TPU v7x, 32 devices: a whole 2x2x4 slice. The times are simulated.
32 devices in a mesh: seg: 4 (over y, x), expert: 8 (over z, core).
Axes of the slice: x: 2, y: 2, z: 4, core: 2. Of those that a mesh axis runs over, the one named last changes fastest.
Arguments:
- frames: bfloat16 [8192, 1536], P(('seg', 'expert')), may hold values from -6 to 6
- expert_ids: int32 [8192, 2], P(('seg', 'expert')), may hold values from 0 to 7, all different within a row; in each aligned block of 256 rows (0 to 255, 256 to 511, ...) at most 96 rows name the same one
- gate_weights: float32 [8192, 2], P(('seg', 'expert')), may hold values from 0.2 to 1
- up_weight: bfloat16 [8, 1536, 2048], P('expert'), may hold values from -0.15625 to 0.15625
- down_weight: bfloat16 [8, 2048, 1536], P('expert'), may hold values from -0.125 to 0.125
- out_weight: bfloat16 [1536, 64], replicated, may hold values from -0.15625 to 0.15625
- in_conv: bfloat16 [7, 64, 2048], replicated, may hold values from -0.25 to 0.25
- snake_first: float32 [2048], replicated, may hold values from 0.5 to 2
- first_up: bfloat16 [16, 2048, 512], P(None, None, 'seg'), may hold values from -0.09375 to 0.09375
Outputs:
- features: float32 [4, 16384, 512], P(None, 'expert', 'seg')
Inputs may be any that keep to these rules, and one draw needn't show every extreme that they name: `expert_ids`: in each aligned block of 256 rows (the rows of one device) no expert is named by more than 96 of the block's choices, and some block reaches 96; the two ids of a token differ.
All inputs are finite; a program needn't handle non-finite values.
Results may differ from a plain program's by a relative error of at most 0.005.
Values may be sent and summed in bfloat16 or wider, within the bound.
No kernel may reach another device: no remote copies, remote signals or barrier semaphores. Data moves between devices by JAX's collectives and lax.ppermute only.
A program may use at most 128 MiB of HBM per device.

v0:
```python
import jax
import jax.numpy as jnp
from jax import lax
from jax.sharding import PartitionSpec as P


def with_halo(value, sides, width):
    for axis, dim in sides:
        size, length = (lax.axis_size(axis), value.shape[dim])
        up = [(i, (i + 1) % size) for i in range(size - 1)]
        down = [(j, i) for i, j in up]
        last = lax.slice_in_dim(value, length - width, length, axis=dim)
        leading = lax.slice_in_dim(value, 0, width, axis=dim)
        before = lax.ppermute(last, axis, up)
        after = lax.ppermute(leading, axis, down)
        value = jnp.concatenate([before, value, after], axis=dim)
    return value


def snake_act(values, alpha_row):
    return values + jnp.sin(alpha_row * values) ** 2 / alpha_row


def slot_dest(expert_ids, num_experts, capacity):
    flat_ids = expert_ids.reshape(-1)
    one_hot = (flat_ids[:, None] == jnp.arange(num_experts, dtype=jnp.int32)[None, :]).astype(
        jnp.int32
    )
    before = jnp.cumsum(one_hot, axis=0) - one_hot
    return flat_ids * capacity + jnp.sum(before * one_hot, axis=1)


def conv_seven(padded, weights, length):
    windows = [
        lax.slice_in_dim(padded, tap_index, tap_index + length, axis=1) for tap_index in range(7)
    ]
    stacked = jnp.concatenate(windows, axis=2)
    return jnp.einsum(
        "klc,co->klo",
        stacked,
        weights.reshape(-1, weights.shape[2]),
        preferred_element_type=jnp.float32,
    )


def upsample(padded, weights, length):
    prev_rows = padded[:, 0:length]
    here_rows = padded[:, 1 : length + 1]
    next_rows = padded[:, 2 : length + 2]
    middle = jnp.einsum(
        "klc,rco->klro", here_rows, weights[4:12], preferred_element_type=jnp.float32
    )
    early_part = jnp.einsum(
        "klc,rco->klro", prev_rows, weights[12:16], preferred_element_type=jnp.float32
    )
    later_part = jnp.einsum(
        "klc,rco->klro", next_rows, weights[0:4], preferred_element_type=jnp.float32
    )
    joined = middle + jnp.concatenate([early_part, later_part], axis=2)
    return joined.reshape(padded.shape[0], length * 8, weights.shape[2])


def local(
    frames,
    expert_ids,
    gate_weights,
    up_weight,
    down_weight,
    out_weight,
    in_conv,
    snake_first,
    first_up,
):
    tok_rows, model_dim = frames.shape
    num_experts = lax.axis_size("expert")
    capacity = 3 * tok_rows // num_experts
    dest_slot = slot_dest(expert_ids, num_experts, capacity)
    source_rows = jnp.repeat(frames, 2, axis=0)
    send_buffer = (
        jnp.zeros((num_experts * capacity, model_dim), jnp.bfloat16).at[dest_slot].set(source_rows)
    )
    send_buffer = send_buffer.reshape(num_experts, capacity, model_dim)
    upper_weight = up_weight[0]
    lower_weight = down_weight[0]
    received = lax.all_to_all(send_buffer, "expert", split_axis=0, concat_axis=0, tiled=True)
    count_src, count_rows, _ = received.shape
    flat_rows = received.reshape(count_src * count_rows, model_dim)
    hidden_units = jax.nn.gelu(
        jnp.dot(flat_rows, upper_weight, preferred_element_type=jnp.float32), approximate=True
    ).astype(jnp.bfloat16)
    expert_out = jnp.dot(hidden_units, lower_weight, preferred_element_type=jnp.float32).astype(
        jnp.bfloat16
    )
    result_rows = jnp.dot(expert_out, out_weight, preferred_element_type=jnp.float32)
    processed = result_rows.reshape(count_src, count_rows, result_rows.shape[1])
    returned = lax.all_to_all(processed, "expert", split_axis=0, concat_axis=0, tiled=True)
    picked = returned.reshape(num_experts * capacity, returned.shape[2])[dest_slot]
    lat_dim = out_weight.shape[1]
    gated = jnp.sum(picked.reshape(tok_rows, 2, lat_dim) * gate_weights[:, :, None], axis=1)
    latent = jnp.dot(frames, out_weight, preferred_element_type=jnp.float32) + gated
    latent_low = latent.astype(jnp.bfloat16)
    lat_padded = with_halo(latent_low, (("expert", 0),), 3)
    first_in = conv_seven(lat_padded[None], in_conv, tok_rows)[0]
    act_first = snake_act(first_in, snake_first).astype(jnp.bfloat16)
    pad_first = with_halo(act_first, (("expert", 0),), 1)
    return upsample(lax.all_gather(pad_first[None], "seg", axis=0, tiled=True), first_up, tok_rows)


def solution(mesh):
    placed = (
        P(("seg", "expert"), None),
        P(("seg", "expert"), None),
        P(("seg", "expert"), None),
        P("expert", None, None),
        P("expert", None, None),
        P(),
        P(),
        P(),
        P(None, None, "seg"),
    )
    return jax.shard_map(
        local, mesh=mesh, in_specs=placed, out_specs=P(None, "expert", "seg"), check_vma=False
    )
```

profile of v0, /device:TPU:0, one launch (start us, length us, event | category | flops | bytes accessed | tf_op | source)
XLA Modules:
  0.0 219.8 jit_solution(14476242708202597146)
XLA Ops:
  8.8 1.1 reduce-window.6
  10.2 2.0 broadcast_in_dim.9
  12.1 1.5 reshape.99
  13.7 5.5 %scatter_custom_fusion = bf16[768,1536]{1,0:T(8,128)(2,1)} fusion(s32[512]{0:T(512)S(1)} %bitcast.81, bf16[512,1536]{1,0:T(8,128)(2,1)} %reshape.99, bf16[]{:T(256)} %constant.9.clone.1), kind=kCustom, calls=%fused_computation.35 | custom fusion | bytes 2359808 | tf_op jit(solution)/shard_map/scatter | solution.py:80
  19.3 61.1 %all_to_all.10 = bf16[8,96,1536]{2,1,0:T(8,128)(2,1)} all-to-all(bf16[8,96,1536]{2,1,0:T(8,128)(2,1)} %bitcast.78), channel_id=1, replica_groups=mesh['seg'=4,'expert'=8] {'expert'}, dimensions={0} | all-to-all | bytes 4718592 | tf_op jit(solution)/shard_map/all_to_all | solution.py:85
  80.4 16.7 %fusion.17 = bf16[768,1536]{1,0:T(8,128)(2,1)} fusion(bf16[1,2048,1536]{2,1,0:T(8,128)(2,1)} %param.13, bf16[768,1536]{1,0:T(8,128)(2,1)} %bitcast.79, bf16[1,1536,2048]{2,1,0:T(8,128)(2,1)} %param.12), kind=kOutput, calls=%fused_computation.25 | convolution fusion | flops 9679011840 | bytes 17301504 | tf_op jit(solution)/shard_map/dot_general | solution.py:91
  97.1 2.5 %fusion.51 = f32[768,64]{0,1:T(8,128)S(1)} fusion(bf16[768,1536]{1,0:T(8,128)(2,1)} %fusion.17, bf16[1536,64]{0,1:T(8,128)(2,1)S(1)} %copy-done.2), kind=kOutput, calls=%fused_computation.67 | convolution fusion | flops 150994944 | bytes 2752512 | tf_op jit(solution)/shard_map/dot_general | solution.py:94
  100.5 3.5 %all-to-all-start.1 = ((f32[8,96,64]{1,2,0:T(8,128)}), f32[8,96,64]{1,2,0:T(8,128)S(1)}, u32[]{:S(2)}, u32[]{:S(2)}) async-start(f32[8,96,64]{1,2,0:T(8,128)} %copy.21), calls=%async_computation.1 | async-start | bytes 524288 | tf_op jit(solution)/shard_map/all_to_all | solution.py:96
  104.9 8.8 %all-to-all-done.1 = f32[8,96,64]{1,2,0:T(8,128)S(1)} async-done(((f32[8,96,64]{1,2,0:T(8,128)}), f32[8,96,64]{1,2,0:T(8,128)S(1)}, u32[]{:S(2)}, u32[]{:S(2)}) %all-to-all-start.1) | async-done | bytes 196640 | tf_op jit(solution)/shard_map/all_to_all | solution.py:96
  113.9 1.0 gather_fusion
  114.9 1.3 multiply_reduce_fusion
  116.8 1.4 collective-permute-start
  118.1 1.3 collective-permute-start.1
  119.5 2.1 collective-permute-done.1
  122.2 8.7 %add_convert_fusion = bf16[256,2048]{1,0:T(8,128)(2,1)S(1)} fusion(f32[2048]{0:T(1024)S(1)} %copy-done.5, bf16[448,2048]{1,0:T(8,128)(2,1)S(1)} %bitcast.76, bf16[1,256,448]{1,2,0:T(8,128)(2,1)S(1)} %slice_dynamic-update-slice_fusion), kind=kOutput, calls=%fused_computation.34 | convolution fusion | flops 472383488 | bytes 3121152 | tf_op jit(solution)/shard_map/klc,co->klo/dot_general | solution.py:38
  130.9 4.4 %collective-permute-start.2 = (bf16[1,2048]{1,0:T(2,128)(2,1)S(1)}, bf16[1,2048]{1,0:T(2,128)(2,1)S(1)}, u32[]{:S(2)}, u32[]{:S(2)}) collective-permute-start(bf16[1,2048]{1,0:T(2,128)(2,1)S(1)} %get-tuple-element.5), channel_id=1, source_target_pairs={{0,1},{1,2},{2,3},{3,4},{4,5},{5,6},{6,7},{8,9},{9,10},{10,11},{11... | collective-permute-start | bytes 12296 | tf_op jit(solution)/shard_map/ppermute | solution.py:14
  135.3 1.5 collective-permute-start.3
  136.8 1.5 collective-permute-done.3
  138.4 1.3 maximum_bitcast_fusion
  139.7 54.8 %all-gather.4.cloned.1.call-done = bf16[4,258,2048]{2,1,0:T(8,128)(2,1)} async-done(((bf16[1,258,2048]{2,1,0:T(8,128)(2,1)}), bf16[4,258,2048]{2,1,0:T(8,128)(2,1)}) %all-gather.4.cloned.1.call-update) | async-done | bytes 4227088 | tf_op jit(solution)/shard_map/all_gather | solution.py:106
  194.5 5.3 %fusion.13 = f32[4,256,4,128]{3,1,2,0:T(8,128)S(1)} fusion(bf16[4,258,2048]{2,1,0:T(8,128)(2,1)} %all-gather.4.cloned.1.call-done, bf16[16,2048,128]{2,1,0:T(8,128)(2,1)} %param.17), kind=kOutput, calls=%fused_computation.18 | convolution fusion | flops 2147483648 | bytes 8388608 | tf_op jit(solution)/shard_map/klc,rco->klro/dot_general | solution.py:53
  199.9 4.1 %fusion.12 = f32[4,256,4,128]{3,1,2,0:T(8,128)S(1)} fusion(bf16[4,258,2048]{2,1,0:T(8,128)(2,1)S(1)} %copy-done.4, bf16[16,2048,128]{2,1,0:T(8,128)(2,1)} %param.17), kind=kOutput, calls=%fused_computation.16 | convolution fusion | flops 2147483648 | bytes 8388608 | tf_op jit(solution)/shard_map/klc,rco->klro/dot_general | solution.py:56
  204.0 4.5 %maximum_add_fusion = f32[4,256,8,128]{3,1,2,0:T(8,128)S(1)} fusion(f32[4,256,4,128]{3,1,2,0:T(8,128)S(1)} %fusion.12, f32[4,256,4,128]{3,1,2,0:T(8,128)S(1)} %fusion.13, bf16[16,2048,128]{2,1,0:T(8,128)(2,1)S(1)} %bitcast.85, bf16[4,258,2048]{2,1,0:T(8,128)(2,1)S(1)} %copy-done.4), kind=kOutput, calls=%fused_computation.21 | convolution fusion | flops 4297064448 | bytes 16777216 | tf_op jit(solution)/shard_map/klc,rco->klro/dot_general | solution.py:50
  208.5 4.4 %copy.30 = f32[4,256,8,128]{3,2,1,0:T(8,128)} copy(f32[4,256,8,128]{3,1,2,0:T(8,128)S(1)} %maximum_add_fusion) | data formatting | bytes 8388608 | tf_op jit(solution)/shard_map/add | solution.py:59
  (50 shorter events, 5.6 us)
Async XLA Ops:
  6.5 115.6 %copy-start = (bf16[7,64,2048]{2,1,0:T(8,128)(2,1)S(1)}, bf16[7,64,2048]{2,1,0:T(8,128)(2,1)}, u32[]{:S(2)}) copy-start(bf16[7,64,2048]{2,1,0:T(8,128)(2,1)} %param.15) | copy-start | bytes 5505028
  80.4 16.7 %copy-start.2 = (bf16[1536,64]{0,1:T(8,128)(2,1)S(1)}, bf16[1536,64]{0,1:T(8,128)(2,1)}, u32[]{:S(2)}) copy-start(bf16[1536,64]{0,1:T(8,128)(2,1)} %param.14) | copy-start | bytes 589828
  97.1 7.0 %copy-start.3 = (f32[256,2]{0,1:T(2,128)S(1)}, f32[256,2]{0,1:T(2,128)}, u32[]{:S(2)}) copy-start(f32[256,2]{0,1:T(2,128)} %param.11) | copy-start | bytes 6148
  99.6 16.8 %copy-start.1 = (bf16[256,1536]{1,0:T(8,128)(2,1)S(1)}, bf16[256,1536]{1,0:T(8,128)(2,1)}, u32[]{:S(2)}) copy-start(bf16[256,1536]{1,0:T(8,128)(2,1)} %param.9) | copy-start | bytes 2359300
  100.5 21.7 %copy-start.5 = (f32[2048]{0:T(1024)S(1)}, f32[2048]{0:T(1024)}, u32[]{:S(2)}) copy-start(f32[2048]{0:T(1024)} %param.16) | copy-start | bytes 24580
  100.5 13.2 %all-to-all-start.1 = ((f32[8,96,64]{1,2,0:T(8,128)}), f32[8,96,64]{1,2,0:T(8,128)S(1)}, u32[]{:S(2)}, u32[]{:S(2)}) async-start(f32[8,96,64]{1,2,0:T(8,128)} %copy.21), calls=%async_computation.1 | async-start | bytes 524288 | tf_op jit(solution)/shard_map/all_to_all | solution.py:96
  104.0 90.5 %all-gather.4.cloned.1.call-start = ((), (), s32[]{:S(2)}) async-start(), calls=%async_computation.2 | async-start | bytes 5406720 | tf_op jit(solution)/shard_map/all_gather | solution.py:106
  116.8 2.7 %collective-permute-start = (bf16[3,64]{0,1:T(8,128)(2,1)S(1)}, bf16[3,64]{0,1:T(8,128)(2,1)S(1)}, u32[]{:S(2)}, u32[]{:S(2)}) collective-permute-start(bf16[3,64]{0,1:T(8,128)(2,1)S(1)} %get-tuple-element.7), channel_id=1, source_target_pairs={{0,1},{1,2},{2,3},{3,4},{4,5},{5,6},{6,7},{8,9},{9,10},{10,11},{11... | collective-permute-start | bytes 1160 | tf_op jit(solution)/shard_map/ppermute | solution.py:14
  118.1 3.4 %collective-permute-start.1 = (bf16[3,64]{0,1:T(8,128)(2,1)S(1)}, bf16[3,64]{0,1:T(8,128)(2,1)S(1)}, u32[]{:S(2)}, u32[]{:S(2)}) collective-permute-start(bf16[3,64]{0,1:T(8,128)(2,1)S(1)} %get-tuple-element.8), channel_id=1, source_target_pairs={{1,0},{2,1},{3,2},{4,3},{5,4},{6,5},{7,6},{9,8},{10,9},{11,10},{12... | collective-permute-start | bytes 1160 | tf_op jit(solution)/shard_map/ppermute | solution.py:15
  130.9 5.9 %collective-permute-start.2 = (bf16[1,2048]{1,0:T(2,128)(2,1)S(1)}, bf16[1,2048]{1,0:T(2,128)(2,1)S(1)}, u32[]{:S(2)}, u32[]{:S(2)}) collective-permute-start(bf16[1,2048]{1,0:T(2,128)(2,1)S(1)} %get-tuple-element.5), channel_id=1, source_target_pairs={{0,1},{1,2},{2,3},{3,4},{4,5},{5,6},{6,7},{8,9},{9,10},{10,11},{11... | collective-permute-start | bytes 12296 | tf_op jit(solution)/shard_map/ppermute | solution.py:14
  135.3 3.1 %collective-permute-start.3 = (bf16[1,2048]{1,0:T(2,128)(2,1)S(1)}, bf16[1,2048]{1,0:T(2,128)(2,1)S(1)}, u32[]{:S(2)}, u32[]{:S(2)}) collective-permute-start(bf16[1,2048]{1,0:T(2,128)(2,1)S(1)} %get-tuple-element.6), channel_id=1, source_target_pairs={{1,0},{2,1},{3,2},{4,3},{5,4},{6,5},{7,6},{9,8},{10,9},{11,10},{12... | collective-permute-start | bytes 12296 | tf_op jit(solution)/shard_map/ppermute | solution.py:15
  194.5 5.3 %copy-start.4 = (bf16[4,258,2048]{2,1,0:T(8,128)(2,1)S(1)}, bf16[4,258,2048]{2,1,0:T(8,128)(2,1)}, u32[]{:S(2)}) copy-start(bf16[4,258,2048]{2,1,0:T(8,128)(2,1)} %all-gather.4.cloned.1.call-done) | copy-start | bytes 12681220
  194.5 9.4 %slice-start = ((s8[8388608]{0:T(1024)(128)(4,1)}), s8[4194304]{0:T(1024)(128)(4,1)S(1)}, s32[]{:S(2)}) async-start(s8[8388608]{0:T(1024)(128)(4,1)} %bitcast.84), calls=%async_computation.3 | async-start | bytes 8388608
  199.9 4.1 %slice-start.1 = ((s8[8388608]{0:T(1024)(128)(4,1)}), s8[4194304]{0:T(1024)(128)(4,1)S(1)}, s32[]{:S(2)}) async-start(s8[8388608]{0:T(1024)(128)(4,1)} %bitcast.84), calls=%async_computation.4 | async-start | bytes 8388608
Sparse Core Ops, SparseCore 0:
  139.8 54.6 all-gather.3
where the time goes:
time: 220 us
  waiting for transfers between devices  67.3 us (31%)
  blocking collectives  61.1 us (28%)
  matrix products  42.2 us (19%)
  local copies, waits for them, and re-layouts  18.6 us (8%)
  between operations  13.7 us (6%)
  starting transfers between devices  12.1 us (6%)
  other arithmetic  4.83 us (2%)
    all_to_all x1, blocking collectives, local(): lax.all_to_all(send_buffer, 'expert', split_axis=0, concat_axis=0, tiled=...  61.1 us
    all_gather x1, waiting for transfers between devices, local(): lax.all_gather(pad_first[None], 'seg', axis=0, tiled=True)  54.8 us
    dot_general x1, matrix products, local(): jnp.dot(hidden_units, lower_weight, preferred_element_type=jnp.float32)  16.7 us
    all_to_all x1, waiting for transfers between devices, local(): lax.all_to_all(processed, 'expert', split_axis=0, concat_axis=0, tiled=True)  8.8 us
    dot_general x1, matrix products, conv_seven(): jnp.einsum('klc,co->klo', stacked, weights.reshape(-1, weights.shape[2]),...  8.72 us
    ppermute x2, starting transfers between devices, with_halo(): before = lax.ppermute(last, axis, up)  5.75 us
    scatter x1, local copies, waits for them, and re-layouts, local(): jnp.zeros((num_experts * capacity, model_dim), jnp.bfloat16).at[dest_slot]  5.52 us
    dot_general x1, matrix products, upsample(): jnp.einsum('klc,rco->klro', prev_rows, weights[12:16], preferred_element_...  5.32 us
  transfers between devices with their start and end apart: 6, of which 4 were waited for; matrix products, arithmetic and copies ran while one was open for 0% of the time, Pallas kernels for 0%

commit v1 on v0

v1 whole, which is shorter than its diff:
```python
import functools
import math

import jax
import jax.numpy as jnp
from jax import lax
from jax.experimental import pallas as pl
from jax.experimental.pallas import tpu as pltpu
from jax.sharding import PartitionSpec as P

F32 = jnp.float32
BF16 = jnp.bfloat16
VMEM = pltpu.VMEM
SIN2 = (
    9.869603157043457,
    -32.469581604003906,
    42.72538375854492,
    -30.085954666137695,
    12.99073314666748,
    -3.2729504108428955,
)
ROUNDER = 12582912.0


def whole():
    return pl.BlockSpec(memory_space=VMEM)


def params(mib):
    return pltpu.CompilerParams(vmem_limit_bytes=mib * 1024 * 1024)


def slots_kernel(me_ref, ids_ref, frames_ref, *out_refs):
    n = len(out_refs)
    rows = frames_ref.shape[0]
    capacity = out_refs[0].shape[0]
    ids = ids_ref[...] ^ me_ref[0]
    step = lax.broadcasted_iota(jnp.int32, (max(n, 16), rows), 0)
    named = (ids[0:1] == step) | (ids[1:2] == step)
    earlier = lax.broadcasted_iota(jnp.int32, (rows, rows), 0) < lax.broadcasted_iota(
        jnp.int32, (rows, rows), 1
    )
    rank = jnp.dot(
        named.astype(F32).astype(BF16), earlier.astype(F32).astype(BF16), preferred_element_type=F32
    )
    rank = jnp.where(named, rank, -1.0)
    slot = lax.broadcasted_iota(jnp.int32, (capacity, rows), 0).astype(F32)
    frames = frames_ref[...]
    for k in range(n):
        pick = (slot == rank[k : k + 1]).astype(F32).astype(BF16)
        out_refs[k][...] = jnp.dot(pick, frames, preferred_element_type=F32).astype(BF16)


def make_slots(me, ids_t, frames, n, capacity):
    rows, width = frames.shape
    return pl.pallas_call(
        slots_kernel,
        out_shape=[jax.ShapeDtypeStruct((capacity, width), BF16)] * n,
        in_specs=[pl.BlockSpec(memory_space=pltpu.SMEM), whole(), whole()],
        out_specs=[whole()] * n,
        compiler_params=params(24),
    )(me, ids_t, frames)


def fold_kernel(down_ref, out_w_ref, folded_ref):
    full = lax.dot_general(
        down_ref[...], out_w_ref[...], (((1,), (1,)), ((), ())), preferred_element_type=F32
    )
    high = full.astype(BF16)
    low = (full - high.astype(F32)).astype(BF16)
    folded_ref[...] = jnp.concatenate([high, low], axis=1)


def fold_weights(down, out_w_t):
    hid, width = down.shape
    lat = out_w_t.shape[0]
    block = 512 if hid % 512 == 0 else hid
    return pl.pallas_call(
        fold_kernel,
        grid=(hid // block,),
        out_shape=jax.ShapeDtypeStruct((hid, 2 * lat), BF16),
        in_specs=[
            pl.BlockSpec((block, width), lambda i: (i, 0)),
            pl.BlockSpec((lat, width), lambda i: (0, 0)),
        ],
        out_specs=pl.BlockSpec((block, 2 * lat), lambda i: (i, 0)),
        compiler_params=params(16),
        cost_estimate=pl.CostEstimate(
            flops=2 * hid * width * 2 * lat, bytes_accessed=2 * hid * width, transcendentals=0
        ),
    )(down, out_w_t)


def table_kernel(me_ref, ids_ref, gates_ref, frames_ref, out_w_ref, pick_ref, scale_ref, base_ref):
    n = pick_ref.shape[0]
    rows = frames_ref.shape[0]
    capacity = pick_ref.shape[2]
    base_ref[...] = lax.dot_general(
        frames_ref[...], out_w_ref[...], (((1,), (1,)), ((), ())), preferred_element_type=F32
    )
    ids = ids_ref[...] ^ me_ref[0]
    step = lax.broadcasted_iota(jnp.int32, (rows, 128), 1)
    first = ids[:, 0:1] == step
    second = ids[:, 1:2] == step
    named = first | second
    earlier = lax.broadcasted_iota(jnp.int32, (rows, rows), 0) > lax.broadcasted_iota(
        jnp.int32, (rows, rows), 1
    )
    rank = jnp.dot(
        earlier.astype(F32).astype(BF16), named.astype(F32).astype(BF16), preferred_element_type=F32
    )
    rank = jnp.where(named, rank, -1.0)
    gates = gates_ref[...]
    scale_ref[...] = jnp.where(first, gates[:, 0:1], jnp.where(second, gates[:, 1:2], 0.0))
    slot = lax.broadcasted_iota(jnp.int32, (rows, capacity), 1).astype(F32)
    for k in range(n):
        pick_ref[k] = (slot == rank[:, k : k + 1]).astype(F32).astype(BF16)


def make_table(me, ids, gates, frames, out_w_t, n, capacity):
    rows, width = frames.shape
    lat = out_w_t.shape[0]
    return pl.pallas_call(
        table_kernel,
        out_shape=[
            jax.ShapeDtypeStruct((n, rows, capacity), BF16),
            jax.ShapeDtypeStruct((rows, 128), F32),
            jax.ShapeDtypeStruct((rows, lat), F32),
        ],
        in_specs=[pl.BlockSpec(memory_space=pltpu.SMEM)] + [whole()] * 4,
        out_specs=[whole()] * 3,
        compiler_params=params(16),
        cost_estimate=pl.CostEstimate(
            flops=2 * rows * width * 128, bytes_accessed=2 * rows * width, transcendentals=0
        ),
    )(me, ids, gates, frames, out_w_t)


def expert_kernel(count, *refs):
    chunk_refs = refs[:count]
    up_ref, folded_ref = refs[count : count + 2]
    out_refs = refs[count + 2 : count + 2 + count]
    total_ref = refs[-1]
    capacity = chunk_refs[0].shape[0]
    hid = up_ref.shape[1]
    block = 256 if hid % 256 == 0 else hid
    rows = jnp.concatenate([ref[...] for ref in chunk_refs], axis=0)
    total_ref[...] = jnp.zeros_like(total_ref)

    @pl.loop(0, hid // block)
    def _(i):
        at = pl.multiple_of(i * block, block)
        v = jnp.dot(rows, up_ref[:, pl.ds(at, block)], preferred_element_type=F32)
        inner = v * (0.7978845608 + (0.7978845608 * 0.044715) * (v * v))
        hidden = (0.5 * v * (1.0 + jnp.tanh(inner))).astype(BF16)
        total_ref[...] += jnp.dot(hidden, folded_ref[pl.ds(at, block), :], preferred_element_type=F32)

    lat = folded_ref.shape[1] // 2
    total = total_ref[...]
    value = total[:, :lat] + total[:, lat:]
    high = value.astype(BF16)
    low = (value - high.astype(F32)).astype(BF16)
    both = jnp.concatenate([high, low], axis=1)
    for j in range(count):
        out_refs[j][...] = both[j * capacity : (j + 1) * capacity]


def run_expert(chunks, up, folded):
    count = len(chunks)
    capacity, width = chunks[0].shape
    hid = up.shape[1]
    return pl.pallas_call(
        functools.partial(expert_kernel, count),
        out_shape=[jax.ShapeDtypeStruct((capacity, folded.shape[1]), BF16)] * count,
        in_specs=[whole()] * (count + 2),
        out_specs=[whole()] * count,
        scratch_shapes=[pltpu.VMEM((count * capacity, folded.shape[1]), F32)],
        compiler_params=params(24),
        cost_estimate=pl.CostEstimate(
            flops=2 * count * capacity * hid * (width + 256),
            bytes_accessed=2 * hid * width,
            transcendentals=count * capacity * hid,
        ),
    )(*chunks, up, folded)


def combine_kernel(n, *refs):
    part_refs = refs[:n]
    pick_ref, scale_ref, base_ref, low_ref = refs[n:]
    lat = base_ref.shape[1]
    latent = base_ref[...]
    for k in range(n):
        picked = jnp.dot(pick_ref[k], part_refs[k][...], preferred_element_type=F32)
        latent = latent + scale_ref[:, k : k + 1] * (picked[:, :lat] + picked[:, lat:])
    low_ref[...] = latent.astype(BF16)


def combine(parts, pick, scale, base):
    n = len(parts)
    return pl.pallas_call(
        functools.partial(combine_kernel, n),
        out_shape=jax.ShapeDtypeStruct(base.shape, BF16),
        in_specs=[whole()] * (n + 3),
        out_specs=whole(),
        compiler_params=params(16),
    )(*parts, pick, scale, base)


def decoder_kernel(segs, place_ref, *refs):
    lat_refs = refs[:segs]
    conv_ref, alpha_ref, up_ref, out_ref = refs[segs : segs + 4]
    padded, prev, here, after, rows_out, sems = refs[segs + 4 :]
    length = here.shape[0]
    channels = conv_ref.shape[1]
    width = up_ref.shape[2]
    lat = lat_refs[0].shape[1]
    taps = conv_ref.shape[0] // lat
    halo = lat_refs[0].shape[0]
    span = length + 16
    block = 256
    own = place_ref[0]
    is_first = place_ref[1] == 0
    is_last = place_ref[1] == place_ref[2] - 1
    frame = lax.broadcasted_iota(jnp.int32, (span, block), 0) - 1
    keep = jnp.logical_not(((frame < 0) & is_first) | ((frame >= length) & is_last))

    def out_copy(k):
        return pltpu.make_async_copy(rows_out.at[k % 2], out_ref.at[own ^ k], sems.at[k % 2])

    for k in range(segs):
        padded[0:halo, :] = lat_refs[k][...].astype(F32)
        padded[halo:, :] = jnp.zeros((padded.shape[0] - halo, lat), F32)
        windows = jnp.concatenate(
            [padded[j : j + span, :] for j in range(taps)], axis=1
        ).astype(BF16)

        @pl.loop(0, channels // block)
        def _(i):
            at = pl.multiple_of(i * block, block)
            v = jnp.dot(windows, conv_ref[:, pl.ds(at, block)], preferred_element_type=F32)
            turns = v * alpha_ref[0:1, pl.ds(at, block)]
            part = turns - ((turns + ROUNDER) - ROUNDER)
            s = part * part
            poly = SIN2[-1]
            for c in SIN2[-2::-1]:
                poly = poly * s + c
            act = v + (poly * s) * alpha_ref[1:2, pl.ds(at, block)]
            act = jnp.where(keep, act, 0.0)
            prev[:, pl.ds(at, block)] = act[0:length].astype(BF16)
            here[:, pl.ds(at, block)] = act[1 : length + 1].astype(BF16)
            after[:, pl.ds(at, block)] = act[2 : length + 2].astype(BF16)

        if k >= 2:
            out_copy(k - 2).wait()
        for r in range(0, 8, 2):
            side, far = (prev, r + 12) if r < 4 else (after, r - 4)
            near_w = jnp.concatenate([up_ref[r + 4], up_ref[r + 5]], axis=1)
            far_w = jnp.concatenate([up_ref[far], up_ref[far + 1]], axis=1)
            res = jnp.dot(here[...], near_w, preferred_element_type=F32) + jnp.dot(
                side[...], far_w, preferred_element_type=F32
            )
            rows_out[k % 2, pl.ds(r, length, stride=8), :] = res[:, :width]
            rows_out[k % 2, pl.ds(r + 1, length, stride=8), :] = res[:, width:]
        out_copy(k).start()
    for k in range(max(0, segs - 2), segs):
        out_copy(k).wait()


def decode(place, slabs, conv, alpha, first_up):
    segs = len(slabs)
    length = slabs[0].shape[0] - 8
    channels = conv.shape[1]
    width = first_up.shape[2]
    lat = slabs[0].shape[1]
    return pl.pallas_call(
        functools.partial(decoder_kernel, segs),
        out_shape=jax.ShapeDtypeStruct((segs, 8 * length, width), F32),
        in_specs=[pl.BlockSpec(memory_space=pltpu.SMEM)] + [whole()] * (segs + 3),
        out_specs=pl.BlockSpec(memory_space=pl.ANY),
        scratch_shapes=[
            pltpu.VMEM((length + 32, lat), F32),
            pltpu.VMEM((length, channels), BF16),
            pltpu.VMEM((length, channels), BF16),
            pltpu.VMEM((length, channels), BF16),
            pltpu.VMEM((2, 8 * length, width), F32),
            pltpu.SemaphoreType.DMA((2,)),
        ],
        compiler_params=params(32),
        cost_estimate=pl.CostEstimate(
            flops=2 * segs * length * channels * (16 * width + 512),
            bytes_accessed=4 * segs * 8 * length * width,
            transcendentals=0,
        ),
    )(place, *slabs, conv, alpha, first_up)


def local(
    frames,
    expert_ids,
    gate_weights,
    up_weight,
    down_weight,
    out_weight,
    in_conv,
    snake_first,
    first_up,
):
    rows, _ = frames.shape
    n = lax.axis_size("expert")
    segs = lax.axis_size("seg")
    capacity = -(-(3 * rows // n) // 16) * 16
    me = lax.axis_index("expert")
    me_array = jnp.full((1,), me, jnp.int32)

    def partner(axis, size, k):
        return [(i, i ^ k) for i in range(size)]

    chunks = make_slots(me_array, expert_ids.T, frames, n, capacity)
    arrived = {0: chunks[0]}
    for k in range(n - 1, 0, -1):
        arrived[k] = lax.ppermute(chunks[k], "expert", partner("expert", n, k))
    out_w_t = out_weight.T
    folded = fold_weights(down_weight[0], out_w_t)
    pick, scale, base = make_table(
        me_array, expert_ids, gate_weights, frames, out_w_t, n, capacity
    )
    parts = {}
    groups = [(0, 1), (2, 3)] + [tuple(range(j, min(j + 4, n))) for j in range(4, n, 4)]
    for group in groups:
        done = run_expert([arrived[k] for k in group], up_weight[0], folded)
        for k, value in zip(group, done):
            parts[k] = value if k == 0 else lax.ppermute(value, "expert", partner("expert", n, k))
    latent_low = combine([parts[k] for k in range(n)], pick, scale, base)

    up_pairs = [(i, i + 1) for i in range(n - 1)]
    down_pairs = [(i + 1, i) for i in range(n - 1)]
    before = lax.ppermute(latent_low[rows - 4 :], "expert", up_pairs)
    later = lax.ppermute(latent_low[:4], "expert", down_pairs)
    slab = jnp.concatenate([before, latent_low, later], axis=0)
    slabs = [slab] + [
        lax.ppermute(slab, "seg", partner("seg", segs, k)) for k in range(1, segs)
    ]
    place = jnp.stack([lax.axis_index("seg"), me, jnp.int32(n)]).astype(jnp.int32)
    alpha = jnp.stack([snake_first * (1.0 / math.pi), 1.0 / snake_first])
    conv = in_conv.reshape(-1, in_conv.shape[2])
    return decode(place, slabs, conv, alpha, first_up)


def solution(mesh):
    placed = (
        P(("seg", "expert"), None),
        P(("seg", "expert"), None),
        P(("seg", "expert"), None),
        P("expert", None, None),
        P("expert", None, None),
        P(),
        P(),
        P(),
        P(None, None, "seg"),
    )
    return jax.shard_map(
        local, mesh=mesh, in_specs=placed, out_specs=P(None, "expert", "seg"), check_vma=False
    )
```

time: 220 us -> 117 us (0.53)
  blocking collectives: 61.1 us -> 0 us
  waiting for transfers between devices: 67.3 us -> 21.3 us
  Pallas kernels: 0 us -> 44 us
  matrix products: 42.2 us -> 0 us
  starting transfers between devices: 12.1 us -> 41.7 us
  between operations: 13.7 us -> 0.41 us
  local copies, waits for them, and re-layouts: 18.6 us -> 9.61 us
  other arithmetic: 4.83 us -> 0.13 us
    all_to_all x1 -> x0, blocking collectives: 61.1 us -> none  [local(): lax.all_to_all(send_buffer, 'expert', split_axis=0, concat_axis=0, tiled=...]
    all_gather x1 -> x0, waiting for transfers between devices: 54.8 us -> none  [local(): lax.all_gather(pad_first[None], 'seg', axis=0, tiled=True)]
    pallas_call x0 -> x8, Pallas kernels: none -> 44 us  [the longest x1 24.2 us: decode(): pl.pallas_call(functools.partial(decoder_kernel, segs), out_shape=jax.Sha...]
    dot_general x7 -> x0, matrix products: 42.2 us -> none  [the longest x1 16.7 us: local(): jnp.dot(hidden_units, lower_weight, preferred_element_type=jnp.float32)]
    ppermute x4 -> x19, starting transfers between devices: 8.56 us -> 41.7 us  [the longest x7 24.6 us: local(): lax.ppermute(value, 'expert', partner('expert', n, k))]
    ppermute x4 -> x19, waiting for transfers between devices: 3.63 us -> 21.3 us  [the longest x7 13.6 us: local(): arrived[k] = lax.ppermute(chunks[k], 'expert', partner('expert', n, k))]
    all_to_all x1 -> x0, waiting for transfers between devices: 8.8 us -> none  [local(): lax.all_to_all(processed, 'expert', split_axis=0, concat_axis=0, tiled=True)]
    unnamed x24 -> x26, local copies, waits for them, and re-layouts: 2.05 us -> 9.6 us
  transfers between devices with their start and end apart: 6 -> 19, of which waited for: 4 -> 6; matrix products, arithmetic and copies ran while one was open for 0% -> 0% of each run, Pallas kernels for 0% -> 15%
where the time goes in v1:
time: 117 us
  Pallas kernels  44 us (38%)
  starting transfers between devices  41.7 us (36%)
  waiting for transfers between devices  21.3 us (18%)
  local copies, waits for them, and re-layouts  9.61 us (8%)
    ppermute x7, starting transfers between devices, local(): lax.ppermute(value, 'expert', partner('expert', n, k))  24.6 us
    pallas_call x1, Pallas kernels, decode(): pl.pallas_call(functools.partial(decoder_kernel, segs), out_shape=jax.Sha...  24.2 us
    pallas_call x3, Pallas kernels, run_expert(): pl.pallas_call(functools.partial(expert_kernel, count), out_shape=[jax.Sh...  14.6 us
    ppermute x7, waiting for transfers between devices, local(): arrived[k] = lax.ppermute(chunks[k], 'expert', partner('expert', n, k))  13.6 us
    ppermute x7, starting transfers between devices, local(): arrived[k] = lax.ppermute(chunks[k], 'expert', partner('expert', n, k))  10.1 us
    unnamed x26, local copies, waits for them, and re-layouts  9.6 us
    ppermute x3, waiting for transfers between devices, local(): lax.ppermute(slab, 'seg', partner('seg', segs, k))  3.87 us
    ppermute x3, starting transfers between devices, local(): lax.ppermute(slab, 'seg', partner('seg', segs, k))  3.55 us
  transfers between devices with their start and end apart: 19, of which 6 were waited for; matrix products, arithmetic and copies ran while one was open for 0% of the time, Pallas kernels for 15%

profile of v1, /device:TPU:0, one launch (start us, length us, event | category | flops | bytes accessed | tf_op | source)
XLA Modules:
  0.0 117.1 jit_solution(17284235412063226737)
XLA Ops:
  0.0 1.3 %copy-done.2 = bf16[256,1536]{1,0:T(8,128)(2,1)S(1)} copy-done((bf16[256,1536]{1,0:T(8,128)(2,1)S(1)}, bf16[256,1536]{1,0:T(8,128)(2,1)}, u32[]{:S(2)}) %copy-start.2) | copy-done | bytes 786456
  2.2 1.3 %shard_map.91 = (bf16[96,1536]{1,0:T(8,128)(2,1)S(1)}, bf16[96,1536]{1,0:T(8,128)(2,1)S(1)}, bf16[96,1536]{1,0:T(8,128)(2,1)S(1)}, bf16[96,1536]{1,0:T(8,128)(2,...) custom-call(s32[1]{0:T(128)} %bitcast.1.me_ref, ...), custom_call_target="tpu_custom_call" | custom-call | tf_op jit(solution)/shard_map/pallas_call | solution.py:56
  4.0 2.6 %collective-permute-start.2 = (bf16[96,1536]{1,0:T(8,128)(2,1)S(1)}, bf16[96,1536]{1,0:T(8,128)(2,1)S(1)}, u32[]{:S(2)}, u32[]{:S(2)}) collective-permute-start(bf16[96,1536]{1,0:T(8,128)(2,1)S(1)} %get-tuple-element.28), channel_id=1, source_target_pairs={{0,2},{1,3},{2,0},{3,1},{4,6},{5,7},{6,4},{7,5},{8,10},{9,11},{10,... | collective-permute-start | bytes 884744 | tf_op jit(solution)/shard_map/ppermute | solution.py:321
  6.7 2.8 %collective-permute-start.6 = (bf16[96,1536]{1,0:T(8,128)(2,1)S(1)}, bf16[96,1536]{1,0:T(8,128)(2,1)S(1)}, u32[]{:S(2)}, u32[]{:S(2)}) collective-permute-start(bf16[96,1536]{1,0:T(8,128)(2,1)S(1)} %get-tuple-element.32), channel_id=1, source_target_pairs={{0,4},{1,5},{2,6},{3,7},{4,0},{5,1},{6,2},{7,3},{8,12},{9,13},{10,... | collective-permute-start | bytes 884744 | tf_op jit(solution)/shard_map/ppermute | solution.py:321
  9.5 3.6 %collective-permute-start.8 = (bf16[96,1536]{1,0:T(8,128)(2,1)S(1)}, bf16[96,1536]{1,0:T(8,128)(2,1)S(1)}, u32[]{:S(2)}, u32[]{:S(2)}) collective-permute-start(bf16[96,1536]{1,0:T(8,128)(2,1)S(1)} %get-tuple-element.34), channel_id=1, source_target_pairs={{0,6},{1,7},{2,4},{3,5},{4,2},{5,3},{6,0},{7,1},{8,14},{9,15},{10,... | collective-permute-start | bytes 884744 | tf_op jit(solution)/shard_map/ppermute | solution.py:321
  13.1 13.6 %collective-permute-done.2.refs_0_ = bf16[96,1536]{1,0:T(8,128)(2,1)S(1)} collective-permute-done((bf16[96,1536]{1,0:T(8,128)(2,1)S(1)}, bf16[96,1536]{1,0:T(8,128)(2,1)S(1)}, u32[]{:S(2)}, u32[]{:S(2)}) %collective-permute-start.2) | collective-permute-done | bytes 294944 | tf_op jit(solution)/shard_map/ppermute | solution.py:321
  27.2 2.8 %copy-done.1 = bf16[1,2048,1536]{2,1,0:T(8,128)(2,1)S(1)} copy-done((bf16[1,2048,1536]{2,1,0:T(8,128)(2,1)S(1)}, bf16[1,2048,1536]{2,1,0:T(8,128)(2,1)}, u32[]{:S(2)}) %copy-start.1) | copy-done | bytes 6291480
  30.9 2.5 %shard_map.92.refs_3_.refs_5_ = bf16[2048,128]{1,0:T(8,128)(2,1)S(1)} custom-call(bf16[2048,1536]{1,0:T(8,128)(2,1)S(1)} %bitcast.12, bf16[64,1536]{1,0:T(8,128)(2,1)S(1)} %bitcast.13), custom_call_target="tpu_custom_call" | custom-call | flops 805306368 | bytes 6291456 | tf_op jit(solution)/shard_map/pallas_call | solution.py:78
  33.4 4.4 %shard_map.93 = (bf16[96,128]{1,0:T(8,128)(2,1)S(1)}, bf16[96,128]{1,0:T(8,128)(2,1)S(1)}) custom-call(bf16[96,1536]{1,0:T(8,128)(2,1)S(1)} %get-tuple-element.24.refs_0_, bf16[96,1536]{1,0:T(8,128)(2,1)S(1)} %collective-permute-done.refs_1_, bf16[1536,2048]{1,0:T(8,128)(2,1)S(1)} %bitcast.9, bf16[2048,128]{1,0:T(8,128)(2,1)S(1)} %shard_map.92.refs_3_.refs_5_), custom_call_target="tpu_custom_call" | custom-call | flops 1409286144 | bytes 6291456 | tf_op jit(solution)/shard_map/pallas_call | solution.py:172
  37.8 1.4 %collective-permute-start.1 = (bf16[96,128]{1,0:T(8,128)(2,1)S(1)}, bf16[96,128]{1,0:T(8,128)(2,1)S(1)}, u32[]{:S(2)}, u32[]{:S(2)}) collective-permute-start(bf16[96,128]{1,0:T(8,128)(2,1)S(1)} %get-tuple-element.27), channel_id=1, source_target_pairs={{0,1},{1,0},{2,3},{3,2},{4,5},{5,4},{6,7},{7,6},{8,9},{9,8},{10,11... | collective-permute-start | bytes 73736 | tf_op jit(solution)/shard_map/ppermute | solution.py:332
  39.2 4.4 %shard_map.94 = (bf16[96,128]{1,0:T(8,128)(2,1)S(1)}, bf16[96,128]{1,0:T(8,128)(2,1)S(1)}) custom-call(bf16[96,1536]{1,0:T(8,128)(2,1)S(1)} %collective-permute-done.2.refs_0_, bf16[96,1536]{1,0:T(8,128)(2,1)S(1)} %collective-permute-done.3.refs_1_, bf16[1536,2048]{1,0:T(8,128)(2,1)S(1)} %bitcast.10, bf16[2048,128]{1,0:T(8,128)(2,1)S(1)} %shard_map.92.refs_3_.refs_5_), custom_call_target="tpu_custom_call" | custom-call | flops 1409286144 | bytes 6291456 | tf_op jit(solution)/shard_map/pallas_call | solution.py:172
  43.7 4.9 %collective-permute-start.5 = (bf16[96,128]{1,0:T(8,128)(2,1)S(1)}, bf16[96,128]{1,0:T(8,128)(2,1)S(1)}, u32[]{:S(2)}, u32[]{:S(2)}) collective-permute-start(bf16[96,128]{1,0:T(8,128)(2,1)S(1)} %get-tuple-element.31), channel_id=1, source_target_pairs={{0,3},{1,2},{2,1},{3,0},{4,7},{5,6},{6,5},{7,4},{8,11},{9,10},{10,... | collective-permute-start | bytes 73736 | tf_op jit(solution)/shard_map/ppermute | solution.py:332
  48.7 5.8 %shard_map.95 = (bf16[96,128]{1,0:T(8,128)(2,1)S(1)}, bf16[96,128]{1,0:T(8,128)(2,1)S(1)}, bf16[96,128]{1,0:T(8,128)(2,1)S(1)}, bf16[96,128]{1,0:T(8,128)(2,1)S(1)}) custom-call(bf16[96,1536]{1,0:T(8,128)(2,1)S(1)} %collective-permute-done.6.refs_0_, bf16[96,1536]{1,0:T(8,128)(2,1)S(1)} %collective-permute-done.7.refs_1_, ...), custom_call_target="tpu_custom_call" | custom-call | flops 2818572288 | bytes 6291456 | tf_op jit(solution)/shard_map/pallas_call | solution.py:172
  54.5 14.9 %collective-permute-start.10 = (bf16[96,128]{1,0:T(8,128)(2,1)S(1)}, bf16[96,128]{1,0:T(8,128)(2,1)S(1)}, u32[]{:S(2)}, u32[]{:S(2)}) collective-permute-start(bf16[96,128]{1,0:T(8,128)(2,1)S(1)} %get-tuple-element.36), channel_id=1, source_target_pairs={{0,4},{1,5},{2,6},{3,7},{4,0},{5,1},{6,2},{7,3},{8,12},{9,13},{10,... | collective-permute-start | bytes 73736 | tf_op jit(solution)/shard_map/ppermute | solution.py:332
  70.4 2.3 %collective-permute-start.13 = (bf16[96,128]{1,0:T(8,128)(2,1)S(1)}, bf16[96,128]{1,0:T(8,128)(2,1)S(1)}, u32[]{:S(2)}, u32[]{:S(2)}) collective-permute-start(bf16[96,128]{1,0:T(8,128)(2,1)S(1)} %get-tuple-element.39), channel_id=1, source_target_pairs={{0,7},{1,6},{2,5},{3,4},{4,3},{5,2},{6,1},{7,0},{8,15},{9,14},{10,... | collective-permute-start | bytes 73736 | tf_op jit(solution)/shard_map/ppermute | solution.py:332
  73.8 1.2 %collective-permute-done.12.refs_6_ = bf16[96,128]{1,0:T(8,128)(2,1)S(1)} collective-permute-done((bf16[96,128]{1,0:T(8,128)(2,1)S(1)}, bf16[96,128]{1,0:T(8,128)(2,1)S(1)}, u32[]{:S(2)}, u32[]{:S(2)}) %collective-permute-start.12) | collective-permute-done | bytes 24608 | tf_op jit(solution)/shard_map/ppermute | solution.py:332
  76.4 2.0 %collective-permute-start.14 = (bf16[4,64]{1,0:T(4,128)(2,1)S(1)}, bf16[4,64]{1,0:T(4,128)(2,1)S(1)}, u32[]{:S(2)}, u32[]{:S(2)}) collective-permute-start(bf16[4,64]{1,0:T(4,128)(2,1)S(1)} %get-tuple-element.43), channel_id=1, source_target_pairs={{0,1},{1,2},{2,3},{3,4},{4,5},{5,6},{6,7},{8,9},{9,10},{10,11},{11... | collective-permute-start | bytes 1544 | tf_op jit(solution)/shard_map/ppermute | solution.py:337
  78.4 1.5 %collective-permute-start.15 = (bf16[4,64]{1,0:T(4,128)(2,1)S(1)}, bf16[4,64]{1,0:T(4,128)(2,1)S(1)}, u32[]{:S(2)}, u32[]{:S(2)}) collective-permute-start(bf16[4,64]{1,0:T(4,128)(2,1)S(1)} %get-tuple-element.44), channel_id=1, source_target_pairs={{1,0},{2,1},{3,2},{4,3},{5,4},{6,5},{7,6},{9,8},{10,9},{11,10},{12... | collective-permute-start | bytes 1544 | tf_op jit(solution)/shard_map/ppermute | solution.py:338
  79.9 1.9 %collective-permute-done.15 = bf16[4,64]{1,0:T(4,128)(2,1)S(1)} collective-permute-done((bf16[4,64]{1,0:T(4,128)(2,1)S(1)}, bf16[4,64]{1,0:T(4,128)(2,1)S(1)}, u32[]{:S(2)}, u32[]{:S(2)}) %collective-permute-start.15) | collective-permute-done | bytes 544 | tf_op jit(solution)/shard_map/ppermute | solution.py:338
  81.9 2.5 %collective-permute-start.18 = (bf16[264,64]{1,0:T(8,128)(2,1)S(1)}, bf16[264,64]{1,0:T(8,128)(2,1)S(1)}, u32[]{:S(2)}, u32[]{:S(2)}) collective-permute-start(bf16[264,64]{1,0:T(8,128)(2,1)S(1)} %pad_maximum_fusion.refs_0_), channel_id=1, source_target_pairs={{0,24},{8,16},{16,8},{24,0},{1,25},{9,17},{17,9},{25,1},{2,26},{10... | collective-permute-start | bytes 101384 | tf_op jit(solution)/shard_map/ppermute | solution.py:341
  85.5 1.6 %collective-permute-done.18.refs_3_ = bf16[264,64]{1,0:T(8,128)(2,1)S(1)} collective-permute-done((bf16[264,64]{1,0:T(8,128)(2,1)S(1)}, bf16[264,64]{1,0:T(8,128)(2,1)S(1)}, u32[]{:S(2)}, u32[]{:S(2)}) %collective-permute-start.18) | collective-permute-done | bytes 33824 | tf_op jit(solution)/shard_map/ppermute | solution.py:341
  87.1 2.2 %collective-permute-done.17.refs_2_ = bf16[264,64]{1,0:T(8,128)(2,1)S(1)} collective-permute-done((bf16[264,64]{1,0:T(8,128)(2,1)S(1)}, bf16[264,64]{1,0:T(8,128)(2,1)S(1)}, u32[]{:S(2)}, u32[]{:S(2)}) %collective-permute-start.17) | collective-permute-done | bytes 33824 | tf_op jit(solution)/shard_map/ppermute | solution.py:341
  89.4 3.4 %copy-done.8 = bf16[16,2048,128]{2,1,0:T(8,128)(2,1)S(1)} copy-done((bf16[16,2048,128]{2,1,0:T(8,128)(2,1)S(1)}, bf16[16,2048,128]{2,1,0:T(8,128)(2,1)}, u32[]{:S(2)}) %copy-start.8) | copy-done | bytes 8388632
  92.8 24.2 %shard_map.98 = f32[4,2048,128]{2,1,0:T(8,128)} custom-call(s32[3]{0:T(128)S(1)} %pad_add_fusion.place_ref, bf16[264,64]{1,0:T(8,128)(2,1)S(1)} %pad_maximum_fusion.refs_0_, bf16[264,64]{1,0:T(8,128)(2,1)S(1)} %collective-permute-done.16.refs_1_, bf16[264,64]{1,0:T(8,128)(2,1)S(1)} %collective-permute-done.17.refs_2_, ...), custom_call_target="tpu_custom_call" | custom-call | flops 10737418240 | bytes 4194304 | tf_op jit(solution)/shard_map/pallas_call | solution.py:275
  (53 shorter events, 7.5 us)
Async XLA Ops:
  0.0 33.4 %copy-start = (bf16[1,1536,2048]{2,1,0:T(8,128)(2,1)S(1)}, bf16[1,1536,2048]{2,1,0:T(8,128)(2,1)}, u32[]{:S(2)}) copy-start(bf16[1,1536,2048]{2,1,0:T(8,128)(2,1)} %param.12) | copy-start | bytes 18874372
  3.5 6.0 %collective-permute-start = (bf16[96,1536]{1,0:T(8,128)(2,1)S(1)}, bf16[96,1536]{1,0:T(8,128)(2,1)S(1)}, u32[]{:S(2)}, u32[]{:S(2)}) collective-permute-start(bf16[96,1536]{1,0:T(8,128)(2,1)S(1)} %get-tuple-element.25), channel_id=1, source_target_pairs={{0,1},{1,0},{2,3},{3,2},{4,5},{5,4},{6,7},{7,6},{8,9},{9,8},{10,11... | collective-permute-start | bytes 884744 | tf_op jit(solution)/shard_map/ppermute | solution.py:321
  4.0 22.7 %collective-permute-start.2 = (bf16[96,1536]{1,0:T(8,128)(2,1)S(1)}, bf16[96,1536]{1,0:T(8,128)(2,1)S(1)}, u32[]{:S(2)}, u32[]{:S(2)}) collective-permute-start(bf16[96,1536]{1,0:T(8,128)(2,1)S(1)} %get-tuple-element.28), channel_id=1, source_target_pairs={{0,2},{1,3},{2,0},{3,1},{4,6},{5,7},{6,4},{7,5},{8,10},{9,11},{10,... | collective-permute-start | bytes 884744 | tf_op jit(solution)/shard_map/ppermute | solution.py:321
  6.6 31.1 %collective-permute-start.3 = (bf16[96,1536]{1,0:T(8,128)(2,1)S(1)}, bf16[96,1536]{1,0:T(8,128)(2,1)S(1)}, u32[]{:S(2)}, u32[]{:S(2)}) collective-permute-start(bf16[96,1536]{1,0:T(8,128)(2,1)S(1)} %get-tuple-element.29), channel_id=1, source_target_pairs={{0,3},{1,2},{2,1},{3,0},{4,7},{5,6},{6,5},{7,4},{8,11},{9,10},{10,... | collective-permute-start | bytes 884744 | tf_op jit(solution)/shard_map/ppermute | solution.py:321
  6.7 36.9 %collective-permute-start.6 = (bf16[96,1536]{1,0:T(8,128)(2,1)S(1)}, bf16[96,1536]{1,0:T(8,128)(2,1)S(1)}, u32[]{:S(2)}, u32[]{:S(2)}) collective-permute-start(bf16[96,1536]{1,0:T(8,128)(2,1)S(1)} %get-tuple-element.32), channel_id=1, source_target_pairs={{0,4},{1,5},{2,6},{3,7},{4,0},{5,1},{6,2},{7,3},{8,12},{9,13},{10,... | collective-permute-start | bytes 884744 | tf_op jit(solution)/shard_map/ppermute | solution.py:321
  9.5 34.2 %collective-permute-start.7 = (bf16[96,1536]{1,0:T(8,128)(2,1)S(1)}, bf16[96,1536]{1,0:T(8,128)(2,1)S(1)}, u32[]{:S(2)}, u32[]{:S(2)}) collective-permute-start(bf16[96,1536]{1,0:T(8,128)(2,1)S(1)} %get-tuple-element.33), channel_id=1, source_target_pairs={{0,5},{1,4},{2,7},{3,6},{4,1},{5,0},{6,3},{7,2},{8,13},{9,12},{10,... | collective-permute-start | bytes 884744 | tf_op jit(solution)/shard_map/ppermute | solution.py:321
  9.5 39.2 %collective-permute-start.8 = (bf16[96,1536]{1,0:T(8,128)(2,1)S(1)}, bf16[96,1536]{1,0:T(8,128)(2,1)S(1)}, u32[]{:S(2)}, u32[]{:S(2)}) collective-permute-start(bf16[96,1536]{1,0:T(8,128)(2,1)S(1)} %get-tuple-element.34), channel_id=1, source_target_pairs={{0,6},{1,7},{2,4},{3,5},{4,2},{5,3},{6,0},{7,1},{8,14},{9,15},{10,... | collective-permute-start | bytes 884744 | tf_op jit(solution)/shard_map/ppermute | solution.py:321
  26.7 22.0 %collective-permute-start.9 = (bf16[96,1536]{1,0:T(8,128)(2,1)S(1)}, bf16[96,1536]{1,0:T(8,128)(2,1)S(1)}, u32[]{:S(2)}, u32[]{:S(2)}) collective-permute-start(bf16[96,1536]{1,0:T(8,128)(2,1)S(1)} %get-tuple-element.35), channel_id=1, source_target_pairs={{0,7},{1,6},{2,5},{3,4},{4,3},{5,2},{6,1},{7,0},{8,15},{9,14},{10,... | collective-permute-start | bytes 884744 | tf_op jit(solution)/shard_map/ppermute | solution.py:321
  37.8 31.6 %collective-permute-start.1 = (bf16[96,128]{1,0:T(8,128)(2,1)S(1)}, bf16[96,128]{1,0:T(8,128)(2,1)S(1)}, u32[]{:S(2)}, u32[]{:S(2)}) collective-permute-start(bf16[96,128]{1,0:T(8,128)(2,1)S(1)} %get-tuple-element.27), channel_id=1, source_target_pairs={{0,1},{1,0},{2,3},{3,2},{4,5},{5,4},{6,7},{7,6},{8,9},{9,8},{10,11... | collective-permute-start | bytes 73736 | tf_op jit(solution)/shard_map/ppermute | solution.py:332
  43.6 29.3 %copy-start.11 = (f32[256,2]{0,1:T(2,128)S(1)}, f32[256,2]{0,1:T(2,128)}, u32[]{:S(2)}) copy-start(f32[256,2]{0,1:T(2,128)} %param.11) | copy-start | bytes 6148
  43.6 29.5 %copy-start.3 = (bf16[256,1536]{1,0:T(8,128)(2,1)S(1)}, bf16[256,1536]{1,0:T(8,128)(2,1)}, u32[]{:S(2)}) copy-start(bf16[256,1536]{1,0:T(8,128)(2,1)} %frames_ref.3) | copy-start | bytes 2359300
  43.6 29.5 %copy-start.5 = (bf16[1536,64]{0,1:T(8,128)(2,1)S(1)}, bf16[1536,64]{0,1:T(8,128)(2,1)}, u32[]{:S(2)}) copy-start(bf16[1536,64]{0,1:T(8,128)(2,1)} %param.14) | copy-start | bytes 589828
  43.6 26.8 %collective-permute-start.4 = (bf16[96,128]{1,0:T(8,128)(2,1)S(1)}, bf16[96,128]{1,0:T(8,128)(2,1)S(1)}, u32[]{:S(2)}, u32[]{:S(2)}) collective-permute-start(bf16[96,128]{1,0:T(8,128)(2,1)S(1)} %get-tuple-element.30), channel_id=1, source_target_pairs={{0,2},{1,3},{2,0},{3,1},{4,6},{5,7},{6,4},{7,5},{8,10},{9,11},{10,... | collective-permute-start | bytes 73736 | tf_op jit(solution)/shard_map/ppermute | solution.py:332
  43.7 45.7 %copy-start.9 = (bf16[7,64,2048]{2,1,0:T(8,128)(2,1)S(1)}, bf16[7,64,2048]{2,1,0:T(8,128)(2,1)}, u32[]{:S(2)}) copy-start(bf16[7,64,2048]{2,1,0:T(8,128)(2,1)} %param.15) | copy-start | bytes 5505028
  43.7 30.1 %collective-permute-start.5 = (bf16[96,128]{1,0:T(8,128)(2,1)S(1)}, bf16[96,128]{1,0:T(8,128)(2,1)S(1)}, u32[]{:S(2)}, u32[]{:S(2)}) collective-permute-start(bf16[96,128]{1,0:T(8,128)(2,1)S(1)} %get-tuple-element.31), channel_id=1, source_target_pairs={{0,3},{1,2},{2,1},{3,0},{4,7},{5,6},{6,5},{7,4},{8,11},{9,10},{10,... | collective-permute-start | bytes 73736 | tf_op jit(solution)/shard_map/ppermute | solution.py:332
  54.5 19.3 %collective-permute-start.10 = (bf16[96,128]{1,0:T(8,128)(2,1)S(1)}, bf16[96,128]{1,0:T(8,128)(2,1)S(1)}, u32[]{:S(2)}, u32[]{:S(2)}) collective-permute-start(bf16[96,128]{1,0:T(8,128)(2,1)S(1)} %get-tuple-element.36), channel_id=1, source_target_pairs={{0,4},{1,5},{2,6},{3,7},{4,0},{5,1},{6,2},{7,3},{8,12},{9,13},{10,... | collective-permute-start | bytes 73736 | tf_op jit(solution)/shard_map/ppermute | solution.py:332
  69.4 4.4 %collective-permute-start.11 = (bf16[96,128]{1,0:T(8,128)(2,1)S(1)}, bf16[96,128]{1,0:T(8,128)(2,1)S(1)}, u32[]{:S(2)}, u32[]{:S(2)}) collective-permute-start(bf16[96,128]{1,0:T(8,128)(2,1)S(1)} %get-tuple-element.37), channel_id=1, source_target_pairs={{0,5},{1,4},{2,7},{3,6},{4,1},{5,0},{6,3},{7,2},{8,13},{9,12},{10,... | collective-permute-start | bytes 73736 | tf_op jit(solution)/shard_map/ppermute | solution.py:332
  69.4 5.6 %collective-permute-start.12 = (bf16[96,128]{1,0:T(8,128)(2,1)S(1)}, bf16[96,128]{1,0:T(8,128)(2,1)S(1)}, u32[]{:S(2)}, u32[]{:S(2)}) collective-permute-start(bf16[96,128]{1,0:T(8,128)(2,1)S(1)} %get-tuple-element.38), channel_id=1, source_target_pairs={{0,6},{1,7},{2,4},{3,5},{4,2},{5,3},{6,0},{7,1},{8,14},{9,15},{10,... | collective-permute-start | bytes 73736 | tf_op jit(solution)/shard_map/ppermute | solution.py:332
  70.4 5.3 %collective-permute-start.13 = (bf16[96,128]{1,0:T(8,128)(2,1)S(1)}, bf16[96,128]{1,0:T(8,128)(2,1)S(1)}, u32[]{:S(2)}, u32[]{:S(2)}) collective-permute-start(bf16[96,128]{1,0:T(8,128)(2,1)S(1)} %get-tuple-element.39), channel_id=1, source_target_pairs={{0,7},{1,6},{2,5},{3,4},{4,3},{5,2},{6,1},{7,0},{8,15},{9,14},{10,... | collective-permute-start | bytes 73736 | tf_op jit(solution)/shard_map/ppermute | solution.py:332
  76.4 3.5 %collective-permute-start.14 = (bf16[4,64]{1,0:T(4,128)(2,1)S(1)}, bf16[4,64]{1,0:T(4,128)(2,1)S(1)}, u32[]{:S(2)}, u32[]{:S(2)}) collective-permute-start(bf16[4,64]{1,0:T(4,128)(2,1)S(1)} %get-tuple-element.43), channel_id=1, source_target_pairs={{0,1},{1,2},{2,3},{3,4},{4,5},{5,6},{6,7},{8,9},{9,10},{10,11},{11... | collective-permute-start | bytes 1544 | tf_op jit(solution)/shard_map/ppermute | solution.py:337
  78.4 3.5 %collective-permute-start.15 = (bf16[4,64]{1,0:T(4,128)(2,1)S(1)}, bf16[4,64]{1,0:T(4,128)(2,1)S(1)}, u32[]{:S(2)}, u32[]{:S(2)}) collective-permute-start(bf16[4,64]{1,0:T(4,128)(2,1)S(1)} %get-tuple-element.44), channel_id=1, source_target_pairs={{1,0},{2,1},{3,2},{4,3},{5,4},{6,5},{7,6},{9,8},{10,9},{11,10},{12... | collective-permute-start | bytes 1544 | tf_op jit(solution)/shard_map/ppermute | solution.py:338
  81.9 5.3 %collective-permute-start.18 = (bf16[264,64]{1,0:T(8,128)(2,1)S(1)}, bf16[264,64]{1,0:T(8,128)(2,1)S(1)}, u32[]{:S(2)}, u32[]{:S(2)}) collective-permute-start(bf16[264,64]{1,0:T(8,128)(2,1)S(1)} %pad_maximum_fusion.refs_0_), channel_id=1, source_target_pairs={{0,24},{8,16},{16,8},{24,0},{1,25},{9,17},{17,9},{25,1},{2,26},{10... | collective-permute-start | bytes 101384 | tf_op jit(solution)/shard_map/ppermute | solution.py:341
  84.4 5.0 %collective-permute-start.17 = (bf16[264,64]{1,0:T(8,128)(2,1)S(1)}, bf16[264,64]{1,0:T(8,128)(2,1)S(1)}, u32[]{:S(2)}, u32[]{:S(2)}) collective-permute-start(bf16[264,64]{1,0:T(8,128)(2,1)S(1)} %pad_maximum_fusion.refs_0_), channel_id=1, source_target_pairs={{0,16},{8,24},{16,0},{24,8},{1,17},{9,25},{17,1},{25,9},{2,18},{10... | collective-permute-start | bytes 101384 | tf_op jit(solution)/shard_map/ppermute | solution.py:341
  84.9 4.5 %collective-permute-start.16 = (bf16[264,64]{1,0:T(8,128)(2,1)S(1)}, bf16[264,64]{1,0:T(8,128)(2,1)S(1)}, u32[]{:S(2)}, u32[]{:S(2)}) collective-permute-start(bf16[264,64]{1,0:T(8,128)(2,1)S(1)} %pad_maximum_fusion.refs_0_), channel_id=1, source_target_pairs={{0,8},{8,0},{16,24},{24,16},{1,9},{9,1},{17,25},{25,17},{2,10},{10... | collective-permute-start | bytes 101384 | tf_op jit(solution)/shard_map/ppermute | solution.py:341
  (7 other events, 67.7 us)

commit v2 on v1

--- a/solution.py
+++ b/solution.py
@@ -206,63 +206,70 @@
     )(*parts, pick, scale, base)
 
 
+def snake(v, turns_row, inverse_row):
+    turns = v * turns_row
+    part = turns - ((turns + ROUNDER) - ROUNDER)
+    s = part * part
+    poly = SIN2[-1]
+    for c in SIN2[-2::-1]:
+        poly = poly * s + c
+    return v + (poly * s) * inverse_row
+
+
 def decoder_kernel(segs, place_ref, *refs):
     lat_refs = refs[:segs]
-    conv_ref, alpha_ref, up_ref, out_ref = refs[segs : segs + 4]
-    padded, prev, here, after, rows_out, sems = refs[segs + 4 :]
-    length = here.shape[0]
-    channels = conv_ref.shape[1]
+    conv_ref, alpha_ref, up_hbm, out_ref = refs[segs : segs + 4]
+    padded, windows, act, up_ref, rows_out, sems, up_sem = refs[segs + 4 :]
+    span, channels = act.shape[1:]
+    length = span - 16
     width = up_ref.shape[2]
-    lat = lat_refs[0].shape[1]
+    halo, lat = lat_refs[0].shape
     taps = conv_ref.shape[0] // lat
-    halo = lat_refs[0].shape[0]
-    span = length + 16
     block = 256
     own = place_ref[0]
     is_first = place_ref[1] == 0
     is_last = place_ref[1] == place_ref[2] - 1
-    frame = lax.broadcasted_iota(jnp.int32, (span, block), 0) - 1
-    keep = jnp.logical_not(((frame < 0) & is_first) | ((frame >= length) & is_last))
+    up_copy = pltpu.make_async_copy(up_hbm, up_ref, up_sem)
+    up_copy.start()
 
     def out_copy(k):
-        return pltpu.make_async_copy(rows_out.at[k % 2], out_ref.at[own ^ k], sems.at[k % 2])
-
+        return pltpu.make_async_copy(rows_out.at[k], out_ref.at[own ^ k], sems.at[k])
+
+    row = lax.broadcasted_iota(jnp.int32, (16, taps * lat), 0)
+    edge_row = lax.broadcasted_iota(jnp.int32, (16, block), 0)
+    gone = ((edge_row == 0) & is_first) | ((edge_row == 1) & is_last)
     for k in range(segs):
         padded[0:halo, :] = lat_refs[k][...].astype(F32)
-        padded[halo:, :] = jnp.zeros((padded.shape[0] - halo, lat), F32)
-        windows = jnp.concatenate(
-            [padded[j : j + span, :] for j in range(taps)], axis=1
-        ).astype(BF16)
-
-        @pl.loop(0, channels // block)
-        def _(i):
-            at = pl.multiple_of(i * block, block)
-            v = jnp.dot(windows, conv_ref[:, pl.ds(at, block)], preferred_element_type=F32)
-            turns = v * alpha_ref[0:1, pl.ds(at, block)]
-            part = turns - ((turns + ROUNDER) - ROUNDER)
-            s = part * part
-            poly = SIN2[-1]
-            for c in SIN2[-2::-1]:
-                poly = poly * s + c
-            act = v + (poly * s) * alpha_ref[1:2, pl.ds(at, block)]
-            act = jnp.where(keep, act, 0.0)
-            prev[:, pl.ds(at, block)] = act[0:length].astype(BF16)
-            here[:, pl.ds(at, block)] = act[1 : length + 1].astype(BF16)
-            after[:, pl.ds(at, block)] = act[2 : length + 2].astype(BF16)
-
-        if k >= 2:
-            out_copy(k - 2).wait()
+
+        def window(start, rows):
+            return jnp.concatenate([padded[start + j : start + j + rows] for j in range(taps)], axis=1)
+
+        windows[k, 0:length] = window(1, length).astype(BF16)
+        edges = jnp.where(row == 0, window(0, 1), jnp.where(row == 1, window(length + 1, 1), 0.0))
+        windows[k, length:] = edges.astype(BF16)
+        for at in range(0, channels, block):
+            cols = slice(at, at + block)
+            v = jnp.dot(windows[k], conv_ref[:, cols], preferred_element_type=F32)
+            value = snake(v, alpha_ref[0:1, cols], alpha_ref[1:2, cols])
+            act[k, 0:length, cols] = value[:length].astype(BF16)
+            act[k, length:, cols] = jnp.where(gone, 0.0, value[length:]).astype(BF16)
+    up_copy.wait()
+    for k in range(segs):
         for r in range(0, 8, 2):
-            side, far = (prev, r + 12) if r < 4 else (after, r - 4)
+            far = r + 12 if r < 4 else r - 4
             near_w = jnp.concatenate([up_ref[r + 4], up_ref[r + 5]], axis=1)
             far_w = jnp.concatenate([up_ref[far], up_ref[far + 1]], axis=1)
-            res = jnp.dot(here[...], near_w, preferred_element_type=F32) + jnp.dot(
-                side[...], far_w, preferred_element_type=F32
-            )
-            rows_out[k % 2, pl.ds(r, length, stride=8), :] = res[:, :width]
-            rows_out[k % 2, pl.ds(r + 1, length, stride=8), :] = res[:, width:]
+            near = jnp.dot(act[k, 0:length], near_w, preferred_element_type=F32)
+            side = jnp.dot(act[k], far_w, preferred_element_type=F32)
+            if r < 4:
+                moved = [side[length : length + 1], side[: length - 1]]
+            else:
+                moved = [side[1:length], side[length + 1 : length + 2]]
+            res = near + jnp.concatenate(moved, axis=0)
+            rows_out[k, pl.ds(r, length, stride=8), :] = res[:, :width]
+            rows_out[k, pl.ds(r + 1, length, stride=8), :] = res[:, width:]
         out_copy(k).start()
-    for k in range(max(0, segs - 2), segs):
+    for k in range(segs):
         out_copy(k).wait()
 
 
@@ -275,17 +282,20 @@
     return pl.pallas_call(
         functools.partial(decoder_kernel, segs),
         out_shape=jax.ShapeDtypeStruct((segs, 8 * length, width), F32),
-        in_specs=[pl.BlockSpec(memory_space=pltpu.SMEM)] + [whole()] * (segs + 3),
+        in_specs=[pl.BlockSpec(memory_space=pltpu.SMEM)]
+        + [whole()] * (segs + 2)
+        + [pl.BlockSpec(memory_space=pl.ANY)],
         out_specs=pl.BlockSpec(memory_space=pl.ANY),
         scratch_shapes=[
-            pltpu.VMEM((length + 32, lat), F32),
-            pltpu.VMEM((length, channels), BF16),
-            pltpu.VMEM((length, channels), BF16),
-            pltpu.VMEM((length, channels), BF16),
-            pltpu.VMEM((2, 8 * length, width), F32),
-            pltpu.SemaphoreType.DMA((2,)),
+            pltpu.VMEM((length + 16, lat), F32),
+            pltpu.VMEM((segs, length + 16, conv.shape[0]), BF16),
+            pltpu.VMEM((segs, length + 16, channels), BF16),
+            pltpu.VMEM(first_up.shape, BF16),
+            pltpu.VMEM((segs, 8 * length, width), F32),
+            pltpu.SemaphoreType.DMA((segs,)),
+            pltpu.SemaphoreType.DMA,
         ],
-        compiler_params=params(32),
+        compiler_params=params(52),
         cost_estimate=pl.CostEstimate(
             flops=2 * segs * length * channels * (16 * width + 512),
             bytes_accessed=4 * segs * 8 * length * width,
@@ -320,12 +330,13 @@
     for k in range(n - 1, 0, -1):
         arrived[k] = lax.ppermute(chunks[k], "expert", partner("expert", n, k))
     out_w_t = out_weight.T
-    folded = fold_weights(down_weight[0], out_w_t)
     pick, scale, base = make_table(
         me_array, expert_ids, gate_weights, frames, out_w_t, n, capacity
     )
+    down, pick = lax.optimization_barrier((down_weight[0], pick))
+    folded = fold_weights(down, out_w_t)
     parts = {}
-    groups = [(0, 1), (2, 3)] + [tuple(range(j, min(j + 4, n))) for j in range(4, n, 4)]
+    groups = [tuple(range(j, j + 2)) for j in range(0, n, 2)]
     for group in groups:
         done = run_expert([arrived[k] for k in group], up_weight[0], folded)
         for k, value in zip(group, done):

time: 117 us -> 107 us (0.915)
  waiting for transfers between devices: 21.3 us -> 12.2 us
  Pallas kernels: 44 us -> 41.3 us
    ppermute x7, waiting for transfers between devices: 13.6 us -> 3.92 us  [local(): arrived[k] = lax.ppermute(chunks[k], 'expert', partner('expert', n, k))]
    pallas_call x1, Pallas kernels: 24.2 us -> 18.3 us  [decode(): pl.pallas_call(functools.partial(decoder_kernel, segs), out_shape=jax.Sha...]
    pallas_call x3 -> x4, Pallas kernels: 14.6 us -> 17.5 us  [run_expert(): pl.pallas_call(functools.partial(expert_kernel, count), out_shape=[jax.Sh...]
    unnamed x26 -> x18, local copies, waits for them, and re-layouts: 9.6 us -> 9.6 us
  transfers between devices with their start and end apart: 19 -> 19, of which waited for: 6 -> 7; matrix products, arithmetic and copies ran while one was open for 0% -> 2% of each run, Pallas kernels for 15% -> 20%
where the time goes in v2:
time: 107 us; the launch traced here: 106 us
  starting transfers between devices  42.6 us (40%)
  Pallas kernels  41.3 us (39%)
  waiting for transfers between devices  12.2 us (11%)
  local copies, waits for them, and re-layouts  9.61 us (9%)
    ppermute x7, starting transfers between devices, local(): lax.ppermute(value, 'expert', partner('expert', n, k))  25.3 us
    pallas_call x1, Pallas kernels, decode(): pl.pallas_call(functools.partial(decoder_kernel, segs), out_shape=jax.Sha...  18.3 us
    pallas_call x4, Pallas kernels, run_expert(): pl.pallas_call(functools.partial(expert_kernel, count), out_shape=[jax.Sh...  17.5 us
    ppermute x7, starting transfers between devices, local(): arrived[k] = lax.ppermute(chunks[k], 'expert', partner('expert', n, k))  10.1 us
    unnamed x18, local copies, waits for them, and re-layouts  9.6 us
    ppermute x3, waiting for transfers between devices, local(): lax.ppermute(slab, 'seg', partner('seg', segs, k))  3.98 us
    ppermute x7, waiting for transfers between devices, local(): arrived[k] = lax.ppermute(chunks[k], 'expert', partner('expert', n, k))  3.92 us
    ppermute x3, starting transfers between devices, local(): lax.ppermute(slab, 'seg', partner('seg', segs, k))  3.55 us
  transfers between devices with their start and end apart: 19, of which 7 were waited for; matrix products, arithmetic and copies ran while one was open for 2% of the time, Pallas kernels for 20%

profile of v2, /device:TPU:0, one launch (start us, length us, event | category | flops | bytes accessed | tf_op | source)
XLA Modules:
  0.0 106.2 jit_solution(15540890017681247897)
XLA Ops:
  1.8 1.5 %shard_map.91 = (bf16[96,1536]{1,0:T(8,128)(2,1)S(1)}, bf16[96,1536]{1,0:T(8,128)(2,1)}, bf16[96,1536]{1,0:T(8,128)(2,1)}, bf16[96,1536]{1,0:T(8,128)(2,1)S(1)},...) custom-call(s32[1]{0:T(128)} %bitcast.1.me_ref, ...), custom_call_target="tpu_custom_call" | custom-call | tf_op jit(solution)/shard_map/pallas_call | solution.py:56
  3.8 2.6 %collective-permute-start.2 = (bf16[96,1536]{1,0:T(8,128)(2,1)}, bf16[96,1536]{1,0:T(8,128)(2,1)S(1)}, u32[]{:S(2)}, u32[]{:S(2)}) collective-permute-start(bf16[96,1536]{1,0:T(8,128)(2,1)} %get-tuple-element.32), channel_id=1, source_target_pairs={{0,2},{1,3},{2,0},{3,1},{4,6},{5,7},{6,4},{7,5},{8,10},{9,11},{10,... | collective-permute-start | bytes 884744 | tf_op jit(solution)/shard_map/ppermute | solution.py:331
  6.5 2.7 %collective-permute-start.6 = (bf16[96,1536]{1,0:T(8,128)(2,1)S(1)}, bf16[96,1536]{1,0:T(8,128)(2,1)S(1)}, u32[]{:S(2)}, u32[]{:S(2)}) collective-permute-start(bf16[96,1536]{1,0:T(8,128)(2,1)S(1)} %get-tuple-element.36), channel_id=1, source_target_pairs={{0,4},{1,5},{2,6},{3,7},{4,0},{5,1},{6,2},{7,3},{8,12},{9,13},{10,... | collective-permute-start | bytes 884744 | tf_op jit(solution)/shard_map/ppermute | solution.py:331
  10.9 1.3 %copy-done.3 = bf16[256,1536]{1,0:T(8,128)(2,1)S(1)} copy-done((bf16[256,1536]{1,0:T(8,128)(2,1)S(1)}, bf16[256,1536]{1,0:T(8,128)(2,1)}, u32[]{:S(2)}) %copy-start.3) | copy-done | bytes 786456
  14.1 2.8 %copy-done.1 = bf16[1,2048,1536]{2,1,0:T(8,128)(2,1)S(1)} copy-done((bf16[1,2048,1536]{2,1,0:T(8,128)(2,1)S(1)}, bf16[1,2048,1536]{2,1,0:T(8,128)(2,1)}, u32[]{:S(2)}) %copy-start.1) | copy-done | bytes 6291480
  17.8 2.5 %shard_map.93.refs_3_ = bf16[2048,128]{1,0:T(8,128)(2,1)S(1)} custom-call(bf16[2048,1536]{1,0:T(8,128)(2,1)S(1)} %bitcast.13, bf16[64,1536]{1,0:T(8,128)(2,1)S(1)} %bitcast.15), custom_call_target="tpu_custom_call" | custom-call | flops 805306368 | bytes 6291456 | tf_op jit(solution)/shard_map/pallas_call | solution.py:78
  20.3 3.6 %collective-permute-start.10 = (bf16[96,1536]{1,0:T(8,128)(2,1)S(1)}, bf16[96,1536]{1,0:T(8,128)(2,1)S(1)}, u32[]{:S(2)}, u32[]{:S(2)}) collective-permute-start(bf16[96,1536]{1,0:T(8,128)(2,1)S(1)} %get-tuple-element.40), channel_id=1, source_target_pairs={{0,6},{1,7},{2,4},{3,5},{4,2},{5,3},{6,0},{7,1},{8,14},{9,15},{10,... | collective-permute-start | bytes 884744 | tf_op jit(solution)/shard_map/ppermute | solution.py:331
  23.9 3.0 %collective-permute-done.2.refs_0_ = bf16[96,1536]{1,0:T(8,128)(2,1)S(1)} collective-permute-done((bf16[96,1536]{1,0:T(8,128)(2,1)}, bf16[96,1536]{1,0:T(8,128)(2,1)S(1)}, u32[]{:S(2)}, u32[]{:S(2)}) %collective-permute-start.2) | collective-permute-done | bytes 294944 | tf_op jit(solution)/shard_map/ppermute | solution.py:331
  27.5 4.4 %shard_map.94 = (bf16[96,128]{1,0:T(8,128)(2,1)S(1)}, bf16[96,128]{1,0:T(8,128)(2,1)S(1)}) custom-call(bf16[96,1536]{1,0:T(8,128)(2,1)S(1)} %get-tuple-element.26.refs_0_, bf16[96,1536]{1,0:T(8,128)(2,1)S(1)} %collective-permute-done.refs_1_, bf16[1536,2048]{1,0:T(8,128)(2,1)S(1)} %bitcast.9, bf16[2048,128]{1,0:T(8,128)(2,1)S(1)} %shard_map.93.refs_3_), custom_call_target="tpu_custom_call" | custom-call | flops 1409286144 | bytes 6291456 | tf_op jit(solution)/shard_map/pallas_call | solution.py:172
  33.1 4.4 %shard_map.95 = (bf16[96,128]{1,0:T(8,128)(2,1)S(1)}, bf16[96,128]{1,0:T(8,128)(2,1)S(1)}) custom-call(bf16[96,1536]{1,0:T(8,128)(2,1)S(1)} %collective-permute-done.2.refs_0_, bf16[96,1536]{1,0:T(8,128)(2,1)S(1)} %collective-permute-done.3.refs_1_, bf16[1536,2048]{1,0:T(8,128)(2,1)S(1)} %bitcast.10, bf16[2048,128]{1,0:T(8,128)(2,1)S(1)} %shard_map.93.refs_3_), custom_call_target="tpu_custom_call" | custom-call | flops 1409286144 | bytes 6291456 | tf_op jit(solution)/shard_map/pallas_call | solution.py:172
  37.6 10.7 %collective-permute-start.5 = (bf16[96,128]{1,0:T(8,128)(2,1)S(1)}, bf16[96,128]{1,0:T(8,128)(2,1)S(1)}, u32[]{:S(2)}, u32[]{:S(2)}) collective-permute-start(bf16[96,128]{1,0:T(8,128)(2,1)S(1)} %get-tuple-element.35), channel_id=1, source_target_pairs={{0,3},{1,2},{2,1},{3,0},{4,7},{5,6},{6,5},{7,4},{8,11},{9,10},{10,... | collective-permute-start | bytes 73736 | tf_op jit(solution)/shard_map/ppermute | solution.py:343
  48.3 4.4 %shard_map.96 = (bf16[96,128]{1,0:T(8,128)(2,1)S(1)}, bf16[96,128]{1,0:T(8,128)(2,1)S(1)}) custom-call(bf16[96,1536]{1,0:T(8,128)(2,1)S(1)} %collective-permute-done.6.refs_0_, bf16[96,1536]{1,0:T(8,128)(2,1)S(1)} %collective-permute-done.7.refs_1_, bf16[1536,2048]{1,0:T(8,128)(2,1)S(1)} %bitcast.11, bf16[2048,128]{1,0:T(8,128)(2,1)S(1)} %shard_map.93.refs_3_), custom_call_target="tpu_custom_call" | custom-call | flops 1409286144 | bytes 6291456 | tf_op jit(solution)/shard_map/pallas_call | solution.py:172
  52.7 5.4 %collective-permute-start.8 = (bf16[96,128]{1,0:T(8,128)(2,1)S(1)}, bf16[96,128]{1,0:T(8,128)(2,1)S(1)}, u32[]{:S(2)}, u32[]{:S(2)}) collective-permute-start(bf16[96,128]{1,0:T(8,128)(2,1)S(1)} %get-tuple-element.38), channel_id=1, source_target_pairs={{0,4},{1,5},{2,6},{3,7},{4,0},{5,1},{6,2},{7,3},{8,12},{9,13},{10,... | collective-permute-start | bytes 73736 | tf_op jit(solution)/shard_map/ppermute | solution.py:343
  58.1 6.0 %collective-permute-start.9 = (bf16[96,128]{1,0:T(8,128)(2,1)S(1)}, bf16[96,128]{1,0:T(8,128)(2,1)S(1)}, u32[]{:S(2)}, u32[]{:S(2)}) collective-permute-start(bf16[96,128]{1,0:T(8,128)(2,1)S(1)} %get-tuple-element.39), channel_id=1, source_target_pairs={{0,5},{1,4},{2,7},{3,6},{4,1},{5,0},{6,3},{7,2},{8,13},{9,12},{10,... | collective-permute-start | bytes 73736 | tf_op jit(solution)/shard_map/ppermute | solution.py:343
  64.0 4.4 %shard_map.97 = (bf16[96,128]{1,0:T(8,128)(2,1)S(1)}, bf16[96,128]{1,0:T(8,128)(2,1)S(1)}) custom-call(bf16[96,1536]{1,0:T(8,128)(2,1)S(1)} %collective-permute-done.10.refs_0_, bf16[96,1536]{1,0:T(8,128)(2,1)S(1)} %collective-permute-done.11.refs_1_, bf16[1536,2048]{1,0:T(8,128)(2,1)S(1)} %bitcast.12, bf16[2048,128]{1,0:T(8,128)(2,1)S(1)} %shard_map.93.refs_3_), custom_call_target="tpu_custom_call" | custom-call | flops 1409286144 | bytes 6291456 | tf_op jit(solution)/shard_map/pallas_call | solution.py:172
  68.5 2.8 %collective-permute-start.13 = (bf16[96,128]{1,0:T(8,128)(2,1)S(1)}, bf16[96,128]{1,0:T(8,128)(2,1)S(1)}, u32[]{:S(2)}, u32[]{:S(2)}) collective-permute-start(bf16[96,128]{1,0:T(8,128)(2,1)S(1)} %get-tuple-element.43), channel_id=1, source_target_pairs={{0,7},{1,6},{2,5},{3,4},{4,3},{5,2},{6,1},{7,0},{8,15},{9,14},{10,... | collective-permute-start | bytes 73736 | tf_op jit(solution)/shard_map/ppermute | solution.py:343
  71.4 2.7 %collective-permute-done.12.refs_6_ = bf16[96,128]{1,0:T(8,128)(2,1)S(1)} collective-permute-done((bf16[96,128]{1,0:T(8,128)(2,1)S(1)}, bf16[96,128]{1,0:T(8,128)(2,1)S(1)}, u32[]{:S(2)}, u32[]{:S(2)}) %collective-permute-start.12) | collective-permute-done | bytes 24608 | tf_op jit(solution)/shard_map/ppermute | solution.py:343
  74.8 2.2 %collective-permute-start.14 = (bf16[4,64]{1,0:T(4,128)(2,1)S(1)}, bf16[4,64]{1,0:T(4,128)(2,1)S(1)}, u32[]{:S(2)}, u32[]{:S(2)}) collective-permute-start(bf16[4,64]{1,0:T(4,128)(2,1)S(1)} %get-tuple-element.47), channel_id=1, source_target_pairs={{0,1},{1,2},{2,3},{3,4},{4,5},{5,6},{6,7},{8,9},{9,10},{10,11},{11... | collective-permute-start | bytes 1544 | tf_op jit(solution)/shard_map/ppermute | solution.py:348
  77.0 1.5 %collective-permute-start.15 = (bf16[4,64]{1,0:T(4,128)(2,1)S(1)}, bf16[4,64]{1,0:T(4,128)(2,1)S(1)}, u32[]{:S(2)}, u32[]{:S(2)}) collective-permute-start(bf16[4,64]{1,0:T(4,128)(2,1)S(1)} %get-tuple-element.48), channel_id=1, source_target_pairs={{1,0},{2,1},{3,2},{4,3},{5,4},{6,5},{7,6},{9,8},{10,9},{11,10},{12... | collective-permute-start | bytes 1544 | tf_op jit(solution)/shard_map/ppermute | solution.py:349
  78.6 1.5 %collective-permute-done.15 = bf16[4,64]{1,0:T(4,128)(2,1)S(1)} collective-permute-done((bf16[4,64]{1,0:T(4,128)(2,1)S(1)}, bf16[4,64]{1,0:T(4,128)(2,1)S(1)}, u32[]{:S(2)}, u32[]{:S(2)}) %collective-permute-start.15) | collective-permute-done | bytes 544 | tf_op jit(solution)/shard_map/ppermute | solution.py:349
  80.1 2.4 %collective-permute-start.18 = (bf16[264,64]{1,0:T(8,128)(2,1)S(1)}, bf16[264,64]{1,0:T(8,128)(2,1)S(1)}, u32[]{:S(2)}, u32[]{:S(2)}) collective-permute-start(bf16[264,64]{1,0:T(8,128)(2,1)S(1)} %pad_maximum_fusion.refs_0_), channel_id=1, source_target_pairs={{0,24},{8,16},{16,8},{24,0},{1,25},{9,17},{17,9},{25,1},{2,26},{10... | collective-permute-start | bytes 101384 | tf_op jit(solution)/shard_map/ppermute | solution.py:352
  83.7 1.6 %collective-permute-done.18.refs_3_ = bf16[264,64]{1,0:T(8,128)(2,1)S(1)} collective-permute-done((bf16[264,64]{1,0:T(8,128)(2,1)S(1)}, bf16[264,64]{1,0:T(8,128)(2,1)S(1)}, u32[]{:S(2)}, u32[]{:S(2)}) %collective-permute-start.18) | collective-permute-done | bytes 33824 | tf_op jit(solution)/shard_map/ppermute | solution.py:352
  85.4 1.9 %collective-permute-done.17.refs_2_ = bf16[264,64]{1,0:T(8,128)(2,1)S(1)} collective-permute-done((bf16[264,64]{1,0:T(8,128)(2,1)S(1)}, bf16[264,64]{1,0:T(8,128)(2,1)S(1)}, u32[]{:S(2)}, u32[]{:S(2)}) %collective-permute-start.17) | collective-permute-done | bytes 33824 | tf_op jit(solution)/shard_map/ppermute | solution.py:352
  87.7 18.3 %shard_map.99 = f32[4,2048,128]{2,1,0:T(8,128)} custom-call(s32[3]{0:T(128)S(1)} %pad_add_fusion.place_ref, bf16[264,64]{1,0:T(8,128)(2,1)S(1)} %pad_maximum_fusion.refs_0_, bf16[264,64]{1,0:T(8,128)(2,1)S(1)} %collective-permute-done.16.refs_1_, bf16[264,64]{1,0:T(8,128)(2,1)S(1)} %collective-permute-done.17.refs_2_, ...), custom_call_target="tpu_custom_call" | custom-call | flops 10737418240 | bytes 4194304 | tf_op jit(solution)/shard_map/pallas_call | solution.py:282
  (46 shorter events, 11.3 us)
Async XLA Ops:
  3.3 17.0 %collective-permute-start = (bf16[96,1536]{1,0:T(8,128)(2,1)}, bf16[96,1536]{1,0:T(8,128)(2,1)S(1)}, u32[]{:S(2)}, u32[]{:S(2)}) collective-permute-start(bf16[96,1536]{1,0:T(8,128)(2,1)} %get-tuple-element.27), channel_id=1, source_target_pairs={{0,1},{1,0},{2,3},{3,2},{4,5},{5,4},{6,7},{7,6},{8,9},{9,8},{10,11... | collective-permute-start | bytes 884744 | tf_op jit(solution)/shard_map/ppermute | solution.py:331
  3.8 23.1 %collective-permute-start.2 = (bf16[96,1536]{1,0:T(8,128)(2,1)}, bf16[96,1536]{1,0:T(8,128)(2,1)S(1)}, u32[]{:S(2)}, u32[]{:S(2)}) collective-permute-start(bf16[96,1536]{1,0:T(8,128)(2,1)} %get-tuple-element.32), channel_id=1, source_target_pairs={{0,2},{1,3},{2,0},{3,1},{4,6},{5,7},{6,4},{7,5},{8,10},{9,11},{10,... | collective-permute-start | bytes 884744 | tf_op jit(solution)/shard_map/ppermute | solution.py:331
  6.3 26.5 %collective-permute-start.3 = (bf16[96,1536]{1,0:T(8,128)(2,1)S(1)}, bf16[96,1536]{1,0:T(8,128)(2,1)S(1)}, u32[]{:S(2)}, u32[]{:S(2)}) collective-permute-start(bf16[96,1536]{1,0:T(8,128)(2,1)S(1)} %get-tuple-element.33), channel_id=1, source_target_pairs={{0,3},{1,2},{2,1},{3,0},{4,7},{5,6},{6,5},{7,4},{8,11},{9,10},{10,... | collective-permute-start | bytes 884744 | tf_op jit(solution)/shard_map/ppermute | solution.py:331
  6.5 31.0 %collective-permute-start.6 = (bf16[96,1536]{1,0:T(8,128)(2,1)S(1)}, bf16[96,1536]{1,0:T(8,128)(2,1)S(1)}, u32[]{:S(2)}, u32[]{:S(2)}) collective-permute-start(bf16[96,1536]{1,0:T(8,128)(2,1)S(1)} %get-tuple-element.36), channel_id=1, source_target_pairs={{0,4},{1,5},{2,6},{3,7},{4,0},{5,1},{6,2},{7,3},{8,12},{9,13},{10,... | collective-permute-start | bytes 884744 | tf_op jit(solution)/shard_map/ppermute | solution.py:331
  9.2 28.4 %collective-permute-start.7 = (bf16[96,1536]{1,0:T(8,128)(2,1)S(1)}, bf16[96,1536]{1,0:T(8,128)(2,1)S(1)}, u32[]{:S(2)}, u32[]{:S(2)}) collective-permute-start(bf16[96,1536]{1,0:T(8,128)(2,1)S(1)} %get-tuple-element.37), channel_id=1, source_target_pairs={{0,5},{1,4},{2,7},{3,6},{4,1},{5,0},{6,3},{7,2},{8,13},{9,12},{10,... | collective-permute-start | bytes 884744 | tf_op jit(solution)/shard_map/ppermute | solution.py:331
  10.9 16.6 %copy-start = (bf16[1,1536,2048]{2,1,0:T(8,128)(2,1)S(1)}, bf16[1,1536,2048]{2,1,0:T(8,128)(2,1)}, u32[]{:S(2)}) copy-start(bf16[1,1536,2048]{2,1,0:T(8,128)(2,1)} %param.12) | copy-start | bytes 18874372
  10.9 1.3 %copy-start.3 = (bf16[256,1536]{1,0:T(8,128)(2,1)S(1)}, bf16[256,1536]{1,0:T(8,128)(2,1)}, u32[]{:S(2)}) copy-start(bf16[256,1536]{1,0:T(8,128)(2,1)} %frames_ref.3) | copy-start | bytes 2359300
  12.2 1.2 %copy-start.4 = (bf16[1536,64]{0,1:T(8,128)(2,1)S(1)}, bf16[1536,64]{0,1:T(8,128)(2,1)}, u32[]{:S(2)}) copy-start(bf16[1536,64]{0,1:T(8,128)(2,1)} %param.14) | copy-start | bytes 589828
  14.1 2.8 %copy-start.1 = (bf16[1,2048,1536]{2,1,0:T(8,128)(2,1)S(1)}, bf16[1,2048,1536]{2,1,0:T(8,128)(2,1)}, u32[]{:S(2)}) copy-start(bf16[1,2048,1536]{2,1,0:T(8,128)(2,1)} %param.13) | copy-start | bytes 18874372
  20.3 32.4 %collective-permute-start.10 = (bf16[96,1536]{1,0:T(8,128)(2,1)S(1)}, bf16[96,1536]{1,0:T(8,128)(2,1)S(1)}, u32[]{:S(2)}, u32[]{:S(2)}) collective-permute-start(bf16[96,1536]{1,0:T(8,128)(2,1)S(1)} %get-tuple-element.40), channel_id=1, source_target_pairs={{0,6},{1,7},{2,4},{3,5},{4,2},{5,3},{6,0},{7,1},{8,14},{9,15},{10,... | collective-permute-start | bytes 884744 | tf_op jit(solution)/shard_map/ppermute | solution.py:331
  26.9 31.2 %collective-permute-start.11 = (bf16[96,1536]{1,0:T(8,128)(2,1)S(1)}, bf16[96,1536]{1,0:T(8,128)(2,1)S(1)}, u32[]{:S(2)}, u32[]{:S(2)}) collective-permute-start(bf16[96,1536]{1,0:T(8,128)(2,1)S(1)} %get-tuple-element.41), channel_id=1, source_target_pairs={{0,7},{1,6},{2,5},{3,4},{4,3},{5,2},{6,1},{7,0},{8,15},{9,14},{10,... | collective-permute-start | bytes 884744 | tf_op jit(solution)/shard_map/ppermute | solution.py:331
  32.8 35.6 %collective-permute-start.1 = (bf16[96,128]{1,0:T(8,128)(2,1)S(1)}, bf16[96,128]{1,0:T(8,128)(2,1)S(1)}, u32[]{:S(2)}, u32[]{:S(2)}) collective-permute-start(bf16[96,128]{1,0:T(8,128)(2,1)S(1)} %get-tuple-element.31), channel_id=1, source_target_pairs={{0,1},{1,0},{2,3},{3,2},{4,5},{5,4},{6,7},{7,6},{8,9},{9,8},{10,11... | collective-permute-start | bytes 73736 | tf_op jit(solution)/shard_map/ppermute | solution.py:343
  37.5 31.0 %collective-permute-start.4 = (bf16[96,128]{1,0:T(8,128)(2,1)S(1)}, bf16[96,128]{1,0:T(8,128)(2,1)S(1)}, u32[]{:S(2)}, u32[]{:S(2)}) collective-permute-start(bf16[96,128]{1,0:T(8,128)(2,1)S(1)} %get-tuple-element.34), channel_id=1, source_target_pairs={{0,2},{1,3},{2,0},{3,1},{4,6},{5,7},{6,4},{7,5},{8,10},{9,11},{10,... | collective-permute-start | bytes 73736 | tf_op jit(solution)/shard_map/ppermute | solution.py:343
  37.6 33.8 %copy-start.7 = (f32[2048]{0:T(1024)S(1)}, f32[2048]{0:T(1024)}, u32[]{:S(2)}) copy-start(f32[2048]{0:T(1024)} %param.16) | copy-start | bytes 24580
  37.6 33.8 %collective-permute-start.5 = (bf16[96,128]{1,0:T(8,128)(2,1)S(1)}, bf16[96,128]{1,0:T(8,128)(2,1)S(1)}, u32[]{:S(2)}, u32[]{:S(2)}) collective-permute-start(bf16[96,128]{1,0:T(8,128)(2,1)S(1)} %get-tuple-element.35), channel_id=1, source_target_pairs={{0,3},{1,2},{2,1},{3,0},{4,7},{5,6},{6,5},{7,4},{8,11},{9,10},{10,... | collective-permute-start | bytes 73736 | tf_op jit(solution)/shard_map/ppermute | solution.py:343
  52.7 18.7 %collective-permute-start.8 = (bf16[96,128]{1,0:T(8,128)(2,1)S(1)}, bf16[96,128]{1,0:T(8,128)(2,1)S(1)}, u32[]{:S(2)}, u32[]{:S(2)}) collective-permute-start(bf16[96,128]{1,0:T(8,128)(2,1)S(1)} %get-tuple-element.38), channel_id=1, source_target_pairs={{0,4},{1,5},{2,6},{3,7},{4,0},{5,1},{6,2},{7,3},{8,12},{9,13},{10,... | collective-permute-start | bytes 73736 | tf_op jit(solution)/shard_map/ppermute | solution.py:343
  58.1 13.3 %collective-permute-start.9 = (bf16[96,128]{1,0:T(8,128)(2,1)S(1)}, bf16[96,128]{1,0:T(8,128)(2,1)S(1)}, u32[]{:S(2)}, u32[]{:S(2)}) collective-permute-start(bf16[96,128]{1,0:T(8,128)(2,1)S(1)} %get-tuple-element.39), channel_id=1, source_target_pairs={{0,5},{1,4},{2,7},{3,6},{4,1},{5,0},{6,3},{7,2},{8,13},{9,12},{10,... | collective-permute-start | bytes 73736 | tf_op jit(solution)/shard_map/ppermute | solution.py:343
  68.4 5.7 %collective-permute-start.12 = (bf16[96,128]{1,0:T(8,128)(2,1)S(1)}, bf16[96,128]{1,0:T(8,128)(2,1)S(1)}, u32[]{:S(2)}, u32[]{:S(2)}) collective-permute-start(bf16[96,128]{1,0:T(8,128)(2,1)S(1)} %get-tuple-element.42), channel_id=1, source_target_pairs={{0,6},{1,7},{2,4},{3,5},{4,2},{5,3},{6,0},{7,1},{8,14},{9,15},{10,... | collective-permute-start | bytes 73736 | tf_op jit(solution)/shard_map/ppermute | solution.py:343
  68.5 5.6 %collective-permute-start.13 = (bf16[96,128]{1,0:T(8,128)(2,1)S(1)}, bf16[96,128]{1,0:T(8,128)(2,1)S(1)}, u32[]{:S(2)}, u32[]{:S(2)}) collective-permute-start(bf16[96,128]{1,0:T(8,128)(2,1)S(1)} %get-tuple-element.43), channel_id=1, source_target_pairs={{0,7},{1,6},{2,5},{3,4},{4,3},{5,2},{6,1},{7,0},{8,15},{9,14},{10,... | collective-permute-start | bytes 73736 | tf_op jit(solution)/shard_map/ppermute | solution.py:343
  74.8 3.7 %collective-permute-start.14 = (bf16[4,64]{1,0:T(4,128)(2,1)S(1)}, bf16[4,64]{1,0:T(4,128)(2,1)S(1)}, u32[]{:S(2)}, u32[]{:S(2)}) collective-permute-start(bf16[4,64]{1,0:T(4,128)(2,1)S(1)} %get-tuple-element.47), channel_id=1, source_target_pairs={{0,1},{1,2},{2,3},{3,4},{4,5},{5,6},{6,7},{8,9},{9,10},{10,11},{11... | collective-permute-start | bytes 1544 | tf_op jit(solution)/shard_map/ppermute | solution.py:348
  77.0 3.0 %collective-permute-start.15 = (bf16[4,64]{1,0:T(4,128)(2,1)S(1)}, bf16[4,64]{1,0:T(4,128)(2,1)S(1)}, u32[]{:S(2)}, u32[]{:S(2)}) collective-permute-start(bf16[4,64]{1,0:T(4,128)(2,1)S(1)} %get-tuple-element.48), channel_id=1, source_target_pairs={{1,0},{2,1},{3,2},{4,3},{5,4},{6,5},{7,6},{9,8},{10,9},{11,10},{12... | collective-permute-start | bytes 1544 | tf_op jit(solution)/shard_map/ppermute | solution.py:349
  80.1 5.3 %collective-permute-start.18 = (bf16[264,64]{1,0:T(8,128)(2,1)S(1)}, bf16[264,64]{1,0:T(8,128)(2,1)S(1)}, u32[]{:S(2)}, u32[]{:S(2)}) collective-permute-start(bf16[264,64]{1,0:T(8,128)(2,1)S(1)} %pad_maximum_fusion.refs_0_), channel_id=1, source_target_pairs={{0,24},{8,16},{16,8},{24,0},{1,25},{9,17},{17,9},{25,1},{2,26},{10... | collective-permute-start | bytes 101384 | tf_op jit(solution)/shard_map/ppermute | solution.py:352
  82.6 4.7 %collective-permute-start.17 = (bf16[264,64]{1,0:T(8,128)(2,1)S(1)}, bf16[264,64]{1,0:T(8,128)(2,1)S(1)}, u32[]{:S(2)}, u32[]{:S(2)}) collective-permute-start(bf16[264,64]{1,0:T(8,128)(2,1)S(1)} %pad_maximum_fusion.refs_0_), channel_id=1, source_target_pairs={{0,16},{8,24},{16,0},{24,8},{1,17},{9,25},{17,1},{25,9},{2,18},{10... | collective-permute-start | bytes 101384 | tf_op jit(solution)/shard_map/ppermute | solution.py:352
  83.1 4.7 %collective-permute-start.16 = (bf16[264,64]{1,0:T(8,128)(2,1)S(1)}, bf16[264,64]{1,0:T(8,128)(2,1)S(1)}, u32[]{:S(2)}, u32[]{:S(2)}) collective-permute-start(bf16[264,64]{1,0:T(8,128)(2,1)S(1)} %pad_maximum_fusion.refs_0_), channel_id=1, source_target_pairs={{0,8},{8,0},{16,24},{24,16},{1,9},{9,1},{17,25},{25,17},{2,10},{10... | collective-permute-start | bytes 101384 | tf_op jit(solution)/shard_map/ppermute | solution.py:352
  (3 other events, 2.7 us)

commit v3 on v2

v3 whole, which is shorter than its diff:
```python
import functools
import math

import jax
import jax.numpy as jnp
from jax import lax
from jax.experimental import pallas as pl
from jax.experimental.pallas import tpu as pltpu
from jax.sharding import PartitionSpec as P

F32 = jnp.float32
BF16 = jnp.bfloat16
VMEM = pltpu.VMEM
SIN2 = (
    9.869603157043457,
    -32.469581604003906,
    42.72538375854492,
    -30.085954666137695,
    12.99073314666748,
    -3.2729504108428955,
)
ROUNDER = 12582912.0


FREE = pl.CostEstimate(flops=0, bytes_accessed=0, transcendentals=0)


def whole():
    return pl.BlockSpec(memory_space=VMEM)


def params(mib):
    return pltpu.CompilerParams(vmem_limit_bytes=mib * 1024 * 1024)


EDGE = 4
EDGE_ROWS = 16


def token_key(token, rows):
    rest = jnp.where(token >= rows - EDGE, token - (rows - 2 * EDGE), token + EDGE)
    return jnp.where(token < EDGE, token, rest)


def one_hot(mask):
    return mask.astype(F32).astype(BF16)


def slots_kernel(steps, origin_ref, *refs):
    sources, out_refs = refs[: -len(steps)], refs[-len(steps) :]
    ids, frames = sources[0][...], sources[1][...]
    if len(sources) > 2:
        second = origin_ref[1] == 1
        ids = jnp.where(second, sources[2][...], ids)
        frames = jnp.where(second, sources[3][...], frames)
    rows = frames.shape[0]
    capacity = out_refs[0].shape[0]
    ids = ids ^ origin_ref[0]
    count = -(-len(steps) // 16) * 16
    step = lax.broadcasted_iota(jnp.int32, (count, rows), 0) + steps[0]
    named = (ids[0:1] == step) | (ids[1:2] == step)
    earlier = token_key(lax.broadcasted_iota(jnp.int32, (rows, rows), 0), rows) < token_key(
        lax.broadcasted_iota(jnp.int32, (rows, rows), 1), rows
    )
    rank = jnp.dot(one_hot(named), one_hot(earlier), preferred_element_type=F32)
    rank = jnp.where(named, rank, -1.0)
    slot = lax.broadcasted_iota(jnp.int32, (capacity, rows), 0).astype(F32)
    for j, ref in enumerate(out_refs):
        pick = one_hot(slot == rank[j : j + 1])
        ref[...] = jnp.dot(pick, frames, preferred_element_type=F32).astype(BF16)


def make_slots(origin, steps, sources, capacity):
    width = sources[1].shape[1]
    return pl.pallas_call(
        functools.partial(slots_kernel, steps),
        out_shape=[jax.ShapeDtypeStruct((capacity, width), BF16)] * len(steps),
        in_specs=[pl.BlockSpec(memory_space=pltpu.SMEM)] + [whole()] * len(sources),
        out_specs=[whole()] * len(steps),
        compiler_params=params(24),
        cost_estimate=FREE,
    )(origin, *sources)


def fold_kernel(down_ref, out_w_ref, folded_ref):
    full = lax.dot_general(
        down_ref[...], out_w_ref[...], (((1,), (1,)), ((), ())), preferred_element_type=F32
    )
    high = full.astype(BF16)
    low = (full - high.astype(F32)).astype(BF16)
    folded_ref[...] = jnp.concatenate([high, low], axis=1)


def fold_weights(down, out_w_t):
    hid, width = down.shape
    lat = out_w_t.shape[0]
    block = 512 if hid % 512 == 0 else hid
    return pl.pallas_call(
        fold_kernel,
        grid=(hid // block,),
        out_shape=jax.ShapeDtypeStruct((hid, 2 * lat), BF16),
        in_specs=[
            pl.BlockSpec((block, width), lambda i: (i, 0)),
            pl.BlockSpec((lat, width), lambda i: (0, 0)),
        ],
        out_specs=pl.BlockSpec((block, 2 * lat), lambda i: (i, 0)),
        compiler_params=params(16),
        cost_estimate=FREE,
    )(down, out_w_t)


def table_kernel(place_ref, ids_ref, gates_ref, pick_ref, scale_ref):
    n, span, columns = pick_ref.shape
    rows = span - 4 * EDGE
    capacity = columns - 2 * EDGE_ROWS

    def code(i):
        own = 1024 + token_key(i - EDGE, rows)
        late = jnp.where(i < rows + 3 * EDGE, i - rows - 2 * EDGE, 3072)
        tail = jnp.where(i < rows + 2 * EDGE, 2048 + i - rows - EDGE, late)
        return jnp.where(i < EDGE, i + EDGE, jnp.where(i < rows + EDGE, own, tail))

    line = lax.broadcasted_iota(jnp.int32, (span, 1), 0)
    line_code = code(line)
    other = code(lax.broadcasted_iota(jnp.int32, (span, span), 1))
    earlier = (other < line_code) & (other >= (line_code >> 10) * 1024)
    before = line_code < 1024
    after = (line_code >= 2048) & (line_code < 3072)
    lost = (before & (place_ref[0] == 0)) | (after & (place_ref[0] == place_ref[1] - 1))
    ids = jnp.where(lost | (line_code >= 3072), -1, ids_ref[...] ^ place_ref[0])
    step = lax.broadcasted_iota(jnp.int32, (span, 128), 1)
    first = ids[:, 0:1] == step
    second = ids[:, 1:2] == step
    named = first | second
    rank = jnp.dot(one_hot(earlier), one_hot(named), preferred_element_type=F32)
    rank = rank + jnp.where(before, capacity, jnp.where(after, capacity + EDGE_ROWS, 0)).astype(F32)
    rank = jnp.where(named, rank, -1.0)
    gates = gates_ref[...]
    scale_ref[...] = jnp.where(first, gates[:, 0:1], jnp.where(second, gates[:, 1:2], 0.0))
    slot = lax.broadcasted_iota(jnp.int32, (span, columns), 1).astype(F32)
    for k in range(n):
        pick_ref[k] = one_hot(slot == rank[:, k : k + 1])


def make_table(place, ids, gates, n, capacity):
    span = ids.shape[0]
    return pl.pallas_call(
        table_kernel,
        out_shape=[
            jax.ShapeDtypeStruct((n, span, capacity + 2 * EDGE_ROWS), BF16),
            jax.ShapeDtypeStruct((span, 128), F32),
        ],
        in_specs=[pl.BlockSpec(memory_space=pltpu.SMEM)] + [whole()] * 2,
        out_specs=[whole()] * 2,
        compiler_params=params(16),
        cost_estimate=FREE,
    )(place, ids, gates)


def expert_rows(rows, up_ref, folded_ref):
    hid = up_ref.shape[1]
    block = 256 if hid % 256 == 0 else hid
    total = None
    for at in range(0, hid, block):
        v = jnp.dot(rows, up_ref[:, at : at + block], preferred_element_type=F32)
        inner = v * (0.7978845608 + (0.7978845608 * 0.044715) * (v * v))
        hidden = (0.5 * v * (1.0 + jnp.tanh(inner))).astype(BF16)
        part = jnp.dot(hidden, folded_ref[at : at + block, :], preferred_element_type=F32)
        total = part if total is None else total + part
    lat = folded_ref.shape[1] // 2
    value = total[:, :lat] + total[:, lat:]
    high = value.astype(BF16)
    low = (value - high.astype(F32)).astype(BF16)
    return jnp.concatenate([high, low], axis=1)


def near_kernel(count, *refs):
    chunk_refs = refs[:count]
    up_ref, folded_ref, out_ref = refs[count:]
    capacity = chunk_refs[0].shape[0]
    rows = jnp.concatenate([ref[...] for ref in chunk_refs], axis=0)
    both = expert_rows(rows, up_ref, folded_ref)
    for j in range(count):
        out_ref[j] = both[j * capacity : (j + 1) * capacity]


def near_group(chunks, up, folded):
    count = len(chunks)
    capacity = chunks[0].shape[0]
    return pl.pallas_call(
        functools.partial(near_kernel, count),
        out_shape=jax.ShapeDtypeStruct((count, capacity, folded.shape[1]), BF16),
        in_specs=[whole()] * (count + 2),
        out_specs=whole(),
        compiler_params=params(24),
        cost_estimate=FREE,
    )(*chunks, up, folded)


def far_kernel(n, *refs):
    quarter, half = n // 4, n // 2
    place_ref, local_ref = refs[:2]
    chunk_refs = refs[2 : 2 + half]
    known_refs = refs[2 + half : 4 + half]
    up_ref, folded_ref = refs[4 + half : 6 + half]
    outs, held = refs[6 + half : -1], refs[-1]
    capacity = local_ref.shape[0]
    me = place_ref[0]
    is_inner = (me >= quarter) & (me < 3 * quarter)
    chunks = [ref[...] for ref in chunk_refs]
    chunks[quarter] = jnp.where(is_inner, local_ref[...], chunks[quarter])
    held[0:quarter] = known_refs[0][...]
    held[quarter:half] = known_refs[1][...]
    both = expert_rows(jnp.concatenate(chunks, axis=0), up_ref, folded_ref)
    for j in range(half):
        held[half + j] = both[j * capacity : (j + 1) * capacity]
    for k, ref in enumerate(outs):
        to = me ^ k
        left = me ^ jnp.where(to > 0, to - 1, to)
        right = me ^ jnp.where(to < n - 1, to + 1, to)
        ref[0:capacity] = held[k]
        ref[capacity : capacity + EDGE_ROWS] = held[left, 0:EDGE_ROWS]
        ref[capacity + EDGE_ROWS :] = held[right, 0:EDGE_ROWS]


def far_group(n, place, local_chunk, chunks, known, up, folded):
    capacity = local_chunk.shape[0]
    lanes = folded.shape[1]
    return pl.pallas_call(
        functools.partial(far_kernel, n),
        out_shape=[jax.ShapeDtypeStruct((capacity + 2 * EDGE_ROWS, lanes), BF16)] * n,
        in_specs=[pl.BlockSpec(memory_space=pltpu.SMEM)] + [whole()] * (n // 2 + 5),
        out_specs=[whole()] * n,
        scratch_shapes=[pltpu.VMEM((n, capacity, lanes), BF16)],
        compiler_params=params(24),
        cost_estimate=FREE,
    )(place, local_chunk, *chunks, *known, up, folded)


def combine_kernel(n, *refs):
    part_refs = refs[:n]
    pick_ref, scale_ref, base_ref, low_ref = refs[n:]
    lat = base_ref.shape[1]
    latent = base_ref[...]
    for k in range(n):
        picked = jnp.dot(pick_ref[k], part_refs[k][...], preferred_element_type=F32)
        latent = latent + scale_ref[:, k : k + 1] * (picked[:, :lat] + picked[:, lat:])
    low_ref[...] = latent.astype(BF16)


def combine(parts, pick, scale, base):
    n = len(parts)
    return pl.pallas_call(
        functools.partial(combine_kernel, n),
        out_shape=jax.ShapeDtypeStruct(base.shape, BF16),
        in_specs=[whole()] * (n + 3),
        out_specs=whole(),
        compiler_params=params(16),
    )(*parts, pick, scale, base)


def snake(v, turns_row, inverse_row):
    turns = v * turns_row
    part = turns - ((turns + ROUNDER) - ROUNDER)
    s = part * part
    poly = SIN2[-1]
    for c in SIN2[-2::-1]:
        poly = poly * s + c
    return v + (poly * s) * inverse_row


def decoder_kernel(segs, place_ref, *refs):
    lat_refs = refs[:segs]
    conv_ref, alpha_ref, up_hbm, out_ref = refs[segs : segs + 4]
    padded, windows, act, up_ref, rows_out, sems, up_sem = refs[segs + 4 :]
    span, channels = act.shape[1:]
    length = span - 16
    width = up_ref.shape[2]
    halo, lat = lat_refs[0].shape
    taps = conv_ref.shape[0] // lat
    block = 256
    own = place_ref[0]
    is_first = place_ref[1] == 0
    is_last = place_ref[1] == place_ref[2] - 1
    up_copy = pltpu.make_async_copy(up_hbm, up_ref, up_sem)
    up_copy.start()

    def out_copy(k):
        return pltpu.make_async_copy(rows_out.at[k], out_ref.at[own ^ k], sems.at[k])

    row = lax.broadcasted_iota(jnp.int32, (16, taps * lat), 0)
    edge_row = lax.broadcasted_iota(jnp.int32, (16, block), 0)
    gone = ((edge_row == 0) & is_first) | ((edge_row == 1) & is_last)
    for k in range(segs):
        padded[0:halo, :] = lat_refs[k][...].astype(F32)

        def window(start, rows):
            return jnp.concatenate([padded[start + j : start + j + rows] for j in range(taps)], axis=1)

        windows[k, 0:length] = window(1, length).astype(BF16)
        edges = jnp.where(row == 0, window(0, 1), jnp.where(row == 1, window(length + 1, 1), 0.0))
        windows[k, length:] = edges.astype(BF16)
        for at in range(0, channels, block):
            cols = slice(at, at + block)
            v = jnp.dot(windows[k], conv_ref[:, cols], preferred_element_type=F32)
            value = snake(v, alpha_ref[0:1, cols], alpha_ref[1:2, cols])
            act[k, 0:length, cols] = value[:length].astype(BF16)
            act[k, length:, cols] = jnp.where(gone, 0.0, value[length:]).astype(BF16)
    up_copy.wait()
    for k in range(segs):
        for r in range(0, 8, 2):
            far = r + 12 if r < 4 else r - 4
            near_w = jnp.concatenate([up_ref[r + 4], up_ref[r + 5]], axis=1)
            far_w = jnp.concatenate([up_ref[far], up_ref[far + 1]], axis=1)
            near = jnp.dot(act[k, 0:length], near_w, preferred_element_type=F32)
            side = jnp.dot(act[k], far_w, preferred_element_type=F32)
            if r < 4:
                moved = [side[length : length + 1], side[: length - 1]]
            else:
                moved = [side[1:length], side[length + 1 : length + 2]]
            res = near + jnp.concatenate(moved, axis=0)
            rows_out[k, pl.ds(r, length, stride=8), :] = res[:, :width]
            rows_out[k, pl.ds(r + 1, length, stride=8), :] = res[:, width:]
        out_copy(k).start()
    for k in range(segs):
        out_copy(k).wait()


def decode(place, slabs, conv, alpha, first_up):
    segs = len(slabs)
    length = slabs[0].shape[0] - 4 * EDGE
    channels = conv.shape[1]
    width = first_up.shape[2]
    lat = slabs[0].shape[1]
    return pl.pallas_call(
        functools.partial(decoder_kernel, segs),
        out_shape=jax.ShapeDtypeStruct((segs, 8 * length, width), F32),
        in_specs=[pl.BlockSpec(memory_space=pltpu.SMEM)]
        + [whole()] * (segs + 2)
        + [pl.BlockSpec(memory_space=pl.ANY)],
        out_specs=pl.BlockSpec(memory_space=pl.ANY),
        scratch_shapes=[
            pltpu.VMEM((length + 16, lat), F32),
            pltpu.VMEM((segs, length + 16, conv.shape[0]), BF16),
            pltpu.VMEM((segs, length + 16, channels), BF16),
            pltpu.VMEM(first_up.shape, BF16),
            pltpu.VMEM((segs, 8 * length, width), F32),
            pltpu.SemaphoreType.DMA((segs,)),
            pltpu.SemaphoreType.DMA,
        ],
        compiler_params=params(52),
        cost_estimate=FREE,
    )(place, *slabs, conv, alpha, first_up)


def local(
    frames,
    expert_ids,
    gate_weights,
    up_weight,
    down_weight,
    out_weight,
    in_conv,
    snake_first,
    first_up,
):
    rows, _ = frames.shape
    n = lax.axis_size("expert")
    segs = lax.axis_size("seg")
    quarter, half = n // 4, n // 2
    capacity = -(-(3 * rows // n) // 16) * 16
    me = lax.axis_index("expert")
    place = jnp.stack([me, jnp.int32(n)]).astype(jnp.int32)
    inner = range(quarter, 3 * quarter)
    across_by = 3 * quarter
    is_inner = ((me >= quarter) & (me < across_by)).astype(jnp.int32)

    def swap(value, k, members=range(n)):
        return lax.ppermute(value, "expert", [(i, i ^ k) for i in members])

    across = swap(frames, across_by, inner)
    ids_t = expert_ids.T
    across_ids = swap(ids_t, across_by, inner)
    own = jnp.stack([me, 0]).astype(jnp.int32)
    chunks = make_slots(own, range(half), (ids_t, frames), capacity)
    near = [chunks[0]] + [swap(chunks[k], k) for k in range(1, half)]
    origin = jnp.stack([me ^ (is_inner * across_by), is_inner]).astype(jnp.int32)
    sent = make_slots(
        origin, range(half, n), (ids_t, frames, across_ids, across), capacity
    )
    far = []
    for k, value in zip(range(half, n), sent):
        pairs = [(i, i ^ (k ^ across_by if i in inner else k)) for i in range(n)]
        far.append(lax.ppermute(value, "expert", [(i, j) for i, j in pairs if i != j]))

    base = jnp.dot(frames, out_weight, preferred_element_type=F32)

    def edges(value):
        return jnp.concatenate([value[:EDGE], value[rows - EDGE :]], axis=0)

    lat = base.shape[1]
    packed = jnp.concatenate(
        [edges(base), edges(expert_ids).astype(F32), edges(gate_weights)], axis=1
    )
    left = lax.ppermute(packed, "expert", [(i, i + 1) for i in range(n - 1)])
    right = lax.ppermute(packed, "expert", [(i + 1, i) for i in range(n - 1)])

    def extended(value, columns, fill):
        parts = [left[EDGE:, columns], value.astype(F32), right[:EDGE, columns], left[:EDGE, columns]]
        rest = jnp.full((EDGE, value.shape[1]), fill, F32)
        return jnp.concatenate(parts + [rest], axis=0)

    ids_all = extended(expert_ids, slice(lat, lat + 2), -1).astype(jnp.int32)
    gates_all = extended(gate_weights, slice(lat + 2, lat + 4), 0)
    base_all = extended(base, slice(0, lat), 0)
    pick, scale = make_table(place, ids_all, gates_all, n, capacity)
    folded = fold_weights(down_weight[0], out_weight.T)

    up = up_weight[0]
    known = [near_group(near[:quarter], up, folded), near_group(near[quarter:], up, folded)]
    place, pick, scale, base_all, known = lax.optimization_barrier(
        (place, pick, scale, base_all, known)
    )
    back = far_group(n, place, sent[quarter], far, known, up, folded)
    parts = [back[0]] + [swap(back[k], k) for k in range(1, n)]
    slab = combine(parts, pick, scale, base_all)

    slabs = [slab] + [
        lax.ppermute(slab, "seg", [(i, i ^ k) for i in range(segs)]) for k in range(1, segs)
    ]
    spot = jnp.stack([lax.axis_index("seg"), me, jnp.int32(n)]).astype(jnp.int32)
    alpha = jnp.stack([snake_first * (1.0 / math.pi), 1.0 / snake_first])
    conv = in_conv.reshape(-1, in_conv.shape[2])
    return decode(spot, slabs, conv, alpha, first_up)


def solution(mesh):
    placed = (
        P(("seg", "expert"), None),
        P(("seg", "expert"), None),
        P(("seg", "expert"), None),
        P("expert", None, None),
        P("expert", None, None),
        P(),
        P(),
        P(),
        P(None, None, "seg"),
    )
    return jax.shard_map(
        local, mesh=mesh, in_specs=placed, out_specs=P(None, "expert", "seg"), check_vma=False
    )
```

time: 107 us -> 111 us (1.037)
  local copies, waits for them, and re-layouts: 9.61 us -> 18.9 us
  starting transfers between devices: 42.6 us -> 33.6 us
  waiting for transfers between devices: 12.2 us -> 15.3 us
  Pallas kernels: 41.3 us -> 39.4 us
  matrix products: 0 us -> 1.51 us
  other arithmetic: 0.13 us -> 1.25 us
    ppermute x19 -> x21, starting transfers between devices: 42.6 us -> 33.6 us  [the longest x12 19.9 us: swap(): return lax.ppermute(value, 'expert', [(i, i ^ k) for i in members])]
    concatenate x0 -> x5, local copies, waits for them, and re-layouts: none -> 5.36 us  [the longest x3 5.19 us: extended(): return jnp.concatenate(parts + [rest], axis=0)]
    ppermute x19 -> x21, waiting for transfers between devices: 12.2 us -> 15.3 us  [the longest x4 6.6 us: local(): lax.ppermute(value, 'expert', [(i, j) for i, j in pairs if i != j])]
    slice x1 -> x7, local copies, waits for them, and re-layouts: 0.01 us -> 2.98 us  [the longest x3 1.54 us: edges(): return jnp.concatenate([value[:EDGE], value[rows - EDGE:]], axis=0)]
    pallas_call x6, Pallas kernels: 19.8 us -> 17.7 us  [the longest x2 7.87 us: near_group(): pl.pallas_call(functools.partial(near_kernel, count), out_shape=jax.Shape...]
    dot_general x0 -> x1, matrix products: none -> 1.51 us  [local(): base = jnp.dot(frames, out_weight, preferred_element_type=F32)]
    unnamed x18 -> x21, local copies, waits for them, and re-layouts: 9.6 us -> 9.8 us
  transfers between devices with their start and end apart: 19 -> 21, of which waited for: 7 -> 8; matrix products, arithmetic and copies ran while one was open for 2% -> 12% of each run, Pallas kernels for 20% -> 14%
where the time goes in v3:
time: 111 us; the launch traced here: 110 us
  Pallas kernels  39.4 us (35%)
  starting transfers between devices  33.6 us (30%)
  local copies, waits for them, and re-layouts  18.9 us (17%)
  waiting for transfers between devices  15.3 us (14%)
  matrix products  1.51 us (1%)
  other arithmetic  1.25 us (1%)
    ppermute x12, starting transfers between devices, swap(): return lax.ppermute(value, 'expert', [(i, i ^ k) for i in members])  19.9 us
    pallas_call x1, Pallas kernels, decode(): pl.pallas_call(functools.partial(decoder_kernel, segs), out_shape=jax.Sha...  18.6 us
    unnamed x21, local copies, waits for them, and re-layouts  9.8 us
    pallas_call x2, Pallas kernels, near_group(): pl.pallas_call(functools.partial(near_kernel, count), out_shape=jax.Shape...  7.87 us
    ppermute x4, waiting for transfers between devices, local(): lax.ppermute(value, 'expert', [(i, j) for i, j in pairs if i != j])  6.6 us
    ppermute x4, starting transfers between devices, local(): lax.ppermute(value, 'expert', [(i, j) for i, j in pairs if i != j])  6.55 us
    concatenate x3, local copies, waits for them, and re-layouts, extended(): return jnp.concatenate(parts + [rest], axis=0)  5.19 us
    ppermute x12, waiting for transfers between devices, swap(): return lax.ppermute(value, 'expert', [(i, i ^ k) for i in members])  5.19 us
  transfers between devices with their start and end apart: 21, of which 8 were waited for; matrix products, arithmetic and copies ran while one was open for 12% of the time, Pallas kernels for 14%

profile of v3, /device:TPU:0, one launch (start us, length us, event | category | flops | bytes accessed | tf_op | source)
XLA Modules:
  0.0 110.5 jit_solution(1239120651726981701)
XLA Ops:
  3.2 1.5 %fusion.6 = f32[256,64]{1,0:T(8,128)S(1)} fusion(bf16[256,1536]{1,0:T(8,128)(2,1)} %refs_1_.3, bf16[1536,64]{0,1:T(8,128)(2,1)} %param.14), kind=kOutput, calls=%fused_computation.16 | convolution fusion | flops 50331648 | bytes 1048576 | tf_op jit(solution)/shard_map/dot_general | solution.py:396
  5.0 2.3 %collective-permute-start = (f32[8,68]{1,0:T(8,128)S(1)}, f32[8,68]{1,0:T(8,128)S(1)}, u32[]{:S(2)}, u32[]{:S(2)}) collective-permute-start(f32[8,68]{1,0:T(8,128)S(1)} %pad_maximum_fusion.1), channel_id=1, source_target_pairs={{0,1},{1,2},{2,3},{3,4},{4,5},{5,6},{6,7},{8,9},{9,10},{10,11},{11... | collective-permute-start | bytes 6536 | tf_op jit(solution)/shard_map/ppermute | solution.py:405
  9.2 2.0 %shard_map.92 = (bf16[96,1536]{1,0:T(8,128)(2,1)S(1)}, bf16[96,1536]{1,0:T(8,128)(2,1)}, bf16[96,1536]{1,0:T(8,128)(2,1)}, bf16[96,1536]{1,0:T(8,128)(2,1)}) custom-call(s32[2]{0:T(128)S(1)} %pad_add_fusion.3.origin_ref, s32[2,256]{1,0:T(2,128)S(1)} %bitcast.19, bf16[256,1536]{1,0:T(8,128)(2,1)S(1)} %copy-done.2), custom_call_target="tpu_custom_call" | custom-call | tf_op jit(solution)/shard_map/pallas_call | solution.py:75
  11.3 7.2 %collective-permute-start.2 = (bf16[96,1536]{1,0:T(8,128)(2,1)}, bf16[96,1536]{1,0:T(8,128)(2,1)S(1)}, u32[]{:S(2)}, u32[]{:S(2)}) collective-permute-start(bf16[96,1536]{1,0:T(8,128)(2,1)} %get-tuple-element.32), channel_id=1, source_target_pairs={{0,1},{1,0},{2,3},{3,2},{4,5},{5,4},{6,7},{7,6},{8,9},{9,8},{10,11... | collective-permute-start | bytes 884744 | tf_op jit(solution)/shard_map/ppermute | solution.py:379
  18.4 1.6 %collective-permute-start.3 = (bf16[96,1536]{1,0:T(8,128)(2,1)}, bf16[96,1536]{1,0:T(8,128)(2,1)S(1)}, u32[]{:S(2)}, u32[]{:S(2)}) collective-permute-start(bf16[96,1536]{1,0:T(8,128)(2,1)} %get-tuple-element.33), channel_id=1, source_target_pairs={{0,2},{1,3},{2,0},{3,1},{4,6},{5,7},{6,4},{7,5},{8,10},{9,11},{10,... | collective-permute-start | bytes 884744 | tf_op jit(solution)/shard_map/ppermute | solution.py:379
  23.1 2.8 %copy-done.4 = bf16[1,2048,1536]{2,1,0:T(8,128)(2,1)S(1)} copy-done((bf16[1,2048,1536]{2,1,0:T(8,128)(2,1)S(1)}, bf16[1,2048,1536]{2,1,0:T(8,128)(2,1)}, u32[]{:S(2)}) %copy-start.4) | copy-done | bytes 6291480
  26.8 2.5 %shard_map.93.refs_3_.refs_9_ = bf16[2048,128]{1,0:T(8,128)(2,1)S(1)} custom-call(bf16[2048,1536]{1,0:T(8,128)(2,1)S(1)} %bitcast.16, bf16[64,1536]{1,0:T(8,128)(2,1)S(1)} %bitcast.17), custom_call_target="tpu_custom_call" | custom-call | tf_op jit(solution)/shard_map/pallas_call | solution.py:98
  32.5 2.1 %shard_map.96 = (bf16[96,1536]{1,0:T(8,128)(2,1)}, bf16[96,1536]{1,0:T(8,128)(2,1)}, bf16[96,1536]{1,0:T(8,128)(2,1)S(1)}, bf16[96,1536]{1,0:T(8,128)(2,1)}) custom-call(s32[2]{0:T(128)S(1)} %pad_add_fusion.4.origin_ref, s32[2,256]{1,0:T(2,128)S(1)} %bitcast.20, bf16[256,1536]{1,0:T(8,128)(2,1)S(1)} %copy-done.3, ...), custom_call_target="tpu_custom_call" | custom-call | tf_op jit(solution)/shard_map/pallas_call | solution.py:75
  36.7 2.0 %collective-permute-start.10 = (bf16[96,1536]{1,0:T(8,128)(2,1)}, bf16[96,1536]{1,0:T(8,128)(2,1)}, u32[]{:S(2)}, u32[]{:S(2)}) collective-permute-start(bf16[96,1536]{1,0:T(8,128)(2,1)} %get-tuple-element.39), channel_id=1, source_target_pairs={{0,7},{1,6},{2,3},{3,2},{4,5},{5,4},{6,1},{7,0},{8,15},{9,14},{10,... | collective-permute-start | bytes 884744 | tf_op jit(solution)/shard_map/ppermute | solution.py:394
  38.7 2.4 %collective-permute-start.9 = (bf16[96,1536]{1,0:T(8,128)(2,1)S(1)}, bf16[96,1536]{1,0:T(8,128)(2,1)}, u32[]{:S(2)}, u32[]{:S(2)}) collective-permute-start(bf16[96,1536]{1,0:T(8,128)(2,1)S(1)} %get-tuple-element.36.refs_1_), channel_id=1, source_target_pairs={{0,6},{1,7},{6,0},{7,1},{8,14},{9,15},{14,8},{15,9},{16,22},{17,23... | collective-permute-start | bytes 884744 | tf_op jit(solution)/shard_map/ppermute | solution.py:394
  41.2 2.3 %concatenate.25 = f32[272,2]{1,0:T(8,128)S(1)} concatenate(f32[4,2]{1,0:T(4,128)} %get-tuple-element.62, f32[256,2]{1,0:T(8,128)} %copy.36, f32[4,2]{1,0:T(4,128)S(1)} %get-tuple-element.64, f32[4,2]{1,0:T(4,128)} %get-tuple-element.61, f32[4,2]{1,0:T(4,128)S(1)} %broadcast.7), dimensions={0} | concatenate | bytes 4352 | tf_op jit(solution)/shard_map/concatenate | solution.py:411
  43.6 2.3 %concatenate.26.gates_ref = f32[272,2]{1,0:T(8,128)S(1)} concatenate(f32[4,2]{1,0:T(4,128)} %get-tuple-element.60, f32[256,2]{1,0:T(8,128)} %copy.37, f32[4,2]{1,0:T(4,128)S(1)} %get-tuple-element.63, f32[4,2]{1,0:T(4,128)} %get-tuple-element.59, f32[4,2]{1,0:T(4,128)S(1)} %broadcast.8), dimensions={0} | concatenate | bytes 4352 | tf_op jit(solution)/shard_map/concatenate | solution.py:411
  48.4 2.8 %copy-done = bf16[1,1536,2048]{2,1,0:T(8,128)(2,1)S(1)} copy-done((bf16[1,1536,2048]{2,1,0:T(8,128)(2,1)S(1)}, bf16[1,1536,2048]{2,1,0:T(8,128)(2,1)}, u32[]{:S(2)}) %copy-start) | copy-done | bytes 6291480
  51.2 3.5 %shard_map.94.refs_6_ = bf16[2,96,128]{2,1,0:T(8,128)(2,1)S(1)} custom-call(bf16[96,1536]{1,0:T(8,128)(2,1)S(1)} %get-tuple-element.31.refs_0_, bf16[96,1536]{1,0:T(8,128)(2,1)S(1)} %collective-permute-done.2.refs_1_, bf16[1536,2048]{1,0:T(8,128)(2,1)S(1)} %bitcast.13, bf16[2048,128]{1,0:T(8,128)(2,1)S(1)} %shard_map.93.refs_3_.refs_9_), custom_call_target="tpu_custom_call" | custom-call | tf_op jit(solution)/shard_map/pallas_call | solution.py:190
  54.7 4.4 %shard_map.95.refs_7_ = bf16[2,96,128]{2,1,0:T(8,128)(2,1)S(1)} custom-call(bf16[96,1536]{1,0:T(8,128)(2,1)S(1)} %collective-permute-done.3.refs_0_, bf16[96,1536]{1,0:T(8,128)(2,1)} %collective-permute-done.4.refs_1_, bf16[1536,2048]{1,0:T(8,128)(2,1)S(1)} %bitcast.14, bf16[2048,128]{1,0:T(8,128)(2,1)S(1)} %shard_map.93.refs_3_.refs_9_), custom_call_target="tpu_custom_call" | custom-call | tf_op jit(solution)/shard_map/pallas_call | solution.py:190
  60.6 5.1 %collective-permute-done.9.refs_4_ = bf16[96,1536]{1,0:T(8,128)(2,1)} collective-permute-done((bf16[96,1536]{1,0:T(8,128)(2,1)S(1)}, bf16[96,1536]{1,0:T(8,128)(2,1)}, u32[]{:S(2)}, u32[]{:S(2)}) %collective-permute-start.9) | collective-permute-done | bytes 294944 | tf_op jit(solution)/shard_map/ppermute | solution.py:394
  65.7 4.4 %shard_map.97 = (bf16[128,128]{1,0:T(8,128)(2,1)S(1)}, bf16[128,128]{1,0:T(8,128)(2,1)S(1)}, bf16[128,128]{1,0:T(8,128)(2,1)S(1)}, bf16[128,128]{1,0:T(8,128)(2,...) custom-call(s32[2]{0:T(128)S(1)} %pad_add_fusion.2.place_ref.refs_0_, ...), custom_call_target="tpu_custom_call" | custom-call | tf_op jit(solution)/shard_map/pallas_call | solution.py:229
  72.1 2.7 %collective-permute-start.14 = (bf16[128,128]{1,0:T(8,128)(2,1)S(1)}, bf16[128,128]{1,0:T(8,128)(2,1)S(1)}, u32[]{:S(2)}, u32[]{:S(2)}) collective-permute-start(bf16[128,128]{1,0:T(8,128)(2,1)S(1)} %get-tuple-element.46), channel_id=1, source_target_pairs={{0,4},{1,5},{2,6},{3,7},{4,0},{5,1},{6,2},{7,3},{8,12},{9,13},{10,... | collective-permute-start | bytes 98312 | tf_op jit(solution)/shard_map/ppermute | solution.py:379
  75.1 3.6 %collective-permute-start.16 = (bf16[128,128]{1,0:T(8,128)(2,1)S(1)}, bf16[128,128]{1,0:T(8,128)(2,1)S(1)}, u32[]{:S(2)}, u32[]{:S(2)}) collective-permute-start(bf16[128,128]{1,0:T(8,128)(2,1)S(1)} %get-tuple-element.48), channel_id=1, source_target_pairs={{0,6},{1,7},{2,4},{3,5},{4,2},{5,3},{6,0},{7,1},{8,14},{9,15},{10,... | collective-permute-start | bytes 98312 | tf_op jit(solution)/shard_map/ppermute | solution.py:379
  79.4 1.9 %collective-permute-done.16.refs_6_ = bf16[128,128]{1,0:T(8,128)(2,1)S(1)} collective-permute-done((bf16[128,128]{1,0:T(8,128)(2,1)S(1)}, bf16[128,128]{1,0:T(8,128)(2,1)S(1)}, u32[]{:S(2)}, u32[]{:S(2)}) %collective-permute-start.16) | collective-permute-done | bytes 32800 | tf_op jit(solution)/shard_map/ppermute | solution.py:379
  81.3 2.5 %collective-permute-done.17.refs_7_ = bf16[128,128]{1,0:T(8,128)(2,1)S(1)} collective-permute-done((bf16[128,128]{1,0:T(8,128)(2,1)S(1)}, bf16[128,128]{1,0:T(8,128)(2,1)S(1)}, u32[]{:S(2)}, u32[]{:S(2)}) %collective-permute-start.17) | collective-permute-done | bytes 32800 | tf_op jit(solution)/shard_map/ppermute | solution.py:379
  84.6 2.4 %collective-permute-start.20 = (bf16[272,64]{1,0:T(8,128)(2,1)S(1)}, bf16[272,64]{1,0:T(8,128)(2,1)S(1)}, u32[]{:S(2)}, u32[]{:S(2)}) collective-permute-start(bf16[272,64]{1,0:T(8,128)(2,1)S(1)} %shard_map.98.refs_0_), channel_id=1, source_target_pairs={{0,24},{8,16},{16,8},{24,0},{1,25},{9,17},{17,9},{25,1},{2,26},{10... | collective-permute-start | bytes 104456 | tf_op jit(solution)/shard_map/ppermute | solution.py:429
  88.2 1.7 %collective-permute-done.20.refs_3_ = bf16[272,64]{1,0:T(8,128)(2,1)S(1)} collective-permute-done((bf16[272,64]{1,0:T(8,128)(2,1)S(1)}, bf16[272,64]{1,0:T(8,128)(2,1)S(1)}, u32[]{:S(2)}, u32[]{:S(2)}) %collective-permute-start.20) | collective-permute-done | bytes 34848 | tf_op jit(solution)/shard_map/ppermute | solution.py:429
  91.7 18.6 %shard_map.99 = f32[4,2048,128]{2,1,0:T(8,128)} custom-call(s32[3]{0:T(128)S(1)} %pad_add_fusion.1.place_ref, bf16[272,64]{1,0:T(8,128)(2,1)S(1)} %shard_map.98.refs_0_, bf16[272,64]{1,0:T(8,128)(2,1)S(1)} %collective-permute-done.18.refs_1_, bf16[272,64]{1,0:T(8,128)(2,1)S(1)} %collective-permute-done.19.refs_2_, ...), custom_call_target="tpu_custom_call" | custom-call | tf_op jit(solution)/shard_map/pallas_call | solution.py:335
  (77 shorter events, 25.5 us)
Async XLA Ops:
  0.0 32.5 %copy-start.7 = (s32[256,2]{0,1:T(2,128)S(1)}, s32[256,2]{0,1:T(2,128)}, u32[]{:S(2)}) copy-start(s32[256,2]{0,1:T(2,128)} %param.10) | copy-start | bytes 6148
  0.0 32.5 %copy-start.3 = (bf16[256,1536]{1,0:T(8,128)(2,1)S(1)}, bf16[256,1536]{1,0:T(8,128)(2,1)}, u32[]{:S(2)}) copy-start(bf16[256,1536]{1,0:T(8,128)(2,1)} %refs_1_.3) | copy-start | bytes 2359300
  0.0 31.3 %collective-permute-start.5 = (s32[2,256]{1,0:T(2,128)}, s32[2,256]{1,0:T(2,128)S(1)}, u32[]{:S(2)}, u32[]{:S(2)}) collective-permute-start(s32[2,256]{1,0:T(2,128)} %bitcast.18), channel_id=1, source_target_pairs={{2,4},{3,5},{4,2},{5,3},{10,12},{11,13},{12,10},{13,11},{18,20},{1... | collective-permute-start | bytes 6152 | tf_op jit(solution)/shard_map/ppermute | solution.py:379
  0.8 31.7 %collective-permute-start.6 = (bf16[256,1536]{1,0:T(8,128)(2,1)}, bf16[256,1536]{1,0:T(8,128)(2,1)S(1)}, u32[]{:S(2)}, u32[]{:S(2)}) collective-permute-start(bf16[256,1536]{1,0:T(8,128)(2,1)} %refs_1_.3), channel_id=1, source_target_pairs={{2,4},{3,5},{4,2},{5,3},{10,12},{11,13},{12,10},{13,11},{18,20},{1... | collective-permute-start | bytes 2359304 | tf_op jit(solution)/shard_map/ppermute | solution.py:379
  5.0 24.3 %collective-permute-start = (f32[8,68]{1,0:T(8,128)S(1)}, f32[8,68]{1,0:T(8,128)S(1)}, u32[]{:S(2)}, u32[]{:S(2)}) collective-permute-start(f32[8,68]{1,0:T(8,128)S(1)} %pad_maximum_fusion.1), channel_id=1, source_target_pairs={{0,1},{1,2},{2,3},{3,4},{4,5},{5,6},{6,7},{8,9},{9,10},{10,11},{11... | collective-permute-start | bytes 6536 | tf_op jit(solution)/shard_map/ppermute | solution.py:405
  11.3 25.5 %collective-permute-start.2 = (bf16[96,1536]{1,0:T(8,128)(2,1)}, bf16[96,1536]{1,0:T(8,128)(2,1)S(1)}, u32[]{:S(2)}, u32[]{:S(2)}) collective-permute-start(bf16[96,1536]{1,0:T(8,128)(2,1)} %get-tuple-element.32), channel_id=1, source_target_pairs={{0,1},{1,0},{2,3},{3,2},{4,5},{5,4},{6,7},{7,6},{8,9},{9,8},{10,11... | collective-permute-start | bytes 884744 | tf_op jit(solution)/shard_map/ppermute | solution.py:379
  18.4 20.3 %collective-permute-start.3 = (bf16[96,1536]{1,0:T(8,128)(2,1)}, bf16[96,1536]{1,0:T(8,128)(2,1)S(1)}, u32[]{:S(2)}, u32[]{:S(2)}) collective-permute-start(bf16[96,1536]{1,0:T(8,128)(2,1)} %get-tuple-element.33), channel_id=1, source_target_pairs={{0,2},{1,3},{2,0},{3,1},{4,6},{5,7},{6,4},{7,5},{8,10},{9,11},{10,... | collective-permute-start | bytes 884744 | tf_op jit(solution)/shard_map/ppermute | solution.py:379
  29.3 6.2 %collective-permute-start.1 = (f32[8,68]{1,0:T(8,128)S(1)}, f32[8,68]{1,0:T(8,128)S(1)}, u32[]{:S(2)}, u32[]{:S(2)}) collective-permute-start(f32[8,68]{1,0:T(8,128)S(1)} %pad_maximum_fusion.1), channel_id=1, source_target_pairs={{1,0},{2,1},{3,2},{4,3},{5,4},{6,5},{7,6},{9,8},{10,9},{11,10},{12... | collective-permute-start | bytes 6536 | tf_op jit(solution)/shard_map/ppermute | solution.py:406
  31.3 23.3 %collective-permute-start.4 = (bf16[96,1536]{1,0:T(8,128)(2,1)}, bf16[96,1536]{1,0:T(8,128)(2,1)}, u32[]{:S(2)}, u32[]{:S(2)}) collective-permute-start(bf16[96,1536]{1,0:T(8,128)(2,1)} %get-tuple-element.34), channel_id=1, source_target_pairs={{0,3},{1,2},{2,1},{3,0},{4,7},{5,6},{6,5},{7,4},{8,11},{9,10},{10,... | collective-permute-start | bytes 884744 | tf_op jit(solution)/shard_map/ppermute | solution.py:379
  34.6 24.5 %collective-permute-start.7 = (bf16[96,1536]{1,0:T(8,128)(2,1)}, bf16[96,1536]{1,0:T(8,128)(2,1)S(1)}, u32[]{:S(2)}, u32[]{:S(2)}) collective-permute-start(bf16[96,1536]{1,0:T(8,128)(2,1)} %get-tuple-element.37), channel_id=1, source_target_pairs={{0,4},{1,5},{2,0},{3,1},{4,6},{5,7},{6,2},{7,3},{8,12},{9,13},{10,... | collective-permute-start | bytes 884744 | tf_op jit(solution)/shard_map/ppermute | solution.py:394
  35.5 23.6 %collective-permute-start.8 = (bf16[96,1536]{1,0:T(8,128)(2,1)}, bf16[96,1536]{1,0:T(8,128)(2,1)S(1)}, u32[]{:S(2)}, u32[]{:S(2)}) collective-permute-start(bf16[96,1536]{1,0:T(8,128)(2,1)} %get-tuple-element.38), channel_id=1, source_target_pairs={{0,5},{1,4},{2,1},{3,0},{4,7},{5,6},{6,3},{7,2},{8,13},{9,12},{10,... | collective-permute-start | bytes 884744 | tf_op jit(solution)/shard_map/ppermute | solution.py:394
  36.7 23.9 %collective-permute-start.10 = (bf16[96,1536]{1,0:T(8,128)(2,1)}, bf16[96,1536]{1,0:T(8,128)(2,1)}, u32[]{:S(2)}, u32[]{:S(2)}) collective-permute-start(bf16[96,1536]{1,0:T(8,128)(2,1)} %get-tuple-element.39), channel_id=1, source_target_pairs={{0,7},{1,6},{2,3},{3,2},{4,5},{5,4},{6,1},{7,0},{8,15},{9,14},{10,... | collective-permute-start | bytes 884744 | tf_op jit(solution)/shard_map/ppermute | solution.py:394
  38.7 27.0 %collective-permute-start.9 = (bf16[96,1536]{1,0:T(8,128)(2,1)S(1)}, bf16[96,1536]{1,0:T(8,128)(2,1)}, u32[]{:S(2)}, u32[]{:S(2)}) collective-permute-start(bf16[96,1536]{1,0:T(8,128)(2,1)S(1)} %get-tuple-element.36.refs_1_), channel_id=1, source_target_pairs={{0,6},{1,7},{6,0},{7,1},{8,14},{9,15},{14,8},{15,9},{16,22},{17,23... | collective-permute-start | bytes 884744 | tf_op jit(solution)/shard_map/ppermute | solution.py:394
  54.6 16.0 %copy-start.9 = (f32[2048]{0:T(1024)S(1)}, f32[2048]{0:T(1024)}, u32[]{:S(2)}) copy-start(f32[2048]{0:T(1024)} %param.16) | copy-start | bytes 24580
  70.2 4.9 %collective-permute-start.11 = (bf16[128,128]{1,0:T(8,128)(2,1)S(1)}, bf16[128,128]{1,0:T(8,128)(2,1)S(1)}, u32[]{:S(2)}, u32[]{:S(2)}) collective-permute-start(bf16[128,128]{1,0:T(8,128)(2,1)S(1)} %get-tuple-element.43), channel_id=1, source_target_pairs={{0,1},{1,0},{2,3},{3,2},{4,5},{5,4},{6,7},{7,6},{8,9},{9,8},{10,11... | collective-permute-start | bytes 98312 | tf_op jit(solution)/shard_map/ppermute | solution.py:379
  70.6 8.0 %collective-permute-start.12 = (bf16[128,128]{1,0:T(8,128)(2,1)S(1)}, bf16[128,128]{1,0:T(8,128)(2,1)S(1)}, u32[]{:S(2)}, u32[]{:S(2)}) collective-permute-start(bf16[128,128]{1,0:T(8,128)(2,1)S(1)} %get-tuple-element.44), channel_id=1, source_target_pairs={{0,2},{1,3},{2,0},{3,1},{4,6},{5,7},{6,4},{7,5},{8,10},{9,11},{10,... | collective-permute-start | bytes 98312 | tf_op jit(solution)/shard_map/ppermute | solution.py:379
  70.7 8.0 %collective-permute-start.13 = (bf16[128,128]{1,0:T(8,128)(2,1)S(1)}, bf16[128,128]{1,0:T(8,128)(2,1)S(1)}, u32[]{:S(2)}, u32[]{:S(2)}) collective-permute-start(bf16[128,128]{1,0:T(8,128)(2,1)S(1)} %get-tuple-element.45), channel_id=1, source_target_pairs={{0,3},{1,2},{2,1},{3,0},{4,7},{5,6},{6,5},{7,4},{8,11},{9,10},{10,... | collective-permute-start | bytes 98312 | tf_op jit(solution)/shard_map/ppermute | solution.py:379
  72.1 6.6 %collective-permute-start.14 = (bf16[128,128]{1,0:T(8,128)(2,1)S(1)}, bf16[128,128]{1,0:T(8,128)(2,1)S(1)}, u32[]{:S(2)}, u32[]{:S(2)}) collective-permute-start(bf16[128,128]{1,0:T(8,128)(2,1)S(1)} %get-tuple-element.46), channel_id=1, source_target_pairs={{0,4},{1,5},{2,6},{3,7},{4,0},{5,1},{6,2},{7,3},{8,12},{9,13},{10,... | collective-permute-start | bytes 98312 | tf_op jit(solution)/shard_map/ppermute | solution.py:379
  74.8 4.6 %collective-permute-start.15 = (bf16[128,128]{1,0:T(8,128)(2,1)S(1)}, bf16[128,128]{1,0:T(8,128)(2,1)S(1)}, u32[]{:S(2)}, u32[]{:S(2)}) collective-permute-start(bf16[128,128]{1,0:T(8,128)(2,1)S(1)} %get-tuple-element.47), channel_id=1, source_target_pairs={{0,5},{1,4},{2,7},{3,6},{4,1},{5,0},{6,3},{7,2},{8,13},{9,12},{10,... | collective-permute-start | bytes 98312 | tf_op jit(solution)/shard_map/ppermute | solution.py:379
  75.1 6.2 %collective-permute-start.16 = (bf16[128,128]{1,0:T(8,128)(2,1)S(1)}, bf16[128,128]{1,0:T(8,128)(2,1)S(1)}, u32[]{:S(2)}, u32[]{:S(2)}) collective-permute-start(bf16[128,128]{1,0:T(8,128)(2,1)S(1)} %get-tuple-element.48), channel_id=1, source_target_pairs={{0,6},{1,7},{2,4},{3,5},{4,2},{5,3},{6,0},{7,1},{8,14},{9,15},{10,... | collective-permute-start | bytes 98312 | tf_op jit(solution)/shard_map/ppermute | solution.py:379
  78.6 5.2 %collective-permute-start.17 = (bf16[128,128]{1,0:T(8,128)(2,1)S(1)}, bf16[128,128]{1,0:T(8,128)(2,1)S(1)}, u32[]{:S(2)}, u32[]{:S(2)}) collective-permute-start(bf16[128,128]{1,0:T(8,128)(2,1)S(1)} %get-tuple-element.49), channel_id=1, source_target_pairs={{0,7},{1,6},{2,5},{3,4},{4,3},{5,2},{6,1},{7,0},{8,15},{9,14},{10,... | collective-permute-start | bytes 98312 | tf_op jit(solution)/shard_map/ppermute | solution.py:379
  84.6 5.3 %collective-permute-start.20 = (bf16[272,64]{1,0:T(8,128)(2,1)S(1)}, bf16[272,64]{1,0:T(8,128)(2,1)S(1)}, u32[]{:S(2)}, u32[]{:S(2)}) collective-permute-start(bf16[272,64]{1,0:T(8,128)(2,1)S(1)} %shard_map.98.refs_0_), channel_id=1, source_target_pairs={{0,24},{8,16},{16,8},{24,0},{1,25},{9,17},{17,9},{25,1},{2,26},{10... | collective-permute-start | bytes 104456 | tf_op jit(solution)/shard_map/ppermute | solution.py:429
  86.9 4.4 %collective-permute-start.19 = (bf16[272,64]{1,0:T(8,128)(2,1)S(1)}, bf16[272,64]{1,0:T(8,128)(2,1)S(1)}, u32[]{:S(2)}, u32[]{:S(2)}) collective-permute-start(bf16[272,64]{1,0:T(8,128)(2,1)S(1)} %shard_map.98.refs_0_), channel_id=1, source_target_pairs={{0,16},{8,24},{16,0},{24,8},{1,17},{9,25},{17,1},{25,9},{2,18},{10... | collective-permute-start | bytes 104456 | tf_op jit(solution)/shard_map/ppermute | solution.py:429
  87.4 4.3 %collective-permute-start.18 = (bf16[272,64]{1,0:T(8,128)(2,1)S(1)}, bf16[272,64]{1,0:T(8,128)(2,1)S(1)}, u32[]{:S(2)}, u32[]{:S(2)}) collective-permute-start(bf16[272,64]{1,0:T(8,128)(2,1)S(1)} %shard_map.98.refs_0_), channel_id=1, source_target_pairs={{0,8},{8,0},{16,24},{24,16},{1,9},{9,1},{17,25},{25,17},{2,10},{10... | collective-permute-start | bytes 104456 | tf_op jit(solution)/shard_map/ppermute | solution.py:429
  (7 other events, 17.5 us)

commit v4 on v3

--- a/solution.py
+++ b/solution.py
@@ -109,10 +109,51 @@
     )(down, out_w_t)
 
 
-def table_kernel(place_ref, ids_ref, gates_ref, pick_ref, scale_ref):
+def info_kernel(frames_ref, out_w_ref, ids_ref, gates_ref, info_ref, edge_ref):
+    rows = frames_ref.shape[0]
+    lat = out_w_ref.shape[0]
+    base = lax.dot_general(
+        frames_ref[...], out_w_ref[...], (((1,), (1,)), ((), ())), preferred_element_type=F32
+    )
+    lines = jnp.concatenate(
+        [ids_ref[...].astype(F32), gates_ref[...], jnp.zeros((124, rows), F32)], axis=0
+    )
+    info_ref[...] = jnp.concatenate([base, jnp.transpose(lines)[:, : 128 - lat]], axis=1)
+    edge_ref[0:EDGE] = info_ref[0:EDGE]
+    edge_ref[EDGE:] = info_ref[rows - EDGE : rows]
+
+
+def make_info(frames, out_w_t, ids_t, gates_t):
+    rows = frames.shape[0]
+    return pl.pallas_call(
+        info_kernel,
+        out_shape=[
+            jax.ShapeDtypeStruct((rows, 128), F32),
+            jax.ShapeDtypeStruct((2 * EDGE, 128), F32),
+        ],
+        in_specs=[whole()] * 4,
+        out_specs=[whole()] * 2,
+        compiler_params=params(16),
+        cost_estimate=FREE,
+    )(frames, out_w_t, ids_t, gates_t)
+
+
+def table_kernel(lat, place_ref, info_ref, left_ref, right_ref, pick_ref, scale_ref, base_ref):
     n, span, columns = pick_ref.shape
-    rows = span - 4 * EDGE
+    rows = info_ref.shape[0]
     capacity = columns - 2 * EDGE_ROWS
+    me, size = place_ref[0], place_ref[1]
+    info = jnp.concatenate(
+        [
+            left_ref[EDGE:],
+            info_ref[...],
+            right_ref[:EDGE],
+            left_ref[:EDGE],
+            jnp.zeros((EDGE, 128), F32),
+        ],
+        axis=0,
+    )
+    base_ref[...] = info[:, :lat]
 
     def code(i):
         own = 1024 + token_key(i - EDGE, rows)
@@ -122,12 +163,15 @@
 
     line = lax.broadcasted_iota(jnp.int32, (span, 1), 0)
     line_code = code(line)
-    other = code(lax.broadcasted_iota(jnp.int32, (span, span), 1))
+    other = code(lax.broadcasted_iota(jnp.int32, (1, span), 1))
     earlier = (other < line_code) & (other >= (line_code >> 10) * 1024)
     before = line_code < 1024
     after = (line_code >= 2048) & (line_code < 3072)
-    lost = (before & (place_ref[0] == 0)) | (after & (place_ref[0] == place_ref[1] - 1))
-    ids = jnp.where(lost | (line_code >= 3072), -1, ids_ref[...] ^ place_ref[0])
+    lost = (before & ((me == 0) | (me == size // 2))) | (
+        after & ((me == size - 1) | (me == size // 2 - 1))
+    )
+    ids = info[:, lat : lat + 2].astype(jnp.int32) ^ me
+    ids = jnp.where(lost | (line_code >= 3072), -1, ids)
     step = lax.broadcasted_iota(jnp.int32, (span, 128), 1)
     first = ids[:, 0:1] == step
     second = ids[:, 1:2] == step
@@ -135,26 +179,28 @@
     rank = jnp.dot(one_hot(earlier), one_hot(named), preferred_element_type=F32)
     rank = rank + jnp.where(before, capacity, jnp.where(after, capacity + EDGE_ROWS, 0)).astype(F32)
     rank = jnp.where(named, rank, -1.0)
-    gates = gates_ref[...]
-    scale_ref[...] = jnp.where(first, gates[:, 0:1], jnp.where(second, gates[:, 1:2], 0.0))
+    scale_ref[...] = jnp.where(
+        first, info[:, lat + 2 : lat + 3], jnp.where(second, info[:, lat + 3 : lat + 4], 0.0)
+    )
     slot = lax.broadcasted_iota(jnp.int32, (span, columns), 1).astype(F32)
     for k in range(n):
         pick_ref[k] = one_hot(slot == rank[:, k : k + 1])
 
 
-def make_table(place, ids, gates, n, capacity):
-    span = ids.shape[0]
-    return pl.pallas_call(
-        table_kernel,
+def make_table(place, info, left, right, lat, n, capacity):
+    span = info.shape[0] + 4 * EDGE
+    return pl.pallas_call(
+        functools.partial(table_kernel, lat),
         out_shape=[
             jax.ShapeDtypeStruct((n, span, capacity + 2 * EDGE_ROWS), BF16),
             jax.ShapeDtypeStruct((span, 128), F32),
-        ],
-        in_specs=[pl.BlockSpec(memory_space=pltpu.SMEM)] + [whole()] * 2,
-        out_specs=[whole()] * 2,
+            jax.ShapeDtypeStruct((span, lat), F32),
+        ],
+        in_specs=[pl.BlockSpec(memory_space=pltpu.SMEM)] + [whole()] * 3,
+        out_specs=[whole()] * 3,
         compiler_params=params(16),
         cost_estimate=FREE,
-    )(place, ids, gates)
+    )(place, info, left, right)
 
 
 def expert_rows(rows, up_ref, folded_ref):
@@ -174,89 +220,82 @@
     return jnp.concatenate([high, low], axis=1)
 
 
-def near_kernel(count, *refs):
-    chunk_refs = refs[:count]
-    up_ref, folded_ref, out_ref = refs[count:]
-    capacity = chunk_refs[0].shape[0]
-    rows = jnp.concatenate([ref[...] for ref in chunk_refs], axis=0)
-    both = expert_rows(rows, up_ref, folded_ref)
-    for j in range(count):
-        out_ref[j] = both[j * capacity : (j + 1) * capacity]
-
-
-def near_group(chunks, up, folded):
-    count = len(chunks)
-    capacity = chunks[0].shape[0]
-    return pl.pallas_call(
-        functools.partial(near_kernel, count),
-        out_shape=jax.ShapeDtypeStruct((count, capacity, folded.shape[1]), BF16),
-        in_specs=[whole()] * (count + 2),
-        out_specs=whole(),
-        compiler_params=params(24),
-        cost_estimate=FREE,
-    )(*chunks, up, folded)
-
-
-def far_kernel(n, *refs):
-    quarter, half = n // 4, n // 2
-    place_ref, local_ref = refs[:2]
-    chunk_refs = refs[2 : 2 + half]
-    known_refs = refs[2 + half : 4 + half]
-    up_ref, folded_ref = refs[4 + half : 6 + half]
-    outs, held = refs[6 + half : -1], refs[-1]
-    capacity = local_ref.shape[0]
-    me = place_ref[0]
-    is_inner = (me >= quarter) & (me < 3 * quarter)
-    chunks = [ref[...] for ref in chunk_refs]
-    chunks[quarter] = jnp.where(is_inner, local_ref[...], chunks[quarter])
-    held[0:quarter] = known_refs[0][...]
-    held[quarter:half] = known_refs[1][...]
-    both = expert_rows(jnp.concatenate(chunks, axis=0), up_ref, folded_ref)
-    for j in range(half):
-        held[half + j] = both[j * capacity : (j + 1) * capacity]
-    for k, ref in enumerate(outs):
+def write_returns(n, me, held, first, outs):
+    capacity = held.shape[1]
+    half = n // 2
+    for j, ref in enumerate(outs):
+        k = first + j
         to = me ^ k
-        left = me ^ jnp.where(to > 0, to - 1, to)
-        right = me ^ jnp.where(to < n - 1, to + 1, to)
+        place = to % half
+        left = me ^ jnp.where(place > 0, to - 1, to)
+        right = me ^ jnp.where(place < half - 1, to + 1, to)
         ref[0:capacity] = held[k]
         ref[capacity : capacity + EDGE_ROWS] = held[left, 0:EDGE_ROWS]
         ref[capacity + EDGE_ROWS :] = held[right, 0:EDGE_ROWS]
 
 
-def far_group(n, place, local_chunk, chunks, known, up, folded):
+def group_kernel(n, far, place_ref, local_ref, *refs):
+    quarter, half = n // 4, n // 2
+    chunk_refs = refs[: half - 1 + far]
+    up_ref, folded_ref = refs[half - 1 + far : half + 1 + far]
+    outs, held = refs[half + 1 + far : -1], refs[-1]
+    capacity = local_ref.shape[0]
+    me = place_ref[0]
+    chunks = [ref[...] for ref in chunk_refs]
+    if far:
+        is_inner = (me >= quarter) & (me < 3 * quarter)
+        chunks[quarter] = jnp.where(is_inner, local_ref[...], chunks[quarter])
+    else:
+        chunks = [local_ref[...]] + chunks
+    both = expert_rows(jnp.concatenate(chunks, axis=0), up_ref, folded_ref)
+    first = half if far else 0
+    for j in range(half):
+        held[first + j] = both[j * capacity : (j + 1) * capacity]
+    write_returns(n, me, held, first, outs)
+
+
+def run_group(n, far, place, local_chunk, chunks, up, folded):
     capacity = local_chunk.shape[0]
     lanes = folded.shape[1]
     return pl.pallas_call(
-        functools.partial(far_kernel, n),
-        out_shape=[jax.ShapeDtypeStruct((capacity + 2 * EDGE_ROWS, lanes), BF16)] * n,
-        in_specs=[pl.BlockSpec(memory_space=pltpu.SMEM)] + [whole()] * (n // 2 + 5),
-        out_specs=[whole()] * n,
+        functools.partial(group_kernel, n, far),
+        out_shape=[jax.ShapeDtypeStruct((capacity + 2 * EDGE_ROWS, lanes), BF16)] * (n // 2),
+        in_specs=[pl.BlockSpec(memory_space=pltpu.SMEM)] + [whole()] * (len(chunks) + 3),
+        out_specs=[whole()] * (n // 2),
         scratch_shapes=[pltpu.VMEM((n, capacity, lanes), BF16)],
         compiler_params=params(24),
         cost_estimate=FREE,
-    )(place, local_chunk, *chunks, *known, up, folded)
-
-
-def combine_kernel(n, *refs):
+    )(place, local_chunk, *chunks, up, folded)
+
+
+def combine_kernel(n, place_ref, *refs):
     part_refs = refs[:n]
-    pick_ref, scale_ref, base_ref, low_ref = refs[n:]
-    lat = base_ref.shape[1]
+    pick_ref, scale_ref, base_ref, low_ref, middle_ref = refs[n:]
+    span, lat = base_ref.shape
     latent = base_ref[...]
     for k in range(n):
         picked = jnp.dot(pick_ref[k], part_refs[k][...], preferred_element_type=F32)
         latent = latent + scale_ref[:, k : k + 1] * (picked[:, :lat] + picked[:, lat:])
-    low_ref[...] = latent.astype(BF16)
-
-
-def combine(parts, pick, scale, base):
+    low = latent.astype(BF16)
+    low_ref[...] = low
+    middle_ref[...] = jnp.where(
+        place_ref[0] >= place_ref[1] // 2, low[:EDGE_ROWS], low[span - EDGE_ROWS :]
+    )
+
+
+def combine(place, parts, pick, scale, base):
     n = len(parts)
     return pl.pallas_call(
         functools.partial(combine_kernel, n),
-        out_shape=jax.ShapeDtypeStruct(base.shape, BF16),
-        in_specs=[whole()] * (n + 3),
-        out_specs=whole(),
+        out_shape=[
+            jax.ShapeDtypeStruct(base.shape, BF16),
+            jax.ShapeDtypeStruct((EDGE_ROWS, base.shape[1]), BF16),
+        ],
+        in_specs=[pl.BlockSpec(memory_space=pltpu.SMEM)] + [whole()] * (n + 3),
+        out_specs=[whole()] * 2,
         compiler_params=params(16),
-    )(*parts, pick, scale, base)
+        cost_estimate=FREE,
+    )(place, *parts, pick, scale, base)
 
 
 def snake(v, turns_row, inverse_row):
@@ -276,7 +315,7 @@
     span, channels = act.shape[1:]
     length = span - 16
     width = up_ref.shape[2]
-    halo, lat = lat_refs[0].shape
+    lat = lat_refs[0].shape[1]
     taps = conv_ref.shape[0] // lat
     block = 256
     own = place_ref[0]
@@ -292,7 +331,16 @@
     edge_row = lax.broadcasted_iota(jnp.int32, (16, block), 0)
     gone = ((edge_row == 0) & is_first) | ((edge_row == 1) & is_last)
     for k in range(segs):
-        padded[0:halo, :] = lat_refs[k][...].astype(F32)
+        slab = lat_refs[k][...].astype(F32)
+        middle = slab[span:]
+        padded[...] = slab[:span]
+        before = jnp.where(place_ref[1] == place_ref[2] // 2, middle[:EDGE], slab[:EDGE])
+        end = length + EDGE
+        after = jnp.where(
+            place_ref[1] == place_ref[2] // 2 - 1, middle[EDGE : 2 * EDGE], slab[end : end + EDGE]
+        )
+        padded[0:EDGE] = before
+        padded[end : end + EDGE] = after
 
         def window(start, rows):
             return jnp.concatenate([padded[start + j : start + j + rows] for j in range(taps)], axis=1)
@@ -328,7 +376,7 @@
 
 def decode(place, slabs, conv, alpha, first_up):
     segs = len(slabs)
-    length = slabs[0].shape[0] - 4 * EDGE
+    length = slabs[0].shape[0] - 4 * EDGE - EDGE_ROWS
     channels = conv.shape[1]
     width = first_up.shape[2]
     lat = slabs[0].shape[1]
@@ -383,8 +431,16 @@
     across_ids = swap(ids_t, across_by, inner)
     own = jnp.stack([me, 0]).astype(jnp.int32)
     chunks = make_slots(own, range(half), (ids_t, frames), capacity)
-    near = [chunks[0]] + [swap(chunks[k], k) for k in range(1, half)]
+    near = [swap(chunks[k], k) for k in range(1, half)]
+    lat = out_weight.shape[1]
+    info, edge = make_info(frames, out_weight.T, ids_t, gate_weights.T)
+    left = lax.ppermute(edge, "expert", [(i, i + 1) for i in range(n - 1)])
+    right = lax.ppermute(edge, "expert", [(i + 1, i) for i in range(n - 1)])
+    folded = fold_weights(down_weight[0], out_weight.T)
     origin = jnp.stack([me ^ (is_inner * across_by), is_inner]).astype(jnp.int32)
+    origin, near, left, right, folded = lax.optimization_barrier(
+        (origin, near, left, right, folded)
+    )
     sent = make_slots(
         origin, range(half, n), (ids_t, frames, across_ids, across), capacity
     )
@@ -392,38 +448,17 @@
     for k, value in zip(range(half, n), sent):
         pairs = [(i, i ^ (k ^ across_by if i in inner else k)) for i in range(n)]
         far.append(lax.ppermute(value, "expert", [(i, j) for i, j in pairs if i != j]))
-
-    base = jnp.dot(frames, out_weight, preferred_element_type=F32)
-
-    def edges(value):
-        return jnp.concatenate([value[:EDGE], value[rows - EDGE :]], axis=0)
-
-    lat = base.shape[1]
-    packed = jnp.concatenate(
-        [edges(base), edges(expert_ids).astype(F32), edges(gate_weights)], axis=1
-    )
-    left = lax.ppermute(packed, "expert", [(i, i + 1) for i in range(n - 1)])
-    right = lax.ppermute(packed, "expert", [(i + 1, i) for i in range(n - 1)])
-
-    def extended(value, columns, fill):
-        parts = [left[EDGE:, columns], value.astype(F32), right[:EDGE, columns], left[:EDGE, columns]]
-        rest = jnp.full((EDGE, value.shape[1]), fill, F32)
-        return jnp.concatenate(parts + [rest], axis=0)
-
-    ids_all = extended(expert_ids, slice(lat, lat + 2), -1).astype(jnp.int32)
-    gates_all = extended(gate_weights, slice(lat + 2, lat + 4), 0)
-    base_all = extended(base, slice(0, lat), 0)
-    pick, scale = make_table(place, ids_all, gates_all, n, capacity)
-    folded = fold_weights(down_weight[0], out_weight.T)
-
     up = up_weight[0]
-    known = [near_group(near[:quarter], up, folded), near_group(near[quarter:], up, folded)]
-    place, pick, scale, base_all, known = lax.optimization_barrier(
-        (place, pick, scale, base_all, known)
-    )
-    back = far_group(n, place, sent[quarter], far, known, up, folded)
-    parts = [back[0]] + [swap(back[k], k) for k in range(1, n)]
-    slab = combine(parts, pick, scale, base_all)
+    info, chunk, _ = lax.optimization_barrier((info, chunks[0], sent))
+    pick, scale, base = make_table(place, info, left, right, lat, n, capacity)
+    back = run_group(n, False, place, chunk, near, up, folded)
+    parts = [back[0]] + [swap(back[k], k) for k in range(1, half)]
+    place, pick, scale, base, parts = lax.optimization_barrier((place, pick, scale, base, parts))
+    back = run_group(n, True, place, sent[quarter], far, up, folded)
+    parts += [swap(back[k], half + k) for k in range(half)]
+    slab, middle = combine(place, parts, pick, scale, base)
+    middle = lax.ppermute(middle, "expert", [(half - 1, half), (half, half - 1)])
+    slab = jnp.concatenate([slab, middle], axis=0)
 
     slabs = [slab] + [
         lax.ppermute(slab, "seg", [(i, i ^ k) for i in range(segs)]) for k in range(1, segs)

time: 111 us -> 113 us (1.018)
  waiting for transfers between devices: 15.3 us -> 27.4 us
  local copies, waits for them, and re-layouts: 18.9 us -> 7.33 us
  starting transfers between devices: 33.6 us -> 41.1 us
  Pallas kernels: 39.4 us -> 36.4 us
  matrix products: 1.51 us -> 0 us
    ppermute x12, waiting for transfers between devices: 5.19 us -> 21.1 us  [swap(): return lax.ppermute(value, 'expert', [(i, i ^ k) for i in members])]
    ppermute x2 -> x3, starting transfers between devices: 3.63 us -> 12.8 us  [the longest x1 10.6 us: local(): left = lax.ppermute(edge, 'expert', [(i, i + 1) for i in range(n - 1)])]
    ppermute x4, waiting for transfers between devices: 6.6 us -> 0.01 us  [local(): lax.ppermute(value, 'expert', [(i, j) for i, j in pairs if i != j])]
    concatenate x5 -> x1, local copies, waits for them, and re-layouts: 5.36 us -> 0.01 us  [local(): slab = jnp.concatenate([slab, middle], axis=0)]
    ppermute x12, starting transfers between devices: 19.9 us -> 14.7 us  [swap(): return lax.ppermute(value, 'expert', [(i, i ^ k) for i in members])]
    ppermute x4, starting transfers between devices: 6.55 us -> 10.1 us  [local(): lax.ppermute(value, 'expert', [(i, j) for i, j in pairs if i != j])]
    pallas_call x5, Pallas kernels: 14.3 us -> 10.8 us  [the longest x2 7.99 us: run_group(): pl.pallas_call(functools.partial(group_kernel, n, far), out_shape=[jax.Sh...]
    slice x7 -> x0, local copies, waits for them, and re-layouts: 2.98 us -> none  [the longest x3 1.54 us: edges(): return jnp.concatenate([value[:EDGE], value[rows - EDGE:]], axis=0)]
  transfers between devices with their start and end apart: 21 -> 22, of which waited for: 8 -> 11; matrix products, arithmetic and copies ran while one was open for 12% -> 0% of each run, Pallas kernels for 14% -> 9%
where the time goes in v4:
time: 113 us
  starting transfers between devices  41.1 us (36%)
  Pallas kernels  36.4 us (32%)
  waiting for transfers between devices  27.4 us (24%)
  local copies, waits for them, and re-layouts  7.33 us (6%)
    ppermute x12, waiting for transfers between devices, swap(): return lax.ppermute(value, 'expert', [(i, i ^ k) for i in members])  21.1 us
    pallas_call x1, Pallas kernels, decode(): pl.pallas_call(functools.partial(decoder_kernel, segs), out_shape=jax.Sha...  19.9 us
    ppermute x12, starting transfers between devices, swap(): return lax.ppermute(value, 'expert', [(i, i ^ k) for i in members])  14.7 us
    ppermute x1, starting transfers between devices, local(): left = lax.ppermute(edge, 'expert', [(i, i + 1) for i in range(n - 1)])  10.6 us
    ppermute x4, starting transfers between devices, local(): lax.ppermute(value, 'expert', [(i, j) for i, j in pairs if i != j])  10.1 us
    pallas_call x2, Pallas kernels, run_group(): pl.pallas_call(functools.partial(group_kernel, n, far), out_shape=[jax.Sh...  7.99 us
    unnamed x21, local copies, waits for them, and re-layouts  7.32 us
    ppermute x3, waiting for transfers between devices, local(): lax.ppermute(slab, 'seg', [(i, i ^ k) for i in range(segs)])  3.75 us
  transfers between devices with their start and end apart: 22, of which 11 were waited for; matrix products, arithmetic and copies ran while one was open for 0% of the time, Pallas kernels for 9%

profile of v4, /device:TPU:0, one launch (start us, length us, event | category | flops | bytes accessed | tf_op | source)
XLA Modules:
  0.0 112.9 jit_solution(10053745633569345042)
XLA Ops:
  2.7 1.8 %shard_map.92 = (bf16[96,1536]{1,0:T(8,128)(2,1)S(1)}, bf16[96,1536]{1,0:T(8,128)(2,1)}, bf16[96,1536]{1,0:T(8,128)(2,1)S(1)}, bf16[96,1536]{1,0:T(8,128)(2,1)S(1)}) custom-call(s32[2]{0:T(128)S(1)} %get-tuple-element.88.origin_ref, s32[2,256]{1,0:T(2,128)S(1)} %bitcast.18, bf16[256,1536]{1,0:T(8,128)(2,1)S(1)} %copy-done.1), custom_call_target="tpu_custom_call" | custom-call | tf_op jit(solution)/shard_map/pallas_call | solution.py:75
  5.0 5.4 %collective-permute-start.1 = (bf16[96,1536]{1,0:T(8,128)(2,1)S(1)}, bf16[96,1536]{1,0:T(8,128)(2,1)S(1)}, u32[]{:S(2)}, u32[]{:S(2)}) collective-permute-start(bf16[96,1536]{1,0:T(8,128)(2,1)S(1)} %get-tuple-element.48), channel_id=1, source_target_pairs={{0,2},{1,3},{2,0},{3,1},{4,6},{5,7},{6,4},{7,5},{8,10},{9,11},{10,... | collective-permute-start | bytes 884744 | tf_op jit(solution)/shard_map/ppermute | solution.py:427
  12.5 1.3 %collective-permute-start.4 = (f32[8,128]{1,0:T(8,128)S(1)}, f32[8,128]{1,0:T(8,128)S(1)}, u32[]{:S(2)}, u32[]{:S(2)}) collective-permute-start(f32[8,128]{1,0:T(8,128)S(1)} %get-tuple-element.50), channel_id=1, source_target_pairs={{1,0},{2,1},{3,2},{4,3},{5,4},{6,5},{7,6},{9,8},{10,9},{11,10},{12... | collective-permute-start | bytes 12296 | tf_op jit(solution)/shard_map/ppermute | solution.py:438
  13.8 1.8 %collective-permute-done.4.right_ref = f32[8,128]{1,0:T(8,128)S(1)} collective-permute-done((f32[8,128]{1,0:T(8,128)S(1)}, f32[8,128]{1,0:T(8,128)S(1)}, u32[]{:S(2)}, u32[]{:S(2)}) %collective-permute-start.4) | collective-permute-done | bytes 4128 | tf_op jit(solution)/shard_map/ppermute | solution.py:438
  15.5 10.6 %collective-permute-start.3 = (f32[8,128]{1,0:T(8,128)S(1)}, f32[8,128]{1,0:T(8,128)S(1)}, u32[]{:S(2)}, u32[]{:S(2)}) collective-permute-start(f32[8,128]{1,0:T(8,128)S(1)} %get-tuple-element.50), channel_id=1, source_target_pairs={{0,1},{1,2},{2,3},{3,4},{4,5},{5,6},{6,7},{8,9},{9,10},{10,11},{11... | collective-permute-start | bytes 12296 | tf_op jit(solution)/shard_map/ppermute | solution.py:437
  27.8 2.9 %copy-done.3 = bf16[1,2048,1536]{2,1,0:T(8,128)(2,1)S(1)} copy-done((bf16[1,2048,1536]{2,1,0:T(8,128)(2,1)S(1)}, bf16[1,2048,1536]{2,1,0:T(8,128)(2,1)}, u32[]{:S(2)}) %copy-start.3) | copy-done | bytes 6291480
  31.7 2.5 %shard_map.93.refs_4_.refs_5_ = bf16[2048,128]{1,0:T(8,128)(2,1)S(1)} custom-call(bf16[2048,1536]{1,0:T(8,128)(2,1)S(1)} %bitcast.14, bf16[64,1536]{1,0:T(8,128)(2,1)S(1)} %bitcast.16), custom_call_target="tpu_custom_call" | custom-call | tf_op jit(solution)/shard_map/pallas_call | solution.py:98
  34.3 1.3 %shard_map.94 = (bf16[96,1536]{1,0:T(8,128)(2,1)S(1)}, bf16[96,1536]{1,0:T(8,128)(2,1)S(1)}, bf16[96,1536]{1,0:T(8,128)(2,1)S(1)}, bf16[96,1536]{1,0:T(8,128)(2,1)S(1)}) custom-call(s32[2]{0:T(128)S(1)} %pad_add_fusion.3.origin_ref, s32[2,256]{1,0:T(2,128)S(1)} %bitcast.20, bf16[256,1536]{1,0:T(8,128)(2,1)S(1)} %copy-done.2, ...), custom_call_target="tpu_custom_call" | custom-call | tf_op jit(solution)/shard_map/pallas_call | solution.py:75
  35.6 4.6 %collective-permute-start.10 = (bf16[96,1536]{1,0:T(8,128)(2,1)S(1)}, bf16[96,1536]{1,0:T(8,128)(2,1)S(1)}, u32[]{:S(2)}, u32[]{:S(2)}) collective-permute-start(bf16[96,1536]{1,0:T(8,128)(2,1)S(1)} %get-tuple-element.52), channel_id=1, source_target_pairs={{0,4},{1,5},{2,0},{3,1},{4,6},{5,7},{6,2},{7,3},{8,12},{9,13},{10,... | collective-permute-start | bytes 884744 | tf_op jit(solution)/shard_map/ppermute | solution.py:450
  40.2 1.2 %collective-permute-start.13 = (bf16[96,1536]{1,0:T(8,128)(2,1)S(1)}, bf16[96,1536]{1,0:T(8,128)(2,1)S(1)}, u32[]{:S(2)}, u32[]{:S(2)}) collective-permute-start(bf16[96,1536]{1,0:T(8,128)(2,1)S(1)} %get-tuple-element.55), channel_id=1, source_target_pairs={{0,7},{1,6},{2,3},{3,2},{4,5},{5,4},{6,1},{7,0},{8,15},{9,14},{10,... | collective-permute-start | bytes 884744 | tf_op jit(solution)/shard_map/ppermute | solution.py:450
  41.5 4.3 %collective-permute-start.12 = (bf16[96,1536]{1,0:T(8,128)(2,1)S(1)}, bf16[96,1536]{1,0:T(8,128)(2,1)S(1)}, u32[]{:S(2)}, u32[]{:S(2)}) collective-permute-start(bf16[96,1536]{1,0:T(8,128)(2,1)S(1)} %get-tuple-element.54.local_ref), channel_id=1, source_target_pairs={{0,6},{1,7},{6,0},{7,1},{8,14},{9,15},{14,8},{15,9},{16,22},{17,23... | collective-permute-start | bytes 884744 | tf_op jit(solution)/shard_map/ppermute | solution.py:450
  45.7 4.0 %shard_map.96 = (bf16[128,128]{1,0:T(8,128)(2,1)S(1)}, bf16[128,128]{1,0:T(8,128)(2,1)S(1)}, bf16[128,128]{1,0:T(8,128)(2,1)S(1)}, bf16[128,128]{1,0:T(8,128)(2,1)S(1)}) custom-call(s32[2]{0:T(128)S(1)} %get-tuple-element.71.place_ref, bf16[96,1536]{1,0:T(8,128)(2,1)S(1)} %get-tuple-element.62.local_ref, bf16[96,1536]{1,0:T(8,128)(2,1)S(1)} %collective-permute-done.refs_0_, ...), custom_call_target="tpu_custom_call" | custom-call | tf_op jit(solution)/shard_map/pallas_call | solution.py:260
  51.0 13.8 %collective-permute-done.8.refs_2_ = bf16[128,128]{1,0:T(8,128)(2,1)S(1)} collective-permute-done((bf16[128,128]{1,0:T(8,128)(2,1)S(1)}, bf16[128,128]{1,0:T(8,128)(2,1)S(1)}, u32[]{:S(2)}, u32[]{:S(2)}) %collective-permute-start.8) | collective-permute-done | bytes 32800 | tf_op jit(solution)/shard_map/ppermute | solution.py:427
  66.1 2.1 %collective-permute-done.9.refs_3_ = bf16[128,128]{1,0:T(8,128)(2,1)S(1)} collective-permute-done((bf16[128,128]{1,0:T(8,128)(2,1)S(1)}, bf16[128,128]{1,0:T(8,128)(2,1)S(1)}, u32[]{:S(2)}, u32[]{:S(2)}) %collective-permute-start.9) | collective-permute-done | bytes 32800 | tf_op jit(solution)/shard_map/ppermute | solution.py:427
  68.2 4.0 %shard_map.97 = (bf16[128,128]{1,0:T(8,128)(2,1)S(1)}, bf16[128,128]{1,0:T(8,128)(2,1)S(1)}, bf16[128,128]{1,0:T(8,128)(2,1)S(1)}, bf16[128,128]{1,0:T(8,128)(2,1)S(1)}) custom-call(s32[2]{0:T(128)S(1)} %get-tuple-element.71.place_ref, bf16[96,1536]{1,0:T(8,128)(2,1)S(1)} %get-tuple-element.54.local_ref, ...), custom_call_target="tpu_custom_call" | custom-call | tf_op jit(solution)/shard_map/pallas_call | solution.py:260
  72.2 3.7 %collective-permute-start.14 = (bf16[128,128]{1,0:T(8,128)(2,1)S(1)}, bf16[128,128]{1,0:T(8,128)(2,1)S(1)}, u32[]{:S(2)}, u32[]{:S(2)}) collective-permute-start(bf16[128,128]{1,0:T(8,128)(2,1)S(1)} %get-tuple-element.76), channel_id=1, source_target_pairs={{0,4},{1,5},{2,6},{3,7},{4,0},{5,1},{6,2},{7,3},{8,12},{9,13},{10,... | collective-permute-start | bytes 98312 | tf_op jit(solution)/shard_map/ppermute | solution.py:427
  75.9 2.1 %collective-permute-start.16 = (bf16[128,128]{1,0:T(8,128)(2,1)S(1)}, bf16[128,128]{1,0:T(8,128)(2,1)S(1)}, u32[]{:S(2)}, u32[]{:S(2)}) collective-permute-start(bf16[128,128]{1,0:T(8,128)(2,1)S(1)} %get-tuple-element.78), channel_id=1, source_target_pairs={{0,6},{1,7},{2,4},{3,5},{4,2},{5,3},{6,0},{7,1},{8,14},{9,15},{10,... | collective-permute-start | bytes 98312 | tf_op jit(solution)/shard_map/ppermute | solution.py:427
  77.9 1.3 %collective-permute-start.17 = (bf16[128,128]{1,0:T(8,128)(2,1)S(1)}, bf16[128,128]{1,0:T(8,128)(2,1)S(1)}, u32[]{:S(2)}, u32[]{:S(2)}) collective-permute-start(bf16[128,128]{1,0:T(8,128)(2,1)S(1)} %get-tuple-element.79), channel_id=1, source_target_pairs={{0,7},{1,6},{2,5},{3,4},{4,3},{5,2},{6,1},{7,0},{8,15},{9,14},{10,... | collective-permute-start | bytes 98312 | tf_op jit(solution)/shard_map/ppermute | solution.py:427
  80.4 1.2 %collective-permute-done.16.refs_6_ = bf16[128,128]{1,0:T(8,128)(2,1)S(1)} collective-permute-done((bf16[128,128]{1,0:T(8,128)(2,1)S(1)}, bf16[128,128]{1,0:T(8,128)(2,1)S(1)}, u32[]{:S(2)}, u32[]{:S(2)}) %collective-permute-start.16) | collective-permute-done | bytes 32800 | tf_op jit(solution)/shard_map/ppermute | solution.py:427
  81.6 1.7 %collective-permute-done.17.refs_7_ = bf16[128,128]{1,0:T(8,128)(2,1)S(1)} collective-permute-done((bf16[128,128]{1,0:T(8,128)(2,1)S(1)}, bf16[128,128]{1,0:T(8,128)(2,1)S(1)}, u32[]{:S(2)}, u32[]{:S(2)}) %collective-permute-start.17) | collective-permute-done | bytes 32800 | tf_op jit(solution)/shard_map/ppermute | solution.py:427
  85.4 2.5 %collective-permute-start.21 = (bf16[288,64]{1,0:T(8,128)(2,1)S(1)}, bf16[288,64]{1,0:T(8,128)(2,1)S(1)}, u32[]{:S(2)}, u32[]{:S(2)}) collective-permute-start(bf16[288,64]{1,0:T(8,128)(2,1)S(1)} %constant_dynamic-update-slice_fusion.refs_0_), channel_id=1, source_target_pairs={{0,24},{8,16},{16,8},{24,0},{1,25},{9,17},{17,9},{25,1},{2,26},{10... | collective-permute-start | bytes 110600 | tf_op jit(solution)/shard_map/ppermute | solution.py:464
  89.0 1.7 %collective-permute-done.21.refs_3_ = bf16[288,64]{1,0:T(8,128)(2,1)S(1)} collective-permute-done((bf16[288,64]{1,0:T(8,128)(2,1)S(1)}, bf16[288,64]{1,0:T(8,128)(2,1)S(1)}, u32[]{:S(2)}, u32[]{:S(2)}) %collective-permute-start.21) | collective-permute-done | bytes 36896 | tf_op jit(solution)/shard_map/ppermute | solution.py:464
  90.8 1.5 %collective-permute-done.20.refs_2_ = bf16[288,64]{1,0:T(8,128)(2,1)S(1)} collective-permute-done((bf16[288,64]{1,0:T(8,128)(2,1)S(1)}, bf16[288,64]{1,0:T(8,128)(2,1)S(1)}, u32[]{:S(2)}, u32[]{:S(2)}) %collective-permute-start.20) | collective-permute-done | bytes 36896 | tf_op jit(solution)/shard_map/ppermute | solution.py:464
  92.8 19.9 %shard_map.99 = f32[4,2048,128]{2,1,0:T(8,128)} custom-call(s32[3]{0:T(128)S(1)} %pad_add_fusion.place_ref, bf16[288,64]{1,0:T(8,128)(2,1)S(1)} %constant_dynamic-update-slice_fusion.refs_0_, bf16[288,64]{1,0:T(8,128)(2,1)S(1)} %collective-permute-done.19.refs_1_, bf16[288,64]{1,0:T(8,128)(2,1)S(1)} %collective-permute-done.20.refs_2_, ...), custom_call_target="tpu_custom_call" | custom-call | tf_op jit(solution)/shard_map/pallas_call | solution.py:383
  (56 shorter events, 15.2 us)
Async XLA Ops:
  0.0 34.3 %copy-start.7 = (s32[256,2]{0,1:T(2,128)S(1)}, s32[256,2]{0,1:T(2,128)}, u32[]{:S(2)}) copy-start(s32[256,2]{0,1:T(2,128)} %param.10) | copy-start | bytes 6148
  0.0 34.3 %collective-permute-start.6 = (bf16[256,1536]{1,0:T(8,128)(2,1)}, bf16[256,1536]{1,0:T(8,128)(2,1)S(1)}, u32[]{:S(2)}, u32[]{:S(2)}) collective-permute-start(bf16[256,1536]{1,0:T(8,128)(2,1)} %refs_1_.3), channel_id=1, source_target_pairs={{2,4},{3,5},{4,2},{5,3},{10,12},{11,13},{12,10},{13,11},{18,20},{1... | collective-permute-start | bytes 2359304 | tf_op jit(solution)/shard_map/ppermute | solution.py:427
  2.7 31.6 %copy-start.2 = (bf16[256,1536]{1,0:T(8,128)(2,1)S(1)}, bf16[256,1536]{1,0:T(8,128)(2,1)}, u32[]{:S(2)}) copy-start(bf16[256,1536]{1,0:T(8,128)(2,1)} %refs_1_.3) | copy-start | bytes 2359300
  4.5 29.7 %collective-permute-start = (bf16[96,1536]{1,0:T(8,128)(2,1)}, bf16[96,1536]{1,0:T(8,128)(2,1)S(1)}, u32[]{:S(2)}, u32[]{:S(2)}) collective-permute-start(bf16[96,1536]{1,0:T(8,128)(2,1)} %get-tuple-element.47), channel_id=1, source_target_pairs={{0,1},{1,0},{2,3},{3,2},{4,5},{5,4},{6,7},{7,6},{8,9},{9,8},{10,11... | collective-permute-start | bytes 884744 | tf_op jit(solution)/shard_map/ppermute | solution.py:427
  5.0 29.2 %collective-permute-start.1 = (bf16[96,1536]{1,0:T(8,128)(2,1)S(1)}, bf16[96,1536]{1,0:T(8,128)(2,1)S(1)}, u32[]{:S(2)}, u32[]{:S(2)}) collective-permute-start(bf16[96,1536]{1,0:T(8,128)(2,1)S(1)} %get-tuple-element.48), channel_id=1, source_target_pairs={{0,2},{1,3},{2,0},{3,1},{4,6},{5,7},{6,4},{7,5},{8,10},{9,11},{10,... | collective-permute-start | bytes 884744 | tf_op jit(solution)/shard_map/ppermute | solution.py:427
  10.3 23.9 %collective-permute-start.2 = (bf16[96,1536]{1,0:T(8,128)(2,1)S(1)}, bf16[96,1536]{1,0:T(8,128)(2,1)S(1)}, u32[]{:S(2)}, u32[]{:S(2)}) collective-permute-start(bf16[96,1536]{1,0:T(8,128)(2,1)S(1)} %get-tuple-element.49), channel_id=1, source_target_pairs={{0,3},{1,2},{2,1},{3,0},{4,7},{5,6},{6,5},{7,4},{8,11},{9,10},{10,... | collective-permute-start | bytes 884744 | tf_op jit(solution)/shard_map/ppermute | solution.py:427
  12.5 3.1 %collective-permute-start.4 = (f32[8,128]{1,0:T(8,128)S(1)}, f32[8,128]{1,0:T(8,128)S(1)}, u32[]{:S(2)}, u32[]{:S(2)}) collective-permute-start(f32[8,128]{1,0:T(8,128)S(1)} %get-tuple-element.50), channel_id=1, source_target_pairs={{1,0},{2,1},{3,2},{4,3},{5,4},{6,5},{7,6},{9,8},{10,9},{11,10},{12... | collective-permute-start | bytes 12296 | tf_op jit(solution)/shard_map/ppermute | solution.py:438
  15.5 11.5 %collective-permute-start.3 = (f32[8,128]{1,0:T(8,128)S(1)}, f32[8,128]{1,0:T(8,128)S(1)}, u32[]{:S(2)}, u32[]{:S(2)}) collective-permute-start(f32[8,128]{1,0:T(8,128)S(1)} %get-tuple-element.50), channel_id=1, source_target_pairs={{0,1},{1,2},{2,3},{3,4},{4,5},{5,6},{6,7},{8,9},{9,10},{10,11},{11... | collective-permute-start | bytes 12296 | tf_op jit(solution)/shard_map/ppermute | solution.py:437
  27.0 7.3 %collective-permute-start.5 = (s32[2,256]{1,0:T(2,128)}, s32[2,256]{1,0:T(2,128)S(1)}, u32[]{:S(2)}, u32[]{:S(2)}) collective-permute-start(s32[2,256]{1,0:T(2,128)} %bitcast.17), channel_id=1, source_target_pairs={{2,4},{3,5},{4,2},{5,3},{10,12},{11,13},{12,10},{13,11},{18,20},{1... | collective-permute-start | bytes 6152 | tf_op jit(solution)/shard_map/ppermute | solution.py:427
  35.6 32.5 %collective-permute-start.10 = (bf16[96,1536]{1,0:T(8,128)(2,1)S(1)}, bf16[96,1536]{1,0:T(8,128)(2,1)S(1)}, u32[]{:S(2)}, u32[]{:S(2)}) collective-permute-start(bf16[96,1536]{1,0:T(8,128)(2,1)S(1)} %get-tuple-element.52), channel_id=1, source_target_pairs={{0,4},{1,5},{2,0},{3,1},{4,6},{5,7},{6,2},{7,3},{8,12},{9,13},{10,... | collective-permute-start | bytes 884744 | tf_op jit(solution)/shard_map/ppermute | solution.py:450
  40.2 28.0 %collective-permute-start.11 = (bf16[96,1536]{1,0:T(8,128)(2,1)S(1)}, bf16[96,1536]{1,0:T(8,128)(2,1)S(1)}, u32[]{:S(2)}, u32[]{:S(2)}) collective-permute-start(bf16[96,1536]{1,0:T(8,128)(2,1)S(1)} %get-tuple-element.53), channel_id=1, source_target_pairs={{0,5},{1,4},{2,1},{3,0},{4,7},{5,6},{6,3},{7,2},{8,13},{9,12},{10,... | collective-permute-start | bytes 884744 | tf_op jit(solution)/shard_map/ppermute | solution.py:450
  40.2 28.0 %collective-permute-start.13 = (bf16[96,1536]{1,0:T(8,128)(2,1)S(1)}, bf16[96,1536]{1,0:T(8,128)(2,1)S(1)}, u32[]{:S(2)}, u32[]{:S(2)}) collective-permute-start(bf16[96,1536]{1,0:T(8,128)(2,1)S(1)} %get-tuple-element.55), channel_id=1, source_target_pairs={{0,7},{1,6},{2,3},{3,2},{4,5},{5,4},{6,1},{7,0},{8,15},{9,14},{10,... | collective-permute-start | bytes 884744 | tf_op jit(solution)/shard_map/ppermute | solution.py:450
  41.5 26.7 %collective-permute-start.12 = (bf16[96,1536]{1,0:T(8,128)(2,1)S(1)}, bf16[96,1536]{1,0:T(8,128)(2,1)S(1)}, u32[]{:S(2)}, u32[]{:S(2)}) collective-permute-start(bf16[96,1536]{1,0:T(8,128)(2,1)S(1)} %get-tuple-element.54.local_ref), channel_id=1, source_target_pairs={{0,6},{1,7},{6,0},{7,1},{8,14},{9,15},{14,8},{15,9},{16,22},{17,23... | collective-permute-start | bytes 884744 | tf_op jit(solution)/shard_map/ppermute | solution.py:450
  49.7 1.3 %collective-permute-start.7 = (bf16[128,128]{1,0:T(8,128)(2,1)S(1)}, bf16[128,128]{1,0:T(8,128)(2,1)S(1)}, u32[]{:S(2)}, u32[]{:S(2)}) collective-permute-start(bf16[128,128]{1,0:T(8,128)(2,1)S(1)} %get-tuple-element.68), channel_id=1, source_target_pairs={{0,1},{1,0},{2,3},{3,2},{4,5},{5,4},{6,7},{7,6},{8,9},{9,8},{10,11... | collective-permute-start | bytes 98312 | tf_op jit(solution)/shard_map/ppermute | solution.py:427
  51.0 13.8 %collective-permute-start.8 = (bf16[128,128]{1,0:T(8,128)(2,1)S(1)}, bf16[128,128]{1,0:T(8,128)(2,1)S(1)}, u32[]{:S(2)}, u32[]{:S(2)}) collective-permute-start(bf16[128,128]{1,0:T(8,128)(2,1)S(1)} %get-tuple-element.69), channel_id=1, source_target_pairs={{0,2},{1,3},{2,0},{3,1},{4,6},{5,7},{6,4},{7,5},{8,10},{9,11},{10,... | collective-permute-start | bytes 98312 | tf_op jit(solution)/shard_map/ppermute | solution.py:427
  64.8 3.3 %collective-permute-start.9 = (bf16[128,128]{1,0:T(8,128)(2,1)S(1)}, bf16[128,128]{1,0:T(8,128)(2,1)S(1)}, u32[]{:S(2)}, u32[]{:S(2)}) collective-permute-start(bf16[128,128]{1,0:T(8,128)(2,1)S(1)} %get-tuple-element.70), channel_id=1, source_target_pairs={{0,3},{1,2},{2,1},{3,0},{4,7},{5,6},{6,5},{7,4},{8,11},{9,10},{10,... | collective-permute-start | bytes 98312 | tf_op jit(solution)/shard_map/ppermute | solution.py:427
  72.2 7.1 %collective-permute-start.14 = (bf16[128,128]{1,0:T(8,128)(2,1)S(1)}, bf16[128,128]{1,0:T(8,128)(2,1)S(1)}, u32[]{:S(2)}, u32[]{:S(2)}) collective-permute-start(bf16[128,128]{1,0:T(8,128)(2,1)S(1)} %get-tuple-element.76), channel_id=1, source_target_pairs={{0,4},{1,5},{2,6},{3,7},{4,0},{5,1},{6,2},{7,3},{8,12},{9,13},{10,... | collective-permute-start | bytes 98312 | tf_op jit(solution)/shard_map/ppermute | solution.py:427
  75.9 4.5 %collective-permute-start.15 = (bf16[128,128]{1,0:T(8,128)(2,1)S(1)}, bf16[128,128]{1,0:T(8,128)(2,1)S(1)}, u32[]{:S(2)}, u32[]{:S(2)}) collective-permute-start(bf16[128,128]{1,0:T(8,128)(2,1)S(1)} %get-tuple-element.77), channel_id=1, source_target_pairs={{0,5},{1,4},{2,7},{3,6},{4,1},{5,0},{6,3},{7,2},{8,13},{9,12},{10,... | collective-permute-start | bytes 98312 | tf_op jit(solution)/shard_map/ppermute | solution.py:427
  75.9 5.8 %collective-permute-start.16 = (bf16[128,128]{1,0:T(8,128)(2,1)S(1)}, bf16[128,128]{1,0:T(8,128)(2,1)S(1)}, u32[]{:S(2)}, u32[]{:S(2)}) collective-permute-start(bf16[128,128]{1,0:T(8,128)(2,1)S(1)} %get-tuple-element.78), channel_id=1, source_target_pairs={{0,6},{1,7},{2,4},{3,5},{4,2},{5,3},{6,0},{7,1},{8,14},{9,15},{10,... | collective-permute-start | bytes 98312 | tf_op jit(solution)/shard_map/ppermute | solution.py:427
  77.9 5.3 %collective-permute-start.17 = (bf16[128,128]{1,0:T(8,128)(2,1)S(1)}, bf16[128,128]{1,0:T(8,128)(2,1)S(1)}, u32[]{:S(2)}, u32[]{:S(2)}) collective-permute-start(bf16[128,128]{1,0:T(8,128)(2,1)S(1)} %get-tuple-element.79), channel_id=1, source_target_pairs={{0,7},{1,6},{2,5},{3,4},{4,3},{5,2},{6,1},{7,0},{8,15},{9,14},{10,... | collective-permute-start | bytes 98312 | tf_op jit(solution)/shard_map/ppermute | solution.py:427
  84.5 0.9 collective-permute-start.18
  85.4 5.4 %collective-permute-start.21 = (bf16[288,64]{1,0:T(8,128)(2,1)S(1)}, bf16[288,64]{1,0:T(8,128)(2,1)S(1)}, u32[]{:S(2)}, u32[]{:S(2)}) collective-permute-start(bf16[288,64]{1,0:T(8,128)(2,1)S(1)} %constant_dynamic-update-slice_fusion.refs_0_), channel_id=1, source_target_pairs={{0,24},{8,16},{16,8},{24,0},{1,25},{9,17},{17,9},{25,1},{2,26},{10... | collective-permute-start | bytes 110600 | tf_op jit(solution)/shard_map/ppermute | solution.py:464
  87.9 4.4 %collective-permute-start.20 = (bf16[288,64]{1,0:T(8,128)(2,1)S(1)}, bf16[288,64]{1,0:T(8,128)(2,1)S(1)}, u32[]{:S(2)}, u32[]{:S(2)}) collective-permute-start(bf16[288,64]{1,0:T(8,128)(2,1)S(1)} %constant_dynamic-update-slice_fusion.refs_0_), channel_id=1, source_target_pairs={{0,16},{8,24},{16,0},{24,8},{1,17},{9,25},{17,1},{25,9},{2,18},{10... | collective-permute-start | bytes 110600 | tf_op jit(solution)/shard_map/ppermute | solution.py:464
  88.4 4.4 %collective-permute-start.19 = (bf16[288,64]{1,0:T(8,128)(2,1)S(1)}, bf16[288,64]{1,0:T(8,128)(2,1)S(1)}, u32[]{:S(2)}, u32[]{:S(2)}) collective-permute-start(bf16[288,64]{1,0:T(8,128)(2,1)S(1)} %constant_dynamic-update-slice_fusion.refs_0_), channel_id=1, source_target_pairs={{0,8},{8,0},{16,24},{24,16},{1,9},{9,1},{17,25},{25,17},{2,10},{10... | collective-permute-start | bytes 110600 | tf_op jit(solution)/shard_map/ppermute | solution.py:464
  (8 other events, 57.5 us)

commit v5 on v4

--- a/solution.py
+++ b/solution.py
@@ -46,10 +46,35 @@
     return mask.astype(F32).astype(BF16)
 
 
+def is_neighbour(k):
+    return k & (k + 1) == 0 and k > 0
+
+
+def edge_rows(frames, ids, gates):
+    rows, width = frames.shape
+    parts = []
+    for choice in range(2):
+        rest = gates[choice : choice + 1]
+        for _ in range(3):
+            part = rest.astype(BF16).astype(F32)
+            parts.append(part)
+            rest = rest - part
+    meta = jnp.concatenate([ids.astype(F32)] + parts, axis=0)
+    meta = jnp.concatenate([meta, jnp.zeros((8, width - rows), F32)], axis=1)
+    ends = [frames[:16].astype(F32)[:EDGE], frames[rows - 16 :].astype(F32)[16 - EDGE :]]
+    return jnp.concatenate(ends + [meta], axis=0).astype(BF16)
+
+
 def slots_kernel(steps, origin_ref, *refs):
     sources, out_refs = refs[: -len(steps)], refs[-len(steps) :]
     ids, frames = sources[0][...], sources[1][...]
-    if len(sources) > 2:
+    if len(sources) == 3:
+        capacity = out_refs[0].shape[0]
+        extra = edge_rows(frames, ids, sources[2][...])
+        for k, ref in zip(steps, out_refs):
+            if is_neighbour(k):
+                ref[capacity:] = extra
+    else:
         second = origin_ref[1] == 1
         ids = jnp.where(second, sources[2][...], ids)
         frames = jnp.where(second, sources[3][...], frames)
@@ -67,14 +92,19 @@
     slot = lax.broadcasted_iota(jnp.int32, (capacity, rows), 0).astype(F32)
     for j, ref in enumerate(out_refs):
         pick = one_hot(slot == rank[j : j + 1])
-        ref[...] = jnp.dot(pick, frames, preferred_element_type=F32).astype(BF16)
+        ref[0:capacity] = jnp.dot(pick, frames, preferred_element_type=F32).astype(BF16)
 
 
 def make_slots(origin, steps, sources, capacity):
     width = sources[1].shape[1]
     return pl.pallas_call(
         functools.partial(slots_kernel, steps),
-        out_shape=[jax.ShapeDtypeStruct((capacity, width), BF16)] * len(steps),
+        out_shape=[
+            jax.ShapeDtypeStruct(
+                (capacity + EDGE_ROWS * (len(sources) == 3 and is_neighbour(k)), width), BF16
+            )
+            for k in steps
+        ],
         in_specs=[pl.BlockSpec(memory_space=pltpu.SMEM)] + [whole()] * len(sources),
         out_specs=[whole()] * len(steps),
         compiler_params=params(24),
@@ -109,52 +139,53 @@
     )(down, out_w_t)
 
 
-def info_kernel(frames_ref, out_w_ref, ids_ref, gates_ref, info_ref, edge_ref):
-    rows = frames_ref.shape[0]
+def table_kernel(
+    links, place_ref, frames_ref, out_w_ref, ids_ref, gates_ref, *refs
+):
+    link_refs = refs[: len(links)]
+    pick_ref, scale_ref, base_ref = refs[len(links) :]
+    n, span, columns = pick_ref.shape
+    rows, width = frames_ref.shape
     lat = out_w_ref.shape[0]
-    base = lax.dot_general(
-        frames_ref[...], out_w_ref[...], (((1,), (1,)), ((), ())), preferred_element_type=F32
-    )
-    lines = jnp.concatenate(
-        [ids_ref[...].astype(F32), gates_ref[...], jnp.zeros((124, rows), F32)], axis=0
-    )
-    info_ref[...] = jnp.concatenate([base, jnp.transpose(lines)[:, : 128 - lat]], axis=1)
-    edge_ref[0:EDGE] = info_ref[0:EDGE]
-    edge_ref[EDGE:] = info_ref[rows - EDGE : rows]
-
-
-def make_info(frames, out_w_t, ids_t, gates_t):
-    rows = frames.shape[0]
-    return pl.pallas_call(
-        info_kernel,
-        out_shape=[
-            jax.ShapeDtypeStruct((rows, 128), F32),
-            jax.ShapeDtypeStruct((2 * EDGE, 128), F32),
-        ],
-        in_specs=[whole()] * 4,
-        out_specs=[whole()] * 2,
-        compiler_params=params(16),
-        cost_estimate=FREE,
-    )(frames, out_w_t, ids_t, gates_t)
-
-
-def table_kernel(lat, place_ref, info_ref, left_ref, right_ref, pick_ref, scale_ref, base_ref):
-    n, span, columns = pick_ref.shape
-    rows = info_ref.shape[0]
     capacity = columns - 2 * EDGE_ROWS
     me, size = place_ref[0], place_ref[1]
+
+    def rows_of(frames, lines):
+        base = lax.dot_general(
+            frames, out_w_ref[...], (((1,), (1,)), ((), ())), preferred_element_type=F32
+        )
+        lines = jnp.concatenate([lines, jnp.zeros((128 - lines.shape[0], rows), F32)], axis=0)
+        return base, jnp.transpose(lines)[:, : 128 - lat]
+
+    def neighbour(other):
+        extra = link_refs[0][capacity:]
+        for k, ref in zip(links[1:], link_refs[1:]):
+            extra = jnp.where((me ^ other) == k, ref[capacity:], extra)
+        meta = extra[:, :rows].astype(F32)[2 * EDGE :]
+        gates = [meta[j : j + 1] + meta[j + 1 : j + 2] + meta[j + 2 : j + 3] for j in (2, 5)]
+        base, lines = rows_of(extra, jnp.concatenate([meta[:2]] + gates, axis=0))
+        return jnp.concatenate(
+            [
+                jnp.concatenate([base[:EDGE], lines[:EDGE]], axis=1),
+                jnp.concatenate([base[EDGE : 2 * EDGE], lines[rows - EDGE :]], axis=1),
+            ],
+            axis=0,
+        )
+
+    left, right = neighbour(me - 1), neighbour(me + 1)
+    own = rows_of(
+        frames_ref[...], jnp.concatenate([ids_ref[...].astype(F32), gates_ref[...]], axis=0)
+    )
     info = jnp.concatenate(
         [
-            left_ref[EDGE:],
-            info_ref[...],
-            right_ref[:EDGE],
-            left_ref[:EDGE],
+            left[EDGE:],
+            jnp.concatenate(own, axis=1),
+            right[:EDGE],
+            left[:EDGE],
             jnp.zeros((EDGE, 128), F32),
         ],
         axis=0,
     )
-    base_ref[...] = info[:, :lat]
-
     def code(i):
         own = 1024 + token_key(i - EDGE, rows)
         late = jnp.where(i < rows + 3 * EDGE, i - rows - 2 * EDGE, 3072)
@@ -170,6 +201,7 @@
     lost = (before & ((me == 0) | (me == size // 2))) | (
         after & ((me == size - 1) | (me == size // 2 - 1))
     )
+    base_ref[...] = jnp.where(lost, 0.0, info[:, :lat])
     ids = info[:, lat : lat + 2].astype(jnp.int32) ^ me
     ids = jnp.where(lost | (line_code >= 3072), -1, ids)
     step = lax.broadcasted_iota(jnp.int32, (span, 128), 1)
@@ -187,20 +219,22 @@
         pick_ref[k] = one_hot(slot == rank[:, k : k + 1])
 
 
-def make_table(place, info, left, right, lat, n, capacity):
-    span = info.shape[0] + 4 * EDGE
+def make_table(place, frames, out_w_t, ids_t, gates_t, neighbours, n, capacity):
+    span = frames.shape[0] + 4 * EDGE
+    lat = out_w_t.shape[0]
+    links = tuple(neighbours)
     return pl.pallas_call(
-        functools.partial(table_kernel, lat),
+        functools.partial(table_kernel, links),
         out_shape=[
             jax.ShapeDtypeStruct((n, span, capacity + 2 * EDGE_ROWS), BF16),
             jax.ShapeDtypeStruct((span, 128), F32),
             jax.ShapeDtypeStruct((span, lat), F32),
         ],
-        in_specs=[pl.BlockSpec(memory_space=pltpu.SMEM)] + [whole()] * 3,
+        in_specs=[pl.BlockSpec(memory_space=pltpu.SMEM)] + [whole()] * (4 + len(links)),
         out_specs=[whole()] * 3,
         compiler_params=params(16),
         cost_estimate=FREE,
-    )(place, info, left, right)
+    )(place, frames, out_w_t, ids_t, gates_t, *[neighbours[k] for k in links])
 
 
 def expert_rows(rows, up_ref, folded_ref):
@@ -246,7 +280,7 @@
         is_inner = (me >= quarter) & (me < 3 * quarter)
         chunks[quarter] = jnp.where(is_inner, local_ref[...], chunks[quarter])
     else:
-        chunks = [local_ref[...]] + chunks
+        chunks = [local_ref[...]] + [chunk[:capacity] for chunk in chunks]
     both = expert_rows(jnp.concatenate(chunks, axis=0), up_ref, folded_ref)
     first = half if far else 0
     for j in range(half):
@@ -430,17 +464,12 @@
     ids_t = expert_ids.T
     across_ids = swap(ids_t, across_by, inner)
     own = jnp.stack([me, 0]).astype(jnp.int32)
-    chunks = make_slots(own, range(half), (ids_t, frames), capacity)
+    gates_t, out_w_t = gate_weights.T, out_weight.T
+    chunks = make_slots(own, range(half), (ids_t, frames, gates_t), capacity)
     near = [swap(chunks[k], k) for k in range(1, half)]
-    lat = out_weight.shape[1]
-    info, edge = make_info(frames, out_weight.T, ids_t, gate_weights.T)
-    left = lax.ppermute(edge, "expert", [(i, i + 1) for i in range(n - 1)])
-    right = lax.ppermute(edge, "expert", [(i + 1, i) for i in range(n - 1)])
-    folded = fold_weights(down_weight[0], out_weight.T)
+    folded = fold_weights(down_weight[0], out_w_t)
     origin = jnp.stack([me ^ (is_inner * across_by), is_inner]).astype(jnp.int32)
-    origin, near, left, right, folded = lax.optimization_barrier(
-        (origin, near, left, right, folded)
-    )
+    origin, folded = lax.optimization_barrier((origin, folded))
     sent = make_slots(
         origin, range(half, n), (ids_t, frames, across_ids, across), capacity
     )
@@ -449,11 +478,14 @@
         pairs = [(i, i ^ (k ^ across_by if i in inner else k)) for i in range(n)]
         far.append(lax.ppermute(value, "expert", [(i, j) for i, j in pairs if i != j]))
     up = up_weight[0]
-    info, chunk, _ = lax.optimization_barrier((info, chunks[0], sent))
-    pick, scale, base = make_table(place, info, left, right, lat, n, capacity)
+    gates_t, chunk, _ = lax.optimization_barrier((gates_t, chunks[0], sent))
+    neighbours = {k: near[k - 1] for k in range(1, half) if is_neighbour(k)}
+    pick, scale, base = make_table(
+        place, frames, out_w_t, ids_t, gates_t, neighbours, n, capacity
+    )
     back = run_group(n, False, place, chunk, near, up, folded)
     parts = [back[0]] + [swap(back[k], k) for k in range(1, half)]
-    place, pick, scale, base, parts = lax.optimization_barrier((place, pick, scale, base, parts))
+    place, pick, scale, base = lax.optimization_barrier((place, pick, scale, base))
     back = run_group(n, True, place, sent[quarter], far, up, folded)
     parts += [swap(back[k], half + k) for k in range(half)]
     slab, middle = combine(place, parts, pick, scale, base)

time: 113 us -> 98.3 us (0.87)
  waiting for transfers between devices: 27.4 us -> 20 us
  starting transfers between devices: 41.1 us -> 34 us
  local copies, waits for them, and re-layouts: 7.33 us -> 6.02 us
    ppermute x12, waiting for transfers between devices: 21.1 us -> 1.91 us  [swap(): return lax.ppermute(value, 'expert', [(i, i ^ k) for i in members])]
    ppermute x4, waiting for transfers between devices: 0.01 us -> 14 us  [local(): lax.ppermute(value, 'expert', [(i, j) for i, j in pairs if i != j])]
    ppermute x2 -> x0, starting transfers between devices: 11.9 us -> none  [the longest x1 10.6 us: local(): left = lax.ppermute(edge, 'expert', [(i, i + 1) for i in range(n - 1)])]
    ppermute x12, starting transfers between devices: 14.7 us -> 18.4 us  [swap(): return lax.ppermute(value, 'expert', [(i, i ^ k) for i in members])]
    ppermute x2 -> x0, waiting for transfers between devices: 2.54 us -> none  [the longest x1 1.76 us: local(): right = lax.ppermute(edge, 'expert', [(i + 1, i) for i in range(n - 1)])]
    unnamed x21 -> x19, local copies, waits for them, and re-layouts: 7.32 us -> 6.01 us
    ppermute x4, starting transfers between devices: 10.1 us -> 11.3 us  [local(): lax.ppermute(value, 'expert', [(i, j) for i, j in pairs if i != j])]
  transfers between devices with their start and end apart: 22 -> 20, of which waited for: 11 -> 8; matrix products, arithmetic and copies ran while one was open for 0% -> 0% of each run, Pallas kernels for 9% -> 16%
where the time goes in v5:
time: 98.3 us; the launch traced here: 97.9 us
  Pallas kernels  37.2 us (38%)
  starting transfers between devices  34 us (35%)
  waiting for transfers between devices  20 us (20%)
  local copies, waits for them, and re-layouts  6.02 us (6%)
    pallas_call x1, Pallas kernels, decode(): pl.pallas_call(functools.partial(decoder_kernel, segs), out_shape=jax.Sha...  19.9 us
    ppermute x12, starting transfers between devices, swap(): return lax.ppermute(value, 'expert', [(i, i ^ k) for i in members])  18.4 us
    ppermute x4, waiting for transfers between devices, local(): lax.ppermute(value, 'expert', [(i, j) for i, j in pairs if i != j])  14 us
    ppermute x4, starting transfers between devices, local(): lax.ppermute(value, 'expert', [(i, j) for i, j in pairs if i != j])  11.3 us
    pallas_call x2, Pallas kernels, run_group(): pl.pallas_call(functools.partial(group_kernel, n, far), out_shape=[jax.Sh...  7.97 us
    unnamed x19, local copies, waits for them, and re-layouts  6.01 us
    ppermute x3, waiting for transfers between devices, local(): lax.ppermute(slab, 'seg', [(i, i ^ k) for i in range(segs)])  4.11 us
    pallas_call x2, Pallas kernels, make_slots(): pl.pallas_call(functools.partial(slots_kernel, steps), out_shape=[jax.Sha...  3.58 us
  transfers between devices with their start and end apart: 20, of which 8 were waited for; matrix products, arithmetic and copies ran while one was open for 0% of the time, Pallas kernels for 16%

profile of v5, /device:TPU:0, one launch (start us, length us, event | category | flops | bytes accessed | tf_op | source)
XLA Modules:
  0.0 97.9 jit_solution(10105811002095414104)
XLA Ops:
  0.8 1.1 %copy-done.1 = bf16[256,1536]{1,0:T(8,128)(2,1)S(1)} copy-done((bf16[256,1536]{1,0:T(8,128)(2,1)S(1)}, bf16[256,1536]{1,0:T(8,128)(2,1)}, u32[]{:S(2)}) %copy-start.1) | copy-done | bytes 786456
  2.6 2.0 %shard_map.91 = (bf16[96,1536]{1,0:T(8,128)(2,1)S(1)}, bf16[112,1536]{1,0:T(8,128)(2,1)}, bf16[96,1536]{1,0:T(8,128)(2,1)S(1)}, bf16[112,1536]{1,0:T(8,128)(2,1)S(1)}) custom-call(s32[2]{0:T(128)S(1)} %pad_add_fusion.2.origin_ref, s32[2,256]{1,0:T(2,128)} %bitcast.3.refs_0_.ids_ref, bf16[256,1536]{1,0:T(8,128)(2,1)S(1)} %copy-done.1, f32[2,256]{1,0:T(2,128)S(1)} %bitcast.17), custom_call_target="tpu_custom_call" | custom-call | tf_op jit(solution)/shard_map/pallas_call | solution.py:100
  5.8 7.1 %collective-permute-start.4 = (bf16[96,1536]{1,0:T(8,128)(2,1)S(1)}, bf16[96,1536]{1,0:T(8,128)(2,1)S(1)}, u32[]{:S(2)}, u32[]{:S(2)}) collective-permute-start(bf16[96,1536]{1,0:T(8,128)(2,1)S(1)} %get-tuple-element.48), channel_id=1, source_target_pairs={{0,2},{1,3},{2,0},{3,1},{4,6},{5,7},{6,4},{7,5},{8,10},{9,11},{10,... | collective-permute-start | bytes 884744 | tf_op jit(solution)/shard_map/ppermute | solution.py:461
  13.0 2.9 %copy-done.3 = bf16[1,2048,1536]{2,1,0:T(8,128)(2,1)S(1)} copy-done((bf16[1,2048,1536]{2,1,0:T(8,128)(2,1)S(1)}, bf16[1,2048,1536]{2,1,0:T(8,128)(2,1)}, u32[]{:S(2)}) %copy-start.3) | copy-done | bytes 6291480
  15.9 1.2 %copy-done.4 = bf16[1536,64]{0,1:T(8,128)(2,1)S(1)} copy-done((bf16[1536,64]{0,1:T(8,128)(2,1)S(1)}, bf16[1536,64]{0,1:T(8,128)(2,1)}, u32[]{:S(2)}) %copy-start.4) | copy-done | bytes 196632
  17.1 2.5 %shard_map.92.refs_4_.refs_5_ = bf16[2048,128]{1,0:T(8,128)(2,1)S(1)} custom-call(bf16[2048,1536]{1,0:T(8,128)(2,1)S(1)} %bitcast.14, bf16[64,1536]{1,0:T(8,128)(2,1)S(1)} %bitcast.15), custom_call_target="tpu_custom_call" | custom-call | tf_op jit(solution)/shard_map/pallas_call | solution.py:128
  19.7 1.5 %shard_map.93 = (bf16[96,1536]{1,0:T(8,128)(2,1)S(1)}, bf16[96,1536]{1,0:T(8,128)(2,1)S(1)}, bf16[96,1536]{1,0:T(8,128)(2,1)S(1)}, bf16[96,1536]{1,0:T(8,128)(2,1)S(1)}) custom-call(s32[2]{0:T(128)S(1)} %pad_add_fusion.3.origin_ref, s32[2,256]{1,0:T(2,128)} %bitcast.3.refs_0_.ids_ref, bf16[256,1536]{1,0:T(8,128)(2,1)S(1)} %copy-done.2, ...), custom_call_target="tpu_custom_call" | custom-call | tf_op jit(solution)/shard_map/pallas_call | solution.py:100
  21.2 5.8 %collective-permute-start.8 = (bf16[96,1536]{1,0:T(8,128)(2,1)S(1)}, bf16[96,1536]{1,0:T(8,128)(2,1)S(1)}, u32[]{:S(2)}, u32[]{:S(2)}) collective-permute-start(bf16[96,1536]{1,0:T(8,128)(2,1)S(1)} %get-tuple-element.36), channel_id=1, source_target_pairs={{0,4},{1,5},{2,0},{3,1},{4,6},{5,7},{6,2},{7,3},{8,12},{9,13},{10,... | collective-permute-start | bytes 884744 | tf_op jit(solution)/shard_map/ppermute | solution.py:479
  27.0 1.1 %collective-permute-start.11 = (bf16[96,1536]{1,0:T(8,128)(2,1)S(1)}, bf16[96,1536]{1,0:T(8,128)(2,1)S(1)}, u32[]{:S(2)}, u32[]{:S(2)}) collective-permute-start(bf16[96,1536]{1,0:T(8,128)(2,1)S(1)} %get-tuple-element.39), channel_id=1, source_target_pairs={{0,7},{1,6},{2,3},{3,2},{4,5},{5,4},{6,1},{7,0},{8,15},{9,14},{10,... | collective-permute-start | bytes 884744 | tf_op jit(solution)/shard_map/ppermute | solution.py:479
  28.1 4.4 %collective-permute-start.10 = (bf16[96,1536]{1,0:T(8,128)(2,1)S(1)}, bf16[96,1536]{1,0:T(8,128)(2,1)S(1)}, u32[]{:S(2)}, u32[]{:S(2)}) collective-permute-start(bf16[96,1536]{1,0:T(8,128)(2,1)S(1)} %get-tuple-element.38.local_ref), channel_id=1, source_target_pairs={{0,6},{1,7},{6,0},{7,1},{8,14},{9,15},{14,8},{15,9},{16,22},{17,23... | collective-permute-start | bytes 884744 | tf_op jit(solution)/shard_map/ppermute | solution.py:479
  32.6 4.0 %shard_map.95 = (bf16[128,128]{1,0:T(8,128)(2,1)S(1)}, bf16[128,128]{1,0:T(8,128)(2,1)S(1)}, bf16[128,128]{1,0:T(8,128)(2,1)S(1)}, bf16[128,128]{1,0:T(8,128)(2,1)S(1)}) custom-call(s32[2]{0:T(128)S(1)} %pad_add_fusion.1.place_ref, bf16[96,1536]{1,0:T(8,128)(2,1)S(1)} %get-tuple-element.47.local_ref, bf16[112,1536]{1,0:T(8,128)(2,1)S(1)} %collective-permute-done.2.refs_0_, ...), custom_call_target="tpu_custom_call" | custom-call | tf_op jit(solution)/shard_map/pallas_call | solution.py:294
  37.4 2.0 %shard_map.94 = (bf16[8,272,128]{2,1,0:T(8,128)(2,1)S(1)}, f32[272,128]{1,0:T(8,128)S(1)}, f32[272,64]{1,0:T(8,128)S(1)}) custom-call(s32[2]{0:T(128)S(1)} %pad_add_fusion.1.place_ref, bf16[256,1536]{1,0:T(8,128)(2,1)S(1)} %copy-done.2, bf16[64,1536]{1,0:T(8,128)(2,1)S(1)} %bitcast.16, s32[2,256]{1,0:T(2,128)} %bitcast.3.refs_0_.ids_ref, ...), custom_call_target="tpu_custom_call" | custom-call | tf_op jit(solution)/shard_map/pallas_call | solution.py:226
  39.5 1.3 %collective-permute-done.9.refs_1_ = bf16[96,1536]{1,0:T(8,128)(2,1)S(1)} collective-permute-done((bf16[96,1536]{1,0:T(8,128)(2,1)S(1)}, bf16[96,1536]{1,0:T(8,128)(2,1)S(1)}, u32[]{:S(2)}, u32[]{:S(2)}) %collective-permute-start.9) | collective-permute-done | bytes 294944 | tf_op jit(solution)/shard_map/ppermute | solution.py:479
  40.8 2.4 %collective-permute-start.7 = (bf16[128,128]{1,0:T(8,128)(2,1)S(1)}, bf16[128,128]{1,0:T(8,128)(2,1)S(1)}, u32[]{:S(2)}, u32[]{:S(2)}) collective-permute-start(bf16[128,128]{1,0:T(8,128)(2,1)S(1)} %get-tuple-element.53), channel_id=1, source_target_pairs={{0,3},{1,2},{2,1},{3,0},{4,7},{5,6},{6,5},{7,4},{8,11},{9,10},{10,... | collective-permute-start | bytes 98312 | tf_op jit(solution)/shard_map/ppermute | solution.py:461
  43.2 5.0 %collective-permute-done.11.refs_3_ = bf16[96,1536]{1,0:T(8,128)(2,1)S(1)} collective-permute-done((bf16[96,1536]{1,0:T(8,128)(2,1)S(1)}, bf16[96,1536]{1,0:T(8,128)(2,1)S(1)}, u32[]{:S(2)}, u32[]{:S(2)}) %collective-permute-start.11) | collective-permute-done | bytes 294944 | tf_op jit(solution)/shard_map/ppermute | solution.py:479
  48.2 7.6 %collective-permute-done.10.refs_2_ = bf16[96,1536]{1,0:T(8,128)(2,1)S(1)} collective-permute-done((bf16[96,1536]{1,0:T(8,128)(2,1)S(1)}, bf16[96,1536]{1,0:T(8,128)(2,1)S(1)}, u32[]{:S(2)}, u32[]{:S(2)}) %collective-permute-start.10) | collective-permute-done | bytes 294944 | tf_op jit(solution)/shard_map/ppermute | solution.py:479
  55.8 4.0 %shard_map.96 = (bf16[128,128]{1,0:T(8,128)(2,1)S(1)}, bf16[128,128]{1,0:T(8,128)(2,1)S(1)}, bf16[128,128]{1,0:T(8,128)(2,1)S(1)}, bf16[128,128]{1,0:T(8,128)(2,1)S(1)}) custom-call(s32[2]{0:T(128)S(1)} %pad_add_fusion.1.place_ref, bf16[96,1536]{1,0:T(8,128)(2,1)S(1)} %get-tuple-element.38.local_ref, bf16[96,1536]{1,0:T(8,128)(2,1)S(1)} %collective-permute-done.8.refs_0_, ...), custom_call_target="tpu_custom_call" | custom-call | tf_op jit(solution)/shard_map/pallas_call | solution.py:294
  61.6 4.4 %collective-permute-start.15 = (bf16[128,128]{1,0:T(8,128)(2,1)S(1)}, bf16[128,128]{1,0:T(8,128)(2,1)S(1)}, u32[]{:S(2)}, u32[]{:S(2)}) collective-permute-start(bf16[128,128]{1,0:T(8,128)(2,1)S(1)} %get-tuple-element.57), channel_id=1, source_target_pairs={{0,7},{1,6},{2,5},{3,4},{4,3},{5,2},{6,1},{7,0},{8,15},{9,14},{10,... | collective-permute-start | bytes 98312 | tf_op jit(solution)/shard_map/ppermute | solution.py:461
  66.6 1.4 %collective-permute-done.15.refs_7_ = bf16[128,128]{1,0:T(8,128)(2,1)S(1)} collective-permute-done((bf16[128,128]{1,0:T(8,128)(2,1)S(1)}, bf16[128,128]{1,0:T(8,128)(2,1)S(1)}, u32[]{:S(2)}, u32[]{:S(2)}) %collective-permute-start.15) | collective-permute-done | bytes 32800 | tf_op jit(solution)/shard_map/ppermute | solution.py:461
  68.0 1.2 %shard_map.97 = (bf16[272,64]{1,0:T(8,128)(2,1)S(1)}, bf16[16,64]{1,0:T(8,128)(2,1)S(1)}) custom-call(s32[2]{0:T(128)S(1)} %pad_add_fusion.1.place_ref, bf16[128,128]{1,0:T(8,128)(2,1)S(1)} %get-tuple-element.50.refs_0_, bf16[128,128]{1,0:T(8,128)(2,1)S(1)} %collective-permute-done.5.refs_1_, bf16[128,128]{1,0:T(8,128)(2,1)S(1)} %collective-permute-done.6.refs_2_, ...), custom_call_target="tpu_custom_call" | custom-call | tf_op jit(solution)/shard_map/pallas_call | solution.py:322
  70.1 2.5 %collective-permute-start.19 = (bf16[288,64]{1,0:T(8,128)(2,1)S(1)}, bf16[288,64]{1,0:T(8,128)(2,1)S(1)}, u32[]{:S(2)}, u32[]{:S(2)}) collective-permute-start(bf16[288,64]{1,0:T(8,128)(2,1)S(1)} %constant_dynamic-update-slice_fusion.refs_0_), channel_id=1, source_target_pairs={{0,24},{8,16},{16,8},{24,0},{1,25},{9,17},{17,9},{25,1},{2,26},{10... | collective-permute-start | bytes 110600 | tf_op jit(solution)/shard_map/ppermute | solution.py:496
  73.7 2.3 %collective-permute-done.19.refs_3_ = bf16[288,64]{1,0:T(8,128)(2,1)S(1)} collective-permute-done((bf16[288,64]{1,0:T(8,128)(2,1)S(1)}, bf16[288,64]{1,0:T(8,128)(2,1)S(1)}, u32[]{:S(2)}, u32[]{:S(2)}) %collective-permute-start.19) | collective-permute-done | bytes 36896 | tf_op jit(solution)/shard_map/ppermute | solution.py:496
  76.1 1.7 %collective-permute-done.18.refs_2_ = bf16[288,64]{1,0:T(8,128)(2,1)S(1)} collective-permute-done((bf16[288,64]{1,0:T(8,128)(2,1)S(1)}, bf16[288,64]{1,0:T(8,128)(2,1)S(1)}, u32[]{:S(2)}, u32[]{:S(2)}) %collective-permute-start.18) | collective-permute-done | bytes 36896 | tf_op jit(solution)/shard_map/ppermute | solution.py:496
  77.8 19.9 %shard_map.98 = f32[4,2048,128]{2,1,0:T(8,128)} custom-call(s32[3]{0:T(128)S(1)} %pad_add_fusion.place_ref, bf16[288,64]{1,0:T(8,128)(2,1)S(1)} %constant_dynamic-update-slice_fusion.refs_0_, bf16[288,64]{1,0:T(8,128)(2,1)S(1)} %collective-permute-done.17.refs_1_, bf16[288,64]{1,0:T(8,128)(2,1)S(1)} %collective-permute-done.18.refs_2_, ...), custom_call_target="tpu_custom_call" | custom-call | tf_op jit(solution)/shard_map/pallas_call | solution.py:417
  (50 shorter events, 8.0 us)
Async XLA Ops:
  0.0 19.7 %collective-permute-start.1 = (bf16[256,1536]{1,0:T(8,128)(2,1)}, bf16[256,1536]{1,0:T(8,128)(2,1)S(1)}, u32[]{:S(2)}, u32[]{:S(2)}) collective-permute-start(bf16[256,1536]{1,0:T(8,128)(2,1)} %frames_ref.1), channel_id=1, source_target_pairs={{2,4},{3,5},{4,2},{5,3},{10,12},{11,13},{12,10},{13,11},{18,20},{1... | collective-permute-start | bytes 2359304 | tf_op jit(solution)/shard_map/ppermute | solution.py:461
  4.6 23.5 %collective-permute-start.2 = (bf16[112,1536]{1,0:T(8,128)(2,1)}, bf16[112,1536]{1,0:T(8,128)(2,1)S(1)}, u32[]{:S(2)}, u32[]{:S(2)}) collective-permute-start(bf16[112,1536]{1,0:T(8,128)(2,1)} %get-tuple-element.41), channel_id=1, source_target_pairs={{0,1},{1,0},{2,3},{3,2},{4,5},{5,4},{6,7},{7,6},{8,9},{9,8},{10,11... | collective-permute-start | bytes 1032200 | tf_op jit(solution)/shard_map/ppermute | solution.py:461
  5.1 14.6 %collective-permute-start = (s32[2,256]{1,0:T(2,128)}, s32[2,256]{1,0:T(2,128)S(1)}, u32[]{:S(2)}, u32[]{:S(2)}) collective-permute-start(s32[2,256]{1,0:T(2,128)} %bitcast.3.refs_0_.ids_ref), channel_id=1, source_target_pairs={{2,4},{3,5},{4,2},{5,3},{10,12},{11,13},{12,10},{13,11},{18,20},{1... | collective-permute-start | bytes 6152 | tf_op jit(solution)/shard_map/ppermute | solution.py:461
  5.8 21.2 %collective-permute-start.4 = (bf16[96,1536]{1,0:T(8,128)(2,1)S(1)}, bf16[96,1536]{1,0:T(8,128)(2,1)S(1)}, u32[]{:S(2)}, u32[]{:S(2)}) collective-permute-start(bf16[96,1536]{1,0:T(8,128)(2,1)S(1)} %get-tuple-element.48), channel_id=1, source_target_pairs={{0,2},{1,3},{2,0},{3,1},{4,6},{5,7},{6,4},{7,5},{8,10},{9,11},{10,... | collective-permute-start | bytes 884744 | tf_op jit(solution)/shard_map/ppermute | solution.py:461
  12.9 19.7 %collective-permute-start.3 = (bf16[112,1536]{1,0:T(8,128)(2,1)S(1)}, bf16[112,1536]{1,0:T(8,128)(2,1)S(1)}, u32[]{:S(2)}, u32[]{:S(2)}) collective-permute-start(bf16[112,1536]{1,0:T(8,128)(2,1)S(1)} %get-tuple-element.42), channel_id=1, source_target_pairs={{0,3},{1,2},{2,1},{3,0},{4,7},{5,6},{6,5},{7,4},{8,11},{9,10},{10,... | collective-permute-start | bytes 1032200 | tf_op jit(solution)/shard_map/ppermute | solution.py:461
  12.9 19.7 %copy-start = (bf16[1,1536,2048]{2,1,0:T(8,128)(2,1)S(1)}, bf16[1,1536,2048]{2,1,0:T(8,128)(2,1)}, u32[]{:S(2)}) copy-start(bf16[1,1536,2048]{2,1,0:T(8,128)(2,1)} %param.12) | copy-start | bytes 18874372
  19.6 17.8 %copy-start.8 = (f32[2048]{0:T(1024)S(1)}, f32[2048]{0:T(1024)}, u32[]{:S(2)}) copy-start(f32[2048]{0:T(1024)} %param.16) | copy-start | bytes 24580
  19.6 17.8 %copy-start.5 = (bf16[1536,64]{0,1:T(8,128)(2,1)S(1)}, bf16[1536,64]{0,1:T(8,128)(2,1)}, u32[]{:S(2)}) copy-start(bf16[1536,64]{0,1:T(8,128)(2,1)} %param.14) | copy-start | bytes 589828
  19.7 17.8 %copy-start.7 = (f32[256,2]{0,1:T(2,128)S(1)}, f32[256,2]{0,1:T(2,128)}, u32[]{:S(2)}) copy-start(f32[256,2]{0,1:T(2,128)} %param.11) | copy-start | bytes 6148
  21.2 15.5 %collective-permute-start.8 = (bf16[96,1536]{1,0:T(8,128)(2,1)S(1)}, bf16[96,1536]{1,0:T(8,128)(2,1)S(1)}, u32[]{:S(2)}, u32[]{:S(2)}) collective-permute-start(bf16[96,1536]{1,0:T(8,128)(2,1)S(1)} %get-tuple-element.36), channel_id=1, source_target_pairs={{0,4},{1,5},{2,0},{3,1},{4,6},{5,7},{6,2},{7,3},{8,12},{9,13},{10,... | collective-permute-start | bytes 884744 | tf_op jit(solution)/shard_map/ppermute | solution.py:479
  27.0 13.8 %collective-permute-start.9 = (bf16[96,1536]{1,0:T(8,128)(2,1)S(1)}, bf16[96,1536]{1,0:T(8,128)(2,1)S(1)}, u32[]{:S(2)}, u32[]{:S(2)}) collective-permute-start(bf16[96,1536]{1,0:T(8,128)(2,1)S(1)} %get-tuple-element.37), channel_id=1, source_target_pairs={{0,5},{1,4},{2,1},{3,0},{4,7},{5,6},{6,3},{7,2},{8,13},{9,12},{10,... | collective-permute-start | bytes 884744 | tf_op jit(solution)/shard_map/ppermute | solution.py:479
  27.0 21.2 %collective-permute-start.11 = (bf16[96,1536]{1,0:T(8,128)(2,1)S(1)}, bf16[96,1536]{1,0:T(8,128)(2,1)S(1)}, u32[]{:S(2)}, u32[]{:S(2)}) collective-permute-start(bf16[96,1536]{1,0:T(8,128)(2,1)S(1)} %get-tuple-element.39), channel_id=1, source_target_pairs={{0,7},{1,6},{2,3},{3,2},{4,5},{5,4},{6,1},{7,0},{8,15},{9,14},{10,... | collective-permute-start | bytes 884744 | tf_op jit(solution)/shard_map/ppermute | solution.py:479
  28.1 27.7 %collective-permute-start.10 = (bf16[96,1536]{1,0:T(8,128)(2,1)S(1)}, bf16[96,1536]{1,0:T(8,128)(2,1)S(1)}, u32[]{:S(2)}, u32[]{:S(2)}) collective-permute-start(bf16[96,1536]{1,0:T(8,128)(2,1)S(1)} %get-tuple-element.38.local_ref), channel_id=1, source_target_pairs={{0,6},{1,7},{6,0},{7,1},{8,14},{9,15},{14,8},{15,9},{16,22},{17,23... | collective-permute-start | bytes 884744 | tf_op jit(solution)/shard_map/ppermute | solution.py:479
  36.6 24.2 %collective-permute-start.5 = (bf16[128,128]{1,0:T(8,128)(2,1)S(1)}, bf16[128,128]{1,0:T(8,128)(2,1)S(1)}, u32[]{:S(2)}, u32[]{:S(2)}) collective-permute-start(bf16[128,128]{1,0:T(8,128)(2,1)S(1)} %get-tuple-element.51), channel_id=1, source_target_pairs={{0,1},{1,0},{2,3},{3,2},{4,5},{5,4},{6,7},{7,6},{8,9},{9,8},{10,11... | collective-permute-start | bytes 98312 | tf_op jit(solution)/shard_map/ppermute | solution.py:461
  36.7 24.9 %collective-permute-start.6 = (bf16[128,128]{1,0:T(8,128)(2,1)S(1)}, bf16[128,128]{1,0:T(8,128)(2,1)S(1)}, u32[]{:S(2)}, u32[]{:S(2)}) collective-permute-start(bf16[128,128]{1,0:T(8,128)(2,1)S(1)} %get-tuple-element.52), channel_id=1, source_target_pairs={{0,2},{1,3},{2,0},{3,1},{4,6},{5,7},{6,4},{7,5},{8,10},{9,11},{10,... | collective-permute-start | bytes 98312 | tf_op jit(solution)/shard_map/ppermute | solution.py:461
  40.8 25.3 %collective-permute-start.7 = (bf16[128,128]{1,0:T(8,128)(2,1)S(1)}, bf16[128,128]{1,0:T(8,128)(2,1)S(1)}, u32[]{:S(2)}, u32[]{:S(2)}) collective-permute-start(bf16[128,128]{1,0:T(8,128)(2,1)S(1)} %get-tuple-element.53), channel_id=1, source_target_pairs={{0,3},{1,2},{2,1},{3,0},{4,7},{5,6},{6,5},{7,4},{8,11},{9,10},{10,... | collective-permute-start | bytes 98312 | tf_op jit(solution)/shard_map/ppermute | solution.py:461
  59.8 6.3 %collective-permute-start.12 = (bf16[128,128]{1,0:T(8,128)(2,1)S(1)}, bf16[128,128]{1,0:T(8,128)(2,1)S(1)}, u32[]{:S(2)}, u32[]{:S(2)}) collective-permute-start(bf16[128,128]{1,0:T(8,128)(2,1)S(1)} %get-tuple-element.54), channel_id=1, source_target_pairs={{0,4},{1,5},{2,6},{3,7},{4,0},{5,1},{6,2},{7,3},{8,12},{9,13},{10,... | collective-permute-start | bytes 98312 | tf_op jit(solution)/shard_map/ppermute | solution.py:461
  59.9 6.2 %collective-permute-start.13 = (bf16[128,128]{1,0:T(8,128)(2,1)S(1)}, bf16[128,128]{1,0:T(8,128)(2,1)S(1)}, u32[]{:S(2)}, u32[]{:S(2)}) collective-permute-start(bf16[128,128]{1,0:T(8,128)(2,1)S(1)} %get-tuple-element.55), channel_id=1, source_target_pairs={{0,5},{1,4},{2,7},{3,6},{4,1},{5,0},{6,3},{7,2},{8,13},{9,12},{10,... | collective-permute-start | bytes 98312 | tf_op jit(solution)/shard_map/ppermute | solution.py:461
  60.8 5.8 %collective-permute-start.14 = (bf16[128,128]{1,0:T(8,128)(2,1)S(1)}, bf16[128,128]{1,0:T(8,128)(2,1)S(1)}, u32[]{:S(2)}, u32[]{:S(2)}) collective-permute-start(bf16[128,128]{1,0:T(8,128)(2,1)S(1)} %get-tuple-element.56), channel_id=1, source_target_pairs={{0,6},{1,7},{2,4},{3,5},{4,2},{5,3},{6,0},{7,1},{8,14},{9,15},{10,... | collective-permute-start | bytes 98312 | tf_op jit(solution)/shard_map/ppermute | solution.py:461
  61.6 6.4 %collective-permute-start.15 = (bf16[128,128]{1,0:T(8,128)(2,1)S(1)}, bf16[128,128]{1,0:T(8,128)(2,1)S(1)}, u32[]{:S(2)}, u32[]{:S(2)}) collective-permute-start(bf16[128,128]{1,0:T(8,128)(2,1)S(1)} %get-tuple-element.57), channel_id=1, source_target_pairs={{0,7},{1,6},{2,5},{3,4},{4,3},{5,2},{6,1},{7,0},{8,15},{9,14},{10,... | collective-permute-start | bytes 98312 | tf_op jit(solution)/shard_map/ppermute | solution.py:461
  69.2 0.9 collective-permute-start.16
  70.1 6.0 %collective-permute-start.19 = (bf16[288,64]{1,0:T(8,128)(2,1)S(1)}, bf16[288,64]{1,0:T(8,128)(2,1)S(1)}, u32[]{:S(2)}, u32[]{:S(2)}) collective-permute-start(bf16[288,64]{1,0:T(8,128)(2,1)S(1)} %constant_dynamic-update-slice_fusion.refs_0_), channel_id=1, source_target_pairs={{0,24},{8,16},{16,8},{24,0},{1,25},{9,17},{17,9},{25,1},{2,26},{10... | collective-permute-start | bytes 110600 | tf_op jit(solution)/shard_map/ppermute | solution.py:496
  72.6 5.2 %collective-permute-start.18 = (bf16[288,64]{1,0:T(8,128)(2,1)S(1)}, bf16[288,64]{1,0:T(8,128)(2,1)S(1)}, u32[]{:S(2)}, u32[]{:S(2)}) collective-permute-start(bf16[288,64]{1,0:T(8,128)(2,1)S(1)} %constant_dynamic-update-slice_fusion.refs_0_), channel_id=1, source_target_pairs={{0,16},{8,24},{16,0},{24,8},{1,17},{9,25},{17,1},{25,9},{2,18},{10... | collective-permute-start | bytes 110600 | tf_op jit(solution)/shard_map/ppermute | solution.py:496
  73.1 4.7 %collective-permute-start.17 = (bf16[288,64]{1,0:T(8,128)(2,1)S(1)}, bf16[288,64]{1,0:T(8,128)(2,1)S(1)}, u32[]{:S(2)}, u32[]{:S(2)}) collective-permute-start(bf16[288,64]{1,0:T(8,128)(2,1)S(1)} %constant_dynamic-update-slice_fusion.refs_0_), channel_id=1, source_target_pairs={{0,8},{8,0},{16,24},{24,16},{1,9},{9,1},{17,25},{25,17},{2,10},{10... | collective-permute-start | bytes 110600 | tf_op jit(solution)/shard_map/ppermute | solution.py:496
  (5 other events, 23.1 us)

commit v6 on v5

--- a/solution.py
+++ b/solution.py
@@ -365,19 +365,24 @@
     edge_row = lax.broadcasted_iota(jnp.int32, (16, block), 0)
     gone = ((edge_row == 0) & is_first) | ((edge_row == 1) & is_last)
     for k in range(segs):
-        slab = lat_refs[k][...].astype(F32)
-        middle = slab[span:]
-        padded[...] = slab[:span]
-        before = jnp.where(place_ref[1] == place_ref[2] // 2, middle[:EDGE], slab[:EDGE])
-        end = length + EDGE
-        after = jnp.where(
-            place_ref[1] == place_ref[2] // 2 - 1, middle[EDGE : 2 * EDGE], slab[end : end + EDGE]
-        )
-        padded[0:EDGE] = before
-        padded[end : end + EDGE] = after
+        padded[k] = lat_refs[k][0:span].astype(F32)
+    end = length + EDGE
+
+    @pl.when(place_ref[1] == place_ref[2] // 2)
+    def _():
+        for k in range(segs):
+            padded[k, 0:EDGE] = lat_refs[k][span:].astype(F32)[:EDGE]
+
+    @pl.when(place_ref[1] == place_ref[2] // 2 - 1)
+    def _():
+        for k in range(segs):
+            padded[k, end : end + EDGE] = lat_refs[k][span:].astype(F32)[EDGE : 2 * EDGE]
+
+    for k in range(segs):
 
         def window(start, rows):
-            return jnp.concatenate([padded[start + j : start + j + rows] for j in range(taps)], axis=1)
+            parts = [padded[k, start + j : start + j + rows] for j in range(taps)]
+            return jnp.concatenate(parts, axis=1)
 
         windows[k, 0:length] = window(1, length).astype(BF16)
         edges = jnp.where(row == 0, window(0, 1), jnp.where(row == 1, window(length + 1, 1), 0.0))
@@ -422,7 +427,7 @@
         + [pl.BlockSpec(memory_space=pl.ANY)],
         out_specs=pl.BlockSpec(memory_space=pl.ANY),
         scratch_shapes=[
-            pltpu.VMEM((length + 16, lat), F32),
+            pltpu.VMEM((segs, length + 16, lat), F32),
             pltpu.VMEM((segs, length + 16, conv.shape[0]), BF16),
             pltpu.VMEM((segs, length + 16, channels), BF16),
             pltpu.VMEM(first_up.shape, BF16),
@@ -467,18 +472,23 @@
     gates_t, out_w_t = gate_weights.T, out_weight.T
     chunks = make_slots(own, range(half), (ids_t, frames, gates_t), capacity)
     near = [swap(chunks[k], k) for k in range(1, half)]
-    folded = fold_weights(down_weight[0], out_w_t)
     origin = jnp.stack([me ^ (is_inner * across_by), is_inner]).astype(jnp.int32)
-    origin, folded = lax.optimization_barrier((origin, folded))
     sent = make_slots(
         origin, range(half, n), (ids_t, frames, across_ids, across), capacity
     )
-    far = []
-    for k, value in zip(range(half, n), sent):
+
+    def cross(value, k):
         pairs = [(i, i ^ (k ^ across_by if i in inner else k)) for i in range(n)]
-        far.append(lax.ppermute(value, "expert", [(i, j) for i, j in pairs if i != j]))
+        return lax.ppermute(value, "expert", [(i, j) for i, j in pairs if i != j])
+
+    far = [cross(sent[k - half], k) for k in range(across_by, n)]
+    late, near = lax.optimization_barrier((sent[:quarter], near))
+    far = [cross(late[k - half], k) for k in range(half, across_by)] + far
     up = up_weight[0]
-    gates_t, chunk, _ = lax.optimization_barrier((gates_t, chunks[0], sent))
+    gates_t, chunk, down, late = lax.optimization_barrier(
+        (gates_t, chunks[0], down_weight[0], late)
+    )
+    folded = fold_weights(down, out_w_t)
     neighbours = {k: near[k - 1] for k in range(1, half) if is_neighbour(k)}
     pick, scale, base = make_table(
         place, frames, out_w_t, ids_t, gates_t, neighbours, n, capacity

time: 98.3 us -> 93.7 us (0.953)
  starting transfers between devices: 34 us -> 31 us
  Pallas kernels: 37.2 us -> 35.5 us
    ppermute x4, waiting for transfers between devices: 14 us -> 7.74 us  [cross(): return lax.ppermute(value, 'expert', [(i, j) for i, j in pairs if i != j])]
    ppermute x12, waiting for transfers between devices: 1.91 us -> 7.88 us  [swap(): return lax.ppermute(value, 'expert', [(i, i ^ k) for i in members])]
    ppermute x4, starting transfers between devices: 11.3 us -> 9.35 us  [cross(): return lax.ppermute(value, 'expert', [(i, j) for i, j in pairs if i != j])]
    pallas_call x1, Pallas kernels: 19.9 us -> 18.5 us  [decode(): pl.pallas_call(functools.partial(decoder_kernel, segs), out_shape=jax.Sha...]
    unnamed x19 -> x21, local copies, waits for them, and re-layouts: 6.01 us -> 6.83 us
  transfers between devices with their start and end apart: 20 -> 20, of which waited for: 8 -> 8; matrix products, arithmetic and copies ran while one was open for 0% -> 0% of each run, Pallas kernels for 16% -> 17%
where the time goes in v6:
time: 93.7 us; the launch traced here: 93.3 us
  Pallas kernels  35.5 us (38%)
  starting transfers between devices  31 us (33%)
  waiting for transfers between devices  19.4 us (21%)
  local copies, waits for them, and re-layouts  6.84 us (7%)
    pallas_call x1, Pallas kernels, decode(): pl.pallas_call(functools.partial(decoder_kernel, segs), out_shape=jax.Sha...  18.5 us
    ppermute x12, starting transfers between devices, swap(): return lax.ppermute(value, 'expert', [(i, i ^ k) for i in members])  17.5 us
    ppermute x4, starting transfers between devices, cross(): return lax.ppermute(value, 'expert', [(i, j) for i, j in pairs if i != j])  9.35 us
    pallas_call x2, Pallas kernels, run_group(): pl.pallas_call(functools.partial(group_kernel, n, far), out_shape=[jax.Sh...  7.95 us
    ppermute x12, waiting for transfers between devices, swap(): return lax.ppermute(value, 'expert', [(i, i ^ k) for i in members])  7.88 us
    ppermute x4, waiting for transfers between devices, cross(): return lax.ppermute(value, 'expert', [(i, j) for i, j in pairs if i != j])  7.74 us
    unnamed x21, local copies, waits for them, and re-layouts  6.83 us
    ppermute x3, waiting for transfers between devices, local(): lax.ppermute(slab, 'seg', [(i, i ^ k) for i in range(segs)])  3.74 us
  transfers between devices with their start and end apart: 20, of which 8 were waited for; matrix products, arithmetic and copies ran while one was open for 0% of the time, Pallas kernels for 17%

profile of v6, /device:TPU:0, one launch (start us, length us, event | category | flops | bytes accessed | tf_op | source)
XLA Modules:
  0.0 93.3 jit_solution(8186511182097355907)
XLA Ops:
  2.6 1.5 %shard_map.91 = (bf16[96,1536]{1,0:T(8,128)(2,1)S(1)}, bf16[112,1536]{1,0:T(8,128)(2,1)S(1)}, bf16[96,1536]{1,0:T(8,128)(2,1)S(1)}, bf16[112,1536]{1,0:T(8,128)(2,1)S(1)}) custom-call(s32[2]{0:T(128)S(1)} %get-tuple-element.74.origin_ref, s32[2,256]{1,0:T(2,128)} %bitcast.3.refs_0_.ids_ref, bf16[256,1536]{1,0:T(8,128)(2,1)S(1)} %copy-done.1, ...), custom_call_target="tpu_custom_call" | custom-call | tf_op jit(solution)/shard_map/pallas_call | solution.py:100
  4.6 5.5 %collective-permute-start.4 = (bf16[112,1536]{1,0:T(8,128)(2,1)S(1)}, bf16[112,1536]{1,0:T(8,128)(2,1)S(1)}, u32[]{:S(2)}, u32[]{:S(2)}) collective-permute-start(bf16[112,1536]{1,0:T(8,128)(2,1)S(1)} %get-tuple-element.43), channel_id=1, source_target_pairs={{0,3},{1,2},{2,1},{3,0},{4,7},{5,6},{6,5},{7,4},{8,11},{9,10},{10,... | collective-permute-start | bytes 1032200 | tf_op jit(solution)/shard_map/ppermute | solution.py:466
  10.7 1.7 %collective-permute-start.3 = (bf16[96,1536]{1,0:T(8,128)(2,1)S(1)}, bf16[96,1536]{1,0:T(8,128)(2,1)S(1)}, u32[]{:S(2)}, u32[]{:S(2)}) collective-permute-start(bf16[96,1536]{1,0:T(8,128)(2,1)S(1)} %get-tuple-element.42), channel_id=1, source_target_pairs={{0,2},{1,3},{2,0},{3,1},{4,6},{5,7},{6,4},{7,5},{8,10},{9,11},{10,... | collective-permute-start | bytes 884744 | tf_op jit(solution)/shard_map/ppermute | solution.py:466
  13.8 1.8 %shard_map.92 = (bf16[96,1536]{1,0:T(8,128)(2,1)S(1)}, bf16[96,1536]{1,0:T(8,128)(2,1)S(1)}, bf16[96,1536]{1,0:T(8,128)(2,1)S(1)}, bf16[96,1536]{1,0:T(8,128)(2,1)S(1)}) custom-call(s32[2]{0:T(128)S(1)} %pad_add_fusion.3.origin_ref, s32[2,256]{1,0:T(2,128)} %bitcast.3.refs_0_.ids_ref, bf16[256,1536]{1,0:T(8,128)(2,1)S(1)} %copy-done.2, ...), custom_call_target="tpu_custom_call" | custom-call | tf_op jit(solution)/shard_map/pallas_call | solution.py:100
  15.6 2.0 %collective-permute-start.11 = (bf16[96,1536]{1,0:T(8,128)(2,1)S(1)}, bf16[96,1536]{1,0:T(8,128)(2,1)S(1)}, u32[]{:S(2)}, u32[]{:S(2)}) collective-permute-start(bf16[96,1536]{1,0:T(8,128)(2,1)S(1)} %get-tuple-element.61), channel_id=1, source_target_pairs={{0,7},{1,6},{2,3},{3,2},{4,5},{5,4},{6,1},{7,0},{8,15},{9,14},{10,... | collective-permute-start | bytes 884744 | tf_op jit(solution)/shard_map/ppermute | solution.py:482
  17.6 3.2 %collective-permute-start.10 = (bf16[96,1536]{1,0:T(8,128)(2,1)S(1)}, bf16[96,1536]{1,0:T(8,128)(2,1)S(1)}, u32[]{:S(2)}, u32[]{:S(2)}) collective-permute-start(bf16[96,1536]{1,0:T(8,128)(2,1)S(1)} %get-tuple-element.60.local_ref), channel_id=1, source_target_pairs={{0,6},{1,7},{6,0},{7,1},{8,14},{9,15},{14,8},{15,9},{16,22},{17,23... | collective-permute-start | bytes 884744 | tf_op jit(solution)/shard_map/ppermute | solution.py:482
  20.9 4.1 %collective-permute-done.3.refs_1_ = bf16[96,1536]{1,0:T(8,128)(2,1)S(1)} collective-permute-done((bf16[96,1536]{1,0:T(8,128)(2,1)S(1)}, bf16[96,1536]{1,0:T(8,128)(2,1)S(1)}, u32[]{:S(2)}, u32[]{:S(2)}) %collective-permute-start.3) | collective-permute-done | bytes 294944 | tf_op jit(solution)/shard_map/ppermute | solution.py:466
  25.0 3.9 %collective-permute-start.8 = (bf16[96,1536]{1,0:T(8,128)(2,1)S(1)}, bf16[96,1536]{1,0:T(8,128)(2,1)S(1)}, u32[]{:S(2)}, u32[]{:S(2)}) collective-permute-start(bf16[96,1536]{1,0:T(8,128)(2,1)S(1)} %get-tuple-element.44), channel_id=1, source_target_pairs={{0,4},{1,5},{2,0},{3,1},{4,6},{5,7},{6,2},{7,3},{8,12},{9,13},{10,... | collective-permute-start | bytes 884744 | tf_op jit(solution)/shard_map/ppermute | solution.py:482
  29.1 2.8 %copy-done.4 = bf16[1,2048,1536]{2,1,0:T(8,128)(2,1)S(1)} copy-done((bf16[1,2048,1536]{2,1,0:T(8,128)(2,1)S(1)}, bf16[1,2048,1536]{2,1,0:T(8,128)(2,1)}, u32[]{:S(2)}) %copy-start.4) | copy-done | bytes 6291480
  32.8 2.5 %shard_map.94.refs_4_.refs_5_ = bf16[2048,128]{1,0:T(8,128)(2,1)S(1)} custom-call(bf16[2048,1536]{1,0:T(8,128)(2,1)S(1)} %bitcast.14, bf16[64,1536]{1,0:T(8,128)(2,1)S(1)} %bitcast.15), custom_call_target="tpu_custom_call" | custom-call | tf_op jit(solution)/shard_map/pallas_call | solution.py:128
  35.4 4.0 %shard_map.95 = (bf16[128,128]{1,0:T(8,128)(2,1)S(1)}, bf16[128,128]{1,0:T(8,128)(2,1)S(1)}, bf16[128,128]{1,0:T(8,128)(2,1)S(1)}, bf16[128,128]{1,0:T(8,128)(2,1)S(1)}) custom-call(s32[2]{0:T(128)S(1)} %get-tuple-element.52.place_ref, bf16[96,1536]{1,0:T(8,128)(2,1)S(1)} %get-tuple-element.53.local_ref, ...), custom_call_target="tpu_custom_call" | custom-call | tf_op jit(solution)/shard_map/pallas_call | solution.py:294
  39.5 1.9 %collective-permute-start.6 = (bf16[128,128]{1,0:T(8,128)(2,1)S(1)}, bf16[128,128]{1,0:T(8,128)(2,1)S(1)}, u32[]{:S(2)}, u32[]{:S(2)}) collective-permute-start(bf16[128,128]{1,0:T(8,128)(2,1)S(1)} %get-tuple-element.58), channel_id=1, source_target_pairs={{0,2},{1,3},{2,0},{3,1},{4,6},{5,7},{6,4},{7,5},{8,10},{9,11},{10,... | collective-permute-start | bytes 98312 | tf_op jit(solution)/shard_map/ppermute | solution.py:466
  41.5 2.0 %shard_map.93 = (bf16[8,272,128]{2,1,0:T(8,128)(2,1)S(1)}, f32[272,128]{1,0:T(8,128)S(1)}, f32[272,64]{1,0:T(8,128)S(1)}) custom-call(s32[2]{0:T(128)S(1)} %get-tuple-element.52.place_ref, bf16[256,1536]{1,0:T(8,128)(2,1)S(1)} %copy-done.3, bf16[64,1536]{1,0:T(8,128)(2,1)S(1)} %bitcast.16, s32[2,256]{1,0:T(2,128)} %bitcast.3.refs_0_.ids_ref, ...), custom_call_target="tpu_custom_call" | custom-call | tf_op jit(solution)/shard_map/pallas_call | solution.py:226
  43.6 1.4 %collective-permute-done.8.refs_0_ = bf16[96,1536]{1,0:T(8,128)(2,1)S(1)} collective-permute-done((bf16[96,1536]{1,0:T(8,128)(2,1)S(1)}, bf16[96,1536]{1,0:T(8,128)(2,1)S(1)}, u32[]{:S(2)}, u32[]{:S(2)}) %collective-permute-start.8) | collective-permute-done | bytes 294944 | tf_op jit(solution)/shard_map/ppermute | solution.py:482
  45.0 6.3 %collective-permute-done.9.refs_1_ = bf16[96,1536]{1,0:T(8,128)(2,1)S(1)} collective-permute-done((bf16[96,1536]{1,0:T(8,128)(2,1)S(1)}, bf16[96,1536]{1,0:T(8,128)(2,1)S(1)}, u32[]{:S(2)}, u32[]{:S(2)}) %collective-permute-start.9) | collective-permute-done | bytes 294944 | tf_op jit(solution)/shard_map/ppermute | solution.py:482
  51.3 3.9 %shard_map.96 = (bf16[128,128]{1,0:T(8,128)(2,1)S(1)}, bf16[128,128]{1,0:T(8,128)(2,1)S(1)}, bf16[128,128]{1,0:T(8,128)(2,1)S(1)}, bf16[128,128]{1,0:T(8,128)(2,1)S(1)}) custom-call(s32[2]{0:T(128)S(1)} %get-tuple-element.52.place_ref, bf16[96,1536]{1,0:T(8,128)(2,1)S(1)} %get-tuple-element.60.local_ref, ...), custom_call_target="tpu_custom_call" | custom-call | tf_op jit(solution)/shard_map/pallas_call | solution.py:294
  57.7 2.5 %collective-permute-start.14 = (bf16[128,128]{1,0:T(8,128)(2,1)S(1)}, bf16[128,128]{1,0:T(8,128)(2,1)S(1)}, u32[]{:S(2)}, u32[]{:S(2)}) collective-permute-start(bf16[128,128]{1,0:T(8,128)(2,1)S(1)} %get-tuple-element.64), channel_id=1, source_target_pairs={{0,6},{1,7},{2,4},{3,5},{4,2},{5,3},{6,0},{7,1},{8,14},{9,15},{10,... | collective-permute-start | bytes 98312 | tf_op jit(solution)/shard_map/ppermute | solution.py:466
  60.2 1.3 %collective-permute-start.15 = (bf16[128,128]{1,0:T(8,128)(2,1)S(1)}, bf16[128,128]{1,0:T(8,128)(2,1)S(1)}, u32[]{:S(2)}, u32[]{:S(2)}) collective-permute-start(bf16[128,128]{1,0:T(8,128)(2,1)S(1)} %get-tuple-element.65), channel_id=1, source_target_pairs={{0,7},{1,6},{2,5},{3,4},{4,3},{5,2},{6,1},{7,0},{8,15},{9,14},{10,... | collective-permute-start | bytes 98312 | tf_op jit(solution)/shard_map/ppermute | solution.py:466
  61.6 1.9 %collective-permute-done.14.refs_6_ = bf16[128,128]{1,0:T(8,128)(2,1)S(1)} collective-permute-done((bf16[128,128]{1,0:T(8,128)(2,1)S(1)}, bf16[128,128]{1,0:T(8,128)(2,1)S(1)}, u32[]{:S(2)}, u32[]{:S(2)}) %collective-permute-start.14) | collective-permute-done | bytes 32800 | tf_op jit(solution)/shard_map/ppermute | solution.py:466
  63.5 1.8 %collective-permute-done.15.refs_7_ = bf16[128,128]{1,0:T(8,128)(2,1)S(1)} collective-permute-done((bf16[128,128]{1,0:T(8,128)(2,1)S(1)}, bf16[128,128]{1,0:T(8,128)(2,1)S(1)}, u32[]{:S(2)}, u32[]{:S(2)}) %collective-permute-start.15) | collective-permute-done | bytes 32800 | tf_op jit(solution)/shard_map/ppermute | solution.py:466
  67.2 2.5 %collective-permute-start.19 = (bf16[288,64]{1,0:T(8,128)(2,1)S(1)}, bf16[288,64]{1,0:T(8,128)(2,1)S(1)}, u32[]{:S(2)}, u32[]{:S(2)}) collective-permute-start(bf16[288,64]{1,0:T(8,128)(2,1)S(1)} %constant_dynamic-update-slice_fusion.refs_0_), channel_id=1, source_target_pairs={{0,24},{8,16},{16,8},{24,0},{1,25},{9,17},{17,9},{25,1},{2,26},{10... | collective-permute-start | bytes 110600 | tf_op jit(solution)/shard_map/ppermute | solution.py:506
  70.9 2.0 %collective-permute-done.19.refs_3_ = bf16[288,64]{1,0:T(8,128)(2,1)S(1)} collective-permute-done((bf16[288,64]{1,0:T(8,128)(2,1)S(1)}, bf16[288,64]{1,0:T(8,128)(2,1)S(1)}, u32[]{:S(2)}, u32[]{:S(2)}) %collective-permute-start.19) | collective-permute-done | bytes 36896 | tf_op jit(solution)/shard_map/ppermute | solution.py:506
  72.8 1.5 %collective-permute-done.18.refs_2_ = bf16[288,64]{1,0:T(8,128)(2,1)S(1)} collective-permute-done((bf16[288,64]{1,0:T(8,128)(2,1)S(1)}, bf16[288,64]{1,0:T(8,128)(2,1)S(1)}, u32[]{:S(2)}, u32[]{:S(2)}) %collective-permute-start.18) | collective-permute-done | bytes 36896 | tf_op jit(solution)/shard_map/ppermute | solution.py:506
  74.6 18.5 %shard_map.98 = f32[4,2048,128]{2,1,0:T(8,128)} custom-call(s32[3]{0:T(128)S(1)} %pad_add_fusion.place_ref, bf16[288,64]{1,0:T(8,128)(2,1)S(1)} %constant_dynamic-update-slice_fusion.refs_0_, bf16[288,64]{1,0:T(8,128)(2,1)S(1)} %collective-permute-done.17.refs_1_, bf16[288,64]{1,0:T(8,128)(2,1)S(1)} %collective-permute-done.18.refs_2_, ...), custom_call_target="tpu_custom_call" | custom-call | tf_op jit(solution)/shard_map/pallas_call | solution.py:422
  (51 shorter events, 12.1 us)
Async XLA Ops:
  0.0 12.6 %collective-permute-start.1 = (bf16[256,1536]{1,0:T(8,128)(2,1)}, bf16[256,1536]{1,0:T(8,128)(2,1)S(1)}, u32[]{:S(2)}, u32[]{:S(2)}) collective-permute-start(bf16[256,1536]{1,0:T(8,128)(2,1)} %frames_ref.1), channel_id=1, source_target_pairs={{2,4},{3,5},{4,2},{5,3},{10,12},{11,13},{12,10},{13,11},{18,20},{1... | collective-permute-start | bytes 2359304 | tf_op jit(solution)/shard_map/ppermute | solution.py:466
  4.1 20.9 %collective-permute-start.2 = (bf16[112,1536]{1,0:T(8,128)(2,1)S(1)}, bf16[112,1536]{1,0:T(8,128)(2,1)S(1)}, u32[]{:S(2)}, u32[]{:S(2)}) collective-permute-start(bf16[112,1536]{1,0:T(8,128)(2,1)S(1)} %get-tuple-element.41), channel_id=1, source_target_pairs={{0,1},{1,0},{2,3},{3,2},{4,5},{5,4},{6,7},{7,6},{8,9},{9,8},{10,11... | collective-permute-start | bytes 1032200 | tf_op jit(solution)/shard_map/ppermute | solution.py:466
  4.6 20.4 %collective-permute-start.4 = (bf16[112,1536]{1,0:T(8,128)(2,1)S(1)}, bf16[112,1536]{1,0:T(8,128)(2,1)S(1)}, u32[]{:S(2)}, u32[]{:S(2)}) collective-permute-start(bf16[112,1536]{1,0:T(8,128)(2,1)S(1)} %get-tuple-element.43), channel_id=1, source_target_pairs={{0,3},{1,2},{2,1},{3,0},{4,7},{5,6},{6,5},{7,4},{8,11},{9,10},{10,... | collective-permute-start | bytes 1032200 | tf_op jit(solution)/shard_map/ppermute | solution.py:466
  10.1 2.5 %collective-permute-start = (s32[2,256]{1,0:T(2,128)}, s32[2,256]{1,0:T(2,128)S(1)}, u32[]{:S(2)}, u32[]{:S(2)}) collective-permute-start(s32[2,256]{1,0:T(2,128)} %bitcast.3.refs_0_.ids_ref), channel_id=1, source_target_pairs={{2,4},{3,5},{4,2},{5,3},{10,12},{11,13},{12,10},{13,11},{18,20},{1... | collective-permute-start | bytes 6152 | tf_op jit(solution)/shard_map/ppermute | solution.py:466
  10.7 14.3 %collective-permute-start.3 = (bf16[96,1536]{1,0:T(8,128)(2,1)S(1)}, bf16[96,1536]{1,0:T(8,128)(2,1)S(1)}, u32[]{:S(2)}, u32[]{:S(2)}) collective-permute-start(bf16[96,1536]{1,0:T(8,128)(2,1)S(1)} %get-tuple-element.42), channel_id=1, source_target_pairs={{0,2},{1,3},{2,0},{3,1},{4,6},{5,7},{6,4},{7,5},{8,10},{9,11},{10,... | collective-permute-start | bytes 884744 | tf_op jit(solution)/shard_map/ppermute | solution.py:466
  12.5 22.9 %copy-start = (bf16[1,1536,2048]{2,1,0:T(8,128)(2,1)S(1)}, bf16[1,1536,2048]{2,1,0:T(8,128)(2,1)}, u32[]{:S(2)}) copy-start(bf16[1,1536,2048]{2,1,0:T(8,128)(2,1)} %param.12) | copy-start | bytes 18874372
  15.6 23.9 %collective-permute-start.11 = (bf16[96,1536]{1,0:T(8,128)(2,1)S(1)}, bf16[96,1536]{1,0:T(8,128)(2,1)S(1)}, u32[]{:S(2)}, u32[]{:S(2)}) collective-permute-start(bf16[96,1536]{1,0:T(8,128)(2,1)S(1)} %get-tuple-element.61), channel_id=1, source_target_pairs={{0,7},{1,6},{2,3},{3,2},{4,5},{5,4},{6,1},{7,0},{8,15},{9,14},{10,... | collective-permute-start | bytes 884744 | tf_op jit(solution)/shard_map/ppermute | solution.py:482
  17.6 25.8 %collective-permute-start.10 = (bf16[96,1536]{1,0:T(8,128)(2,1)S(1)}, bf16[96,1536]{1,0:T(8,128)(2,1)S(1)}, u32[]{:S(2)}, u32[]{:S(2)}) collective-permute-start(bf16[96,1536]{1,0:T(8,128)(2,1)S(1)} %get-tuple-element.60.local_ref), channel_id=1, source_target_pairs={{0,6},{1,7},{6,0},{7,1},{8,14},{9,15},{14,8},{15,9},{16,22},{17,23... | collective-permute-start | bytes 884744 | tf_op jit(solution)/shard_map/ppermute | solution.py:482
  25.0 20.0 %collective-permute-start.8 = (bf16[96,1536]{1,0:T(8,128)(2,1)S(1)}, bf16[96,1536]{1,0:T(8,128)(2,1)S(1)}, u32[]{:S(2)}, u32[]{:S(2)}) collective-permute-start(bf16[96,1536]{1,0:T(8,128)(2,1)S(1)} %get-tuple-element.44), channel_id=1, source_target_pairs={{0,4},{1,5},{2,0},{3,1},{4,6},{5,7},{6,2},{7,3},{8,12},{9,13},{10,... | collective-permute-start | bytes 884744 | tf_op jit(solution)/shard_map/ppermute | solution.py:482
  28.9 22.4 %collective-permute-start.9 = (bf16[96,1536]{1,0:T(8,128)(2,1)S(1)}, bf16[96,1536]{1,0:T(8,128)(2,1)S(1)}, u32[]{:S(2)}, u32[]{:S(2)}) collective-permute-start(bf16[96,1536]{1,0:T(8,128)(2,1)S(1)} %get-tuple-element.45), channel_id=1, source_target_pairs={{0,5},{1,4},{2,1},{3,0},{4,7},{5,6},{6,3},{7,2},{8,13},{9,12},{10,... | collective-permute-start | bytes 884744 | tf_op jit(solution)/shard_map/ppermute | solution.py:482
  32.8 8.6 %copy-start.3 = (bf16[256,1536]{1,0:T(8,128)(2,1)S(1)}, bf16[256,1536]{1,0:T(8,128)(2,1)}, u32[]{:S(2)}) copy-start(bf16[256,1536]{1,0:T(8,128)(2,1)} %frames_ref.1) | copy-start | bytes 2359300
  32.8 8.6 %copy-start.6 = (bf16[1536,64]{0,1:T(8,128)(2,1)S(1)}, bf16[1536,64]{0,1:T(8,128)(2,1)}, u32[]{:S(2)}) copy-start(bf16[1536,64]{0,1:T(8,128)(2,1)} %param.14) | copy-start | bytes 589828
  32.8 8.6 %copy-start.8 = (f32[256,2]{0,1:T(2,128)S(1)}, f32[256,2]{0,1:T(2,128)}, u32[]{:S(2)}) copy-start(f32[256,2]{0,1:T(2,128)} %param.11) | copy-start | bytes 6148
  39.4 18.3 %collective-permute-start.5 = (bf16[128,128]{1,0:T(8,128)(2,1)S(1)}, bf16[128,128]{1,0:T(8,128)(2,1)S(1)}, u32[]{:S(2)}, u32[]{:S(2)}) collective-permute-start(bf16[128,128]{1,0:T(8,128)(2,1)S(1)} %get-tuple-element.57), channel_id=1, source_target_pairs={{0,1},{1,0},{2,3},{3,2},{4,5},{5,4},{6,7},{7,6},{8,9},{9,8},{10,11... | collective-permute-start | bytes 98312 | tf_op jit(solution)/shard_map/ppermute | solution.py:466
  39.5 20.7 %collective-permute-start.6 = (bf16[128,128]{1,0:T(8,128)(2,1)S(1)}, bf16[128,128]{1,0:T(8,128)(2,1)S(1)}, u32[]{:S(2)}, u32[]{:S(2)}) collective-permute-start(bf16[128,128]{1,0:T(8,128)(2,1)S(1)} %get-tuple-element.58), channel_id=1, source_target_pairs={{0,2},{1,3},{2,0},{3,1},{4,6},{5,7},{6,4},{7,5},{8,10},{9,11},{10,... | collective-permute-start | bytes 98312 | tf_op jit(solution)/shard_map/ppermute | solution.py:466
  43.5 18.1 %collective-permute-start.7 = (bf16[128,128]{1,0:T(8,128)(2,1)S(1)}, bf16[128,128]{1,0:T(8,128)(2,1)S(1)}, u32[]{:S(2)}, u32[]{:S(2)}) collective-permute-start(bf16[128,128]{1,0:T(8,128)(2,1)S(1)} %get-tuple-element.59), channel_id=1, source_target_pairs={{0,3},{1,2},{2,1},{3,0},{4,7},{5,6},{6,5},{7,4},{8,11},{9,10},{10,... | collective-permute-start | bytes 98312 | tf_op jit(solution)/shard_map/ppermute | solution.py:466
  55.2 6.3 %collective-permute-start.12 = (bf16[128,128]{1,0:T(8,128)(2,1)S(1)}, bf16[128,128]{1,0:T(8,128)(2,1)S(1)}, u32[]{:S(2)}, u32[]{:S(2)}) collective-permute-start(bf16[128,128]{1,0:T(8,128)(2,1)S(1)} %get-tuple-element.62), channel_id=1, source_target_pairs={{0,4},{1,5},{2,6},{3,7},{4,0},{5,1},{6,2},{7,3},{8,12},{9,13},{10,... | collective-permute-start | bytes 98312 | tf_op jit(solution)/shard_map/ppermute | solution.py:466
  56.4 5.2 %collective-permute-start.13 = (bf16[128,128]{1,0:T(8,128)(2,1)S(1)}, bf16[128,128]{1,0:T(8,128)(2,1)S(1)}, u32[]{:S(2)}, u32[]{:S(2)}) collective-permute-start(bf16[128,128]{1,0:T(8,128)(2,1)S(1)} %get-tuple-element.63), channel_id=1, source_target_pairs={{0,5},{1,4},{2,7},{3,6},{4,1},{5,0},{6,3},{7,2},{8,13},{9,12},{10,... | collective-permute-start | bytes 98312 | tf_op jit(solution)/shard_map/ppermute | solution.py:466
  57.7 5.8 %collective-permute-start.14 = (bf16[128,128]{1,0:T(8,128)(2,1)S(1)}, bf16[128,128]{1,0:T(8,128)(2,1)S(1)}, u32[]{:S(2)}, u32[]{:S(2)}) collective-permute-start(bf16[128,128]{1,0:T(8,128)(2,1)S(1)} %get-tuple-element.64), channel_id=1, source_target_pairs={{0,6},{1,7},{2,4},{3,5},{4,2},{5,3},{6,0},{7,1},{8,14},{9,15},{10,... | collective-permute-start | bytes 98312 | tf_op jit(solution)/shard_map/ppermute | solution.py:466
  60.2 5.1 %collective-permute-start.15 = (bf16[128,128]{1,0:T(8,128)(2,1)S(1)}, bf16[128,128]{1,0:T(8,128)(2,1)S(1)}, u32[]{:S(2)}, u32[]{:S(2)}) collective-permute-start(bf16[128,128]{1,0:T(8,128)(2,1)S(1)} %get-tuple-element.65), channel_id=1, source_target_pairs={{0,7},{1,6},{2,5},{3,4},{4,3},{5,2},{6,1},{7,0},{8,15},{9,14},{10,... | collective-permute-start | bytes 98312 | tf_op jit(solution)/shard_map/ppermute | solution.py:466
  66.5 0.7 collective-permute-start.16
  67.2 5.6 %collective-permute-start.19 = (bf16[288,64]{1,0:T(8,128)(2,1)S(1)}, bf16[288,64]{1,0:T(8,128)(2,1)S(1)}, u32[]{:S(2)}, u32[]{:S(2)}) collective-permute-start(bf16[288,64]{1,0:T(8,128)(2,1)S(1)} %constant_dynamic-update-slice_fusion.refs_0_), channel_id=1, source_target_pairs={{0,24},{8,16},{16,8},{24,0},{1,25},{9,17},{17,9},{25,1},{2,26},{10... | collective-permute-start | bytes 110600 | tf_op jit(solution)/shard_map/ppermute | solution.py:506
  69.7 4.6 %collective-permute-start.18 = (bf16[288,64]{1,0:T(8,128)(2,1)S(1)}, bf16[288,64]{1,0:T(8,128)(2,1)S(1)}, u32[]{:S(2)}, u32[]{:S(2)}) collective-permute-start(bf16[288,64]{1,0:T(8,128)(2,1)S(1)} %constant_dynamic-update-slice_fusion.refs_0_), channel_id=1, source_target_pairs={{0,16},{8,24},{16,0},{24,8},{1,17},{9,25},{17,1},{25,9},{2,18},{10... | collective-permute-start | bytes 110600 | tf_op jit(solution)/shard_map/ppermute | solution.py:506
  70.3 4.4 %collective-permute-start.17 = (bf16[288,64]{1,0:T(8,128)(2,1)S(1)}, bf16[288,64]{1,0:T(8,128)(2,1)S(1)}, u32[]{:S(2)}, u32[]{:S(2)}) collective-permute-start(bf16[288,64]{1,0:T(8,128)(2,1)S(1)} %constant_dynamic-update-slice_fusion.refs_0_), channel_id=1, source_target_pairs={{0,8},{8,0},{16,24},{24,16},{1,9},{9,1},{17,25},{25,17},{2,10},{10... | collective-permute-start | bytes 110600 | tf_op jit(solution)/shard_map/ppermute | solution.py:506
  (6 other events, 15.4 us)

commit v7 on v6

--- a/solution.py
+++ b/solution.py
@@ -65,10 +65,10 @@
     return jnp.concatenate(ends + [meta], axis=0).astype(BF16)
 
 
-def slots_kernel(steps, origin_ref, *refs):
+def slots_kernel(steps, first, origin_ref, *refs):
     sources, out_refs = refs[: -len(steps)], refs[-len(steps) :]
     ids, frames = sources[0][...], sources[1][...]
-    if len(sources) == 3:
+    if first:
         capacity = out_refs[0].shape[0]
         extra = edge_rows(frames, ids, sources[2][...])
         for k, ref in zip(steps, out_refs):
@@ -97,16 +97,13 @@
 
 def make_slots(origin, steps, sources, capacity):
     width = sources[1].shape[1]
+    first = len(sources) == 3
+    heights = [capacity + EDGE_ROWS * (first and is_neighbour(k)) for k in steps]
     return pl.pallas_call(
-        functools.partial(slots_kernel, steps),
-        out_shape=[
-            jax.ShapeDtypeStruct(
-                (capacity + EDGE_ROWS * (len(sources) == 3 and is_neighbour(k)), width), BF16
-            )
-            for k in steps
-        ],
+        functools.partial(slots_kernel, steps, first),
+        out_shape=[jax.ShapeDtypeStruct((height, width), BF16) for height in heights],
         in_specs=[pl.BlockSpec(memory_space=pltpu.SMEM)] + [whole()] * len(sources),
-        out_specs=[whole()] * len(steps),
+        out_specs=[whole()] * len(heights),
         compiler_params=params(24),
         cost_estimate=FREE,
     )(origin, *sources)
@@ -306,11 +303,12 @@
     part_refs = refs[:n]
     pick_ref, scale_ref, base_ref, low_ref, middle_ref = refs[n:]
     span, lat = base_ref.shape
-    latent = base_ref[...]
+    total = None
     for k in range(n):
         picked = jnp.dot(pick_ref[k], part_refs[k][...], preferred_element_type=F32)
-        latent = latent + scale_ref[:, k : k + 1] * (picked[:, :lat] + picked[:, lat:])
-    low = latent.astype(BF16)
+        scaled = scale_ref[:, k : k + 1] * picked
+        total = scaled if total is None else total + scaled
+    low = (base_ref[...] + (total[:, :lat] + total[:, lat:])).astype(BF16)
     low_ref[...] = low
     middle_ref[...] = jnp.where(
         place_ref[0] >= place_ref[1] // 2, low[:EDGE_ROWS], low[span - EDGE_ROWS :]
@@ -343,9 +341,9 @@
 
 
 def decoder_kernel(segs, place_ref, *refs):
-    lat_refs = refs[:segs]
-    conv_ref, alpha_ref, up_hbm, out_ref = refs[segs : segs + 4]
-    padded, windows, act, up_ref, rows_out, sems, up_sem = refs[segs + 4 :]
+    lat_refs, middle_refs = refs[:segs], refs[segs : 2 * segs]
+    conv_ref, alpha_ref, up_hbm, out_ref = refs[2 * segs : 2 * segs + 4]
+    padded, windows, act, up_ref, rows_out, sems, up_sem = refs[2 * segs + 4 :]
     span, channels = act.shape[1:]
     length = span - 16
     width = up_ref.shape[2]
@@ -365,18 +363,18 @@
     edge_row = lax.broadcasted_iota(jnp.int32, (16, block), 0)
     gone = ((edge_row == 0) & is_first) | ((edge_row == 1) & is_last)
     for k in range(segs):
-        padded[k] = lat_refs[k][0:span].astype(F32)
+        padded[k] = lat_refs[k][...].astype(F32)
     end = length + EDGE
 
     @pl.when(place_ref[1] == place_ref[2] // 2)
     def _():
         for k in range(segs):
-            padded[k, 0:EDGE] = lat_refs[k][span:].astype(F32)[:EDGE]
+            padded[k, 0:EDGE] = middle_refs[k][...].astype(F32)[:EDGE]
 
     @pl.when(place_ref[1] == place_ref[2] // 2 - 1)
     def _():
         for k in range(segs):
-            padded[k, end : end + EDGE] = lat_refs[k][span:].astype(F32)[EDGE : 2 * EDGE]
+            padded[k, end : end + EDGE] = middle_refs[k][...].astype(F32)[EDGE : 2 * EDGE]
 
     for k in range(segs):
 
@@ -414,8 +412,8 @@
 
 
 def decode(place, slabs, conv, alpha, first_up):
-    segs = len(slabs)
-    length = slabs[0].shape[0] - 4 * EDGE - EDGE_ROWS
+    segs = len(slabs) // 2
+    length = slabs[0].shape[0] - 4 * EDGE
     channels = conv.shape[1]
     width = first_up.shape[2]
     lat = slabs[0].shape[1]
@@ -423,7 +421,7 @@
         functools.partial(decoder_kernel, segs),
         out_shape=jax.ShapeDtypeStruct((segs, 8 * length, width), F32),
         in_specs=[pl.BlockSpec(memory_space=pltpu.SMEM)]
-        + [whole()] * (segs + 2)
+        + [whole()] * (2 * segs + 2)
         + [pl.BlockSpec(memory_space=pl.ANY)],
         out_specs=pl.BlockSpec(memory_space=pl.ANY),
         scratch_shapes=[
@@ -499,12 +497,16 @@
     back = run_group(n, True, place, sent[quarter], far, up, folded)
     parts += [swap(back[k], half + k) for k in range(half)]
     slab, middle = combine(place, parts, pick, scale, base)
-    middle = lax.ppermute(middle, "expert", [(half - 1, half), (half, half - 1)])
-    slab = jnp.concatenate([slab, middle], axis=0)
+
+    def over_middle(k):
+        ends = ((half - 1, half), (half, half - 1))
+        pairs = [(i * n + a, (i ^ k) * n + b) for i in range(segs) for a, b in ends]
+        return lax.ppermute(middle, ("seg", "expert"), pairs)
 
     slabs = [slab] + [
         lax.ppermute(slab, "seg", [(i, i ^ k) for i in range(segs)]) for k in range(1, segs)
     ]
+    slabs += [over_middle(k) for k in range(segs)]
     spot = jnp.stack([lax.axis_index("seg"), me, jnp.int32(n)]).astype(jnp.int32)
     alpha = jnp.stack([snake_first * (1.0 / math.pi), 1.0 / snake_first])
     conv = in_conv.reshape(-1, in_conv.shape[2])

time: 93.7 us -> 101 us (1.078)
  the two profiles are of different devices: /device:TPU:0 before, /device:TPU:20 now
where the time goes in v7:
time: 101 us; the launch traced here: 100 us
  Pallas kernels  35.1 us (35%)
  starting transfers between devices  33.5 us (33%)
  waiting for transfers between devices  24.6 us (24%)
  local copies, waits for them, and re-layouts  6.68 us (7%)
    pallas_call x1, Pallas kernels, decode(): pl.pallas_call(functools.partial(decoder_kernel, segs), out_shape=jax.Sha...  18.6 us
    ppermute x12, starting transfers between devices, swap(): return lax.ppermute(value, 'expert', [(i, i ^ k) for i in members])  14.5 us
    ppermute x12, waiting for transfers between devices, swap(): return lax.ppermute(value, 'expert', [(i, i ^ k) for i in members])  13.5 us
    ppermute x4, starting transfers between devices, over_middle(): return lax.ppermute(middle, ('seg', 'expert'), pairs)  12.9 us
    pallas_call x2, Pallas kernels, run_group(): pl.pallas_call(functools.partial(group_kernel, n, far), out_shape=[jax.Sh...  7.98 us
    ppermute x4, waiting for transfers between devices, cross(): return lax.ppermute(value, 'expert', [(i, j) for i, j in pairs if i != j])  7.4 us
    unnamed x20, local copies, waits for them, and re-layouts  6.68 us
    ppermute x3, waiting for transfers between devices, local(): lax.ppermute(slab, 'seg', [(i, i ^ k) for i in range(segs)])  3.69 us
  transfers between devices with their start and end apart: 23, of which 9 were waited for; matrix products, arithmetic and copies ran while one was open for 0% of the time, Pallas kernels for 15%

profile of v7, /device:TPU:20, one launch (start us, length us, event | category | flops | bytes accessed | tf_op | source)
XLA Modules:
  0.0 100.5 jit_solution(16095927652901516901)
XLA Ops:
  0.0 2.3 %collective-permute-start.1 = (bf16[256,1536]{1,0:T(8,128)(2,1)}, bf16[256,1536]{1,0:T(8,128)(2,1)S(1)}, u32[]{:S(2)}, u32[]{:S(2)}) collective-permute-start(bf16[256,1536]{1,0:T(8,128)(2,1)} %frames_ref.1), channel_id=1, source_target_pairs={{2,4},{3,5},{4,2},{5,3},{10,12},{11,13},{12,10},{13,11},{18,20},{1... | collective-permute-start | bytes 2359304 | tf_op jit(solution)/shard_map/ppermute | solution.py:464
  4.3 1.5 %shard_map.91 = (bf16[96,1536]{1,0:T(8,128)(2,1)S(1)}, bf16[112,1536]{1,0:T(8,128)(2,1)S(1)}, bf16[96,1536]{1,0:T(8,128)(2,1)S(1)}, bf16[112,1536]{1,0:T(8,128)(2,1)S(1)}) custom-call(s32[2]{0:T(128)S(1)} %get-tuple-element.74.origin_ref, s32[2,256]{1,0:T(2,128)} %bitcast.3.refs_0_.ids_ref, bf16[256,1536]{1,0:T(8,128)(2,1)S(1)} %copy-done.1, ...), custom_call_target="tpu_custom_call" | custom-call | tf_op jit(solution)/shard_map/pallas_call | solution.py:102
  5.9 2.1 %collective-permute-start.3 = (bf16[96,1536]{1,0:T(8,128)(2,1)S(1)}, bf16[96,1536]{1,0:T(8,128)(2,1)S(1)}, u32[]{:S(2)}, u32[]{:S(2)}) collective-permute-start(bf16[96,1536]{1,0:T(8,128)(2,1)S(1)} %get-tuple-element.42), channel_id=1, source_target_pairs={{0,2},{1,3},{2,0},{3,1},{4,6},{5,7},{6,4},{7,5},{8,10},{9,11},{10,... | collective-permute-start | bytes 884744 | tf_op jit(solution)/shard_map/ppermute | solution.py:464
  8.0 3.5 %collective-permute-start = (s32[2,256]{1,0:T(2,128)}, s32[2,256]{1,0:T(2,128)S(1)}, u32[]{:S(2)}, u32[]{:S(2)}) collective-permute-start(s32[2,256]{1,0:T(2,128)} %bitcast.3.refs_0_.ids_ref), channel_id=1, source_target_pairs={{2,4},{3,5},{4,2},{5,3},{10,12},{11,13},{12,10},{13,11},{18,20},{1... | collective-permute-start | bytes 6152 | tf_op jit(solution)/shard_map/ppermute | solution.py:464
  11.5 9.9 %collective-permute-done.refs_2_ = s32[2,256]{1,0:T(2,128)S(1)} collective-permute-done((s32[2,256]{1,0:T(2,128)}, s32[2,256]{1,0:T(2,128)S(1)}, u32[]{:S(2)}, u32[]{:S(2)}) %collective-permute-start) | collective-permute-done | bytes 2080 | tf_op jit(solution)/shard_map/ppermute | solution.py:464
  22.6 1.5 %shard_map.92 = (bf16[96,1536]{1,0:T(8,128)(2,1)S(1)}, bf16[96,1536]{1,0:T(8,128)(2,1)S(1)}, bf16[96,1536]{1,0:T(8,128)(2,1)S(1)}, bf16[96,1536]{1,0:T(8,128)(2,1)S(1)}) custom-call(s32[2]{0:T(128)S(1)} %pad_add_fusion.3.origin_ref, s32[2,256]{1,0:T(2,128)} %bitcast.3.refs_0_.ids_ref, bf16[256,1536]{1,0:T(8,128)(2,1)S(1)} %copy-done.2, ...), custom_call_target="tpu_custom_call" | custom-call | tf_op jit(solution)/shard_map/pallas_call | solution.py:102
  24.9 1.7 %collective-permute-start.9 = (bf16[96,1536]{1,0:T(8,128)(2,1)S(1)}, bf16[96,1536]{1,0:T(8,128)(2,1)S(1)}, u32[]{:S(2)}, u32[]{:S(2)}) collective-permute-start(bf16[96,1536]{1,0:T(8,128)(2,1)S(1)} %get-tuple-element.45), channel_id=1, source_target_pairs={{0,5},{1,4},{2,1},{3,0},{4,7},{5,6},{6,3},{7,2},{8,13},{9,12},{10,... | collective-permute-start | bytes 884744 | tf_op jit(solution)/shard_map/ppermute | solution.py:480
  26.6 2.8 %copy-done.4 = bf16[1,2048,1536]{2,1,0:T(8,128)(2,1)S(1)} copy-done((bf16[1,2048,1536]{2,1,0:T(8,128)(2,1)S(1)}, bf16[1,2048,1536]{2,1,0:T(8,128)(2,1)}, u32[]{:S(2)}) %copy-start.4) | copy-done | bytes 6291480
  30.4 2.5 %shard_map.94.refs_4_.refs_5_ = bf16[2048,128]{1,0:T(8,128)(2,1)S(1)} custom-call(bf16[2048,1536]{1,0:T(8,128)(2,1)S(1)} %bitcast.14, bf16[64,1536]{1,0:T(8,128)(2,1)S(1)} %bitcast.15), custom_call_target="tpu_custom_call" | custom-call | tf_op jit(solution)/shard_map/pallas_call | solution.py:125
  32.9 4.0 %shard_map.95 = (bf16[128,128]{1,0:T(8,128)(2,1)S(1)}, bf16[128,128]{1,0:T(8,128)(2,1)S(1)}, bf16[128,128]{1,0:T(8,128)(2,1)S(1)}, bf16[128,128]{1,0:T(8,128)(2,1)S(1)}) custom-call(s32[2]{0:T(128)S(1)} %get-tuple-element.52.place_ref, bf16[96,1536]{1,0:T(8,128)(2,1)S(1)} %get-tuple-element.53.local_ref, ...), custom_call_target="tpu_custom_call" | custom-call | tf_op jit(solution)/shard_map/pallas_call | solution.py:291
  37.4 2.0 %shard_map.93 = (bf16[8,272,128]{2,1,0:T(8,128)(2,1)S(1)}, f32[272,128]{1,0:T(8,128)S(1)}, f32[272,64]{1,0:T(8,128)S(1)}) custom-call(s32[2]{0:T(128)S(1)} %get-tuple-element.52.place_ref, bf16[256,1536]{1,0:T(8,128)(2,1)S(1)} %copy-done.3, bf16[64,1536]{1,0:T(8,128)(2,1)S(1)} %bitcast.16, s32[2,256]{1,0:T(2,128)} %bitcast.3.refs_0_.ids_ref, ...), custom_call_target="tpu_custom_call" | custom-call | tf_op jit(solution)/shard_map/pallas_call | solution.py:223
  39.4 1.5 %collective-permute-start.7 = (bf16[128,128]{1,0:T(8,128)(2,1)S(1)}, bf16[128,128]{1,0:T(8,128)(2,1)S(1)}, u32[]{:S(2)}, u32[]{:S(2)}) collective-permute-start(bf16[128,128]{1,0:T(8,128)(2,1)S(1)} %get-tuple-element.59), channel_id=1, source_target_pairs={{0,3},{1,2},{2,1},{3,0},{4,7},{5,6},{6,5},{7,4},{8,11},{9,10},{10,... | collective-permute-start | bytes 98312 | tf_op jit(solution)/shard_map/ppermute | solution.py:464
  40.9 2.2 %collective-permute-done.8.refs_0_ = bf16[96,1536]{1,0:T(8,128)(2,1)S(1)} collective-permute-done((bf16[96,1536]{1,0:T(8,128)(2,1)S(1)}, bf16[96,1536]{1,0:T(8,128)(2,1)S(1)}, u32[]{:S(2)}, u32[]{:S(2)}) %collective-permute-start.8) | collective-permute-done | bytes 294944 | tf_op jit(solution)/shard_map/ppermute | solution.py:480
  43.1 5.2 %collective-permute-done.9.refs_1_ = bf16[96,1536]{1,0:T(8,128)(2,1)S(1)} collective-permute-done((bf16[96,1536]{1,0:T(8,128)(2,1)S(1)}, bf16[96,1536]{1,0:T(8,128)(2,1)S(1)}, u32[]{:S(2)}, u32[]{:S(2)}) %collective-permute-start.9) | collective-permute-done | bytes 294944 | tf_op jit(solution)/shard_map/ppermute | solution.py:480
  48.3 4.0 %shard_map.96 = (bf16[128,128]{1,0:T(8,128)(2,1)S(1)}, bf16[128,128]{1,0:T(8,128)(2,1)S(1)}, bf16[128,128]{1,0:T(8,128)(2,1)S(1)}, bf16[128,128]{1,0:T(8,128)(2,1)S(1)}) custom-call(s32[2]{0:T(128)S(1)} %get-tuple-element.52.place_ref, bf16[96,1536]{1,0:T(8,128)(2,1)S(1)} %get-tuple-element.60.local_ref, ...), custom_call_target="tpu_custom_call" | custom-call | tf_op jit(solution)/shard_map/pallas_call | solution.py:291
  52.3 1.9 %collective-permute-start.12 = (bf16[128,128]{1,0:T(8,128)(2,1)S(1)}, bf16[128,128]{1,0:T(8,128)(2,1)S(1)}, u32[]{:S(2)}, u32[]{:S(2)}) collective-permute-start(bf16[128,128]{1,0:T(8,128)(2,1)S(1)} %get-tuple-element.62), channel_id=1, source_target_pairs={{0,4},{1,5},{2,6},{3,7},{4,0},{5,1},{6,2},{7,3},{8,12},{9,13},{10,... | collective-permute-start | bytes 98312 | tf_op jit(solution)/shard_map/ppermute | solution.py:464
  61.4 4.1 %collective-permute-start.22 = (bf16[16,64]{1,0:T(8,128)(2,1)S(1)}, bf16[16,64]{1,0:T(8,128)(2,1)S(1)}, u32[]{:S(2)}, u32[]{:S(2)}) collective-permute-start(bf16[16,64]{1,0:T(8,128)(2,1)S(1)} %get-tuple-element.70), channel_id=1, source_target_pairs={{3,28},{4,27},{11,20},{12,19},{19,12},{20,11},{27,4},{28,3}} | collective-permute-start | bytes 6152 | tf_op jit(solution)/shard_map/ppermute | solution.py:504
  65.5 3.3 %collective-permute-start.21 = (bf16[16,64]{1,0:T(8,128)(2,1)S(1)}, bf16[16,64]{1,0:T(8,128)(2,1)S(1)}, u32[]{:S(2)}, u32[]{:S(2)}) collective-permute-start(bf16[16,64]{1,0:T(8,128)(2,1)S(1)} %get-tuple-element.70), channel_id=1, source_target_pairs={{3,20},{4,19},{11,28},{12,27},{19,4},{20,3},{27,12},{28,11}} | collective-permute-start | bytes 6152 | tf_op jit(solution)/shard_map/ppermute | solution.py:504
  68.9 3.2 %collective-permute-start.20 = (bf16[16,64]{1,0:T(8,128)(2,1)S(1)}, bf16[16,64]{1,0:T(8,128)(2,1)S(1)}, u32[]{:S(2)}, u32[]{:S(2)}) collective-permute-start(bf16[16,64]{1,0:T(8,128)(2,1)S(1)} %get-tuple-element.70), channel_id=1, source_target_pairs={{3,12},{4,11},{11,4},{12,3},{19,28},{20,27},{27,20},{28,19}} | collective-permute-start | bytes 6152 | tf_op jit(solution)/shard_map/ppermute | solution.py:504
  72.1 2.3 %collective-permute-start.19 = (bf16[16,64]{1,0:T(8,128)(2,1)S(1)}, bf16[16,64]{1,0:T(8,128)(2,1)S(1)}, u32[]{:S(2)}, u32[]{:S(2)}) collective-permute-start(bf16[16,64]{1,0:T(8,128)(2,1)S(1)} %get-tuple-element.70), channel_id=1, source_target_pairs={{3,4},{4,3},{11,12},{12,11},{19,20},{20,19},{27,28},{28,27}} | collective-permute-start | bytes 6152 | tf_op jit(solution)/shard_map/ppermute | solution.py:504
  74.4 1.5 %collective-permute-start.18 = (bf16[272,64]{1,0:T(8,128)(2,1)S(1)}, bf16[272,64]{1,0:T(8,128)(2,1)S(1)}, u32[]{:S(2)}, u32[]{:S(2)}) collective-permute-start(bf16[272,64]{1,0:T(8,128)(2,1)S(1)} %get-tuple-element.69.refs_0_), channel_id=1, source_target_pairs={{0,24},{8,16},{16,8},{24,0},{1,25},{9,17},{17,9},{25,1},{2,26},{10... | collective-permute-start | bytes 104456 | tf_op jit(solution)/shard_map/ppermute | solution.py:507
  75.9 1.5 %collective-permute-start.17 = (bf16[272,64]{1,0:T(8,128)(2,1)S(1)}, bf16[272,64]{1,0:T(8,128)(2,1)S(1)}, u32[]{:S(2)}, u32[]{:S(2)}) collective-permute-start(bf16[272,64]{1,0:T(8,128)(2,1)S(1)} %get-tuple-element.69.refs_0_), channel_id=1, source_target_pairs={{0,16},{8,24},{16,0},{24,8},{1,17},{9,25},{17,1},{25,9},{2,18},{10... | collective-permute-start | bytes 104456 | tf_op jit(solution)/shard_map/ppermute | solution.py:507
  78.1 1.6 %collective-permute-done.18.refs_3_ = bf16[272,64]{1,0:T(8,128)(2,1)S(1)} collective-permute-done((bf16[272,64]{1,0:T(8,128)(2,1)S(1)}, bf16[272,64]{1,0:T(8,128)(2,1)S(1)}, u32[]{:S(2)}, u32[]{:S(2)}) %collective-permute-start.18) | collective-permute-done | bytes 34848 | tf_op jit(solution)/shard_map/ppermute | solution.py:507
  81.8 18.6 %shard_map.98 = f32[4,2048,128]{2,1,0:T(8,128)} custom-call(s32[3]{0:T(128)S(1)} %pad_add_fusion.place_ref, bf16[272,64]{1,0:T(8,128)(2,1)S(1)} %get-tuple-element.69.refs_0_, bf16[272,64]{1,0:T(8,128)(2,1)S(1)} %collective-permute-done.16.refs_1_, bf16[272,64]{1,0:T(8,128)(2,1)S(1)} %collective-permute-done.17.refs_2_, ...), custom_call_target="tpu_custom_call" | custom-call | tf_op jit(solution)/shard_map/pallas_call | solution.py:420
  (55 shorter events, 15.4 us)
Async XLA Ops:
  0.0 21.4 %collective-permute-start.1 = (bf16[256,1536]{1,0:T(8,128)(2,1)}, bf16[256,1536]{1,0:T(8,128)(2,1)S(1)}, u32[]{:S(2)}, u32[]{:S(2)}) collective-permute-start(bf16[256,1536]{1,0:T(8,128)(2,1)} %frames_ref.1), channel_id=1, source_target_pairs={{2,4},{3,5},{4,2},{5,3},{10,12},{11,13},{12,10},{13,11},{18,20},{1... | collective-permute-start | bytes 2359304 | tf_op jit(solution)/shard_map/ppermute | solution.py:464
  5.7 19.1 %collective-permute-start.2 = (bf16[112,1536]{1,0:T(8,128)(2,1)S(1)}, bf16[112,1536]{1,0:T(8,128)(2,1)S(1)}, u32[]{:S(2)}, u32[]{:S(2)}) collective-permute-start(bf16[112,1536]{1,0:T(8,128)(2,1)S(1)} %get-tuple-element.41), channel_id=1, source_target_pairs={{0,1},{1,0},{2,3},{3,2},{4,5},{5,4},{6,7},{7,6},{8,9},{9,8},{10,11... | collective-permute-start | bytes 1032200 | tf_op jit(solution)/shard_map/ppermute | solution.py:464
  5.8 19.0 %collective-permute-start.4 = (bf16[112,1536]{1,0:T(8,128)(2,1)S(1)}, bf16[112,1536]{1,0:T(8,128)(2,1)S(1)}, u32[]{:S(2)}, u32[]{:S(2)}) collective-permute-start(bf16[112,1536]{1,0:T(8,128)(2,1)S(1)} %get-tuple-element.43), channel_id=1, source_target_pairs={{0,3},{1,2},{2,1},{3,0},{4,7},{5,6},{6,5},{7,4},{8,11},{9,10},{10,... | collective-permute-start | bytes 1032200 | tf_op jit(solution)/shard_map/ppermute | solution.py:464
  5.9 18.9 %collective-permute-start.3 = (bf16[96,1536]{1,0:T(8,128)(2,1)S(1)}, bf16[96,1536]{1,0:T(8,128)(2,1)S(1)}, u32[]{:S(2)}, u32[]{:S(2)}) collective-permute-start(bf16[96,1536]{1,0:T(8,128)(2,1)S(1)} %get-tuple-element.42), channel_id=1, source_target_pairs={{0,2},{1,3},{2,0},{3,1},{4,6},{5,7},{6,4},{7,5},{8,10},{9,11},{10,... | collective-permute-start | bytes 884744 | tf_op jit(solution)/shard_map/ppermute | solution.py:464
  8.0 13.5 %collective-permute-start = (s32[2,256]{1,0:T(2,128)}, s32[2,256]{1,0:T(2,128)S(1)}, u32[]{:S(2)}, u32[]{:S(2)}) collective-permute-start(s32[2,256]{1,0:T(2,128)} %bitcast.3.refs_0_.ids_ref), channel_id=1, source_target_pairs={{2,4},{3,5},{4,2},{5,3},{10,12},{11,13},{12,10},{13,11},{18,20},{1... | collective-permute-start | bytes 6152 | tf_op jit(solution)/shard_map/ppermute | solution.py:464
  11.5 21.4 %copy-start = (bf16[1,1536,2048]{2,1,0:T(8,128)(2,1)S(1)}, bf16[1,1536,2048]{2,1,0:T(8,128)(2,1)}, u32[]{:S(2)}) copy-start(bf16[1,1536,2048]{2,1,0:T(8,128)(2,1)} %param.12) | copy-start | bytes 18874372
  24.1 13.2 %collective-permute-start.11 = (bf16[96,1536]{1,0:T(8,128)(2,1)S(1)}, bf16[96,1536]{1,0:T(8,128)(2,1)S(1)}, u32[]{:S(2)}, u32[]{:S(2)}) collective-permute-start(bf16[96,1536]{1,0:T(8,128)(2,1)S(1)} %get-tuple-element.61), channel_id=1, source_target_pairs={{0,7},{1,6},{2,3},{3,2},{4,5},{5,4},{6,1},{7,0},{8,15},{9,14},{10,... | collective-permute-start | bytes 884744 | tf_op jit(solution)/shard_map/ppermute | solution.py:480
  24.1 15.3 %collective-permute-start.10 = (bf16[96,1536]{1,0:T(8,128)(2,1)S(1)}, bf16[96,1536]{1,0:T(8,128)(2,1)S(1)}, u32[]{:S(2)}, u32[]{:S(2)}) collective-permute-start(bf16[96,1536]{1,0:T(8,128)(2,1)S(1)} %get-tuple-element.60.local_ref), channel_id=1, source_target_pairs={{0,6},{1,7},{6,0},{7,1},{8,14},{9,15},{14,8},{15,9},{16,22},{17,23... | collective-permute-start | bytes 884744 | tf_op jit(solution)/shard_map/ppermute | solution.py:480
  24.9 18.3 %collective-permute-start.8 = (bf16[96,1536]{1,0:T(8,128)(2,1)S(1)}, bf16[96,1536]{1,0:T(8,128)(2,1)S(1)}, u32[]{:S(2)}, u32[]{:S(2)}) collective-permute-start(bf16[96,1536]{1,0:T(8,128)(2,1)S(1)} %get-tuple-element.44), channel_id=1, source_target_pairs={{0,4},{1,5},{2,0},{3,1},{4,6},{5,7},{6,2},{7,3},{8,12},{9,13},{10,... | collective-permute-start | bytes 884744 | tf_op jit(solution)/shard_map/ppermute | solution.py:480
  24.9 23.4 %collective-permute-start.9 = (bf16[96,1536]{1,0:T(8,128)(2,1)S(1)}, bf16[96,1536]{1,0:T(8,128)(2,1)S(1)}, u32[]{:S(2)}, u32[]{:S(2)}) collective-permute-start(bf16[96,1536]{1,0:T(8,128)(2,1)S(1)} %get-tuple-element.45), channel_id=1, source_target_pairs={{0,5},{1,4},{2,1},{3,0},{4,7},{5,6},{6,3},{7,2},{8,13},{9,12},{10,... | collective-permute-start | bytes 884744 | tf_op jit(solution)/shard_map/ppermute | solution.py:480
  36.9 18.6 %collective-permute-start.5 = (bf16[128,128]{1,0:T(8,128)(2,1)S(1)}, bf16[128,128]{1,0:T(8,128)(2,1)S(1)}, u32[]{:S(2)}, u32[]{:S(2)}) collective-permute-start(bf16[128,128]{1,0:T(8,128)(2,1)S(1)} %get-tuple-element.57), channel_id=1, source_target_pairs={{0,1},{1,0},{2,3},{3,2},{4,5},{5,4},{6,7},{7,6},{8,9},{9,8},{10,11... | collective-permute-start | bytes 98312 | tf_op jit(solution)/shard_map/ppermute | solution.py:464
  37.3 18.7 %collective-permute-start.6 = (bf16[128,128]{1,0:T(8,128)(2,1)S(1)}, bf16[128,128]{1,0:T(8,128)(2,1)S(1)}, u32[]{:S(2)}, u32[]{:S(2)}) collective-permute-start(bf16[128,128]{1,0:T(8,128)(2,1)S(1)} %get-tuple-element.58), channel_id=1, source_target_pairs={{0,2},{1,3},{2,0},{3,1},{4,6},{5,7},{6,4},{7,5},{8,10},{9,11},{10,... | collective-permute-start | bytes 98312 | tf_op jit(solution)/shard_map/ppermute | solution.py:464
  39.4 17.4 %collective-permute-start.7 = (bf16[128,128]{1,0:T(8,128)(2,1)S(1)}, bf16[128,128]{1,0:T(8,128)(2,1)S(1)}, u32[]{:S(2)}, u32[]{:S(2)}) collective-permute-start(bf16[128,128]{1,0:T(8,128)(2,1)S(1)} %get-tuple-element.59), channel_id=1, source_target_pairs={{0,3},{1,2},{2,1},{3,0},{4,7},{5,6},{6,5},{7,4},{8,11},{9,10},{10,... | collective-permute-start | bytes 98312 | tf_op jit(solution)/shard_map/ppermute | solution.py:464
  52.3 5.3 %collective-permute-start.12 = (bf16[128,128]{1,0:T(8,128)(2,1)S(1)}, bf16[128,128]{1,0:T(8,128)(2,1)S(1)}, u32[]{:S(2)}, u32[]{:S(2)}) collective-permute-start(bf16[128,128]{1,0:T(8,128)(2,1)S(1)} %get-tuple-element.62), channel_id=1, source_target_pairs={{0,4},{1,5},{2,6},{3,7},{4,0},{5,1},{6,2},{7,3},{8,12},{9,13},{10,... | collective-permute-start | bytes 98312 | tf_op jit(solution)/shard_map/ppermute | solution.py:464
  54.2 4.7 %collective-permute-start.13 = (bf16[128,128]{1,0:T(8,128)(2,1)S(1)}, bf16[128,128]{1,0:T(8,128)(2,1)S(1)}, u32[]{:S(2)}, u32[]{:S(2)}) collective-permute-start(bf16[128,128]{1,0:T(8,128)(2,1)S(1)} %get-tuple-element.63), channel_id=1, source_target_pairs={{0,5},{1,4},{2,7},{3,6},{4,1},{5,0},{6,3},{7,2},{8,13},{9,12},{10,... | collective-permute-start | bytes 98312 | tf_op jit(solution)/shard_map/ppermute | solution.py:464
  55.5 4.8 %collective-permute-start.14 = (bf16[128,128]{1,0:T(8,128)(2,1)S(1)}, bf16[128,128]{1,0:T(8,128)(2,1)S(1)}, u32[]{:S(2)}, u32[]{:S(2)}) collective-permute-start(bf16[128,128]{1,0:T(8,128)(2,1)S(1)} %get-tuple-element.64), channel_id=1, source_target_pairs={{0,6},{1,7},{2,4},{3,5},{4,2},{5,3},{6,0},{7,1},{8,14},{9,15},{10,... | collective-permute-start | bytes 98312 | tf_op jit(solution)/shard_map/ppermute | solution.py:464
  56.0 4.4 %collective-permute-start.15 = (bf16[128,128]{1,0:T(8,128)(2,1)S(1)}, bf16[128,128]{1,0:T(8,128)(2,1)S(1)}, u32[]{:S(2)}, u32[]{:S(2)}) collective-permute-start(bf16[128,128]{1,0:T(8,128)(2,1)S(1)} %get-tuple-element.65), channel_id=1, source_target_pairs={{0,7},{1,6},{2,5},{3,4},{4,3},{5,2},{6,1},{7,0},{8,15},{9,14},{10,... | collective-permute-start | bytes 98312 | tf_op jit(solution)/shard_map/ppermute | solution.py:464
  61.4 14.5 %collective-permute-start.22 = (bf16[16,64]{1,0:T(8,128)(2,1)S(1)}, bf16[16,64]{1,0:T(8,128)(2,1)S(1)}, u32[]{:S(2)}, u32[]{:S(2)}) collective-permute-start(bf16[16,64]{1,0:T(8,128)(2,1)S(1)} %get-tuple-element.70), channel_id=1, source_target_pairs={{3,28},{4,27},{11,20},{12,19},{19,12},{20,11},{27,4},{28,3}} | collective-permute-start | bytes 6152 | tf_op jit(solution)/shard_map/ppermute | solution.py:504
  65.5 11.9 %collective-permute-start.21 = (bf16[16,64]{1,0:T(8,128)(2,1)S(1)}, bf16[16,64]{1,0:T(8,128)(2,1)S(1)}, u32[]{:S(2)}, u32[]{:S(2)}) collective-permute-start(bf16[16,64]{1,0:T(8,128)(2,1)S(1)} %get-tuple-element.70), channel_id=1, source_target_pairs={{3,20},{4,19},{11,28},{12,27},{19,4},{20,3},{27,12},{28,11}} | collective-permute-start | bytes 6152 | tf_op jit(solution)/shard_map/ppermute | solution.py:504
  68.9 9.2 %collective-permute-start.20 = (bf16[16,64]{1,0:T(8,128)(2,1)S(1)}, bf16[16,64]{1,0:T(8,128)(2,1)S(1)}, u32[]{:S(2)}, u32[]{:S(2)}) collective-permute-start(bf16[16,64]{1,0:T(8,128)(2,1)S(1)} %get-tuple-element.70), channel_id=1, source_target_pairs={{3,12},{4,11},{11,4},{12,3},{19,28},{20,27},{27,20},{28,19}} | collective-permute-start | bytes 6152 | tf_op jit(solution)/shard_map/ppermute | solution.py:504
  72.1 6.0 %collective-permute-start.19 = (bf16[16,64]{1,0:T(8,128)(2,1)S(1)}, bf16[16,64]{1,0:T(8,128)(2,1)S(1)}, u32[]{:S(2)}, u32[]{:S(2)}) collective-permute-start(bf16[16,64]{1,0:T(8,128)(2,1)S(1)} %get-tuple-element.70), channel_id=1, source_target_pairs={{3,4},{4,3},{11,12},{12,11},{19,20},{20,19},{27,28},{28,27}} | collective-permute-start | bytes 6152 | tf_op jit(solution)/shard_map/ppermute | solution.py:504
  74.4 5.3 %collective-permute-start.18 = (bf16[272,64]{1,0:T(8,128)(2,1)S(1)}, bf16[272,64]{1,0:T(8,128)(2,1)S(1)}, u32[]{:S(2)}, u32[]{:S(2)}) collective-permute-start(bf16[272,64]{1,0:T(8,128)(2,1)S(1)} %get-tuple-element.69.refs_0_), channel_id=1, source_target_pairs={{0,24},{8,16},{16,8},{24,0},{1,25},{9,17},{17,9},{25,1},{2,26},{10... | collective-permute-start | bytes 104456 | tf_op jit(solution)/shard_map/ppermute | solution.py:507
  75.9 4.5 %collective-permute-start.17 = (bf16[272,64]{1,0:T(8,128)(2,1)S(1)}, bf16[272,64]{1,0:T(8,128)(2,1)S(1)}, u32[]{:S(2)}, u32[]{:S(2)}) collective-permute-start(bf16[272,64]{1,0:T(8,128)(2,1)S(1)} %get-tuple-element.69.refs_0_), channel_id=1, source_target_pairs={{0,16},{8,24},{16,0},{24,8},{1,17},{9,25},{17,1},{25,9},{2,18},{10... | collective-permute-start | bytes 104456 | tf_op jit(solution)/shard_map/ppermute | solution.py:507
  77.5 4.3 %collective-permute-start.16 = (bf16[272,64]{1,0:T(8,128)(2,1)S(1)}, bf16[272,64]{1,0:T(8,128)(2,1)S(1)}, u32[]{:S(2)}, u32[]{:S(2)}) collective-permute-start(bf16[272,64]{1,0:T(8,128)(2,1)S(1)} %get-tuple-element.69.refs_0_), channel_id=1, source_target_pairs={{0,8},{8,0},{16,24},{24,16},{1,9},{9,1},{17,25},{25,17},{2,10},{10... | collective-permute-start | bytes 104456 | tf_op jit(solution)/shard_map/ppermute | solution.py:507
  (9 other events, 47.6 us)

commit v8 on v6

--- a/solution.py
+++ b/solution.py
@@ -19,7 +19,6 @@
     12.99073314666748,
     -3.2729504108428955,
 )
-ROUNDER = 12582912.0
 
 
 FREE = pl.CostEstimate(flops=0, bytes_accessed=0, transcendentals=0)
@@ -306,24 +305,29 @@
     part_refs = refs[:n]
     pick_ref, scale_ref, base_ref, low_ref, middle_ref = refs[n:]
     span, lat = base_ref.shape
-    latent = base_ref[...]
+    packed = low_ref.shape[0]
+    total = None
     for k in range(n):
         picked = jnp.dot(pick_ref[k], part_refs[k][...], preferred_element_type=F32)
-        latent = latent + scale_ref[:, k : k + 1] * (picked[:, :lat] + picked[:, lat:])
-    low = latent.astype(BF16)
-    low_ref[...] = low
-    middle_ref[...] = jnp.where(
+        scaled = scale_ref[:, k : k + 1] * picked
+        total = scaled if total is None else total + scaled
+    low = (base_ref[...] + (total[:, :lat] + total[:, lat:])).astype(BF16)
+    low_ref[...] = jnp.concatenate([low[:packed], low[span - packed :]], axis=1)
+    edge = jnp.where(
         place_ref[0] >= place_ref[1] // 2, low[:EDGE_ROWS], low[span - EDGE_ROWS :]
     )
+    middle_ref[...] = jnp.concatenate([edge, edge], axis=1)
 
 
 def combine(place, parts, pick, scale, base):
     n = len(parts)
+    span, lat = base.shape
+    packed = -(-span // 32) * 16
     return pl.pallas_call(
         functools.partial(combine_kernel, n),
         out_shape=[
-            jax.ShapeDtypeStruct(base.shape, BF16),
-            jax.ShapeDtypeStruct((EDGE_ROWS, base.shape[1]), BF16),
+            jax.ShapeDtypeStruct((packed, 2 * lat), BF16),
+            jax.ShapeDtypeStruct((EDGE_ROWS, 2 * lat), BF16),
         ],
         in_specs=[pl.BlockSpec(memory_space=pltpu.SMEM)] + [whole()] * (n + 3),
         out_specs=[whole()] * 2,
@@ -334,7 +338,7 @@
 
 def snake(v, turns_row, inverse_row):
     turns = v * turns_row
-    part = turns - ((turns + ROUNDER) - ROUNDER)
+    part = turns - jnp.round(turns)
     s = part * part
     poly = SIN2[-1]
     for c in SIN2[-2::-1]:
@@ -342,65 +346,94 @@
     return v + (poly * s) * inverse_row
 
 
-def decoder_kernel(segs, place_ref, *refs):
-    lat_refs = refs[:segs]
-    conv_ref, alpha_ref, up_hbm, out_ref = refs[segs : segs + 4]
-    padded, windows, act, up_ref, rows_out, sems, up_sem = refs[segs + 4 :]
-    span, channels = act.shape[1:]
-    length = span - 16
-    width = up_ref.shape[2]
-    lat = lat_refs[0].shape[1]
+def unpack_slab(place_ref, slab_ref, padded):
+    span, lat = padded.shape
+    packed = slab_ref.shape[0] - EDGE_ROWS
+    end = span - 3 * EDGE
+    padded[0:packed] = slab_ref[0:packed, :lat].astype(F32)
+    padded[span - packed :] = slab_ref[0:packed, lat:].astype(F32)
+
+    @pl.when(place_ref[1] == place_ref[2] // 2)
+    def _():
+        padded[0:EDGE] = slab_ref[packed:, :lat].astype(F32)[:EDGE]
+
+    @pl.when(place_ref[1] == place_ref[2] // 2 - 1)
+    def _():
+        padded[end : end + EDGE] = slab_ref[packed:, :lat].astype(F32)[EDGE : 2 * EDGE]
+
+
+def convolve(place_ref, padded, windows, conv_ref, alpha_ref, act):
+    span, lat = padded.shape
+    length = span - 4 * EDGE
+    channels = conv_ref.shape[1]
     taps = conv_ref.shape[0] // lat
     block = 256
-    own = place_ref[0]
     is_first = place_ref[1] == 0
     is_last = place_ref[1] == place_ref[2] - 1
-    up_copy = pltpu.make_async_copy(up_hbm, up_ref, up_sem)
-    up_copy.start()
-
-    def out_copy(k):
-        return pltpu.make_async_copy(rows_out.at[k], out_ref.at[own ^ k], sems.at[k])
-
     row = lax.broadcasted_iota(jnp.int32, (16, taps * lat), 0)
     edge_row = lax.broadcasted_iota(jnp.int32, (16, block), 0)
     gone = ((edge_row == 0) & is_first) | ((edge_row == 1) & is_last)
-    for k in range(segs):
-        padded[k] = lat_refs[k][0:span].astype(F32)
-    end = length + EDGE
-
-    @pl.when(place_ref[1] == place_ref[2] // 2)
-    def _():
-        for k in range(segs):
-            padded[k, 0:EDGE] = lat_refs[k][span:].astype(F32)[:EDGE]
-
-    @pl.when(place_ref[1] == place_ref[2] // 2 - 1)
-    def _():
-        for k in range(segs):
-            padded[k, end : end + EDGE] = lat_refs[k][span:].astype(F32)[EDGE : 2 * EDGE]
-
-    for k in range(segs):
-
-        def window(start, rows):
-            parts = [padded[k, start + j : start + j + rows] for j in range(taps)]
-            return jnp.concatenate(parts, axis=1)
-
-        windows[k, 0:length] = window(1, length).astype(BF16)
-        edges = jnp.where(row == 0, window(0, 1), jnp.where(row == 1, window(length + 1, 1), 0.0))
-        windows[k, length:] = edges.astype(BF16)
-        for at in range(0, channels, block):
-            cols = slice(at, at + block)
-            v = jnp.dot(windows[k], conv_ref[:, cols], preferred_element_type=F32)
-            value = snake(v, alpha_ref[0:1, cols], alpha_ref[1:2, cols])
-            act[k, 0:length, cols] = value[:length].astype(BF16)
-            act[k, length:, cols] = jnp.where(gone, 0.0, value[length:]).astype(BF16)
+
+    def window(start, rows):
+        return jnp.concatenate([padded[start + j : start + j + rows] for j in range(taps)], axis=1)
+
+    windows[0:length] = window(1, length).astype(BF16)
+    edges = jnp.where(row == 0, window(0, 1), jnp.where(row == 1, window(length + 1, 1), 0.0))
+    windows[length:] = edges.astype(BF16)
+    for at in range(0, channels, block):
+        cols = slice(at, at + block)
+        v = jnp.dot(windows[...], conv_ref[:, cols], preferred_element_type=F32)
+        value = snake(v, alpha_ref[0:1, cols], alpha_ref[1:2, cols])
+        act[0:length, cols] = value[:length].astype(BF16)
+        act[length:, cols] = jnp.where(gone, 0.0, value[length:]).astype(BF16)
+
+
+def own_kernel(place_ref, slab_ref, conv_ref, alpha_ref, act_ref, padded, windows):
+    unpack_slab(place_ref, slab_ref, padded)
+    convolve(place_ref, padded, windows, conv_ref, alpha_ref, act_ref)
+
+
+def activate_own(place, slab, conv, alpha, span):
+    lat = slab.shape[1] // 2
+    taps_lat, channels = conv.shape
+    return pl.pallas_call(
+        own_kernel,
+        out_shape=jax.ShapeDtypeStruct((span, channels), BF16),
+        in_specs=[pl.BlockSpec(memory_space=pltpu.SMEM)] + [whole()] * 3,
+        out_specs=whole(),
+        scratch_shapes=[pltpu.VMEM((span, lat), F32), pltpu.VMEM((span, taps_lat), BF16)],
+        compiler_params=params(16),
+        cost_estimate=FREE,
+    )(place, slab, conv, alpha)
+
+
+def decoder_kernel(segs, place_ref, own_ref, *refs):
+    slab_refs = refs[: segs - 1]
+    conv_ref, alpha_ref, up_hbm, out_ref = refs[segs - 1 : segs + 3]
+    padded, windows, others, up_ref, rows_out, sems, up_sem = refs[segs + 3 :]
+    span = own_ref.shape[0]
+    length = span - 4 * EDGE
+    width = up_ref.shape[2]
+    own = place_ref[0]
+    up_copy = pltpu.make_async_copy(up_hbm, up_ref, up_sem)
+    up_copy.start()
+
+    def out_copy(k):
+        return pltpu.make_async_copy(rows_out.at[k], out_ref.at[own ^ k], sems.at[k])
+
+    for k in range(segs - 1):
+        unpack_slab(place_ref, slab_refs[k], padded.at[k])
+    for k in range(segs - 1):
+        convolve(place_ref, padded.at[k], windows.at[k], conv_ref, alpha_ref, others.at[k])
     up_copy.wait()
     for k in range(segs):
+        act = own_ref if k == 0 else others.at[k - 1]
         for r in range(0, 8, 2):
             far = r + 12 if r < 4 else r - 4
             near_w = jnp.concatenate([up_ref[r + 4], up_ref[r + 5]], axis=1)
             far_w = jnp.concatenate([up_ref[far], up_ref[far + 1]], axis=1)
-            near = jnp.dot(act[k, 0:length], near_w, preferred_element_type=F32)
-            side = jnp.dot(act[k], far_w, preferred_element_type=F32)
+            near = jnp.dot(act[0:length], near_w, preferred_element_type=F32)
+            side = jnp.dot(act[...], far_w, preferred_element_type=F32)
             if r < 4:
                 moved = [side[length : length + 1], side[: length - 1]]
             else:
@@ -413,12 +446,12 @@
         out_copy(k).wait()
 
 
-def decode(place, slabs, conv, alpha, first_up):
-    segs = len(slabs)
-    length = slabs[0].shape[0] - 4 * EDGE - EDGE_ROWS
-    channels = conv.shape[1]
+def decode(place, own, slabs, conv, alpha, first_up):
+    segs = len(slabs) + 1
+    span, channels = own.shape
+    length = span - 4 * EDGE
     width = first_up.shape[2]
-    lat = slabs[0].shape[1]
+    lat = slabs[0].shape[1] // 2
     return pl.pallas_call(
         functools.partial(decoder_kernel, segs),
         out_shape=jax.ShapeDtypeStruct((segs, 8 * length, width), F32),
@@ -427,9 +460,9 @@
         + [pl.BlockSpec(memory_space=pl.ANY)],
         out_specs=pl.BlockSpec(memory_space=pl.ANY),
         scratch_shapes=[
-            pltpu.VMEM((segs, length + 16, lat), F32),
-            pltpu.VMEM((segs, length + 16, conv.shape[0]), BF16),
-            pltpu.VMEM((segs, length + 16, channels), BF16),
+            pltpu.VMEM((segs - 1, span, lat), F32),
+            pltpu.VMEM((segs - 1, span, conv.shape[0]), BF16),
+            pltpu.VMEM((segs - 1, span, channels), BF16),
             pltpu.VMEM(first_up.shape, BF16),
             pltpu.VMEM((segs, 8 * length, width), F32),
             pltpu.SemaphoreType.DMA((segs,)),
@@ -437,7 +470,7 @@
         ],
         compiler_params=params(52),
         cost_estimate=FREE,
-    )(place, *slabs, conv, alpha, first_up)
+    )(place, own, *slabs, conv, alpha, first_up)
 
 
 def local(
@@ -502,13 +535,14 @@
     middle = lax.ppermute(middle, "expert", [(half - 1, half), (half, half - 1)])
     slab = jnp.concatenate([slab, middle], axis=0)
 
-    slabs = [slab] + [
+    others = [
         lax.ppermute(slab, "seg", [(i, i ^ k) for i in range(segs)]) for k in range(1, segs)
     ]
     spot = jnp.stack([lax.axis_index("seg"), me, jnp.int32(n)]).astype(jnp.int32)
     alpha = jnp.stack([snake_first * (1.0 / math.pi), 1.0 / snake_first])
     conv = in_conv.reshape(-1, in_conv.shape[2])
-    return decode(spot, slabs, conv, alpha, first_up)
+    act = activate_own(spot, slab, conv, alpha, base.shape[0])
+    return decode(spot, act, others, conv, alpha, first_up)
 
 
 def solution(mesh):

time: 93.7 us -> 91.6 us (0.978)
  waiting for transfers between devices: 19.4 us -> 16.6 us
    ppermute x3, waiting for transfers between devices: 3.74 us -> 1.02 us  [local(): lax.ppermute(slab, 'seg', [(i, i ^ k) for i in range(segs)])]
    pallas_call x0 -> x1, Pallas kernels: none -> 2.35 us  [activate_own(): pl.pallas_call(own_kernel, out_shape=jax.ShapeDtypeStruct((span, channels...]
    pallas_call x1, Pallas kernels: 18.5 us -> 16.9 us  [decode(): pl.pallas_call(functools.partial(decoder_kernel, segs), out_shape=jax.Sha...]
    unnamed x21 -> x23, local copies, waits for them, and re-layouts: 6.83 us -> 6.84 us
  transfers between devices with their start and end apart: 20 -> 20, of which waited for: 8 -> 7; matrix products, arithmetic and copies ran while one was open for 0% -> 0% of each run, Pallas kernels for 17% -> 20%
where the time goes in v8:
time: 91.6 us; the launch traced here: 91.2 us
  Pallas kernels  36.1 us (39%)
  starting transfers between devices  31 us (34%)
  waiting for transfers between devices  16.6 us (18%)
  local copies, waits for them, and re-layouts  6.85 us (7%)
    ppermute x12, starting transfers between devices, swap(): return lax.ppermute(value, 'expert', [(i, i ^ k) for i in members])  17.5 us
    pallas_call x1, Pallas kernels, decode(): pl.pallas_call(functools.partial(decoder_kernel, segs), out_shape=jax.Sha...  16.9 us
    ppermute x4, starting transfers between devices, cross(): return lax.ppermute(value, 'expert', [(i, j) for i, j in pairs if i != j])  9.35 us
    pallas_call x2, Pallas kernels, run_group(): pl.pallas_call(functools.partial(group_kernel, n, far), out_shape=[jax.Sh...  7.95 us
    ppermute x12, waiting for transfers between devices, swap(): return lax.ppermute(value, 'expert', [(i, i ^ k) for i in members])  7.88 us
    ppermute x4, waiting for transfers between devices, cross(): return lax.ppermute(value, 'expert', [(i, j) for i, j in pairs if i != j])  7.7 us
    unnamed x23, local copies, waits for them, and re-layouts  6.84 us
    ppermute x3, starting transfers between devices, local(): lax.ppermute(slab, 'seg', [(i, i ^ k) for i in range(segs)])  3.55 us
  transfers between devices with their start and end apart: 20, of which 7 were waited for; matrix products, arithmetic and copies ran while one was open for 0% of the time, Pallas kernels for 20%

profile of v8, /device:TPU:0, one launch (start us, length us, event | category | flops | bytes accessed | tf_op | source)
XLA Modules:
  0.0 91.2 jit_solution(12562572397696018617)
XLA Ops:
  2.6 1.5 %shard_map.91 = (bf16[96,1536]{1,0:T(8,128)(2,1)S(1)}, bf16[112,1536]{1,0:T(8,128)(2,1)S(1)}, bf16[96,1536]{1,0:T(8,128)(2,1)S(1)}, bf16[112,1536]{1,0:T(8,128)(2,1)S(1)}) custom-call(s32[2]{0:T(128)S(1)} %get-tuple-element.74.origin_ref, s32[2,256]{1,0:T(2,128)} %bitcast.3.refs_0_.ids_ref, bf16[256,1536]{1,0:T(8,128)(2,1)S(1)} %copy-done.2, ...), custom_call_target="tpu_custom_call" | custom-call | tf_op jit(solution)/shard_map/pallas_call | solution.py:99
  4.6 5.5 %collective-permute-start.4 = (bf16[112,1536]{1,0:T(8,128)(2,1)S(1)}, bf16[112,1536]{1,0:T(8,128)(2,1)S(1)}, u32[]{:S(2)}, u32[]{:S(2)}) collective-permute-start(bf16[112,1536]{1,0:T(8,128)(2,1)S(1)} %get-tuple-element.43), channel_id=1, source_target_pairs={{0,3},{1,2},{2,1},{3,0},{4,7},{5,6},{6,5},{7,4},{8,11},{9,10},{10,... | collective-permute-start | bytes 1032200 | tf_op jit(solution)/shard_map/ppermute | solution.py:499
  10.7 1.7 %collective-permute-start.3 = (bf16[96,1536]{1,0:T(8,128)(2,1)S(1)}, bf16[96,1536]{1,0:T(8,128)(2,1)S(1)}, u32[]{:S(2)}, u32[]{:S(2)}) collective-permute-start(bf16[96,1536]{1,0:T(8,128)(2,1)S(1)} %get-tuple-element.42), channel_id=1, source_target_pairs={{0,2},{1,3},{2,0},{3,1},{4,6},{5,7},{6,4},{7,5},{8,10},{9,11},{10,... | collective-permute-start | bytes 884744 | tf_op jit(solution)/shard_map/ppermute | solution.py:499
  13.8 1.8 %shard_map.92 = (bf16[96,1536]{1,0:T(8,128)(2,1)S(1)}, bf16[96,1536]{1,0:T(8,128)(2,1)S(1)}, bf16[96,1536]{1,0:T(8,128)(2,1)S(1)}, bf16[96,1536]{1,0:T(8,128)(2,1)S(1)}) custom-call(s32[2]{0:T(128)S(1)} %pad_add_fusion.3.origin_ref, s32[2,256]{1,0:T(2,128)} %bitcast.3.refs_0_.ids_ref, bf16[256,1536]{1,0:T(8,128)(2,1)S(1)} %copy-done.3, ...), custom_call_target="tpu_custom_call" | custom-call | tf_op jit(solution)/shard_map/pallas_call | solution.py:99
  15.6 2.0 %collective-permute-start.11 = (bf16[96,1536]{1,0:T(8,128)(2,1)S(1)}, bf16[96,1536]{1,0:T(8,128)(2,1)S(1)}, u32[]{:S(2)}, u32[]{:S(2)}) collective-permute-start(bf16[96,1536]{1,0:T(8,128)(2,1)S(1)} %get-tuple-element.61), channel_id=1, source_target_pairs={{0,7},{1,6},{2,3},{3,2},{4,5},{5,4},{6,1},{7,0},{8,15},{9,14},{10,... | collective-permute-start | bytes 884744 | tf_op jit(solution)/shard_map/ppermute | solution.py:515
  17.6 3.2 %collective-permute-start.10 = (bf16[96,1536]{1,0:T(8,128)(2,1)S(1)}, bf16[96,1536]{1,0:T(8,128)(2,1)S(1)}, u32[]{:S(2)}, u32[]{:S(2)}) collective-permute-start(bf16[96,1536]{1,0:T(8,128)(2,1)S(1)} %get-tuple-element.60.local_ref), channel_id=1, source_target_pairs={{0,6},{1,7},{6,0},{7,1},{8,14},{9,15},{14,8},{15,9},{16,22},{17,23... | collective-permute-start | bytes 884744 | tf_op jit(solution)/shard_map/ppermute | solution.py:515
  20.9 4.1 %collective-permute-done.3.refs_1_ = bf16[96,1536]{1,0:T(8,128)(2,1)S(1)} collective-permute-done((bf16[96,1536]{1,0:T(8,128)(2,1)S(1)}, bf16[96,1536]{1,0:T(8,128)(2,1)S(1)}, u32[]{:S(2)}, u32[]{:S(2)}) %collective-permute-start.3) | collective-permute-done | bytes 294944 | tf_op jit(solution)/shard_map/ppermute | solution.py:499
  25.0 3.9 %collective-permute-start.8 = (bf16[96,1536]{1,0:T(8,128)(2,1)S(1)}, bf16[96,1536]{1,0:T(8,128)(2,1)S(1)}, u32[]{:S(2)}, u32[]{:S(2)}) collective-permute-start(bf16[96,1536]{1,0:T(8,128)(2,1)S(1)} %get-tuple-element.44), channel_id=1, source_target_pairs={{0,4},{1,5},{2,0},{3,1},{4,6},{5,7},{6,2},{7,3},{8,12},{9,13},{10,... | collective-permute-start | bytes 884744 | tf_op jit(solution)/shard_map/ppermute | solution.py:515
  29.1 2.8 %copy-done.5 = bf16[1,2048,1536]{2,1,0:T(8,128)(2,1)S(1)} copy-done((bf16[1,2048,1536]{2,1,0:T(8,128)(2,1)S(1)}, bf16[1,2048,1536]{2,1,0:T(8,128)(2,1)}, u32[]{:S(2)}) %copy-start.5) | copy-done | bytes 6291480
  32.8 2.5 %shard_map.94.refs_4_.refs_5_ = bf16[2048,128]{1,0:T(8,128)(2,1)S(1)} custom-call(bf16[2048,1536]{1,0:T(8,128)(2,1)S(1)} %bitcast.16, bf16[64,1536]{1,0:T(8,128)(2,1)S(1)} %bitcast.17), custom_call_target="tpu_custom_call" | custom-call | tf_op jit(solution)/shard_map/pallas_call | solution.py:127
  35.4 4.0 %shard_map.95 = (bf16[128,128]{1,0:T(8,128)(2,1)S(1)}, bf16[128,128]{1,0:T(8,128)(2,1)S(1)}, bf16[128,128]{1,0:T(8,128)(2,1)S(1)}, bf16[128,128]{1,0:T(8,128)(2,1)S(1)}) custom-call(s32[2]{0:T(128)S(1)} %get-tuple-element.52.place_ref, bf16[96,1536]{1,0:T(8,128)(2,1)S(1)} %get-tuple-element.53.local_ref, ...), custom_call_target="tpu_custom_call" | custom-call | tf_op jit(solution)/shard_map/pallas_call | solution.py:293
  39.5 1.9 %collective-permute-start.6 = (bf16[128,128]{1,0:T(8,128)(2,1)S(1)}, bf16[128,128]{1,0:T(8,128)(2,1)S(1)}, u32[]{:S(2)}, u32[]{:S(2)}) collective-permute-start(bf16[128,128]{1,0:T(8,128)(2,1)S(1)} %get-tuple-element.58), channel_id=1, source_target_pairs={{0,2},{1,3},{2,0},{3,1},{4,6},{5,7},{6,4},{7,5},{8,10},{9,11},{10,... | collective-permute-start | bytes 98312 | tf_op jit(solution)/shard_map/ppermute | solution.py:499
  41.5 2.0 %shard_map.93 = (bf16[8,272,128]{2,1,0:T(8,128)(2,1)S(1)}, f32[272,128]{1,0:T(8,128)S(1)}, f32[272,64]{1,0:T(8,128)S(1)}) custom-call(s32[2]{0:T(128)S(1)} %get-tuple-element.52.place_ref, bf16[256,1536]{1,0:T(8,128)(2,1)S(1)} %copy-done.4, bf16[64,1536]{1,0:T(8,128)(2,1)S(1)} %bitcast.18, s32[2,256]{1,0:T(2,128)} %bitcast.3.refs_0_.ids_ref, ...), custom_call_target="tpu_custom_call" | custom-call | tf_op jit(solution)/shard_map/pallas_call | solution.py:225
  43.6 1.4 %collective-permute-done.8.refs_0_ = bf16[96,1536]{1,0:T(8,128)(2,1)S(1)} collective-permute-done((bf16[96,1536]{1,0:T(8,128)(2,1)S(1)}, bf16[96,1536]{1,0:T(8,128)(2,1)S(1)}, u32[]{:S(2)}, u32[]{:S(2)}) %collective-permute-start.8) | collective-permute-done | bytes 294944 | tf_op jit(solution)/shard_map/ppermute | solution.py:515
  45.0 6.3 %collective-permute-done.9.refs_1_ = bf16[96,1536]{1,0:T(8,128)(2,1)S(1)} collective-permute-done((bf16[96,1536]{1,0:T(8,128)(2,1)S(1)}, bf16[96,1536]{1,0:T(8,128)(2,1)S(1)}, u32[]{:S(2)}, u32[]{:S(2)}) %collective-permute-start.9) | collective-permute-done | bytes 294944 | tf_op jit(solution)/shard_map/ppermute | solution.py:515
  51.3 3.9 %shard_map.96 = (bf16[128,128]{1,0:T(8,128)(2,1)S(1)}, bf16[128,128]{1,0:T(8,128)(2,1)S(1)}, bf16[128,128]{1,0:T(8,128)(2,1)S(1)}, bf16[128,128]{1,0:T(8,128)(2,1)S(1)}) custom-call(s32[2]{0:T(128)S(1)} %get-tuple-element.52.place_ref, bf16[96,1536]{1,0:T(8,128)(2,1)S(1)} %get-tuple-element.60.local_ref, ...), custom_call_target="tpu_custom_call" | custom-call | tf_op jit(solution)/shard_map/pallas_call | solution.py:293
  56.4 1.3 %collective-permute-start.13 = (bf16[128,128]{1,0:T(8,128)(2,1)S(1)}, bf16[128,128]{1,0:T(8,128)(2,1)S(1)}, u32[]{:S(2)}, u32[]{:S(2)}) collective-permute-start(bf16[128,128]{1,0:T(8,128)(2,1)S(1)} %get-tuple-element.63), channel_id=1, source_target_pairs={{0,5},{1,4},{2,7},{3,6},{4,1},{5,0},{6,3},{7,2},{8,13},{9,12},{10,... | collective-permute-start | bytes 98312 | tf_op jit(solution)/shard_map/ppermute | solution.py:499
  57.7 2.5 %collective-permute-start.14 = (bf16[128,128]{1,0:T(8,128)(2,1)S(1)}, bf16[128,128]{1,0:T(8,128)(2,1)S(1)}, u32[]{:S(2)}, u32[]{:S(2)}) collective-permute-start(bf16[128,128]{1,0:T(8,128)(2,1)S(1)} %get-tuple-element.64), channel_id=1, source_target_pairs={{0,6},{1,7},{2,4},{3,5},{4,2},{5,3},{6,0},{7,1},{8,14},{9,15},{10,... | collective-permute-start | bytes 98312 | tf_op jit(solution)/shard_map/ppermute | solution.py:499
  60.2 1.3 %collective-permute-start.15 = (bf16[128,128]{1,0:T(8,128)(2,1)S(1)}, bf16[128,128]{1,0:T(8,128)(2,1)S(1)}, u32[]{:S(2)}, u32[]{:S(2)}) collective-permute-start(bf16[128,128]{1,0:T(8,128)(2,1)S(1)} %get-tuple-element.65), channel_id=1, source_target_pairs={{0,7},{1,6},{2,5},{3,4},{4,3},{5,2},{6,1},{7,0},{8,15},{9,14},{10,... | collective-permute-start | bytes 98312 | tf_op jit(solution)/shard_map/ppermute | solution.py:499
  61.6 1.9 %collective-permute-done.14.refs_6_ = bf16[128,128]{1,0:T(8,128)(2,1)S(1)} collective-permute-done((bf16[128,128]{1,0:T(8,128)(2,1)S(1)}, bf16[128,128]{1,0:T(8,128)(2,1)S(1)}, u32[]{:S(2)}, u32[]{:S(2)}) %collective-permute-start.14) | collective-permute-done | bytes 32800 | tf_op jit(solution)/shard_map/ppermute | solution.py:499
  63.5 1.8 %collective-permute-done.15.refs_7_ = bf16[128,128]{1,0:T(8,128)(2,1)S(1)} collective-permute-done((bf16[128,128]{1,0:T(8,128)(2,1)S(1)}, bf16[128,128]{1,0:T(8,128)(2,1)S(1)}, u32[]{:S(2)}, u32[]{:S(2)}) %collective-permute-start.15) | collective-permute-done | bytes 32800 | tf_op jit(solution)/shard_map/ppermute | solution.py:499
  67.1 2.5 %collective-permute-start.19 = (bf16[160,128]{1,0:T(8,128)(2,1)S(1)}, bf16[160,128]{1,0:T(8,128)(2,1)S(1)}, u32[]{:S(2)}, u32[]{:S(2)}) collective-permute-start(bf16[160,128]{1,0:T(8,128)(2,1)S(1)} %constant_dynamic-update-slice_fusion.slab_ref), channel_id=1, source_target_pairs={{0,24},{8,16},{16,8},{24,0},{1,25},{9,17},{17,9},{25,1},{2,26},{10... | collective-permute-start | bytes 122888 | tf_op jit(solution)/shard_map/ppermute | solution.py:539
  70.8 2.4 %shard_map.98.own_ref = bf16[272,2048]{1,0:T(8,128)(2,1)S(1)} custom-call(s32[3]{0:T(128)S(1)} %pad_add_fusion.place_ref, bf16[160,128]{1,0:T(8,128)(2,1)S(1)} %constant_dynamic-update-slice_fusion.slab_ref, bf16[448,2048]{1,0:T(8,128)(2,1)S(1)} %bitcast.15, f32[2,2048]{1,0:T(2,128)S(1)} %pad_maximum_fusion.alpha_ref.refs_4_), custom_call_target="tpu_custom_call" | custom-call | tf_op jit(solution)/shard_map/pallas_call | solution.py:399
  74.1 16.9 %shard_map.99 = f32[4,2048,128]{2,1,0:T(8,128)} custom-call(s32[3]{0:T(128)S(1)} %pad_add_fusion.place_ref, bf16[272,2048]{1,0:T(8,128)(2,1)S(1)} %shard_map.98.own_ref, bf16[160,128]{1,0:T(8,128)(2,1)S(1)} %collective-permute-done.17.refs_0_, bf16[160,128]{1,0:T(8,128)(2,1)S(1)} %collective-permute-done.18.refs_1_, ...), custom_call_target="tpu_custom_call" | custom-call | tf_op jit(solution)/shard_map/pallas_call | solution.py:455
  (54 shorter events, 11.6 us)
Async XLA Ops:
  0.0 12.6 %collective-permute-start.1 = (bf16[256,1536]{1,0:T(8,128)(2,1)}, bf16[256,1536]{1,0:T(8,128)(2,1)S(1)}, u32[]{:S(2)}, u32[]{:S(2)}) collective-permute-start(bf16[256,1536]{1,0:T(8,128)(2,1)} %frames_ref.1), channel_id=1, source_target_pairs={{2,4},{3,5},{4,2},{5,3},{10,12},{11,13},{12,10},{13,11},{18,20},{1... | collective-permute-start | bytes 2359304 | tf_op jit(solution)/shard_map/ppermute | solution.py:499
  4.1 20.9 %collective-permute-start.2 = (bf16[112,1536]{1,0:T(8,128)(2,1)S(1)}, bf16[112,1536]{1,0:T(8,128)(2,1)S(1)}, u32[]{:S(2)}, u32[]{:S(2)}) collective-permute-start(bf16[112,1536]{1,0:T(8,128)(2,1)S(1)} %get-tuple-element.41), channel_id=1, source_target_pairs={{0,1},{1,0},{2,3},{3,2},{4,5},{5,4},{6,7},{7,6},{8,9},{9,8},{10,11... | collective-permute-start | bytes 1032200 | tf_op jit(solution)/shard_map/ppermute | solution.py:499
  4.6 20.4 %collective-permute-start.4 = (bf16[112,1536]{1,0:T(8,128)(2,1)S(1)}, bf16[112,1536]{1,0:T(8,128)(2,1)S(1)}, u32[]{:S(2)}, u32[]{:S(2)}) collective-permute-start(bf16[112,1536]{1,0:T(8,128)(2,1)S(1)} %get-tuple-element.43), channel_id=1, source_target_pairs={{0,3},{1,2},{2,1},{3,0},{4,7},{5,6},{6,5},{7,4},{8,11},{9,10},{10,... | collective-permute-start | bytes 1032200 | tf_op jit(solution)/shard_map/ppermute | solution.py:499
  10.1 2.5 %collective-permute-start = (s32[2,256]{1,0:T(2,128)}, s32[2,256]{1,0:T(2,128)S(1)}, u32[]{:S(2)}, u32[]{:S(2)}) collective-permute-start(s32[2,256]{1,0:T(2,128)} %bitcast.3.refs_0_.ids_ref), channel_id=1, source_target_pairs={{2,4},{3,5},{4,2},{5,3},{10,12},{11,13},{12,10},{13,11},{18,20},{1... | collective-permute-start | bytes 6152 | tf_op jit(solution)/shard_map/ppermute | solution.py:499
  10.7 14.3 %collective-permute-start.3 = (bf16[96,1536]{1,0:T(8,128)(2,1)S(1)}, bf16[96,1536]{1,0:T(8,128)(2,1)S(1)}, u32[]{:S(2)}, u32[]{:S(2)}) collective-permute-start(bf16[96,1536]{1,0:T(8,128)(2,1)S(1)} %get-tuple-element.42), channel_id=1, source_target_pairs={{0,2},{1,3},{2,0},{3,1},{4,6},{5,7},{6,4},{7,5},{8,10},{9,11},{10,... | collective-permute-start | bytes 884744 | tf_op jit(solution)/shard_map/ppermute | solution.py:499
  12.5 22.9 %copy-start = (bf16[1,1536,2048]{2,1,0:T(8,128)(2,1)S(1)}, bf16[1,1536,2048]{2,1,0:T(8,128)(2,1)}, u32[]{:S(2)}) copy-start(bf16[1,1536,2048]{2,1,0:T(8,128)(2,1)} %param.12) | copy-start | bytes 18874372
  15.6 23.9 %collective-permute-start.11 = (bf16[96,1536]{1,0:T(8,128)(2,1)S(1)}, bf16[96,1536]{1,0:T(8,128)(2,1)S(1)}, u32[]{:S(2)}, u32[]{:S(2)}) collective-permute-start(bf16[96,1536]{1,0:T(8,128)(2,1)S(1)} %get-tuple-element.61), channel_id=1, source_target_pairs={{0,7},{1,6},{2,3},{3,2},{4,5},{5,4},{6,1},{7,0},{8,15},{9,14},{10,... | collective-permute-start | bytes 884744 | tf_op jit(solution)/shard_map/ppermute | solution.py:515
  17.6 25.9 %collective-permute-start.10 = (bf16[96,1536]{1,0:T(8,128)(2,1)S(1)}, bf16[96,1536]{1,0:T(8,128)(2,1)S(1)}, u32[]{:S(2)}, u32[]{:S(2)}) collective-permute-start(bf16[96,1536]{1,0:T(8,128)(2,1)S(1)} %get-tuple-element.60.local_ref), channel_id=1, source_target_pairs={{0,6},{1,7},{6,0},{7,1},{8,14},{9,15},{14,8},{15,9},{16,22},{17,23... | collective-permute-start | bytes 884744 | tf_op jit(solution)/shard_map/ppermute | solution.py:515
  25.0 20.0 %collective-permute-start.8 = (bf16[96,1536]{1,0:T(8,128)(2,1)S(1)}, bf16[96,1536]{1,0:T(8,128)(2,1)S(1)}, u32[]{:S(2)}, u32[]{:S(2)}) collective-permute-start(bf16[96,1536]{1,0:T(8,128)(2,1)S(1)} %get-tuple-element.44), channel_id=1, source_target_pairs={{0,4},{1,5},{2,0},{3,1},{4,6},{5,7},{6,2},{7,3},{8,12},{9,13},{10,... | collective-permute-start | bytes 884744 | tf_op jit(solution)/shard_map/ppermute | solution.py:515
  28.9 22.4 %collective-permute-start.9 = (bf16[96,1536]{1,0:T(8,128)(2,1)S(1)}, bf16[96,1536]{1,0:T(8,128)(2,1)S(1)}, u32[]{:S(2)}, u32[]{:S(2)}) collective-permute-start(bf16[96,1536]{1,0:T(8,128)(2,1)S(1)} %get-tuple-element.45), channel_id=1, source_target_pairs={{0,5},{1,4},{2,1},{3,0},{4,7},{5,6},{6,3},{7,2},{8,13},{9,12},{10,... | collective-permute-start | bytes 884744 | tf_op jit(solution)/shard_map/ppermute | solution.py:515
  32.8 8.6 %copy-start.7 = (bf16[1536,64]{0,1:T(8,128)(2,1)S(1)}, bf16[1536,64]{0,1:T(8,128)(2,1)}, u32[]{:S(2)}) copy-start(bf16[1536,64]{0,1:T(8,128)(2,1)} %param.14) | copy-start | bytes 589828
  32.8 8.6 %copy-start.9 = (f32[256,2]{0,1:T(2,128)S(1)}, f32[256,2]{0,1:T(2,128)}, u32[]{:S(2)}) copy-start(f32[256,2]{0,1:T(2,128)} %param.11) | copy-start | bytes 6148
  39.4 31.4 %copy-start.1 = (bf16[7,64,2048]{2,1,0:T(8,128)(2,1)S(1)}, bf16[7,64,2048]{2,1,0:T(8,128)(2,1)}, u32[]{:S(2)}) copy-start(bf16[7,64,2048]{2,1,0:T(8,128)(2,1)} %param.15) | copy-start | bytes 5505028
  39.4 18.3 %collective-permute-start.5 = (bf16[128,128]{1,0:T(8,128)(2,1)S(1)}, bf16[128,128]{1,0:T(8,128)(2,1)S(1)}, u32[]{:S(2)}, u32[]{:S(2)}) collective-permute-start(bf16[128,128]{1,0:T(8,128)(2,1)S(1)} %get-tuple-element.57), channel_id=1, source_target_pairs={{0,1},{1,0},{2,3},{3,2},{4,5},{5,4},{6,7},{7,6},{8,9},{9,8},{10,11... | collective-permute-start | bytes 98312 | tf_op jit(solution)/shard_map/ppermute | solution.py:499
  39.5 20.6 %collective-permute-start.6 = (bf16[128,128]{1,0:T(8,128)(2,1)S(1)}, bf16[128,128]{1,0:T(8,128)(2,1)S(1)}, u32[]{:S(2)}, u32[]{:S(2)}) collective-permute-start(bf16[128,128]{1,0:T(8,128)(2,1)S(1)} %get-tuple-element.58), channel_id=1, source_target_pairs={{0,2},{1,3},{2,0},{3,1},{4,6},{5,7},{6,4},{7,5},{8,10},{9,11},{10,... | collective-permute-start | bytes 98312 | tf_op jit(solution)/shard_map/ppermute | solution.py:499
  43.5 18.0 %collective-permute-start.7 = (bf16[128,128]{1,0:T(8,128)(2,1)S(1)}, bf16[128,128]{1,0:T(8,128)(2,1)S(1)}, u32[]{:S(2)}, u32[]{:S(2)}) collective-permute-start(bf16[128,128]{1,0:T(8,128)(2,1)S(1)} %get-tuple-element.59), channel_id=1, source_target_pairs={{0,3},{1,2},{2,1},{3,0},{4,7},{5,6},{6,5},{7,4},{8,11},{9,10},{10,... | collective-permute-start | bytes 98312 | tf_op jit(solution)/shard_map/ppermute | solution.py:499
  55.2 6.3 %collective-permute-start.12 = (bf16[128,128]{1,0:T(8,128)(2,1)S(1)}, bf16[128,128]{1,0:T(8,128)(2,1)S(1)}, u32[]{:S(2)}, u32[]{:S(2)}) collective-permute-start(bf16[128,128]{1,0:T(8,128)(2,1)S(1)} %get-tuple-element.62), channel_id=1, source_target_pairs={{0,4},{1,5},{2,6},{3,7},{4,0},{5,1},{6,2},{7,3},{8,12},{9,13},{10,... | collective-permute-start | bytes 98312 | tf_op jit(solution)/shard_map/ppermute | solution.py:499
  56.4 5.2 %collective-permute-start.13 = (bf16[128,128]{1,0:T(8,128)(2,1)S(1)}, bf16[128,128]{1,0:T(8,128)(2,1)S(1)}, u32[]{:S(2)}, u32[]{:S(2)}) collective-permute-start(bf16[128,128]{1,0:T(8,128)(2,1)S(1)} %get-tuple-element.63), channel_id=1, source_target_pairs={{0,5},{1,4},{2,7},{3,6},{4,1},{5,0},{6,3},{7,2},{8,13},{9,12},{10,... | collective-permute-start | bytes 98312 | tf_op jit(solution)/shard_map/ppermute | solution.py:499
  57.7 5.8 %collective-permute-start.14 = (bf16[128,128]{1,0:T(8,128)(2,1)S(1)}, bf16[128,128]{1,0:T(8,128)(2,1)S(1)}, u32[]{:S(2)}, u32[]{:S(2)}) collective-permute-start(bf16[128,128]{1,0:T(8,128)(2,1)S(1)} %get-tuple-element.64), channel_id=1, source_target_pairs={{0,6},{1,7},{2,4},{3,5},{4,2},{5,3},{6,0},{7,1},{8,14},{9,15},{10,... | collective-permute-start | bytes 98312 | tf_op jit(solution)/shard_map/ppermute | solution.py:499
  60.2 5.1 %collective-permute-start.15 = (bf16[128,128]{1,0:T(8,128)(2,1)S(1)}, bf16[128,128]{1,0:T(8,128)(2,1)S(1)}, u32[]{:S(2)}, u32[]{:S(2)}) collective-permute-start(bf16[128,128]{1,0:T(8,128)(2,1)S(1)} %get-tuple-element.65), channel_id=1, source_target_pairs={{0,7},{1,6},{2,5},{3,4},{4,3},{5,2},{6,1},{7,0},{8,15},{9,14},{10,... | collective-permute-start | bytes 98312 | tf_op jit(solution)/shard_map/ppermute | solution.py:499
  66.4 0.7 collective-permute-start.16
  67.1 6.0 %collective-permute-start.19 = (bf16[160,128]{1,0:T(8,128)(2,1)S(1)}, bf16[160,128]{1,0:T(8,128)(2,1)S(1)}, u32[]{:S(2)}, u32[]{:S(2)}) collective-permute-start(bf16[160,128]{1,0:T(8,128)(2,1)S(1)} %constant_dynamic-update-slice_fusion.slab_ref), channel_id=1, source_target_pairs={{0,24},{8,16},{16,8},{24,0},{1,25},{9,17},{17,9},{25,1},{2,26},{10... | collective-permute-start | bytes 122888 | tf_op jit(solution)/shard_map/ppermute | solution.py:539
  69.6 4.0 %collective-permute-start.18 = (bf16[160,128]{1,0:T(8,128)(2,1)S(1)}, bf16[160,128]{1,0:T(8,128)(2,1)S(1)}, u32[]{:S(2)}, u32[]{:S(2)}) collective-permute-start(bf16[160,128]{1,0:T(8,128)(2,1)S(1)} %constant_dynamic-update-slice_fusion.slab_ref), channel_id=1, source_target_pairs={{0,16},{8,24},{16,0},{24,8},{1,17},{9,25},{17,1},{25,9},{2,18},{10... | collective-permute-start | bytes 122888 | tf_op jit(solution)/shard_map/ppermute | solution.py:539
  70.1 4.0 %collective-permute-start.17 = (bf16[160,128]{1,0:T(8,128)(2,1)S(1)}, bf16[160,128]{1,0:T(8,128)(2,1)S(1)}, u32[]{:S(2)}, u32[]{:S(2)}) collective-permute-start(bf16[160,128]{1,0:T(8,128)(2,1)S(1)} %constant_dynamic-update-slice_fusion.slab_ref), channel_id=1, source_target_pairs={{0,8},{8,0},{16,24},{24,16},{1,9},{9,1},{17,25},{25,17},{2,10},{10... | collective-permute-start | bytes 122888 | tf_op jit(solution)/shard_map/ppermute | solution.py:539
  (7 other events, 24.1 us)

commit v9 on v8

--- a/solution.py
+++ b/solution.py
@@ -407,16 +407,32 @@
     )(place, slab, conv, alpha)
 
 
+def stage_kernel(source_ref, target_ref, sem):
+    copy = pltpu.make_async_copy(source_ref, target_ref, sem)
+    copy.start()
+    copy.wait()
+
+
+def stage(value):
+    return pl.pallas_call(
+        stage_kernel,
+        out_shape=jax.ShapeDtypeStruct(value.shape, value.dtype),
+        in_specs=[pl.BlockSpec(memory_space=pl.ANY)],
+        out_specs=whole(),
+        scratch_shapes=[pltpu.SemaphoreType.DMA],
+        compiler_params=params(16),
+        cost_estimate=FREE,
+    )(value)
+
+
 def decoder_kernel(segs, place_ref, own_ref, *refs):
     slab_refs = refs[: segs - 1]
-    conv_ref, alpha_ref, up_hbm, out_ref = refs[segs - 1 : segs + 3]
-    padded, windows, others, up_ref, rows_out, sems, up_sem = refs[segs + 3 :]
+    conv_ref, alpha_ref, up_ref, out_ref = refs[segs - 1 : segs + 3]
+    padded, windows, others, rows_out, sems = refs[segs + 3 :]
     span = own_ref.shape[0]
     length = span - 4 * EDGE
     width = up_ref.shape[2]
     own = place_ref[0]
-    up_copy = pltpu.make_async_copy(up_hbm, up_ref, up_sem)
-    up_copy.start()
 
     def out_copy(k):
         return pltpu.make_async_copy(rows_out.at[k], out_ref.at[own ^ k], sems.at[k])
@@ -425,7 +441,6 @@
         unpack_slab(place_ref, slab_refs[k], padded.at[k])
     for k in range(segs - 1):
         convolve(place_ref, padded.at[k], windows.at[k], conv_ref, alpha_ref, others.at[k])
-    up_copy.wait()
     for k in range(segs):
         act = own_ref if k == 0 else others.at[k - 1]
         for r in range(0, 8, 2):
@@ -456,19 +471,16 @@
         functools.partial(decoder_kernel, segs),
         out_shape=jax.ShapeDtypeStruct((segs, 8 * length, width), F32),
         in_specs=[pl.BlockSpec(memory_space=pltpu.SMEM)]
-        + [whole()] * (segs + 2)
-        + [pl.BlockSpec(memory_space=pl.ANY)],
+        + [whole()] * (segs + 3),
         out_specs=pl.BlockSpec(memory_space=pl.ANY),
         scratch_shapes=[
             pltpu.VMEM((segs - 1, span, lat), F32),
             pltpu.VMEM((segs - 1, span, conv.shape[0]), BF16),
             pltpu.VMEM((segs - 1, span, channels), BF16),
-            pltpu.VMEM(first_up.shape, BF16),
             pltpu.VMEM((segs, 8 * length, width), F32),
             pltpu.SemaphoreType.DMA((segs,)),
-            pltpu.SemaphoreType.DMA,
         ],
-        compiler_params=params(52),
+        compiler_params=params(32),
         cost_estimate=FREE,
     )(place, own, *slabs, conv, alpha, first_up)
 
@@ -527,8 +539,10 @@
         place, frames, out_w_t, ids_t, gates_t, neighbours, n, capacity
     )
     back = run_group(n, False, place, chunk, near, up, folded)
+    back, first_up = lax.optimization_barrier((back, first_up))
+    staged = stage(first_up)
     parts = [back[0]] + [swap(back[k], k) for k in range(1, half)]
-    place, pick, scale, base = lax.optimization_barrier((place, pick, scale, base))
+    place, pick, scale, base, staged = lax.optimization_barrier((place, pick, scale, base, staged))
     back = run_group(n, True, place, sent[quarter], far, up, folded)
     parts += [swap(back[k], half + k) for k in range(half)]
     slab, middle = combine(place, parts, pick, scale, base)
@@ -542,7 +556,7 @@
     alpha = jnp.stack([snake_first * (1.0 / math.pi), 1.0 / snake_first])
     conv = in_conv.reshape(-1, in_conv.shape[2])
     act = activate_own(spot, slab, conv, alpha, base.shape[0])
-    return decode(spot, act, others, conv, alpha, first_up)
+    return decode(spot, act, others, conv, alpha, staged)
 
 
 def solution(mesh):

time: 91.6 us -> 93.2 us (1.017)
  local copies, waits for them, and re-layouts: 6.85 us -> 13.5 us
  waiting for transfers between devices: 16.6 us -> 12.8 us
  Pallas kernels: 36.1 us -> 34.8 us
    unnamed x23 -> x29, local copies, waits for them, and re-layouts: 6.84 us -> 13.5 us
    ppermute x4, waiting for transfers between devices: 7.7 us -> 3.92 us  [cross(): return lax.ppermute(value, 'expert', [(i, j) for i, j in pairs if i != j])]
    pallas_call x1, Pallas kernels: 16.9 us -> 15.1 us  [decode(): pl.pallas_call(functools.partial(decoder_kernel, segs), out_shape=jax.Sha...]
  transfers between devices with their start and end apart: 20 -> 20, of which waited for: 7 -> 6; matrix products, arithmetic and copies ran while one was open for 0% -> 0% of each run, Pallas kernels for 20% -> 20%
where the time goes in v9:
time: 93.2 us; the launch traced here: 92.8 us
  Pallas kernels  34.8 us (37%)
  starting transfers between devices  31 us (33%)
  local copies, waits for them, and re-layouts  13.5 us (14%)
  waiting for transfers between devices  12.8 us (14%)
    ppermute x12, starting transfers between devices, swap(): return lax.ppermute(value, 'expert', [(i, i ^ k) for i in members])  17.4 us
    pallas_call x1, Pallas kernels, decode(): pl.pallas_call(functools.partial(decoder_kernel, segs), out_shape=jax.Sha...  15.1 us
    unnamed x29, local copies, waits for them, and re-layouts  13.5 us
    ppermute x4, starting transfers between devices, cross(): return lax.ppermute(value, 'expert', [(i, j) for i, j in pairs if i != j])  9.35 us
    pallas_call x2, Pallas kernels, run_group(): pl.pallas_call(functools.partial(group_kernel, n, far), out_shape=[jax.Sh...  7.96 us
    ppermute x12, waiting for transfers between devices, swap(): return lax.ppermute(value, 'expert', [(i, i ^ k) for i in members])  7.88 us
    ppermute x4, waiting for transfers between devices, cross(): return lax.ppermute(value, 'expert', [(i, j) for i, j in pairs if i != j])  3.92 us
    ppermute x3, starting transfers between devices, local(): lax.ppermute(slab, 'seg', [(i, i ^ k) for i in range(segs)])  3.57 us
  transfers between devices with their start and end apart: 20, of which 6 were waited for; matrix products, arithmetic and copies ran while one was open for 0% of the time, Pallas kernels for 20%

profile of v9, /device:TPU:0, one launch (start us, length us, event | category | flops | bytes accessed | tf_op | source)
XLA Modules:
  0.0 92.8 jit_solution(3388424938882986839)
XLA Ops:
  2.6 1.5 %shard_map.91 = (bf16[96,1536]{1,0:T(8,128)(2,1)S(1)}, bf16[112,1536]{1,0:T(8,128)(2,1)S(1)}, bf16[96,1536]{1,0:T(8,128)(2,1)S(1)}, bf16[112,1536]{1,0:T(8,128)(2,1)S(1)}) custom-call(s32[2]{0:T(128)S(1)} %get-tuple-element.86.origin_ref, s32[2,256]{1,0:T(2,128)} %bitcast.3.refs_0_.ids_ref, bf16[256,1536]{1,0:T(8,128)(2,1)S(1)} %copy-done.5, ...), custom_call_target="tpu_custom_call" | custom-call | tf_op jit(solution)/shard_map/pallas_call | solution.py:99
  4.6 5.5 %collective-permute-start.4 = (bf16[112,1536]{1,0:T(8,128)(2,1)S(1)}, bf16[112,1536]{1,0:T(8,128)(2,1)S(1)}, u32[]{:S(2)}, u32[]{:S(2)}) collective-permute-start(bf16[112,1536]{1,0:T(8,128)(2,1)S(1)} %get-tuple-element.49), channel_id=1, source_target_pairs={{0,3},{1,2},{2,1},{3,0},{4,7},{5,6},{6,5},{7,4},{8,11},{9,10},{10,... | collective-permute-start | bytes 1032200 | tf_op jit(solution)/shard_map/ppermute | solution.py:511
  10.7 1.7 %collective-permute-start.3 = (bf16[96,1536]{1,0:T(8,128)(2,1)S(1)}, bf16[96,1536]{1,0:T(8,128)(2,1)S(1)}, u32[]{:S(2)}, u32[]{:S(2)}) collective-permute-start(bf16[96,1536]{1,0:T(8,128)(2,1)S(1)} %get-tuple-element.48), channel_id=1, source_target_pairs={{0,2},{1,3},{2,0},{3,1},{4,6},{5,7},{6,4},{7,5},{8,10},{9,11},{10,... | collective-permute-start | bytes 884744 | tf_op jit(solution)/shard_map/ppermute | solution.py:511
  13.8 1.8 %shard_map.92 = (bf16[96,1536]{1,0:T(8,128)(2,1)S(1)}, bf16[96,1536]{1,0:T(8,128)(2,1)S(1)}, bf16[96,1536]{1,0:T(8,128)(2,1)S(1)}, bf16[96,1536]{1,0:T(8,128)(2,1)S(1)}) custom-call(s32[2]{0:T(128)S(1)} %pad_add_fusion.3.origin_ref, s32[2,256]{1,0:T(2,128)} %bitcast.3.refs_0_.ids_ref, bf16[256,1536]{1,0:T(8,128)(2,1)S(1)} %copy-done.6, ...), custom_call_target="tpu_custom_call" | custom-call | tf_op jit(solution)/shard_map/pallas_call | solution.py:99
  15.6 2.0 %collective-permute-start.11 = (bf16[96,1536]{1,0:T(8,128)(2,1)S(1)}, bf16[96,1536]{1,0:T(8,128)(2,1)S(1)}, u32[]{:S(2)}, u32[]{:S(2)}) collective-permute-start(bf16[96,1536]{1,0:T(8,128)(2,1)S(1)} %get-tuple-element.72), channel_id=1, source_target_pairs={{0,7},{1,6},{2,3},{3,2},{4,5},{5,4},{6,1},{7,0},{8,15},{9,14},{10,... | collective-permute-start | bytes 884744 | tf_op jit(solution)/shard_map/ppermute | solution.py:527
  17.6 3.2 %collective-permute-start.10 = (bf16[96,1536]{1,0:T(8,128)(2,1)S(1)}, bf16[96,1536]{1,0:T(8,128)(2,1)S(1)}, u32[]{:S(2)}, u32[]{:S(2)}) collective-permute-start(bf16[96,1536]{1,0:T(8,128)(2,1)S(1)} %get-tuple-element.71.local_ref), channel_id=1, source_target_pairs={{0,6},{1,7},{6,0},{7,1},{8,14},{9,15},{14,8},{15,9},{16,22},{17,23... | collective-permute-start | bytes 884744 | tf_op jit(solution)/shard_map/ppermute | solution.py:527
  20.9 4.1 %collective-permute-done.3.refs_1_ = bf16[96,1536]{1,0:T(8,128)(2,1)S(1)} collective-permute-done((bf16[96,1536]{1,0:T(8,128)(2,1)S(1)}, bf16[96,1536]{1,0:T(8,128)(2,1)S(1)}, u32[]{:S(2)}, u32[]{:S(2)}) %collective-permute-start.3) | collective-permute-done | bytes 294944 | tf_op jit(solution)/shard_map/ppermute | solution.py:511
  25.0 3.9 %collective-permute-start.8 = (bf16[96,1536]{1,0:T(8,128)(2,1)S(1)}, bf16[96,1536]{1,0:T(8,128)(2,1)S(1)}, u32[]{:S(2)}, u32[]{:S(2)}) collective-permute-start(bf16[96,1536]{1,0:T(8,128)(2,1)S(1)} %get-tuple-element.50), channel_id=1, source_target_pairs={{0,4},{1,5},{2,0},{3,1},{4,6},{5,7},{6,2},{7,3},{8,12},{9,13},{10,... | collective-permute-start | bytes 884744 | tf_op jit(solution)/shard_map/ppermute | solution.py:527
  29.1 2.8 %copy-done.8 = bf16[1,2048,1536]{2,1,0:T(8,128)(2,1)S(1)} copy-done((bf16[1,2048,1536]{2,1,0:T(8,128)(2,1)S(1)}, bf16[1,2048,1536]{2,1,0:T(8,128)(2,1)}, u32[]{:S(2)}) %copy-start.8) | copy-done | bytes 6291480
  32.8 2.5 %shard_map.94.refs_4_.refs_5_ = bf16[2048,128]{1,0:T(8,128)(2,1)S(1)} custom-call(bf16[2048,1536]{1,0:T(8,128)(2,1)S(1)} %bitcast.16, bf16[64,1536]{1,0:T(8,128)(2,1)S(1)} %bitcast.17), custom_call_target="tpu_custom_call" | custom-call | tf_op jit(solution)/shard_map/pallas_call | solution.py:127
  35.4 4.0 %shard_map.95 = (bf16[128,128]{1,0:T(8,128)(2,1)S(1)}, bf16[128,128]{1,0:T(8,128)(2,1)S(1)}, bf16[128,128]{1,0:T(8,128)(2,1)S(1)}, bf16[128,128]{1,0:T(8,128)(2,1)S(1)}) custom-call(s32[2]{0:T(128)S(1)} %get-tuple-element.66.place_ref, bf16[96,1536]{1,0:T(8,128)(2,1)S(1)} %get-tuple-element.58.local_ref, ...), custom_call_target="tpu_custom_call" | custom-call | tf_op jit(solution)/shard_map/pallas_call | solution.py:293
  39.5 1.9 %collective-permute-start.6 = (bf16[128,128]{1,0:T(8,128)(2,1)S(1)}, bf16[128,128]{1,0:T(8,128)(2,1)S(1)}, u32[]{:S(2)}, u32[]{:S(2)}) collective-permute-start(bf16[128,128]{1,0:T(8,128)(2,1)S(1)} %get-tuple-element.69), channel_id=1, source_target_pairs={{0,2},{1,3},{2,0},{3,1},{4,6},{5,7},{6,4},{7,5},{8,10},{9,11},{10,... | collective-permute-start | bytes 98312 | tf_op jit(solution)/shard_map/ppermute | solution.py:511
  41.5 2.0 %shard_map.93 = (bf16[8,272,128]{2,1,0:T(8,128)(2,1)S(1)}, f32[272,128]{1,0:T(8,128)S(1)}, f32[272,64]{1,0:T(8,128)S(1)}) custom-call(s32[2]{0:T(128)S(1)} %get-tuple-element.66.place_ref, bf16[256,1536]{1,0:T(8,128)(2,1)S(1)} %copy-done.7, bf16[64,1536]{1,0:T(8,128)(2,1)S(1)} %bitcast.18, s32[2,256]{1,0:T(2,128)} %bitcast.3.refs_0_.ids_ref, ...), custom_call_target="tpu_custom_call" | custom-call | tf_op jit(solution)/shard_map/pallas_call | solution.py:225
  44.1 3.3 %copy-done = bf16[16,2048,128]{2,1,0:T(8,128)(2,1)} copy-done((bf16[16,2048,128]{2,1,0:T(8,128)(2,1)}, bf16[16,2048,128]{2,1,0:T(8,128)(2,1)S(1)}, u32[]{:S(2)}) %copy-start) | copy-done | bytes 8388632
  47.4 3.9 %collective-permute-done.9.refs_1_ = bf16[96,1536]{1,0:T(8,128)(2,1)S(1)} collective-permute-done((bf16[96,1536]{1,0:T(8,128)(2,1)S(1)}, bf16[96,1536]{1,0:T(8,128)(2,1)S(1)}, u32[]{:S(2)}, u32[]{:S(2)}) %collective-permute-start.9) | collective-permute-done | bytes 294944 | tf_op jit(solution)/shard_map/ppermute | solution.py:527
  51.3 3.9 %shard_map.97 = (bf16[128,128]{1,0:T(8,128)(2,1)S(1)}, bf16[128,128]{1,0:T(8,128)(2,1)S(1)}, bf16[128,128]{1,0:T(8,128)(2,1)S(1)}, bf16[128,128]{1,0:T(8,128)(2,1)S(1)}) custom-call(s32[2]{0:T(128)S(1)} %get-tuple-element.66.place_ref, bf16[96,1536]{1,0:T(8,128)(2,1)S(1)} %get-tuple-element.71.local_ref, ...), custom_call_target="tpu_custom_call" | custom-call | tf_op jit(solution)/shard_map/pallas_call | solution.py:293
  57.7 2.5 %collective-permute-start.14 = (bf16[128,128]{1,0:T(8,128)(2,1)S(1)}, bf16[128,128]{1,0:T(8,128)(2,1)S(1)}, u32[]{:S(2)}, u32[]{:S(2)}) collective-permute-start(bf16[128,128]{1,0:T(8,128)(2,1)S(1)} %get-tuple-element.75), channel_id=1, source_target_pairs={{0,6},{1,7},{2,4},{3,5},{4,2},{5,3},{6,0},{7,1},{8,14},{9,15},{10,... | collective-permute-start | bytes 98312 | tf_op jit(solution)/shard_map/ppermute | solution.py:511
  60.2 1.4 %collective-permute-start.15 = (bf16[128,128]{1,0:T(8,128)(2,1)S(1)}, bf16[128,128]{1,0:T(8,128)(2,1)S(1)}, u32[]{:S(2)}, u32[]{:S(2)}) collective-permute-start(bf16[128,128]{1,0:T(8,128)(2,1)S(1)} %get-tuple-element.76), channel_id=1, source_target_pairs={{0,7},{1,6},{2,5},{3,4},{4,3},{5,2},{6,1},{7,0},{8,15},{9,14},{10,... | collective-permute-start | bytes 98312 | tf_op jit(solution)/shard_map/ppermute | solution.py:511
  61.6 1.9 %collective-permute-done.14.refs_6_ = bf16[128,128]{1,0:T(8,128)(2,1)S(1)} collective-permute-done((bf16[128,128]{1,0:T(8,128)(2,1)S(1)}, bf16[128,128]{1,0:T(8,128)(2,1)S(1)}, u32[]{:S(2)}, u32[]{:S(2)}) %collective-permute-start.14) | collective-permute-done | bytes 32800 | tf_op jit(solution)/shard_map/ppermute | solution.py:511
  63.5 1.8 %collective-permute-done.15.refs_7_ = bf16[128,128]{1,0:T(8,128)(2,1)S(1)} collective-permute-done((bf16[128,128]{1,0:T(8,128)(2,1)S(1)}, bf16[128,128]{1,0:T(8,128)(2,1)S(1)}, u32[]{:S(2)}, u32[]{:S(2)}) %collective-permute-start.15) | collective-permute-done | bytes 32800 | tf_op jit(solution)/shard_map/ppermute | solution.py:511
  67.1 2.5 %collective-permute-start.19 = (bf16[160,128]{1,0:T(8,128)(2,1)S(1)}, bf16[160,128]{1,0:T(8,128)(2,1)S(1)}, u32[]{:S(2)}, u32[]{:S(2)}) collective-permute-start(bf16[160,128]{1,0:T(8,128)(2,1)S(1)} %constant_dynamic-update-slice_fusion.slab_ref), channel_id=1, source_target_pairs={{0,24},{8,16},{16,8},{24,0},{1,25},{9,17},{17,9},{25,1},{2,26},{10... | collective-permute-start | bytes 122888 | tf_op jit(solution)/shard_map/ppermute | solution.py:553
  70.8 2.4 %shard_map.99.own_ref = bf16[272,2048]{1,0:T(8,128)(2,1)S(1)} custom-call(s32[3]{0:T(128)S(1)} %pad_add_fusion.place_ref, bf16[160,128]{1,0:T(8,128)(2,1)S(1)} %constant_dynamic-update-slice_fusion.slab_ref, bf16[448,2048]{1,0:T(8,128)(2,1)S(1)} %bitcast.14, f32[2,2048]{1,0:T(2,128)S(1)} %pad_maximum_fusion.alpha_ref.refs_4_), custom_call_target="tpu_custom_call" | custom-call | tf_op jit(solution)/shard_map/pallas_call | solution.py:399
  74.1 3.4 %copy-done.1 = bf16[16,2048,128]{2,1,0:T(8,128)(2,1)S(1)} copy-done((bf16[16,2048,128]{2,1,0:T(8,128)(2,1)S(1)}, bf16[16,2048,128]{2,1,0:T(8,128)(2,1)}, u32[]{:S(2)}) %copy-start.1) | copy-done | bytes 8388632
  77.5 15.1 %shard_map.100 = f32[4,2048,128]{2,1,0:T(8,128)} custom-call(s32[3]{0:T(128)S(1)} %pad_add_fusion.place_ref, bf16[272,2048]{1,0:T(8,128)(2,1)S(1)} %shard_map.99.own_ref, bf16[160,128]{1,0:T(8,128)(2,1)S(1)} %collective-permute-done.17.refs_0_, bf16[160,128]{1,0:T(8,128)(2,1)S(1)} %collective-permute-done.18.refs_1_, ...), custom_call_target="tpu_custom_call" | custom-call | tf_op jit(solution)/shard_map/pallas_call | solution.py:470
  (61 shorter events, 13.3 us)
Async XLA Ops:
  0.0 12.6 %collective-permute-start.1 = (bf16[256,1536]{1,0:T(8,128)(2,1)}, bf16[256,1536]{1,0:T(8,128)(2,1)S(1)}, u32[]{:S(2)}, u32[]{:S(2)}) collective-permute-start(bf16[256,1536]{1,0:T(8,128)(2,1)} %frames_ref.1), channel_id=1, source_target_pairs={{2,4},{3,5},{4,2},{5,3},{10,12},{11,13},{12,10},{13,11},{18,20},{1... | collective-permute-start | bytes 2359304 | tf_op jit(solution)/shard_map/ppermute | solution.py:511
  4.1 20.9 %collective-permute-start.2 = (bf16[112,1536]{1,0:T(8,128)(2,1)S(1)}, bf16[112,1536]{1,0:T(8,128)(2,1)S(1)}, u32[]{:S(2)}, u32[]{:S(2)}) collective-permute-start(bf16[112,1536]{1,0:T(8,128)(2,1)S(1)} %get-tuple-element.47), channel_id=1, source_target_pairs={{0,1},{1,0},{2,3},{3,2},{4,5},{5,4},{6,7},{7,6},{8,9},{9,8},{10,11... | collective-permute-start | bytes 1032200 | tf_op jit(solution)/shard_map/ppermute | solution.py:511
  4.6 20.4 %collective-permute-start.4 = (bf16[112,1536]{1,0:T(8,128)(2,1)S(1)}, bf16[112,1536]{1,0:T(8,128)(2,1)S(1)}, u32[]{:S(2)}, u32[]{:S(2)}) collective-permute-start(bf16[112,1536]{1,0:T(8,128)(2,1)S(1)} %get-tuple-element.49), channel_id=1, source_target_pairs={{0,3},{1,2},{2,1},{3,0},{4,7},{5,6},{6,5},{7,4},{8,11},{9,10},{10,... | collective-permute-start | bytes 1032200 | tf_op jit(solution)/shard_map/ppermute | solution.py:511
  10.1 2.5 %collective-permute-start = (s32[2,256]{1,0:T(2,128)}, s32[2,256]{1,0:T(2,128)S(1)}, u32[]{:S(2)}, u32[]{:S(2)}) collective-permute-start(s32[2,256]{1,0:T(2,128)} %bitcast.3.refs_0_.ids_ref), channel_id=1, source_target_pairs={{2,4},{3,5},{4,2},{5,3},{10,12},{11,13},{12,10},{13,11},{18,20},{1... | collective-permute-start | bytes 6152 | tf_op jit(solution)/shard_map/ppermute | solution.py:511
  10.7 14.3 %collective-permute-start.3 = (bf16[96,1536]{1,0:T(8,128)(2,1)S(1)}, bf16[96,1536]{1,0:T(8,128)(2,1)S(1)}, u32[]{:S(2)}, u32[]{:S(2)}) collective-permute-start(bf16[96,1536]{1,0:T(8,128)(2,1)S(1)} %get-tuple-element.48), channel_id=1, source_target_pairs={{0,2},{1,3},{2,0},{3,1},{4,6},{5,7},{6,4},{7,5},{8,10},{9,11},{10,... | collective-permute-start | bytes 884744 | tf_op jit(solution)/shard_map/ppermute | solution.py:511
  12.5 22.9 %copy-start.2 = (bf16[1,1536,2048]{2,1,0:T(8,128)(2,1)S(1)}, bf16[1,1536,2048]{2,1,0:T(8,128)(2,1)}, u32[]{:S(2)}) copy-start(bf16[1,1536,2048]{2,1,0:T(8,128)(2,1)} %param.12) | copy-start | bytes 18874372
  15.6 23.9 %collective-permute-start.11 = (bf16[96,1536]{1,0:T(8,128)(2,1)S(1)}, bf16[96,1536]{1,0:T(8,128)(2,1)S(1)}, u32[]{:S(2)}, u32[]{:S(2)}) collective-permute-start(bf16[96,1536]{1,0:T(8,128)(2,1)S(1)} %get-tuple-element.72), channel_id=1, source_target_pairs={{0,7},{1,6},{2,3},{3,2},{4,5},{5,4},{6,1},{7,0},{8,15},{9,14},{10,... | collective-permute-start | bytes 884744 | tf_op jit(solution)/shard_map/ppermute | solution.py:527
  17.6 29.7 %collective-permute-start.10 = (bf16[96,1536]{1,0:T(8,128)(2,1)S(1)}, bf16[96,1536]{1,0:T(8,128)(2,1)S(1)}, u32[]{:S(2)}, u32[]{:S(2)}) collective-permute-start(bf16[96,1536]{1,0:T(8,128)(2,1)S(1)} %get-tuple-element.71.local_ref), channel_id=1, source_target_pairs={{0,6},{1,7},{6,0},{7,1},{8,14},{9,15},{14,8},{15,9},{16,22},{17,23... | collective-permute-start | bytes 884744 | tf_op jit(solution)/shard_map/ppermute | solution.py:527
  25.0 22.4 %collective-permute-start.8 = (bf16[96,1536]{1,0:T(8,128)(2,1)S(1)}, bf16[96,1536]{1,0:T(8,128)(2,1)S(1)}, u32[]{:S(2)}, u32[]{:S(2)}) collective-permute-start(bf16[96,1536]{1,0:T(8,128)(2,1)S(1)} %get-tuple-element.50), channel_id=1, source_target_pairs={{0,4},{1,5},{2,0},{3,1},{4,6},{5,7},{6,2},{7,3},{8,12},{9,13},{10,... | collective-permute-start | bytes 884744 | tf_op jit(solution)/shard_map/ppermute | solution.py:527
  28.9 22.4 %collective-permute-start.9 = (bf16[96,1536]{1,0:T(8,128)(2,1)S(1)}, bf16[96,1536]{1,0:T(8,128)(2,1)S(1)}, u32[]{:S(2)}, u32[]{:S(2)}) collective-permute-start(bf16[96,1536]{1,0:T(8,128)(2,1)S(1)} %get-tuple-element.51), channel_id=1, source_target_pairs={{0,5},{1,4},{2,1},{3,0},{4,7},{5,6},{6,3},{7,2},{8,13},{9,12},{10,... | collective-permute-start | bytes 884744 | tf_op jit(solution)/shard_map/ppermute | solution.py:527
  32.8 8.6 %copy-start.10 = (bf16[1536,64]{0,1:T(8,128)(2,1)S(1)}, bf16[1536,64]{0,1:T(8,128)(2,1)}, u32[]{:S(2)}) copy-start(bf16[1536,64]{0,1:T(8,128)(2,1)} %param.14) | copy-start | bytes 589828
  32.8 8.6 %copy-start.12 = (f32[256,2]{0,1:T(2,128)S(1)}, f32[256,2]{0,1:T(2,128)}, u32[]{:S(2)}) copy-start(f32[256,2]{0,1:T(2,128)} %param.11) | copy-start | bytes 6148
  39.4 18.3 %collective-permute-start.5 = (bf16[128,128]{1,0:T(8,128)(2,1)S(1)}, bf16[128,128]{1,0:T(8,128)(2,1)S(1)}, u32[]{:S(2)}, u32[]{:S(2)}) collective-permute-start(bf16[128,128]{1,0:T(8,128)(2,1)S(1)} %get-tuple-element.68), channel_id=1, source_target_pairs={{0,1},{1,0},{2,3},{3,2},{4,5},{5,4},{6,7},{7,6},{8,9},{9,8},{10,11... | collective-permute-start | bytes 98312 | tf_op jit(solution)/shard_map/ppermute | solution.py:511
  39.5 20.6 %collective-permute-start.6 = (bf16[128,128]{1,0:T(8,128)(2,1)S(1)}, bf16[128,128]{1,0:T(8,128)(2,1)S(1)}, u32[]{:S(2)}, u32[]{:S(2)}) collective-permute-start(bf16[128,128]{1,0:T(8,128)(2,1)S(1)} %get-tuple-element.69), channel_id=1, source_target_pairs={{0,2},{1,3},{2,0},{3,1},{4,6},{5,7},{6,4},{7,5},{8,10},{9,11},{10,... | collective-permute-start | bytes 98312 | tf_op jit(solution)/shard_map/ppermute | solution.py:511
  47.4 23.4 %copy-start.4 = (bf16[7,64,2048]{2,1,0:T(8,128)(2,1)S(1)}, bf16[7,64,2048]{2,1,0:T(8,128)(2,1)}, u32[]{:S(2)}) copy-start(bf16[7,64,2048]{2,1,0:T(8,128)(2,1)} %param.15) | copy-start | bytes 5505028
  47.4 14.2 %collective-permute-start.7 = (bf16[128,128]{1,0:T(8,128)(2,1)S(1)}, bf16[128,128]{1,0:T(8,128)(2,1)S(1)}, u32[]{:S(2)}, u32[]{:S(2)}) collective-permute-start(bf16[128,128]{1,0:T(8,128)(2,1)S(1)} %get-tuple-element.70), channel_id=1, source_target_pairs={{0,3},{1,2},{2,1},{3,0},{4,7},{5,6},{6,5},{7,4},{8,11},{9,10},{10,... | collective-permute-start | bytes 98312 | tf_op jit(solution)/shard_map/ppermute | solution.py:511
  55.2 6.3 %collective-permute-start.12 = (bf16[128,128]{1,0:T(8,128)(2,1)S(1)}, bf16[128,128]{1,0:T(8,128)(2,1)S(1)}, u32[]{:S(2)}, u32[]{:S(2)}) collective-permute-start(bf16[128,128]{1,0:T(8,128)(2,1)S(1)} %get-tuple-element.73), channel_id=1, source_target_pairs={{0,4},{1,5},{2,6},{3,7},{4,0},{5,1},{6,2},{7,3},{8,12},{9,13},{10,... | collective-permute-start | bytes 98312 | tf_op jit(solution)/shard_map/ppermute | solution.py:511
  56.4 5.2 %collective-permute-start.13 = (bf16[128,128]{1,0:T(8,128)(2,1)S(1)}, bf16[128,128]{1,0:T(8,128)(2,1)S(1)}, u32[]{:S(2)}, u32[]{:S(2)}) collective-permute-start(bf16[128,128]{1,0:T(8,128)(2,1)S(1)} %get-tuple-element.74), channel_id=1, source_target_pairs={{0,5},{1,4},{2,7},{3,6},{4,1},{5,0},{6,3},{7,2},{8,13},{9,12},{10,... | collective-permute-start | bytes 98312 | tf_op jit(solution)/shard_map/ppermute | solution.py:511
  57.7 5.8 %collective-permute-start.14 = (bf16[128,128]{1,0:T(8,128)(2,1)S(1)}, bf16[128,128]{1,0:T(8,128)(2,1)S(1)}, u32[]{:S(2)}, u32[]{:S(2)}) collective-permute-start(bf16[128,128]{1,0:T(8,128)(2,1)S(1)} %get-tuple-element.75), channel_id=1, source_target_pairs={{0,6},{1,7},{2,4},{3,5},{4,2},{5,3},{6,0},{7,1},{8,14},{9,15},{10,... | collective-permute-start | bytes 98312 | tf_op jit(solution)/shard_map/ppermute | solution.py:511
  60.2 5.2 %collective-permute-start.15 = (bf16[128,128]{1,0:T(8,128)(2,1)S(1)}, bf16[128,128]{1,0:T(8,128)(2,1)S(1)}, u32[]{:S(2)}, u32[]{:S(2)}) collective-permute-start(bf16[128,128]{1,0:T(8,128)(2,1)S(1)} %get-tuple-element.76), channel_id=1, source_target_pairs={{0,7},{1,6},{2,5},{3,4},{4,3},{5,2},{6,1},{7,0},{8,15},{9,14},{10,... | collective-permute-start | bytes 98312 | tf_op jit(solution)/shard_map/ppermute | solution.py:511
  66.4 0.7 collective-permute-start.16
  67.1 6.0 %collective-permute-start.19 = (bf16[160,128]{1,0:T(8,128)(2,1)S(1)}, bf16[160,128]{1,0:T(8,128)(2,1)S(1)}, u32[]{:S(2)}, u32[]{:S(2)}) collective-permute-start(bf16[160,128]{1,0:T(8,128)(2,1)S(1)} %constant_dynamic-update-slice_fusion.slab_ref), channel_id=1, source_target_pairs={{0,24},{8,16},{16,8},{24,0},{1,25},{9,17},{17,9},{25,1},{2,26},{10... | collective-permute-start | bytes 122888 | tf_op jit(solution)/shard_map/ppermute | solution.py:553
  69.6 4.0 %collective-permute-start.18 = (bf16[160,128]{1,0:T(8,128)(2,1)S(1)}, bf16[160,128]{1,0:T(8,128)(2,1)S(1)}, u32[]{:S(2)}, u32[]{:S(2)}) collective-permute-start(bf16[160,128]{1,0:T(8,128)(2,1)S(1)} %constant_dynamic-update-slice_fusion.slab_ref), channel_id=1, source_target_pairs={{0,16},{8,24},{16,0},{24,8},{1,17},{9,25},{17,1},{25,9},{2,18},{10... | collective-permute-start | bytes 122888 | tf_op jit(solution)/shard_map/ppermute | solution.py:553
  70.1 4.0 %collective-permute-start.17 = (bf16[160,128]{1,0:T(8,128)(2,1)S(1)}, bf16[160,128]{1,0:T(8,128)(2,1)S(1)}, u32[]{:S(2)}, u32[]{:S(2)}) collective-permute-start(bf16[160,128]{1,0:T(8,128)(2,1)S(1)} %constant_dynamic-update-slice_fusion.slab_ref), channel_id=1, source_target_pairs={{0,8},{8,0},{16,24},{24,16},{1,9},{9,1},{17,25},{25,17},{2,10},{10... | collective-permute-start | bytes 122888 | tf_op jit(solution)/shard_map/ppermute | solution.py:553
  (10 other events, 38.9 us)

commit v10 on v8

--- a/solution.py
+++ b/solution.py
@@ -388,35 +388,46 @@
         act[length:, cols] = jnp.where(gone, 0.0, value[length:]).astype(BF16)
 
 
-def own_kernel(place_ref, slab_ref, conv_ref, alpha_ref, act_ref, padded, windows):
+def own_kernel(place_ref, slab_ref, conv_ref, alpha_ref, up_ref, act_ref, staged_ref, *scratch):
+    padded, windows, sem = scratch
+    copy = pltpu.make_async_copy(up_ref, staged_ref, sem)
+    copy.start()
     unpack_slab(place_ref, slab_ref, padded)
     convolve(place_ref, padded, windows, conv_ref, alpha_ref, act_ref)
-
-
-def activate_own(place, slab, conv, alpha, span):
+    copy.wait()
+
+
+def activate_own(place, slab, conv, alpha, first_up, span):
     lat = slab.shape[1] // 2
     taps_lat, channels = conv.shape
     return pl.pallas_call(
         own_kernel,
-        out_shape=jax.ShapeDtypeStruct((span, channels), BF16),
-        in_specs=[pl.BlockSpec(memory_space=pltpu.SMEM)] + [whole()] * 3,
-        out_specs=whole(),
-        scratch_shapes=[pltpu.VMEM((span, lat), F32), pltpu.VMEM((span, taps_lat), BF16)],
-        compiler_params=params(16),
-        cost_estimate=FREE,
-    )(place, slab, conv, alpha)
+        out_shape=[
+            jax.ShapeDtypeStruct((span, channels), BF16),
+            jax.ShapeDtypeStruct(first_up.shape, BF16),
+        ],
+        in_specs=[pl.BlockSpec(memory_space=pltpu.SMEM)]
+        + [whole()] * 3
+        + [pl.BlockSpec(memory_space=pl.ANY)],
+        out_specs=[whole()] * 2,
+        scratch_shapes=[
+            pltpu.VMEM((span, lat), F32),
+            pltpu.VMEM((span, taps_lat), BF16),
+            pltpu.SemaphoreType.DMA,
+        ],
+        compiler_params=params(24),
+        cost_estimate=FREE,
+    )(place, slab, conv, alpha, first_up)
 
 
 def decoder_kernel(segs, place_ref, own_ref, *refs):
     slab_refs = refs[: segs - 1]
-    conv_ref, alpha_ref, up_hbm, out_ref = refs[segs - 1 : segs + 3]
-    padded, windows, others, up_ref, rows_out, sems, up_sem = refs[segs + 3 :]
+    conv_ref, alpha_ref, up_ref, out_ref = refs[segs - 1 : segs + 3]
+    padded, windows, others, rows_out, sems = refs[segs + 3 :]
     span = own_ref.shape[0]
     length = span - 4 * EDGE
     width = up_ref.shape[2]
     own = place_ref[0]
-    up_copy = pltpu.make_async_copy(up_hbm, up_ref, up_sem)
-    up_copy.start()
 
     def out_copy(k):
         return pltpu.make_async_copy(rows_out.at[k], out_ref.at[own ^ k], sems.at[k])
@@ -425,7 +436,6 @@
         unpack_slab(place_ref, slab_refs[k], padded.at[k])
     for k in range(segs - 1):
         convolve(place_ref, padded.at[k], windows.at[k], conv_ref, alpha_ref, others.at[k])
-    up_copy.wait()
     for k in range(segs):
         act = own_ref if k == 0 else others.at[k - 1]
         for r in range(0, 8, 2):
@@ -456,19 +466,16 @@
         functools.partial(decoder_kernel, segs),
         out_shape=jax.ShapeDtypeStruct((segs, 8 * length, width), F32),
         in_specs=[pl.BlockSpec(memory_space=pltpu.SMEM)]
-        + [whole()] * (segs + 2)
-        + [pl.BlockSpec(memory_space=pl.ANY)],
+        + [whole()] * (segs + 3),
         out_specs=pl.BlockSpec(memory_space=pl.ANY),
         scratch_shapes=[
             pltpu.VMEM((segs - 1, span, lat), F32),
             pltpu.VMEM((segs - 1, span, conv.shape[0]), BF16),
             pltpu.VMEM((segs - 1, span, channels), BF16),
-            pltpu.VMEM(first_up.shape, BF16),
             pltpu.VMEM((segs, 8 * length, width), F32),
             pltpu.SemaphoreType.DMA((segs,)),
-            pltpu.SemaphoreType.DMA,
-        ],
-        compiler_params=params(52),
+        ],
+        compiler_params=params(32),
         cost_estimate=FREE,
     )(place, own, *slabs, conv, alpha, first_up)
 
@@ -541,8 +548,8 @@
     spot = jnp.stack([lax.axis_index("seg"), me, jnp.int32(n)]).astype(jnp.int32)
     alpha = jnp.stack([snake_first * (1.0 / math.pi), 1.0 / snake_first])
     conv = in_conv.reshape(-1, in_conv.shape[2])
-    act = activate_own(spot, slab, conv, alpha, base.shape[0])
-    return decode(spot, act, others, conv, alpha, first_up)
+    act, staged = activate_own(spot, slab, conv, alpha, first_up, base.shape[0])
+    return decode(spot, act, others, conv, alpha, staged)
 
 
 def solution(mesh):

time: 91.6 us -> 92.9 us (1.014)
  local copies, waits for them, and re-layouts: 6.85 us -> 10.2 us
  Pallas kernels: 36.1 us -> 34.9 us
  waiting for transfers between devices: 16.6 us -> 15.6 us
    unnamed x23 -> x25, local copies, waits for them, and re-layouts: 6.84 us -> 10.2 us
    pallas_call x1, Pallas kernels: 16.9 us -> 15.1 us  [decode(): pl.pallas_call(functools.partial(decoder_kernel, segs), out_shape=jax.Sha...]
    ppermute x3, waiting for transfers between devices: 1.02 us -> 0.01 us  [local(): lax.ppermute(slab, 'seg', [(i, i ^ k) for i in range(segs)])]
  transfers between devices with their start and end apart: 20 -> 20, of which waited for: 7 -> 5; matrix products, arithmetic and copies ran while one was open for 0% -> 0% of each run, Pallas kernels for 20% -> 20%
where the time goes in v10:
time: 92.9 us; the launch traced here: 92.4 us
  Pallas kernels  34.9 us (38%)
  starting transfers between devices  31 us (33%)
  waiting for transfers between devices  15.6 us (17%)
  local copies, waits for them, and re-layouts  10.2 us (11%)
    ppermute x12, starting transfers between devices, swap(): return lax.ppermute(value, 'expert', [(i, i ^ k) for i in members])  17.5 us
    pallas_call x1, Pallas kernels, decode(): pl.pallas_call(functools.partial(decoder_kernel, segs), out_shape=jax.Sha...  15.1 us
    unnamed x25, local copies, waits for them, and re-layouts  10.2 us
    ppermute x4, starting transfers between devices, cross(): return lax.ppermute(value, 'expert', [(i, j) for i, j in pairs if i != j])  9.35 us
    pallas_call x2, Pallas kernels, run_group(): pl.pallas_call(functools.partial(group_kernel, n, far), out_shape=[jax.Sh...  7.95 us
    ppermute x12, waiting for transfers between devices, swap(): return lax.ppermute(value, 'expert', [(i, i ^ k) for i in members])  7.88 us
    ppermute x4, waiting for transfers between devices, cross(): return lax.ppermute(value, 'expert', [(i, j) for i, j in pairs if i != j])  7.7 us
    ppermute x3, starting transfers between devices, local(): lax.ppermute(slab, 'seg', [(i, i ^ k) for i in range(segs)])  3.55 us
  transfers between devices with their start and end apart: 20, of which 5 were waited for; matrix products, arithmetic and copies ran while one was open for 0% of the time, Pallas kernels for 20%

profile of v10, /device:TPU:0, one launch (start us, length us, event | category | flops | bytes accessed | tf_op | source)
XLA Modules:
  0.0 92.4 jit_solution(11003881274490815707)
XLA Ops:
  2.6 1.5 %shard_map.91 = (bf16[96,1536]{1,0:T(8,128)(2,1)S(1)}, bf16[112,1536]{1,0:T(8,128)(2,1)S(1)}, bf16[96,1536]{1,0:T(8,128)(2,1)S(1)}, bf16[112,1536]{1,0:T(8,128)(2,1)S(1)}) custom-call(s32[2]{0:T(128)S(1)} %get-tuple-element.78.origin_ref, s32[2,256]{1,0:T(2,128)} %bitcast.3.refs_0_.ids_ref, bf16[256,1536]{1,0:T(8,128)(2,1)S(1)} %copy-done.3, ...), custom_call_target="tpu_custom_call" | custom-call | tf_op jit(solution)/shard_map/pallas_call | solution.py:99
  4.6 5.5 %collective-permute-start.4 = (bf16[112,1536]{1,0:T(8,128)(2,1)S(1)}, bf16[112,1536]{1,0:T(8,128)(2,1)S(1)}, u32[]{:S(2)}, u32[]{:S(2)}) collective-permute-start(bf16[112,1536]{1,0:T(8,128)(2,1)S(1)} %get-tuple-element.45), channel_id=1, source_target_pairs={{0,3},{1,2},{2,1},{3,0},{4,7},{5,6},{6,5},{7,4},{8,11},{9,10},{10,... | collective-permute-start | bytes 1032200 | tf_op jit(solution)/shard_map/ppermute | solution.py:506
  10.7 1.7 %collective-permute-start.3 = (bf16[96,1536]{1,0:T(8,128)(2,1)S(1)}, bf16[96,1536]{1,0:T(8,128)(2,1)S(1)}, u32[]{:S(2)}, u32[]{:S(2)}) collective-permute-start(bf16[96,1536]{1,0:T(8,128)(2,1)S(1)} %get-tuple-element.44), channel_id=1, source_target_pairs={{0,2},{1,3},{2,0},{3,1},{4,6},{5,7},{6,4},{7,5},{8,10},{9,11},{10,... | collective-permute-start | bytes 884744 | tf_op jit(solution)/shard_map/ppermute | solution.py:506
  13.8 1.8 %shard_map.92 = (bf16[96,1536]{1,0:T(8,128)(2,1)S(1)}, bf16[96,1536]{1,0:T(8,128)(2,1)S(1)}, bf16[96,1536]{1,0:T(8,128)(2,1)S(1)}, bf16[96,1536]{1,0:T(8,128)(2,1)S(1)}) custom-call(s32[2]{0:T(128)S(1)} %pad_add_fusion.3.origin_ref, s32[2,256]{1,0:T(2,128)} %bitcast.3.refs_0_.ids_ref, bf16[256,1536]{1,0:T(8,128)(2,1)S(1)} %copy-done.4, ...), custom_call_target="tpu_custom_call" | custom-call | tf_op jit(solution)/shard_map/pallas_call | solution.py:99
  15.6 2.0 %collective-permute-start.11 = (bf16[96,1536]{1,0:T(8,128)(2,1)S(1)}, bf16[96,1536]{1,0:T(8,128)(2,1)S(1)}, u32[]{:S(2)}, u32[]{:S(2)}) collective-permute-start(bf16[96,1536]{1,0:T(8,128)(2,1)S(1)} %get-tuple-element.63), channel_id=1, source_target_pairs={{0,7},{1,6},{2,3},{3,2},{4,5},{5,4},{6,1},{7,0},{8,15},{9,14},{10,... | collective-permute-start | bytes 884744 | tf_op jit(solution)/shard_map/ppermute | solution.py:522
  17.6 3.2 %collective-permute-start.10 = (bf16[96,1536]{1,0:T(8,128)(2,1)S(1)}, bf16[96,1536]{1,0:T(8,128)(2,1)S(1)}, u32[]{:S(2)}, u32[]{:S(2)}) collective-permute-start(bf16[96,1536]{1,0:T(8,128)(2,1)S(1)} %get-tuple-element.62.local_ref), channel_id=1, source_target_pairs={{0,6},{1,7},{6,0},{7,1},{8,14},{9,15},{14,8},{15,9},{16,22},{17,23... | collective-permute-start | bytes 884744 | tf_op jit(solution)/shard_map/ppermute | solution.py:522
  20.9 4.1 %collective-permute-done.3.refs_1_ = bf16[96,1536]{1,0:T(8,128)(2,1)S(1)} collective-permute-done((bf16[96,1536]{1,0:T(8,128)(2,1)S(1)}, bf16[96,1536]{1,0:T(8,128)(2,1)S(1)}, u32[]{:S(2)}, u32[]{:S(2)}) %collective-permute-start.3) | collective-permute-done | bytes 294944 | tf_op jit(solution)/shard_map/ppermute | solution.py:506
  25.0 3.9 %collective-permute-start.8 = (bf16[96,1536]{1,0:T(8,128)(2,1)S(1)}, bf16[96,1536]{1,0:T(8,128)(2,1)S(1)}, u32[]{:S(2)}, u32[]{:S(2)}) collective-permute-start(bf16[96,1536]{1,0:T(8,128)(2,1)S(1)} %get-tuple-element.46), channel_id=1, source_target_pairs={{0,4},{1,5},{2,0},{3,1},{4,6},{5,7},{6,2},{7,3},{8,12},{9,13},{10,... | collective-permute-start | bytes 884744 | tf_op jit(solution)/shard_map/ppermute | solution.py:522
  29.1 2.8 %copy-done.6 = bf16[1,2048,1536]{2,1,0:T(8,128)(2,1)S(1)} copy-done((bf16[1,2048,1536]{2,1,0:T(8,128)(2,1)S(1)}, bf16[1,2048,1536]{2,1,0:T(8,128)(2,1)}, u32[]{:S(2)}) %copy-start.6) | copy-done | bytes 6291480
  32.8 2.5 %shard_map.94.refs_4_.refs_5_ = bf16[2048,128]{1,0:T(8,128)(2,1)S(1)} custom-call(bf16[2048,1536]{1,0:T(8,128)(2,1)S(1)} %bitcast.16, bf16[64,1536]{1,0:T(8,128)(2,1)S(1)} %bitcast.17), custom_call_target="tpu_custom_call" | custom-call | tf_op jit(solution)/shard_map/pallas_call | solution.py:127
  35.4 4.0 %shard_map.95 = (bf16[128,128]{1,0:T(8,128)(2,1)S(1)}, bf16[128,128]{1,0:T(8,128)(2,1)S(1)}, bf16[128,128]{1,0:T(8,128)(2,1)S(1)}, bf16[128,128]{1,0:T(8,128)(2,1)S(1)}) custom-call(s32[2]{0:T(128)S(1)} %get-tuple-element.54.place_ref, bf16[96,1536]{1,0:T(8,128)(2,1)S(1)} %get-tuple-element.55.local_ref, ...), custom_call_target="tpu_custom_call" | custom-call | tf_op jit(solution)/shard_map/pallas_call | solution.py:293
  39.5 1.9 %collective-permute-start.6 = (bf16[128,128]{1,0:T(8,128)(2,1)S(1)}, bf16[128,128]{1,0:T(8,128)(2,1)S(1)}, u32[]{:S(2)}, u32[]{:S(2)}) collective-permute-start(bf16[128,128]{1,0:T(8,128)(2,1)S(1)} %get-tuple-element.60), channel_id=1, source_target_pairs={{0,2},{1,3},{2,0},{3,1},{4,6},{5,7},{6,4},{7,5},{8,10},{9,11},{10,... | collective-permute-start | bytes 98312 | tf_op jit(solution)/shard_map/ppermute | solution.py:506
  41.5 2.0 %shard_map.93 = (bf16[8,272,128]{2,1,0:T(8,128)(2,1)S(1)}, f32[272,128]{1,0:T(8,128)S(1)}, f32[272,64]{1,0:T(8,128)S(1)}) custom-call(s32[2]{0:T(128)S(1)} %get-tuple-element.54.place_ref, bf16[256,1536]{1,0:T(8,128)(2,1)S(1)} %copy-done.5, bf16[64,1536]{1,0:T(8,128)(2,1)S(1)} %bitcast.18, s32[2,256]{1,0:T(2,128)} %bitcast.3.refs_0_.ids_ref, ...), custom_call_target="tpu_custom_call" | custom-call | tf_op jit(solution)/shard_map/pallas_call | solution.py:225
  43.6 1.4 %collective-permute-done.8.refs_0_ = bf16[96,1536]{1,0:T(8,128)(2,1)S(1)} collective-permute-done((bf16[96,1536]{1,0:T(8,128)(2,1)S(1)}, bf16[96,1536]{1,0:T(8,128)(2,1)S(1)}, u32[]{:S(2)}, u32[]{:S(2)}) %collective-permute-start.8) | collective-permute-done | bytes 294944 | tf_op jit(solution)/shard_map/ppermute | solution.py:522
  45.0 6.3 %collective-permute-done.9.refs_1_ = bf16[96,1536]{1,0:T(8,128)(2,1)S(1)} collective-permute-done((bf16[96,1536]{1,0:T(8,128)(2,1)S(1)}, bf16[96,1536]{1,0:T(8,128)(2,1)S(1)}, u32[]{:S(2)}, u32[]{:S(2)}) %collective-permute-start.9) | collective-permute-done | bytes 294944 | tf_op jit(solution)/shard_map/ppermute | solution.py:522
  51.3 3.9 %shard_map.96 = (bf16[128,128]{1,0:T(8,128)(2,1)S(1)}, bf16[128,128]{1,0:T(8,128)(2,1)S(1)}, bf16[128,128]{1,0:T(8,128)(2,1)S(1)}, bf16[128,128]{1,0:T(8,128)(2,1)S(1)}) custom-call(s32[2]{0:T(128)S(1)} %get-tuple-element.54.place_ref, bf16[96,1536]{1,0:T(8,128)(2,1)S(1)} %get-tuple-element.62.local_ref, ...), custom_call_target="tpu_custom_call" | custom-call | tf_op jit(solution)/shard_map/pallas_call | solution.py:293
  57.7 2.5 %collective-permute-start.14 = (bf16[128,128]{1,0:T(8,128)(2,1)S(1)}, bf16[128,128]{1,0:T(8,128)(2,1)S(1)}, u32[]{:S(2)}, u32[]{:S(2)}) collective-permute-start(bf16[128,128]{1,0:T(8,128)(2,1)S(1)} %get-tuple-element.66), channel_id=1, source_target_pairs={{0,6},{1,7},{2,4},{3,5},{4,2},{5,3},{6,0},{7,1},{8,14},{9,15},{10,... | collective-permute-start | bytes 98312 | tf_op jit(solution)/shard_map/ppermute | solution.py:506
  60.2 1.3 %collective-permute-start.15 = (bf16[128,128]{1,0:T(8,128)(2,1)S(1)}, bf16[128,128]{1,0:T(8,128)(2,1)S(1)}, u32[]{:S(2)}, u32[]{:S(2)}) collective-permute-start(bf16[128,128]{1,0:T(8,128)(2,1)S(1)} %get-tuple-element.67), channel_id=1, source_target_pairs={{0,7},{1,6},{2,5},{3,4},{4,3},{5,2},{6,1},{7,0},{8,15},{9,14},{10,... | collective-permute-start | bytes 98312 | tf_op jit(solution)/shard_map/ppermute | solution.py:506
  61.6 1.9 %collective-permute-done.14.refs_6_ = bf16[128,128]{1,0:T(8,128)(2,1)S(1)} collective-permute-done((bf16[128,128]{1,0:T(8,128)(2,1)S(1)}, bf16[128,128]{1,0:T(8,128)(2,1)S(1)}, u32[]{:S(2)}, u32[]{:S(2)}) %collective-permute-start.14) | collective-permute-done | bytes 32800 | tf_op jit(solution)/shard_map/ppermute | solution.py:506
  63.5 1.8 %collective-permute-done.15.refs_7_ = bf16[128,128]{1,0:T(8,128)(2,1)S(1)} collective-permute-done((bf16[128,128]{1,0:T(8,128)(2,1)S(1)}, bf16[128,128]{1,0:T(8,128)(2,1)S(1)}, u32[]{:S(2)}, u32[]{:S(2)}) %collective-permute-start.15) | collective-permute-done | bytes 32800 | tf_op jit(solution)/shard_map/ppermute | solution.py:506
  67.1 2.5 %collective-permute-start.19 = (bf16[160,128]{1,0:T(8,128)(2,1)S(1)}, bf16[160,128]{1,0:T(8,128)(2,1)S(1)}, u32[]{:S(2)}, u32[]{:S(2)}) collective-permute-start(bf16[160,128]{1,0:T(8,128)(2,1)S(1)} %constant_dynamic-update-slice_fusion.slab_ref), channel_id=1, source_target_pairs={{0,24},{8,16},{16,8},{24,0},{1,25},{9,17},{17,9},{25,1},{2,26},{10... | collective-permute-start | bytes 122888 | tf_op jit(solution)/shard_map/ppermute | solution.py:546
  70.8 3.4 %copy-done.1 = bf16[16,2048,128]{2,1,0:T(8,128)(2,1)S(1)} copy-done((bf16[16,2048,128]{2,1,0:T(8,128)(2,1)S(1)}, bf16[16,2048,128]{2,1,0:T(8,128)(2,1)}, u32[]{:S(2)}) %copy-start.1) | copy-done | bytes 8388632
  74.1 2.9 %shard_map.98 = (bf16[272,2048]{1,0:T(8,128)(2,1)S(1)}, bf16[16,2048,128]{2,1,0:T(8,128)(2,1)S(1)}) custom-call(s32[3]{0:T(128)S(1)} %pad_add_fusion.place_ref, bf16[160,128]{1,0:T(8,128)(2,1)S(1)} %constant_dynamic-update-slice_fusion.slab_ref, bf16[448,2048]{1,0:T(8,128)(2,1)S(1)} %bitcast.14, f32[2,2048]{1,0:T(2,128)S(1)} %pad_maximum_fusion.alpha_ref.refs_4_, ...), custom_call_target="tpu_custom_call" | custom-call | tf_op jit(solution)/shard_map/pallas_call | solution.py:403
  77.1 15.1 %shard_map.99 = f32[4,2048,128]{2,1,0:T(8,128)} custom-call(s32[3]{0:T(128)S(1)} %pad_add_fusion.place_ref, bf16[272,2048]{1,0:T(8,128)(2,1)S(1)} %get-tuple-element.73.own_ref, bf16[160,128]{1,0:T(8,128)(2,1)S(1)} %collective-permute-done.17.refs_0_, bf16[160,128]{1,0:T(8,128)(2,1)S(1)} %collective-permute-done.18.refs_1_, ...), custom_call_target="tpu_custom_call" | custom-call | tf_op jit(solution)/shard_map/pallas_call | solution.py:465
  (56 shorter events, 11.9 us)
Async XLA Ops:
  0.0 12.6 %collective-permute-start.1 = (bf16[256,1536]{1,0:T(8,128)(2,1)}, bf16[256,1536]{1,0:T(8,128)(2,1)S(1)}, u32[]{:S(2)}, u32[]{:S(2)}) collective-permute-start(bf16[256,1536]{1,0:T(8,128)(2,1)} %frames_ref.1), channel_id=1, source_target_pairs={{2,4},{3,5},{4,2},{5,3},{10,12},{11,13},{12,10},{13,11},{18,20},{1... | collective-permute-start | bytes 2359304 | tf_op jit(solution)/shard_map/ppermute | solution.py:506
  4.1 20.9 %collective-permute-start.2 = (bf16[112,1536]{1,0:T(8,128)(2,1)S(1)}, bf16[112,1536]{1,0:T(8,128)(2,1)S(1)}, u32[]{:S(2)}, u32[]{:S(2)}) collective-permute-start(bf16[112,1536]{1,0:T(8,128)(2,1)S(1)} %get-tuple-element.43), channel_id=1, source_target_pairs={{0,1},{1,0},{2,3},{3,2},{4,5},{5,4},{6,7},{7,6},{8,9},{9,8},{10,11... | collective-permute-start | bytes 1032200 | tf_op jit(solution)/shard_map/ppermute | solution.py:506
  4.6 20.4 %collective-permute-start.4 = (bf16[112,1536]{1,0:T(8,128)(2,1)S(1)}, bf16[112,1536]{1,0:T(8,128)(2,1)S(1)}, u32[]{:S(2)}, u32[]{:S(2)}) collective-permute-start(bf16[112,1536]{1,0:T(8,128)(2,1)S(1)} %get-tuple-element.45), channel_id=1, source_target_pairs={{0,3},{1,2},{2,1},{3,0},{4,7},{5,6},{6,5},{7,4},{8,11},{9,10},{10,... | collective-permute-start | bytes 1032200 | tf_op jit(solution)/shard_map/ppermute | solution.py:506
  10.1 2.5 %collective-permute-start = (s32[2,256]{1,0:T(2,128)}, s32[2,256]{1,0:T(2,128)S(1)}, u32[]{:S(2)}, u32[]{:S(2)}) collective-permute-start(s32[2,256]{1,0:T(2,128)} %bitcast.3.refs_0_.ids_ref), channel_id=1, source_target_pairs={{2,4},{3,5},{4,2},{5,3},{10,12},{11,13},{12,10},{13,11},{18,20},{1... | collective-permute-start | bytes 6152 | tf_op jit(solution)/shard_map/ppermute | solution.py:506
  10.7 14.3 %collective-permute-start.3 = (bf16[96,1536]{1,0:T(8,128)(2,1)S(1)}, bf16[96,1536]{1,0:T(8,128)(2,1)S(1)}, u32[]{:S(2)}, u32[]{:S(2)}) collective-permute-start(bf16[96,1536]{1,0:T(8,128)(2,1)S(1)} %get-tuple-element.44), channel_id=1, source_target_pairs={{0,2},{1,3},{2,0},{3,1},{4,6},{5,7},{6,4},{7,5},{8,10},{9,11},{10,... | collective-permute-start | bytes 884744 | tf_op jit(solution)/shard_map/ppermute | solution.py:506
  12.5 22.9 %copy-start = (bf16[1,1536,2048]{2,1,0:T(8,128)(2,1)S(1)}, bf16[1,1536,2048]{2,1,0:T(8,128)(2,1)}, u32[]{:S(2)}) copy-start(bf16[1,1536,2048]{2,1,0:T(8,128)(2,1)} %param.12) | copy-start | bytes 18874372
  15.6 23.9 %collective-permute-start.11 = (bf16[96,1536]{1,0:T(8,128)(2,1)S(1)}, bf16[96,1536]{1,0:T(8,128)(2,1)S(1)}, u32[]{:S(2)}, u32[]{:S(2)}) collective-permute-start(bf16[96,1536]{1,0:T(8,128)(2,1)S(1)} %get-tuple-element.63), channel_id=1, source_target_pairs={{0,7},{1,6},{2,3},{3,2},{4,5},{5,4},{6,1},{7,0},{8,15},{9,14},{10,... | collective-permute-start | bytes 884744 | tf_op jit(solution)/shard_map/ppermute | solution.py:522
  17.6 25.9 %collective-permute-start.10 = (bf16[96,1536]{1,0:T(8,128)(2,1)S(1)}, bf16[96,1536]{1,0:T(8,128)(2,1)S(1)}, u32[]{:S(2)}, u32[]{:S(2)}) collective-permute-start(bf16[96,1536]{1,0:T(8,128)(2,1)S(1)} %get-tuple-element.62.local_ref), channel_id=1, source_target_pairs={{0,6},{1,7},{6,0},{7,1},{8,14},{9,15},{14,8},{15,9},{16,22},{17,23... | collective-permute-start | bytes 884744 | tf_op jit(solution)/shard_map/ppermute | solution.py:522
  25.0 20.0 %collective-permute-start.8 = (bf16[96,1536]{1,0:T(8,128)(2,1)S(1)}, bf16[96,1536]{1,0:T(8,128)(2,1)S(1)}, u32[]{:S(2)}, u32[]{:S(2)}) collective-permute-start(bf16[96,1536]{1,0:T(8,128)(2,1)S(1)} %get-tuple-element.46), channel_id=1, source_target_pairs={{0,4},{1,5},{2,0},{3,1},{4,6},{5,7},{6,2},{7,3},{8,12},{9,13},{10,... | collective-permute-start | bytes 884744 | tf_op jit(solution)/shard_map/ppermute | solution.py:522
  28.9 22.4 %collective-permute-start.9 = (bf16[96,1536]{1,0:T(8,128)(2,1)S(1)}, bf16[96,1536]{1,0:T(8,128)(2,1)S(1)}, u32[]{:S(2)}, u32[]{:S(2)}) collective-permute-start(bf16[96,1536]{1,0:T(8,128)(2,1)S(1)} %get-tuple-element.47), channel_id=1, source_target_pairs={{0,5},{1,4},{2,1},{3,0},{4,7},{5,6},{6,3},{7,2},{8,13},{9,12},{10,... | collective-permute-start | bytes 884744 | tf_op jit(solution)/shard_map/ppermute | solution.py:522
  32.8 8.6 %copy-start.8 = (bf16[1536,64]{0,1:T(8,128)(2,1)S(1)}, bf16[1536,64]{0,1:T(8,128)(2,1)}, u32[]{:S(2)}) copy-start(bf16[1536,64]{0,1:T(8,128)(2,1)} %param.14) | copy-start | bytes 589828
  32.8 8.6 %copy-start.10 = (f32[256,2]{0,1:T(2,128)S(1)}, f32[256,2]{0,1:T(2,128)}, u32[]{:S(2)}) copy-start(f32[256,2]{0,1:T(2,128)} %param.11) | copy-start | bytes 6148
  39.4 31.4 %copy-start.2 = (bf16[7,64,2048]{2,1,0:T(8,128)(2,1)S(1)}, bf16[7,64,2048]{2,1,0:T(8,128)(2,1)}, u32[]{:S(2)}) copy-start(bf16[7,64,2048]{2,1,0:T(8,128)(2,1)} %param.15) | copy-start | bytes 5505028
  39.4 18.3 %collective-permute-start.5 = (bf16[128,128]{1,0:T(8,128)(2,1)S(1)}, bf16[128,128]{1,0:T(8,128)(2,1)S(1)}, u32[]{:S(2)}, u32[]{:S(2)}) collective-permute-start(bf16[128,128]{1,0:T(8,128)(2,1)S(1)} %get-tuple-element.59), channel_id=1, source_target_pairs={{0,1},{1,0},{2,3},{3,2},{4,5},{5,4},{6,7},{7,6},{8,9},{9,8},{10,11... | collective-permute-start | bytes 98312 | tf_op jit(solution)/shard_map/ppermute | solution.py:506
  39.5 20.6 %collective-permute-start.6 = (bf16[128,128]{1,0:T(8,128)(2,1)S(1)}, bf16[128,128]{1,0:T(8,128)(2,1)S(1)}, u32[]{:S(2)}, u32[]{:S(2)}) collective-permute-start(bf16[128,128]{1,0:T(8,128)(2,1)S(1)} %get-tuple-element.60), channel_id=1, source_target_pairs={{0,2},{1,3},{2,0},{3,1},{4,6},{5,7},{6,4},{7,5},{8,10},{9,11},{10,... | collective-permute-start | bytes 98312 | tf_op jit(solution)/shard_map/ppermute | solution.py:506
  43.5 18.0 %collective-permute-start.7 = (bf16[128,128]{1,0:T(8,128)(2,1)S(1)}, bf16[128,128]{1,0:T(8,128)(2,1)S(1)}, u32[]{:S(2)}, u32[]{:S(2)}) collective-permute-start(bf16[128,128]{1,0:T(8,128)(2,1)S(1)} %get-tuple-element.61), channel_id=1, source_target_pairs={{0,3},{1,2},{2,1},{3,0},{4,7},{5,6},{6,5},{7,4},{8,11},{9,10},{10,... | collective-permute-start | bytes 98312 | tf_op jit(solution)/shard_map/ppermute | solution.py:506
  55.2 6.3 %collective-permute-start.12 = (bf16[128,128]{1,0:T(8,128)(2,1)S(1)}, bf16[128,128]{1,0:T(8,128)(2,1)S(1)}, u32[]{:S(2)}, u32[]{:S(2)}) collective-permute-start(bf16[128,128]{1,0:T(8,128)(2,1)S(1)} %get-tuple-element.64), channel_id=1, source_target_pairs={{0,4},{1,5},{2,6},{3,7},{4,0},{5,1},{6,2},{7,3},{8,12},{9,13},{10,... | collective-permute-start | bytes 98312 | tf_op jit(solution)/shard_map/ppermute | solution.py:506
  56.4 5.2 %collective-permute-start.13 = (bf16[128,128]{1,0:T(8,128)(2,1)S(1)}, bf16[128,128]{1,0:T(8,128)(2,1)S(1)}, u32[]{:S(2)}, u32[]{:S(2)}) collective-permute-start(bf16[128,128]{1,0:T(8,128)(2,1)S(1)} %get-tuple-element.65), channel_id=1, source_target_pairs={{0,5},{1,4},{2,7},{3,6},{4,1},{5,0},{6,3},{7,2},{8,13},{9,12},{10,... | collective-permute-start | bytes 98312 | tf_op jit(solution)/shard_map/ppermute | solution.py:506
  57.7 5.8 %collective-permute-start.14 = (bf16[128,128]{1,0:T(8,128)(2,1)S(1)}, bf16[128,128]{1,0:T(8,128)(2,1)S(1)}, u32[]{:S(2)}, u32[]{:S(2)}) collective-permute-start(bf16[128,128]{1,0:T(8,128)(2,1)S(1)} %get-tuple-element.66), channel_id=1, source_target_pairs={{0,6},{1,7},{2,4},{3,5},{4,2},{5,3},{6,0},{7,1},{8,14},{9,15},{10,... | collective-permute-start | bytes 98312 | tf_op jit(solution)/shard_map/ppermute | solution.py:506
  60.2 5.1 %collective-permute-start.15 = (bf16[128,128]{1,0:T(8,128)(2,1)S(1)}, bf16[128,128]{1,0:T(8,128)(2,1)S(1)}, u32[]{:S(2)}, u32[]{:S(2)}) collective-permute-start(bf16[128,128]{1,0:T(8,128)(2,1)S(1)} %get-tuple-element.67), channel_id=1, source_target_pairs={{0,7},{1,6},{2,5},{3,4},{4,3},{5,2},{6,1},{7,0},{8,15},{9,14},{10,... | collective-permute-start | bytes 98312 | tf_op jit(solution)/shard_map/ppermute | solution.py:506
  66.4 0.7 collective-permute-start.16
  67.1 9.9 %collective-permute-start.19 = (bf16[160,128]{1,0:T(8,128)(2,1)S(1)}, bf16[160,128]{1,0:T(8,128)(2,1)S(1)}, u32[]{:S(2)}, u32[]{:S(2)}) collective-permute-start(bf16[160,128]{1,0:T(8,128)(2,1)S(1)} %constant_dynamic-update-slice_fusion.slab_ref), channel_id=1, source_target_pairs={{0,24},{8,16},{16,8},{24,0},{1,25},{9,17},{17,9},{25,1},{2,26},{10... | collective-permute-start | bytes 122888 | tf_op jit(solution)/shard_map/ppermute | solution.py:546
  69.6 7.4 %collective-permute-start.18 = (bf16[160,128]{1,0:T(8,128)(2,1)S(1)}, bf16[160,128]{1,0:T(8,128)(2,1)S(1)}, u32[]{:S(2)}, u32[]{:S(2)}) collective-permute-start(bf16[160,128]{1,0:T(8,128)(2,1)S(1)} %constant_dynamic-update-slice_fusion.slab_ref), channel_id=1, source_target_pairs={{0,16},{8,24},{16,0},{24,8},{1,17},{9,25},{17,1},{25,9},{2,18},{10... | collective-permute-start | bytes 122888 | tf_op jit(solution)/shard_map/ppermute | solution.py:546
  70.1 7.0 %collective-permute-start.17 = (bf16[160,128]{1,0:T(8,128)(2,1)S(1)}, bf16[160,128]{1,0:T(8,128)(2,1)S(1)}, u32[]{:S(2)}, u32[]{:S(2)}) collective-permute-start(bf16[160,128]{1,0:T(8,128)(2,1)S(1)} %constant_dynamic-update-slice_fusion.slab_ref), channel_id=1, source_target_pairs={{0,8},{8,0},{16,24},{24,16},{1,9},{9,1},{17,25},{25,17},{2,10},{10... | collective-permute-start | bytes 122888 | tf_op jit(solution)/shard_map/ppermute | solution.py:546
  (8 other events, 27.4 us)

commit v11 on v10

--- a/solution.py
+++ b/solution.py
@@ -415,7 +415,7 @@
             pltpu.VMEM((span, taps_lat), BF16),
             pltpu.SemaphoreType.DMA,
         ],
-        compiler_params=params(24),
+        compiler_params=params(47),
         cost_estimate=FREE,
     )(place, slab, conv, alpha, first_up)
 

time: 92.9 us -> 97.2 us (1.046)
  Pallas kernels: 34.9 us -> 39.2 us
    pallas_call x1, Pallas kernels: 2.92 us -> 7.21 us  [activate_own(): pl.pallas_call(own_kernel, out_shape=[jax.ShapeDtypeStruct((span, channel...]
  transfers between devices with their start and end apart: 20 -> 20, of which waited for: 5 -> 5; matrix products, arithmetic and copies ran while one was open for 0% -> 0% of each run, Pallas kernels for 20% -> 24%
where the time goes in v11:
time: 97.2 us; the launch traced here: 96.7 us
  Pallas kernels  39.2 us (40%)
  starting transfers between devices  31 us (32%)
  waiting for transfers between devices  15.6 us (16%)
  local copies, waits for them, and re-layouts  10.2 us (10%)
    ppermute x12, starting transfers between devices, swap(): return lax.ppermute(value, 'expert', [(i, i ^ k) for i in members])  17.5 us
    pallas_call x1, Pallas kernels, decode(): pl.pallas_call(functools.partial(decoder_kernel, segs), out_shape=jax.Sha...  15.1 us
    unnamed x25, local copies, waits for them, and re-layouts  10.2 us
    ppermute x4, starting transfers between devices, cross(): return lax.ppermute(value, 'expert', [(i, j) for i, j in pairs if i != j])  9.35 us
    pallas_call x2, Pallas kernels, run_group(): pl.pallas_call(functools.partial(group_kernel, n, far), out_shape=[jax.Sh...  7.95 us
    ppermute x12, waiting for transfers between devices, swap(): return lax.ppermute(value, 'expert', [(i, i ^ k) for i in members])  7.88 us
    ppermute x4, waiting for transfers between devices, cross(): return lax.ppermute(value, 'expert', [(i, j) for i, j in pairs if i != j])  7.7 us
    pallas_call x1, Pallas kernels, activate_own(): pl.pallas_call(own_kernel, out_shape=[jax.ShapeDtypeStruct((span, channel...  7.21 us
  transfers between devices with their start and end apart: 20, of which 5 were waited for; matrix products, arithmetic and copies ran while one was open for 0% of the time, Pallas kernels for 24%

profile of v11, /device:TPU:0, one launch (start us, length us, event | category | flops | bytes accessed | tf_op | source)
XLA Modules:
  0.0 96.7 jit_solution(1520230594511228276)
XLA Ops:
  2.6 1.5 %shard_map.91 = (bf16[96,1536]{1,0:T(8,128)(2,1)S(1)}, bf16[112,1536]{1,0:T(8,128)(2,1)S(1)}, bf16[96,1536]{1,0:T(8,128)(2,1)S(1)}, bf16[112,1536]{1,0:T(8,128)(2,1)S(1)}) custom-call(s32[2]{0:T(128)S(1)} %get-tuple-element.78.origin_ref, s32[2,256]{1,0:T(2,128)} %bitcast.3.refs_0_.ids_ref, bf16[256,1536]{1,0:T(8,128)(2,1)S(1)} %copy-done.3, ...), custom_call_target="tpu_custom_call" | custom-call | tf_op jit(solution)/shard_map/pallas_call | solution.py:99
  4.6 5.5 %collective-permute-start.4 = (bf16[112,1536]{1,0:T(8,128)(2,1)S(1)}, bf16[112,1536]{1,0:T(8,128)(2,1)S(1)}, u32[]{:S(2)}, u32[]{:S(2)}) collective-permute-start(bf16[112,1536]{1,0:T(8,128)(2,1)S(1)} %get-tuple-element.45), channel_id=1, source_target_pairs={{0,3},{1,2},{2,1},{3,0},{4,7},{5,6},{6,5},{7,4},{8,11},{9,10},{10,... | collective-permute-start | bytes 1032200 | tf_op jit(solution)/shard_map/ppermute | solution.py:506
  10.7 1.7 %collective-permute-start.3 = (bf16[96,1536]{1,0:T(8,128)(2,1)S(1)}, bf16[96,1536]{1,0:T(8,128)(2,1)S(1)}, u32[]{:S(2)}, u32[]{:S(2)}) collective-permute-start(bf16[96,1536]{1,0:T(8,128)(2,1)S(1)} %get-tuple-element.44), channel_id=1, source_target_pairs={{0,2},{1,3},{2,0},{3,1},{4,6},{5,7},{6,4},{7,5},{8,10},{9,11},{10,... | collective-permute-start | bytes 884744 | tf_op jit(solution)/shard_map/ppermute | solution.py:506
  13.8 1.8 %shard_map.92 = (bf16[96,1536]{1,0:T(8,128)(2,1)S(1)}, bf16[96,1536]{1,0:T(8,128)(2,1)S(1)}, bf16[96,1536]{1,0:T(8,128)(2,1)S(1)}, bf16[96,1536]{1,0:T(8,128)(2,1)S(1)}) custom-call(s32[2]{0:T(128)S(1)} %pad_add_fusion.3.origin_ref, s32[2,256]{1,0:T(2,128)} %bitcast.3.refs_0_.ids_ref, bf16[256,1536]{1,0:T(8,128)(2,1)S(1)} %copy-done.4, ...), custom_call_target="tpu_custom_call" | custom-call | tf_op jit(solution)/shard_map/pallas_call | solution.py:99
  15.6 2.0 %collective-permute-start.11 = (bf16[96,1536]{1,0:T(8,128)(2,1)S(1)}, bf16[96,1536]{1,0:T(8,128)(2,1)S(1)}, u32[]{:S(2)}, u32[]{:S(2)}) collective-permute-start(bf16[96,1536]{1,0:T(8,128)(2,1)S(1)} %get-tuple-element.63), channel_id=1, source_target_pairs={{0,7},{1,6},{2,3},{3,2},{4,5},{5,4},{6,1},{7,0},{8,15},{9,14},{10,... | collective-permute-start | bytes 884744 | tf_op jit(solution)/shard_map/ppermute | solution.py:522
  17.6 3.2 %collective-permute-start.10 = (bf16[96,1536]{1,0:T(8,128)(2,1)S(1)}, bf16[96,1536]{1,0:T(8,128)(2,1)S(1)}, u32[]{:S(2)}, u32[]{:S(2)}) collective-permute-start(bf16[96,1536]{1,0:T(8,128)(2,1)S(1)} %get-tuple-element.62.local_ref), channel_id=1, source_target_pairs={{0,6},{1,7},{6,0},{7,1},{8,14},{9,15},{14,8},{15,9},{16,22},{17,23... | collective-permute-start | bytes 884744 | tf_op jit(solution)/shard_map/ppermute | solution.py:522
  20.9 4.1 %collective-permute-done.3.refs_1_ = bf16[96,1536]{1,0:T(8,128)(2,1)S(1)} collective-permute-done((bf16[96,1536]{1,0:T(8,128)(2,1)S(1)}, bf16[96,1536]{1,0:T(8,128)(2,1)S(1)}, u32[]{:S(2)}, u32[]{:S(2)}) %collective-permute-start.3) | collective-permute-done | bytes 294944 | tf_op jit(solution)/shard_map/ppermute | solution.py:506
  25.0 3.9 %collective-permute-start.8 = (bf16[96,1536]{1,0:T(8,128)(2,1)S(1)}, bf16[96,1536]{1,0:T(8,128)(2,1)S(1)}, u32[]{:S(2)}, u32[]{:S(2)}) collective-permute-start(bf16[96,1536]{1,0:T(8,128)(2,1)S(1)} %get-tuple-element.46), channel_id=1, source_target_pairs={{0,4},{1,5},{2,0},{3,1},{4,6},{5,7},{6,2},{7,3},{8,12},{9,13},{10,... | collective-permute-start | bytes 884744 | tf_op jit(solution)/shard_map/ppermute | solution.py:522
  29.1 2.8 %copy-done.6 = bf16[1,2048,1536]{2,1,0:T(8,128)(2,1)S(1)} copy-done((bf16[1,2048,1536]{2,1,0:T(8,128)(2,1)S(1)}, bf16[1,2048,1536]{2,1,0:T(8,128)(2,1)}, u32[]{:S(2)}) %copy-start.6) | copy-done | bytes 6291480
  32.8 2.5 %shard_map.94.refs_4_.refs_5_ = bf16[2048,128]{1,0:T(8,128)(2,1)S(1)} custom-call(bf16[2048,1536]{1,0:T(8,128)(2,1)S(1)} %bitcast.16, bf16[64,1536]{1,0:T(8,128)(2,1)S(1)} %bitcast.17), custom_call_target="tpu_custom_call" | custom-call | tf_op jit(solution)/shard_map/pallas_call | solution.py:127
  35.4 4.0 %shard_map.95 = (bf16[128,128]{1,0:T(8,128)(2,1)S(1)}, bf16[128,128]{1,0:T(8,128)(2,1)S(1)}, bf16[128,128]{1,0:T(8,128)(2,1)S(1)}, bf16[128,128]{1,0:T(8,128)(2,1)S(1)}) custom-call(s32[2]{0:T(128)S(1)} %get-tuple-element.54.place_ref, bf16[96,1536]{1,0:T(8,128)(2,1)S(1)} %get-tuple-element.55.local_ref, ...), custom_call_target="tpu_custom_call" | custom-call | tf_op jit(solution)/shard_map/pallas_call | solution.py:293
  39.5 1.9 %collective-permute-start.6 = (bf16[128,128]{1,0:T(8,128)(2,1)S(1)}, bf16[128,128]{1,0:T(8,128)(2,1)S(1)}, u32[]{:S(2)}, u32[]{:S(2)}) collective-permute-start(bf16[128,128]{1,0:T(8,128)(2,1)S(1)} %get-tuple-element.60), channel_id=1, source_target_pairs={{0,2},{1,3},{2,0},{3,1},{4,6},{5,7},{6,4},{7,5},{8,10},{9,11},{10,... | collective-permute-start | bytes 98312 | tf_op jit(solution)/shard_map/ppermute | solution.py:506
  41.5 2.0 %shard_map.93 = (bf16[8,272,128]{2,1,0:T(8,128)(2,1)S(1)}, f32[272,128]{1,0:T(8,128)S(1)}, f32[272,64]{1,0:T(8,128)S(1)}) custom-call(s32[2]{0:T(128)S(1)} %get-tuple-element.54.place_ref, bf16[256,1536]{1,0:T(8,128)(2,1)S(1)} %copy-done.5, bf16[64,1536]{1,0:T(8,128)(2,1)S(1)} %bitcast.18, s32[2,256]{1,0:T(2,128)} %bitcast.3.refs_0_.ids_ref, ...), custom_call_target="tpu_custom_call" | custom-call | tf_op jit(solution)/shard_map/pallas_call | solution.py:225
  43.6 1.4 %collective-permute-done.8.refs_0_ = bf16[96,1536]{1,0:T(8,128)(2,1)S(1)} collective-permute-done((bf16[96,1536]{1,0:T(8,128)(2,1)S(1)}, bf16[96,1536]{1,0:T(8,128)(2,1)S(1)}, u32[]{:S(2)}, u32[]{:S(2)}) %collective-permute-start.8) | collective-permute-done | bytes 294944 | tf_op jit(solution)/shard_map/ppermute | solution.py:522
  45.0 6.3 %collective-permute-done.9.refs_1_ = bf16[96,1536]{1,0:T(8,128)(2,1)S(1)} collective-permute-done((bf16[96,1536]{1,0:T(8,128)(2,1)S(1)}, bf16[96,1536]{1,0:T(8,128)(2,1)S(1)}, u32[]{:S(2)}, u32[]{:S(2)}) %collective-permute-start.9) | collective-permute-done | bytes 294944 | tf_op jit(solution)/shard_map/ppermute | solution.py:522
  51.3 3.9 %shard_map.96 = (bf16[128,128]{1,0:T(8,128)(2,1)S(1)}, bf16[128,128]{1,0:T(8,128)(2,1)S(1)}, bf16[128,128]{1,0:T(8,128)(2,1)S(1)}, bf16[128,128]{1,0:T(8,128)(2,1)S(1)}) custom-call(s32[2]{0:T(128)S(1)} %get-tuple-element.54.place_ref, bf16[96,1536]{1,0:T(8,128)(2,1)S(1)} %get-tuple-element.62.local_ref, ...), custom_call_target="tpu_custom_call" | custom-call | tf_op jit(solution)/shard_map/pallas_call | solution.py:293
  57.7 2.5 %collective-permute-start.14 = (bf16[128,128]{1,0:T(8,128)(2,1)S(1)}, bf16[128,128]{1,0:T(8,128)(2,1)S(1)}, u32[]{:S(2)}, u32[]{:S(2)}) collective-permute-start(bf16[128,128]{1,0:T(8,128)(2,1)S(1)} %get-tuple-element.66), channel_id=1, source_target_pairs={{0,6},{1,7},{2,4},{3,5},{4,2},{5,3},{6,0},{7,1},{8,14},{9,15},{10,... | collective-permute-start | bytes 98312 | tf_op jit(solution)/shard_map/ppermute | solution.py:506
  60.2 1.3 %collective-permute-start.15 = (bf16[128,128]{1,0:T(8,128)(2,1)S(1)}, bf16[128,128]{1,0:T(8,128)(2,1)S(1)}, u32[]{:S(2)}, u32[]{:S(2)}) collective-permute-start(bf16[128,128]{1,0:T(8,128)(2,1)S(1)} %get-tuple-element.67), channel_id=1, source_target_pairs={{0,7},{1,6},{2,5},{3,4},{4,3},{5,2},{6,1},{7,0},{8,15},{9,14},{10,... | collective-permute-start | bytes 98312 | tf_op jit(solution)/shard_map/ppermute | solution.py:506
  61.6 1.9 %collective-permute-done.14.refs_6_ = bf16[128,128]{1,0:T(8,128)(2,1)S(1)} collective-permute-done((bf16[128,128]{1,0:T(8,128)(2,1)S(1)}, bf16[128,128]{1,0:T(8,128)(2,1)S(1)}, u32[]{:S(2)}, u32[]{:S(2)}) %collective-permute-start.14) | collective-permute-done | bytes 32800 | tf_op jit(solution)/shard_map/ppermute | solution.py:506
  63.5 1.8 %collective-permute-done.15.refs_7_ = bf16[128,128]{1,0:T(8,128)(2,1)S(1)} collective-permute-done((bf16[128,128]{1,0:T(8,128)(2,1)S(1)}, bf16[128,128]{1,0:T(8,128)(2,1)S(1)}, u32[]{:S(2)}, u32[]{:S(2)}) %collective-permute-start.15) | collective-permute-done | bytes 32800 | tf_op jit(solution)/shard_map/ppermute | solution.py:506
  67.1 2.5 %collective-permute-start.19 = (bf16[160,128]{1,0:T(8,128)(2,1)S(1)}, bf16[160,128]{1,0:T(8,128)(2,1)S(1)}, u32[]{:S(2)}, u32[]{:S(2)}) collective-permute-start(bf16[160,128]{1,0:T(8,128)(2,1)S(1)} %constant_dynamic-update-slice_fusion.slab_ref), channel_id=1, source_target_pairs={{0,24},{8,16},{16,8},{24,0},{1,25},{9,17},{17,9},{25,1},{2,26},{10... | collective-permute-start | bytes 122888 | tf_op jit(solution)/shard_map/ppermute | solution.py:546
  70.8 7.2 %shard_map.98 = (bf16[272,2048]{1,0:T(8,128)(2,1)S(1)}, bf16[16,2048,128]{2,1,0:T(8,128)(2,1)}) custom-call(s32[3]{0:T(128)S(1)} %pad_add_fusion.place_ref, bf16[160,128]{1,0:T(8,128)(2,1)S(1)} %constant_dynamic-update-slice_fusion.slab_ref, bf16[448,2048]{1,0:T(8,128)(2,1)S(1)} %bitcast.14, f32[2,2048]{1,0:T(2,128)S(1)} %pad_maximum_fusion.alpha_ref.refs_4_, ...), custom_call_target="tpu_custom_call" | custom-call | tf_op jit(solution)/shard_map/pallas_call | solution.py:403
  78.0 3.4 %copy-done.1 = bf16[16,2048,128]{2,1,0:T(8,128)(2,1)S(1)} copy-done((bf16[16,2048,128]{2,1,0:T(8,128)(2,1)S(1)}, bf16[16,2048,128]{2,1,0:T(8,128)(2,1)}, u32[]{:S(2)}) %copy-start.1) | copy-done | bytes 8388632
  81.4 15.1 %shard_map.99 = f32[4,2048,128]{2,1,0:T(8,128)} custom-call(s32[3]{0:T(128)S(1)} %pad_add_fusion.place_ref, bf16[272,2048]{1,0:T(8,128)(2,1)S(1)} %get-tuple-element.73.own_ref, bf16[160,128]{1,0:T(8,128)(2,1)S(1)} %collective-permute-done.17.refs_0_, bf16[160,128]{1,0:T(8,128)(2,1)S(1)} %collective-permute-done.18.refs_1_, ...), custom_call_target="tpu_custom_call" | custom-call | tf_op jit(solution)/shard_map/pallas_call | solution.py:465
  (56 shorter events, 11.9 us)
Async XLA Ops:
  0.0 12.6 %collective-permute-start.1 = (bf16[256,1536]{1,0:T(8,128)(2,1)}, bf16[256,1536]{1,0:T(8,128)(2,1)S(1)}, u32[]{:S(2)}, u32[]{:S(2)}) collective-permute-start(bf16[256,1536]{1,0:T(8,128)(2,1)} %frames_ref.1), channel_id=1, source_target_pairs={{2,4},{3,5},{4,2},{5,3},{10,12},{11,13},{12,10},{13,11},{18,20},{1... | collective-permute-start | bytes 2359304 | tf_op jit(solution)/shard_map/ppermute | solution.py:506
  4.1 20.9 %collective-permute-start.2 = (bf16[112,1536]{1,0:T(8,128)(2,1)S(1)}, bf16[112,1536]{1,0:T(8,128)(2,1)S(1)}, u32[]{:S(2)}, u32[]{:S(2)}) collective-permute-start(bf16[112,1536]{1,0:T(8,128)(2,1)S(1)} %get-tuple-element.43), channel_id=1, source_target_pairs={{0,1},{1,0},{2,3},{3,2},{4,5},{5,4},{6,7},{7,6},{8,9},{9,8},{10,11... | collective-permute-start | bytes 1032200 | tf_op jit(solution)/shard_map/ppermute | solution.py:506
  4.6 20.4 %collective-permute-start.4 = (bf16[112,1536]{1,0:T(8,128)(2,1)S(1)}, bf16[112,1536]{1,0:T(8,128)(2,1)S(1)}, u32[]{:S(2)}, u32[]{:S(2)}) collective-permute-start(bf16[112,1536]{1,0:T(8,128)(2,1)S(1)} %get-tuple-element.45), channel_id=1, source_target_pairs={{0,3},{1,2},{2,1},{3,0},{4,7},{5,6},{6,5},{7,4},{8,11},{9,10},{10,... | collective-permute-start | bytes 1032200 | tf_op jit(solution)/shard_map/ppermute | solution.py:506
  10.1 2.5 %collective-permute-start = (s32[2,256]{1,0:T(2,128)}, s32[2,256]{1,0:T(2,128)S(1)}, u32[]{:S(2)}, u32[]{:S(2)}) collective-permute-start(s32[2,256]{1,0:T(2,128)} %bitcast.3.refs_0_.ids_ref), channel_id=1, source_target_pairs={{2,4},{3,5},{4,2},{5,3},{10,12},{11,13},{12,10},{13,11},{18,20},{1... | collective-permute-start | bytes 6152 | tf_op jit(solution)/shard_map/ppermute | solution.py:506
  10.7 14.3 %collective-permute-start.3 = (bf16[96,1536]{1,0:T(8,128)(2,1)S(1)}, bf16[96,1536]{1,0:T(8,128)(2,1)S(1)}, u32[]{:S(2)}, u32[]{:S(2)}) collective-permute-start(bf16[96,1536]{1,0:T(8,128)(2,1)S(1)} %get-tuple-element.44), channel_id=1, source_target_pairs={{0,2},{1,3},{2,0},{3,1},{4,6},{5,7},{6,4},{7,5},{8,10},{9,11},{10,... | collective-permute-start | bytes 884744 | tf_op jit(solution)/shard_map/ppermute | solution.py:506
  12.5 22.9 %copy-start = (bf16[1,1536,2048]{2,1,0:T(8,128)(2,1)S(1)}, bf16[1,1536,2048]{2,1,0:T(8,128)(2,1)}, u32[]{:S(2)}) copy-start(bf16[1,1536,2048]{2,1,0:T(8,128)(2,1)} %param.12) | copy-start | bytes 18874372
  15.6 23.9 %collective-permute-start.11 = (bf16[96,1536]{1,0:T(8,128)(2,1)S(1)}, bf16[96,1536]{1,0:T(8,128)(2,1)S(1)}, u32[]{:S(2)}, u32[]{:S(2)}) collective-permute-start(bf16[96,1536]{1,0:T(8,128)(2,1)S(1)} %get-tuple-element.63), channel_id=1, source_target_pairs={{0,7},{1,6},{2,3},{3,2},{4,5},{5,4},{6,1},{7,0},{8,15},{9,14},{10,... | collective-permute-start | bytes 884744 | tf_op jit(solution)/shard_map/ppermute | solution.py:522
  17.6 25.9 %collective-permute-start.10 = (bf16[96,1536]{1,0:T(8,128)(2,1)S(1)}, bf16[96,1536]{1,0:T(8,128)(2,1)S(1)}, u32[]{:S(2)}, u32[]{:S(2)}) collective-permute-start(bf16[96,1536]{1,0:T(8,128)(2,1)S(1)} %get-tuple-element.62.local_ref), channel_id=1, source_target_pairs={{0,6},{1,7},{6,0},{7,1},{8,14},{9,15},{14,8},{15,9},{16,22},{17,23... | collective-permute-start | bytes 884744 | tf_op jit(solution)/shard_map/ppermute | solution.py:522
  25.0 20.0 %collective-permute-start.8 = (bf16[96,1536]{1,0:T(8,128)(2,1)S(1)}, bf16[96,1536]{1,0:T(8,128)(2,1)S(1)}, u32[]{:S(2)}, u32[]{:S(2)}) collective-permute-start(bf16[96,1536]{1,0:T(8,128)(2,1)S(1)} %get-tuple-element.46), channel_id=1, source_target_pairs={{0,4},{1,5},{2,0},{3,1},{4,6},{5,7},{6,2},{7,3},{8,12},{9,13},{10,... | collective-permute-start | bytes 884744 | tf_op jit(solution)/shard_map/ppermute | solution.py:522
  28.9 22.4 %collective-permute-start.9 = (bf16[96,1536]{1,0:T(8,128)(2,1)S(1)}, bf16[96,1536]{1,0:T(8,128)(2,1)S(1)}, u32[]{:S(2)}, u32[]{:S(2)}) collective-permute-start(bf16[96,1536]{1,0:T(8,128)(2,1)S(1)} %get-tuple-element.47), channel_id=1, source_target_pairs={{0,5},{1,4},{2,1},{3,0},{4,7},{5,6},{6,3},{7,2},{8,13},{9,12},{10,... | collective-permute-start | bytes 884744 | tf_op jit(solution)/shard_map/ppermute | solution.py:522
  32.8 8.6 %copy-start.8 = (bf16[1536,64]{0,1:T(8,128)(2,1)S(1)}, bf16[1536,64]{0,1:T(8,128)(2,1)}, u32[]{:S(2)}) copy-start(bf16[1536,64]{0,1:T(8,128)(2,1)} %param.14) | copy-start | bytes 589828
  32.8 8.6 %copy-start.10 = (f32[256,2]{0,1:T(2,128)S(1)}, f32[256,2]{0,1:T(2,128)}, u32[]{:S(2)}) copy-start(f32[256,2]{0,1:T(2,128)} %param.11) | copy-start | bytes 6148
  39.4 31.4 %copy-start.2 = (bf16[7,64,2048]{2,1,0:T(8,128)(2,1)S(1)}, bf16[7,64,2048]{2,1,0:T(8,128)(2,1)}, u32[]{:S(2)}) copy-start(bf16[7,64,2048]{2,1,0:T(8,128)(2,1)} %param.15) | copy-start | bytes 5505028
  39.4 18.3 %collective-permute-start.5 = (bf16[128,128]{1,0:T(8,128)(2,1)S(1)}, bf16[128,128]{1,0:T(8,128)(2,1)S(1)}, u32[]{:S(2)}, u32[]{:S(2)}) collective-permute-start(bf16[128,128]{1,0:T(8,128)(2,1)S(1)} %get-tuple-element.59), channel_id=1, source_target_pairs={{0,1},{1,0},{2,3},{3,2},{4,5},{5,4},{6,7},{7,6},{8,9},{9,8},{10,11... | collective-permute-start | bytes 98312 | tf_op jit(solution)/shard_map/ppermute | solution.py:506
  39.5 20.6 %collective-permute-start.6 = (bf16[128,128]{1,0:T(8,128)(2,1)S(1)}, bf16[128,128]{1,0:T(8,128)(2,1)S(1)}, u32[]{:S(2)}, u32[]{:S(2)}) collective-permute-start(bf16[128,128]{1,0:T(8,128)(2,1)S(1)} %get-tuple-element.60), channel_id=1, source_target_pairs={{0,2},{1,3},{2,0},{3,1},{4,6},{5,7},{6,4},{7,5},{8,10},{9,11},{10,... | collective-permute-start | bytes 98312 | tf_op jit(solution)/shard_map/ppermute | solution.py:506
  43.5 18.0 %collective-permute-start.7 = (bf16[128,128]{1,0:T(8,128)(2,1)S(1)}, bf16[128,128]{1,0:T(8,128)(2,1)S(1)}, u32[]{:S(2)}, u32[]{:S(2)}) collective-permute-start(bf16[128,128]{1,0:T(8,128)(2,1)S(1)} %get-tuple-element.61), channel_id=1, source_target_pairs={{0,3},{1,2},{2,1},{3,0},{4,7},{5,6},{6,5},{7,4},{8,11},{9,10},{10,... | collective-permute-start | bytes 98312 | tf_op jit(solution)/shard_map/ppermute | solution.py:506
  55.2 6.3 %collective-permute-start.12 = (bf16[128,128]{1,0:T(8,128)(2,1)S(1)}, bf16[128,128]{1,0:T(8,128)(2,1)S(1)}, u32[]{:S(2)}, u32[]{:S(2)}) collective-permute-start(bf16[128,128]{1,0:T(8,128)(2,1)S(1)} %get-tuple-element.64), channel_id=1, source_target_pairs={{0,4},{1,5},{2,6},{3,7},{4,0},{5,1},{6,2},{7,3},{8,12},{9,13},{10,... | collective-permute-start | bytes 98312 | tf_op jit(solution)/shard_map/ppermute | solution.py:506
  56.4 5.2 %collective-permute-start.13 = (bf16[128,128]{1,0:T(8,128)(2,1)S(1)}, bf16[128,128]{1,0:T(8,128)(2,1)S(1)}, u32[]{:S(2)}, u32[]{:S(2)}) collective-permute-start(bf16[128,128]{1,0:T(8,128)(2,1)S(1)} %get-tuple-element.65), channel_id=1, source_target_pairs={{0,5},{1,4},{2,7},{3,6},{4,1},{5,0},{6,3},{7,2},{8,13},{9,12},{10,... | collective-permute-start | bytes 98312 | tf_op jit(solution)/shard_map/ppermute | solution.py:506
  57.7 5.8 %collective-permute-start.14 = (bf16[128,128]{1,0:T(8,128)(2,1)S(1)}, bf16[128,128]{1,0:T(8,128)(2,1)S(1)}, u32[]{:S(2)}, u32[]{:S(2)}) collective-permute-start(bf16[128,128]{1,0:T(8,128)(2,1)S(1)} %get-tuple-element.66), channel_id=1, source_target_pairs={{0,6},{1,7},{2,4},{3,5},{4,2},{5,3},{6,0},{7,1},{8,14},{9,15},{10,... | collective-permute-start | bytes 98312 | tf_op jit(solution)/shard_map/ppermute | solution.py:506
  60.2 5.1 %collective-permute-start.15 = (bf16[128,128]{1,0:T(8,128)(2,1)S(1)}, bf16[128,128]{1,0:T(8,128)(2,1)S(1)}, u32[]{:S(2)}, u32[]{:S(2)}) collective-permute-start(bf16[128,128]{1,0:T(8,128)(2,1)S(1)} %get-tuple-element.67), channel_id=1, source_target_pairs={{0,7},{1,6},{2,5},{3,4},{4,3},{5,2},{6,1},{7,0},{8,15},{9,14},{10,... | collective-permute-start | bytes 98312 | tf_op jit(solution)/shard_map/ppermute | solution.py:506
  66.4 0.7 collective-permute-start.16
  67.1 10.9 %collective-permute-start.19 = (bf16[160,128]{1,0:T(8,128)(2,1)S(1)}, bf16[160,128]{1,0:T(8,128)(2,1)S(1)}, u32[]{:S(2)}, u32[]{:S(2)}) collective-permute-start(bf16[160,128]{1,0:T(8,128)(2,1)S(1)} %constant_dynamic-update-slice_fusion.slab_ref), channel_id=1, source_target_pairs={{0,24},{8,16},{16,8},{24,0},{1,25},{9,17},{17,9},{25,1},{2,26},{10... | collective-permute-start | bytes 122888 | tf_op jit(solution)/shard_map/ppermute | solution.py:546
  69.6 8.4 %collective-permute-start.18 = (bf16[160,128]{1,0:T(8,128)(2,1)S(1)}, bf16[160,128]{1,0:T(8,128)(2,1)S(1)}, u32[]{:S(2)}, u32[]{:S(2)}) collective-permute-start(bf16[160,128]{1,0:T(8,128)(2,1)S(1)} %constant_dynamic-update-slice_fusion.slab_ref), channel_id=1, source_target_pairs={{0,16},{8,24},{16,0},{24,8},{1,17},{9,25},{17,1},{25,9},{2,18},{10... | collective-permute-start | bytes 122888 | tf_op jit(solution)/shard_map/ppermute | solution.py:546
  70.1 7.9 %collective-permute-start.17 = (bf16[160,128]{1,0:T(8,128)(2,1)S(1)}, bf16[160,128]{1,0:T(8,128)(2,1)S(1)}, u32[]{:S(2)}, u32[]{:S(2)}) collective-permute-start(bf16[160,128]{1,0:T(8,128)(2,1)S(1)} %constant_dynamic-update-slice_fusion.slab_ref), channel_id=1, source_target_pairs={{0,8},{8,0},{16,24},{24,16},{1,9},{9,1},{17,25},{25,17},{2,10},{10... | collective-permute-start | bytes 122888 | tf_op jit(solution)/shard_map/ppermute | solution.py:546
  (8 other events, 27.4 us)

commit v12 on v8

--- a/solution.py
+++ b/solution.py
@@ -410,13 +410,20 @@
 def decoder_kernel(segs, place_ref, own_ref, *refs):
     slab_refs = refs[: segs - 1]
     conv_ref, alpha_ref, up_hbm, out_ref = refs[segs - 1 : segs + 3]
-    padded, windows, others, up_ref, rows_out, sems, up_sem = refs[segs + 3 :]
+    padded, windows, others, up_ref, rows_out, sems, up_sems = refs[segs + 3 :]
     span = own_ref.shape[0]
     length = span - 4 * EDGE
     width = up_ref.shape[2]
     own = place_ref[0]
-    up_copy = pltpu.make_async_copy(up_hbm, up_ref, up_sem)
-    up_copy.start()
+    pairs = [first for r in range(0, 8, 2) for first in (r + 4, r + 12 if r < 4 else r - 4)]
+    up_copies = [
+        pltpu.make_async_copy(
+            up_hbm.at[pl.ds(first, 2)], up_ref.at[pl.ds(first, 2)], up_sems.at[j]
+        )
+        for j, first in enumerate(pairs)
+    ]
+    for copy in up_copies:
+        copy.start()
 
     def out_copy(k):
         return pltpu.make_async_copy(rows_out.at[k], out_ref.at[own ^ k], sems.at[k])
@@ -425,11 +432,13 @@
         unpack_slab(place_ref, slab_refs[k], padded.at[k])
     for k in range(segs - 1):
         convolve(place_ref, padded.at[k], windows.at[k], conv_ref, alpha_ref, others.at[k])
-    up_copy.wait()
     for k in range(segs):
         act = own_ref if k == 0 else others.at[k - 1]
         for r in range(0, 8, 2):
             far = r + 12 if r < 4 else r - 4
+            if k == 0:
+                up_copies[r].wait()
+                up_copies[r + 1].wait()
             near_w = jnp.concatenate([up_ref[r + 4], up_ref[r + 5]], axis=1)
             far_w = jnp.concatenate([up_ref[far], up_ref[far + 1]], axis=1)
             near = jnp.dot(act[0:length], near_w, preferred_element_type=F32)
@@ -466,7 +475,7 @@
             pltpu.VMEM(first_up.shape, BF16),
             pltpu.VMEM((segs, 8 * length, width), F32),
             pltpu.SemaphoreType.DMA((segs,)),
-            pltpu.SemaphoreType.DMA,
+            pltpu.SemaphoreType.DMA((8,)),
         ],
         compiler_params=params(52),
         cost_estimate=FREE,

time: 91.6 us -> 92.3 us (level)
  no operation moved by 1% of the time
where the time goes in v12:
time: 92.3 us; the launch traced here: 91.8 us
  Pallas kernels  36.7 us (40%)
  starting transfers between devices  31 us (34%)
  waiting for transfers between devices  16.6 us (18%)
  local copies, waits for them, and re-layouts  6.85 us (7%)
    pallas_call x1, Pallas kernels, decode(): pl.pallas_call(functools.partial(decoder_kernel, segs), out_shape=jax.Sha...  17.5 us
    ppermute x12, starting transfers between devices, swap(): return lax.ppermute(value, 'expert', [(i, i ^ k) for i in members])  17.5 us
    ppermute x4, starting transfers between devices, cross(): return lax.ppermute(value, 'expert', [(i, j) for i, j in pairs if i != j])  9.35 us
    pallas_call x2, Pallas kernels, run_group(): pl.pallas_call(functools.partial(group_kernel, n, far), out_shape=[jax.Sh...  7.95 us
    ppermute x12, waiting for transfers between devices, swap(): return lax.ppermute(value, 'expert', [(i, i ^ k) for i in members])  7.88 us
    ppermute x4, waiting for transfers between devices, cross(): return lax.ppermute(value, 'expert', [(i, j) for i, j in pairs if i != j])  7.7 us
    unnamed x23, local copies, waits for them, and re-layouts  6.84 us
    ppermute x3, starting transfers between devices, local(): lax.ppermute(slab, 'seg', [(i, i ^ k) for i in range(segs)])  3.55 us
  transfers between devices with their start and end apart: 20, of which 7 were waited for; matrix products, arithmetic and copies ran while one was open for 0% of the time, Pallas kernels for 20%

profile of v12, /device:TPU:0, one launch (start us, length us, event | category | flops | bytes accessed | tf_op | source)
XLA Modules:
  0.0 91.8 jit_solution(3163362281377320207)
XLA Ops:
  2.6 1.5 %shard_map.91 = (bf16[96,1536]{1,0:T(8,128)(2,1)S(1)}, bf16[112,1536]{1,0:T(8,128)(2,1)S(1)}, bf16[96,1536]{1,0:T(8,128)(2,1)S(1)}, bf16[112,1536]{1,0:T(8,128)(2,1)S(1)}) custom-call(s32[2]{0:T(128)S(1)} %get-tuple-element.74.origin_ref, s32[2,256]{1,0:T(2,128)} %bitcast.3.refs_0_.ids_ref, bf16[256,1536]{1,0:T(8,128)(2,1)S(1)} %copy-done.2, ...), custom_call_target="tpu_custom_call" | custom-call | tf_op jit(solution)/shard_map/pallas_call | solution.py:99
  4.6 5.5 %collective-permute-start.4 = (bf16[112,1536]{1,0:T(8,128)(2,1)S(1)}, bf16[112,1536]{1,0:T(8,128)(2,1)S(1)}, u32[]{:S(2)}, u32[]{:S(2)}) collective-permute-start(bf16[112,1536]{1,0:T(8,128)(2,1)S(1)} %get-tuple-element.43), channel_id=1, source_target_pairs={{0,3},{1,2},{2,1},{3,0},{4,7},{5,6},{6,5},{7,4},{8,11},{9,10},{10,... | collective-permute-start | bytes 1032200 | tf_op jit(solution)/shard_map/ppermute | solution.py:508
  10.7 1.7 %collective-permute-start.3 = (bf16[96,1536]{1,0:T(8,128)(2,1)S(1)}, bf16[96,1536]{1,0:T(8,128)(2,1)S(1)}, u32[]{:S(2)}, u32[]{:S(2)}) collective-permute-start(bf16[96,1536]{1,0:T(8,128)(2,1)S(1)} %get-tuple-element.42), channel_id=1, source_target_pairs={{0,2},{1,3},{2,0},{3,1},{4,6},{5,7},{6,4},{7,5},{8,10},{9,11},{10,... | collective-permute-start | bytes 884744 | tf_op jit(solution)/shard_map/ppermute | solution.py:508
  13.8 1.8 %shard_map.92 = (bf16[96,1536]{1,0:T(8,128)(2,1)S(1)}, bf16[96,1536]{1,0:T(8,128)(2,1)S(1)}, bf16[96,1536]{1,0:T(8,128)(2,1)S(1)}, bf16[96,1536]{1,0:T(8,128)(2,1)S(1)}) custom-call(s32[2]{0:T(128)S(1)} %pad_add_fusion.3.origin_ref, s32[2,256]{1,0:T(2,128)} %bitcast.3.refs_0_.ids_ref, bf16[256,1536]{1,0:T(8,128)(2,1)S(1)} %copy-done.3, ...), custom_call_target="tpu_custom_call" | custom-call | tf_op jit(solution)/shard_map/pallas_call | solution.py:99
  15.6 2.0 %collective-permute-start.11 = (bf16[96,1536]{1,0:T(8,128)(2,1)S(1)}, bf16[96,1536]{1,0:T(8,128)(2,1)S(1)}, u32[]{:S(2)}, u32[]{:S(2)}) collective-permute-start(bf16[96,1536]{1,0:T(8,128)(2,1)S(1)} %get-tuple-element.61), channel_id=1, source_target_pairs={{0,7},{1,6},{2,3},{3,2},{4,5},{5,4},{6,1},{7,0},{8,15},{9,14},{10,... | collective-permute-start | bytes 884744 | tf_op jit(solution)/shard_map/ppermute | solution.py:524
  17.6 3.2 %collective-permute-start.10 = (bf16[96,1536]{1,0:T(8,128)(2,1)S(1)}, bf16[96,1536]{1,0:T(8,128)(2,1)S(1)}, u32[]{:S(2)}, u32[]{:S(2)}) collective-permute-start(bf16[96,1536]{1,0:T(8,128)(2,1)S(1)} %get-tuple-element.60.local_ref), channel_id=1, source_target_pairs={{0,6},{1,7},{6,0},{7,1},{8,14},{9,15},{14,8},{15,9},{16,22},{17,23... | collective-permute-start | bytes 884744 | tf_op jit(solution)/shard_map/ppermute | solution.py:524
  20.9 4.1 %collective-permute-done.3.refs_1_ = bf16[96,1536]{1,0:T(8,128)(2,1)S(1)} collective-permute-done((bf16[96,1536]{1,0:T(8,128)(2,1)S(1)}, bf16[96,1536]{1,0:T(8,128)(2,1)S(1)}, u32[]{:S(2)}, u32[]{:S(2)}) %collective-permute-start.3) | collective-permute-done | bytes 294944 | tf_op jit(solution)/shard_map/ppermute | solution.py:508
  25.0 3.9 %collective-permute-start.8 = (bf16[96,1536]{1,0:T(8,128)(2,1)S(1)}, bf16[96,1536]{1,0:T(8,128)(2,1)S(1)}, u32[]{:S(2)}, u32[]{:S(2)}) collective-permute-start(bf16[96,1536]{1,0:T(8,128)(2,1)S(1)} %get-tuple-element.44), channel_id=1, source_target_pairs={{0,4},{1,5},{2,0},{3,1},{4,6},{5,7},{6,2},{7,3},{8,12},{9,13},{10,... | collective-permute-start | bytes 884744 | tf_op jit(solution)/shard_map/ppermute | solution.py:524
  29.1 2.8 %copy-done.5 = bf16[1,2048,1536]{2,1,0:T(8,128)(2,1)S(1)} copy-done((bf16[1,2048,1536]{2,1,0:T(8,128)(2,1)S(1)}, bf16[1,2048,1536]{2,1,0:T(8,128)(2,1)}, u32[]{:S(2)}) %copy-start.5) | copy-done | bytes 6291480
  32.8 2.5 %shard_map.94.refs_4_.refs_5_ = bf16[2048,128]{1,0:T(8,128)(2,1)S(1)} custom-call(bf16[2048,1536]{1,0:T(8,128)(2,1)S(1)} %bitcast.16, bf16[64,1536]{1,0:T(8,128)(2,1)S(1)} %bitcast.17), custom_call_target="tpu_custom_call" | custom-call | tf_op jit(solution)/shard_map/pallas_call | solution.py:127
  35.4 4.0 %shard_map.95 = (bf16[128,128]{1,0:T(8,128)(2,1)S(1)}, bf16[128,128]{1,0:T(8,128)(2,1)S(1)}, bf16[128,128]{1,0:T(8,128)(2,1)S(1)}, bf16[128,128]{1,0:T(8,128)(2,1)S(1)}) custom-call(s32[2]{0:T(128)S(1)} %get-tuple-element.52.place_ref, bf16[96,1536]{1,0:T(8,128)(2,1)S(1)} %get-tuple-element.53.local_ref, ...), custom_call_target="tpu_custom_call" | custom-call | tf_op jit(solution)/shard_map/pallas_call | solution.py:293
  39.5 1.9 %collective-permute-start.6 = (bf16[128,128]{1,0:T(8,128)(2,1)S(1)}, bf16[128,128]{1,0:T(8,128)(2,1)S(1)}, u32[]{:S(2)}, u32[]{:S(2)}) collective-permute-start(bf16[128,128]{1,0:T(8,128)(2,1)S(1)} %get-tuple-element.58), channel_id=1, source_target_pairs={{0,2},{1,3},{2,0},{3,1},{4,6},{5,7},{6,4},{7,5},{8,10},{9,11},{10,... | collective-permute-start | bytes 98312 | tf_op jit(solution)/shard_map/ppermute | solution.py:508
  41.5 2.0 %shard_map.93 = (bf16[8,272,128]{2,1,0:T(8,128)(2,1)S(1)}, f32[272,128]{1,0:T(8,128)S(1)}, f32[272,64]{1,0:T(8,128)S(1)}) custom-call(s32[2]{0:T(128)S(1)} %get-tuple-element.52.place_ref, bf16[256,1536]{1,0:T(8,128)(2,1)S(1)} %copy-done.4, bf16[64,1536]{1,0:T(8,128)(2,1)S(1)} %bitcast.18, s32[2,256]{1,0:T(2,128)} %bitcast.3.refs_0_.ids_ref, ...), custom_call_target="tpu_custom_call" | custom-call | tf_op jit(solution)/shard_map/pallas_call | solution.py:225
  43.6 1.4 %collective-permute-done.8.refs_0_ = bf16[96,1536]{1,0:T(8,128)(2,1)S(1)} collective-permute-done((bf16[96,1536]{1,0:T(8,128)(2,1)S(1)}, bf16[96,1536]{1,0:T(8,128)(2,1)S(1)}, u32[]{:S(2)}, u32[]{:S(2)}) %collective-permute-start.8) | collective-permute-done | bytes 294944 | tf_op jit(solution)/shard_map/ppermute | solution.py:524
  45.0 6.3 %collective-permute-done.9.refs_1_ = bf16[96,1536]{1,0:T(8,128)(2,1)S(1)} collective-permute-done((bf16[96,1536]{1,0:T(8,128)(2,1)S(1)}, bf16[96,1536]{1,0:T(8,128)(2,1)S(1)}, u32[]{:S(2)}, u32[]{:S(2)}) %collective-permute-start.9) | collective-permute-done | bytes 294944 | tf_op jit(solution)/shard_map/ppermute | solution.py:524
  51.3 3.9 %shard_map.96 = (bf16[128,128]{1,0:T(8,128)(2,1)S(1)}, bf16[128,128]{1,0:T(8,128)(2,1)S(1)}, bf16[128,128]{1,0:T(8,128)(2,1)S(1)}, bf16[128,128]{1,0:T(8,128)(2,1)S(1)}) custom-call(s32[2]{0:T(128)S(1)} %get-tuple-element.52.place_ref, bf16[96,1536]{1,0:T(8,128)(2,1)S(1)} %get-tuple-element.60.local_ref, ...), custom_call_target="tpu_custom_call" | custom-call | tf_op jit(solution)/shard_map/pallas_call | solution.py:293
  56.4 1.3 %collective-permute-start.13 = (bf16[128,128]{1,0:T(8,128)(2,1)S(1)}, bf16[128,128]{1,0:T(8,128)(2,1)S(1)}, u32[]{:S(2)}, u32[]{:S(2)}) collective-permute-start(bf16[128,128]{1,0:T(8,128)(2,1)S(1)} %get-tuple-element.63), channel_id=1, source_target_pairs={{0,5},{1,4},{2,7},{3,6},{4,1},{5,0},{6,3},{7,2},{8,13},{9,12},{10,... | collective-permute-start | bytes 98312 | tf_op jit(solution)/shard_map/ppermute | solution.py:508
  57.7 2.5 %collective-permute-start.14 = (bf16[128,128]{1,0:T(8,128)(2,1)S(1)}, bf16[128,128]{1,0:T(8,128)(2,1)S(1)}, u32[]{:S(2)}, u32[]{:S(2)}) collective-permute-start(bf16[128,128]{1,0:T(8,128)(2,1)S(1)} %get-tuple-element.64), channel_id=1, source_target_pairs={{0,6},{1,7},{2,4},{3,5},{4,2},{5,3},{6,0},{7,1},{8,14},{9,15},{10,... | collective-permute-start | bytes 98312 | tf_op jit(solution)/shard_map/ppermute | solution.py:508
  60.2 1.3 %collective-permute-start.15 = (bf16[128,128]{1,0:T(8,128)(2,1)S(1)}, bf16[128,128]{1,0:T(8,128)(2,1)S(1)}, u32[]{:S(2)}, u32[]{:S(2)}) collective-permute-start(bf16[128,128]{1,0:T(8,128)(2,1)S(1)} %get-tuple-element.65), channel_id=1, source_target_pairs={{0,7},{1,6},{2,5},{3,4},{4,3},{5,2},{6,1},{7,0},{8,15},{9,14},{10,... | collective-permute-start | bytes 98312 | tf_op jit(solution)/shard_map/ppermute | solution.py:508
  61.6 1.9 %collective-permute-done.14.refs_6_ = bf16[128,128]{1,0:T(8,128)(2,1)S(1)} collective-permute-done((bf16[128,128]{1,0:T(8,128)(2,1)S(1)}, bf16[128,128]{1,0:T(8,128)(2,1)S(1)}, u32[]{:S(2)}, u32[]{:S(2)}) %collective-permute-start.14) | collective-permute-done | bytes 32800 | tf_op jit(solution)/shard_map/ppermute | solution.py:508
  63.5 1.8 %collective-permute-done.15.refs_7_ = bf16[128,128]{1,0:T(8,128)(2,1)S(1)} collective-permute-done((bf16[128,128]{1,0:T(8,128)(2,1)S(1)}, bf16[128,128]{1,0:T(8,128)(2,1)S(1)}, u32[]{:S(2)}, u32[]{:S(2)}) %collective-permute-start.15) | collective-permute-done | bytes 32800 | tf_op jit(solution)/shard_map/ppermute | solution.py:508
  67.1 2.5 %collective-permute-start.19 = (bf16[160,128]{1,0:T(8,128)(2,1)S(1)}, bf16[160,128]{1,0:T(8,128)(2,1)S(1)}, u32[]{:S(2)}, u32[]{:S(2)}) collective-permute-start(bf16[160,128]{1,0:T(8,128)(2,1)S(1)} %constant_dynamic-update-slice_fusion.slab_ref), channel_id=1, source_target_pairs={{0,24},{8,16},{16,8},{24,0},{1,25},{9,17},{17,9},{25,1},{2,26},{10... | collective-permute-start | bytes 122888 | tf_op jit(solution)/shard_map/ppermute | solution.py:548
  70.8 2.4 %shard_map.98.own_ref = bf16[272,2048]{1,0:T(8,128)(2,1)S(1)} custom-call(s32[3]{0:T(128)S(1)} %pad_add_fusion.place_ref, bf16[160,128]{1,0:T(8,128)(2,1)S(1)} %constant_dynamic-update-slice_fusion.slab_ref, bf16[448,2048]{1,0:T(8,128)(2,1)S(1)} %bitcast.15, f32[2,2048]{1,0:T(2,128)S(1)} %pad_maximum_fusion.alpha_ref.refs_4_), custom_call_target="tpu_custom_call" | custom-call | tf_op jit(solution)/shard_map/pallas_call | solution.py:399
  74.1 17.5 %shard_map.99 = f32[4,2048,128]{2,1,0:T(8,128)} custom-call(s32[3]{0:T(128)S(1)} %pad_add_fusion.place_ref, bf16[272,2048]{1,0:T(8,128)(2,1)S(1)} %shard_map.98.own_ref, bf16[160,128]{1,0:T(8,128)(2,1)S(1)} %collective-permute-done.17.refs_0_, bf16[160,128]{1,0:T(8,128)(2,1)S(1)} %collective-permute-done.18.refs_1_, ...), custom_call_target="tpu_custom_call" | custom-call | tf_op jit(solution)/shard_map/pallas_call | solution.py:464
  (54 shorter events, 11.6 us)
Async XLA Ops:
  0.0 12.6 %collective-permute-start.1 = (bf16[256,1536]{1,0:T(8,128)(2,1)}, bf16[256,1536]{1,0:T(8,128)(2,1)S(1)}, u32[]{:S(2)}, u32[]{:S(2)}) collective-permute-start(bf16[256,1536]{1,0:T(8,128)(2,1)} %frames_ref.1), channel_id=1, source_target_pairs={{2,4},{3,5},{4,2},{5,3},{10,12},{11,13},{12,10},{13,11},{18,20},{1... | collective-permute-start | bytes 2359304 | tf_op jit(solution)/shard_map/ppermute | solution.py:508
  4.1 20.9 %collective-permute-start.2 = (bf16[112,1536]{1,0:T(8,128)(2,1)S(1)}, bf16[112,1536]{1,0:T(8,128)(2,1)S(1)}, u32[]{:S(2)}, u32[]{:S(2)}) collective-permute-start(bf16[112,1536]{1,0:T(8,128)(2,1)S(1)} %get-tuple-element.41), channel_id=1, source_target_pairs={{0,1},{1,0},{2,3},{3,2},{4,5},{5,4},{6,7},{7,6},{8,9},{9,8},{10,11... | collective-permute-start | bytes 1032200 | tf_op jit(solution)/shard_map/ppermute | solution.py:508
  4.6 20.4 %collective-permute-start.4 = (bf16[112,1536]{1,0:T(8,128)(2,1)S(1)}, bf16[112,1536]{1,0:T(8,128)(2,1)S(1)}, u32[]{:S(2)}, u32[]{:S(2)}) collective-permute-start(bf16[112,1536]{1,0:T(8,128)(2,1)S(1)} %get-tuple-element.43), channel_id=1, source_target_pairs={{0,3},{1,2},{2,1},{3,0},{4,7},{5,6},{6,5},{7,4},{8,11},{9,10},{10,... | collective-permute-start | bytes 1032200 | tf_op jit(solution)/shard_map/ppermute | solution.py:508
  10.1 2.5 %collective-permute-start = (s32[2,256]{1,0:T(2,128)}, s32[2,256]{1,0:T(2,128)S(1)}, u32[]{:S(2)}, u32[]{:S(2)}) collective-permute-start(s32[2,256]{1,0:T(2,128)} %bitcast.3.refs_0_.ids_ref), channel_id=1, source_target_pairs={{2,4},{3,5},{4,2},{5,3},{10,12},{11,13},{12,10},{13,11},{18,20},{1... | collective-permute-start | bytes 6152 | tf_op jit(solution)/shard_map/ppermute | solution.py:508
  10.7 14.3 %collective-permute-start.3 = (bf16[96,1536]{1,0:T(8,128)(2,1)S(1)}, bf16[96,1536]{1,0:T(8,128)(2,1)S(1)}, u32[]{:S(2)}, u32[]{:S(2)}) collective-permute-start(bf16[96,1536]{1,0:T(8,128)(2,1)S(1)} %get-tuple-element.42), channel_id=1, source_target_pairs={{0,2},{1,3},{2,0},{3,1},{4,6},{5,7},{6,4},{7,5},{8,10},{9,11},{10,... | collective-permute-start | bytes 884744 | tf_op jit(solution)/shard_map/ppermute | solution.py:508
  12.5 22.9 %copy-start = (bf16[1,1536,2048]{2,1,0:T(8,128)(2,1)S(1)}, bf16[1,1536,2048]{2,1,0:T(8,128)(2,1)}, u32[]{:S(2)}) copy-start(bf16[1,1536,2048]{2,1,0:T(8,128)(2,1)} %param.12) | copy-start | bytes 18874372
  15.6 23.9 %collective-permute-start.11 = (bf16[96,1536]{1,0:T(8,128)(2,1)S(1)}, bf16[96,1536]{1,0:T(8,128)(2,1)S(1)}, u32[]{:S(2)}, u32[]{:S(2)}) collective-permute-start(bf16[96,1536]{1,0:T(8,128)(2,1)S(1)} %get-tuple-element.61), channel_id=1, source_target_pairs={{0,7},{1,6},{2,3},{3,2},{4,5},{5,4},{6,1},{7,0},{8,15},{9,14},{10,... | collective-permute-start | bytes 884744 | tf_op jit(solution)/shard_map/ppermute | solution.py:524
  17.6 25.9 %collective-permute-start.10 = (bf16[96,1536]{1,0:T(8,128)(2,1)S(1)}, bf16[96,1536]{1,0:T(8,128)(2,1)S(1)}, u32[]{:S(2)}, u32[]{:S(2)}) collective-permute-start(bf16[96,1536]{1,0:T(8,128)(2,1)S(1)} %get-tuple-element.60.local_ref), channel_id=1, source_target_pairs={{0,6},{1,7},{6,0},{7,1},{8,14},{9,15},{14,8},{15,9},{16,22},{17,23... | collective-permute-start | bytes 884744 | tf_op jit(solution)/shard_map/ppermute | solution.py:524
  25.0 20.0 %collective-permute-start.8 = (bf16[96,1536]{1,0:T(8,128)(2,1)S(1)}, bf16[96,1536]{1,0:T(8,128)(2,1)S(1)}, u32[]{:S(2)}, u32[]{:S(2)}) collective-permute-start(bf16[96,1536]{1,0:T(8,128)(2,1)S(1)} %get-tuple-element.44), channel_id=1, source_target_pairs={{0,4},{1,5},{2,0},{3,1},{4,6},{5,7},{6,2},{7,3},{8,12},{9,13},{10,... | collective-permute-start | bytes 884744 | tf_op jit(solution)/shard_map/ppermute | solution.py:524
  28.9 22.4 %collective-permute-start.9 = (bf16[96,1536]{1,0:T(8,128)(2,1)S(1)}, bf16[96,1536]{1,0:T(8,128)(2,1)S(1)}, u32[]{:S(2)}, u32[]{:S(2)}) collective-permute-start(bf16[96,1536]{1,0:T(8,128)(2,1)S(1)} %get-tuple-element.45), channel_id=1, source_target_pairs={{0,5},{1,4},{2,1},{3,0},{4,7},{5,6},{6,3},{7,2},{8,13},{9,12},{10,... | collective-permute-start | bytes 884744 | tf_op jit(solution)/shard_map/ppermute | solution.py:524
  32.8 8.6 %copy-start.7 = (bf16[1536,64]{0,1:T(8,128)(2,1)S(1)}, bf16[1536,64]{0,1:T(8,128)(2,1)}, u32[]{:S(2)}) copy-start(bf16[1536,64]{0,1:T(8,128)(2,1)} %param.14) | copy-start | bytes 589828
  32.8 8.6 %copy-start.9 = (f32[256,2]{0,1:T(2,128)S(1)}, f32[256,2]{0,1:T(2,128)}, u32[]{:S(2)}) copy-start(f32[256,2]{0,1:T(2,128)} %param.11) | copy-start | bytes 6148
  39.4 31.4 %copy-start.1 = (bf16[7,64,2048]{2,1,0:T(8,128)(2,1)S(1)}, bf16[7,64,2048]{2,1,0:T(8,128)(2,1)}, u32[]{:S(2)}) copy-start(bf16[7,64,2048]{2,1,0:T(8,128)(2,1)} %param.15) | copy-start | bytes 5505028
  39.4 18.3 %collective-permute-start.5 = (bf16[128,128]{1,0:T(8,128)(2,1)S(1)}, bf16[128,128]{1,0:T(8,128)(2,1)S(1)}, u32[]{:S(2)}, u32[]{:S(2)}) collective-permute-start(bf16[128,128]{1,0:T(8,128)(2,1)S(1)} %get-tuple-element.57), channel_id=1, source_target_pairs={{0,1},{1,0},{2,3},{3,2},{4,5},{5,4},{6,7},{7,6},{8,9},{9,8},{10,11... | collective-permute-start | bytes 98312 | tf_op jit(solution)/shard_map/ppermute | solution.py:508
  39.5 20.6 %collective-permute-start.6 = (bf16[128,128]{1,0:T(8,128)(2,1)S(1)}, bf16[128,128]{1,0:T(8,128)(2,1)S(1)}, u32[]{:S(2)}, u32[]{:S(2)}) collective-permute-start(bf16[128,128]{1,0:T(8,128)(2,1)S(1)} %get-tuple-element.58), channel_id=1, source_target_pairs={{0,2},{1,3},{2,0},{3,1},{4,6},{5,7},{6,4},{7,5},{8,10},{9,11},{10,... | collective-permute-start | bytes 98312 | tf_op jit(solution)/shard_map/ppermute | solution.py:508
  43.5 18.0 %collective-permute-start.7 = (bf16[128,128]{1,0:T(8,128)(2,1)S(1)}, bf16[128,128]{1,0:T(8,128)(2,1)S(1)}, u32[]{:S(2)}, u32[]{:S(2)}) collective-permute-start(bf16[128,128]{1,0:T(8,128)(2,1)S(1)} %get-tuple-element.59), channel_id=1, source_target_pairs={{0,3},{1,2},{2,1},{3,0},{4,7},{5,6},{6,5},{7,4},{8,11},{9,10},{10,... | collective-permute-start | bytes 98312 | tf_op jit(solution)/shard_map/ppermute | solution.py:508
  55.2 6.3 %collective-permute-start.12 = (bf16[128,128]{1,0:T(8,128)(2,1)S(1)}, bf16[128,128]{1,0:T(8,128)(2,1)S(1)}, u32[]{:S(2)}, u32[]{:S(2)}) collective-permute-start(bf16[128,128]{1,0:T(8,128)(2,1)S(1)} %get-tuple-element.62), channel_id=1, source_target_pairs={{0,4},{1,5},{2,6},{3,7},{4,0},{5,1},{6,2},{7,3},{8,12},{9,13},{10,... | collective-permute-start | bytes 98312 | tf_op jit(solution)/shard_map/ppermute | solution.py:508
  56.4 5.2 %collective-permute-start.13 = (bf16[128,128]{1,0:T(8,128)(2,1)S(1)}, bf16[128,128]{1,0:T(8,128)(2,1)S(1)}, u32[]{:S(2)}, u32[]{:S(2)}) collective-permute-start(bf16[128,128]{1,0:T(8,128)(2,1)S(1)} %get-tuple-element.63), channel_id=1, source_target_pairs={{0,5},{1,4},{2,7},{3,6},{4,1},{5,0},{6,3},{7,2},{8,13},{9,12},{10,... | collective-permute-start | bytes 98312 | tf_op jit(solution)/shard_map/ppermute | solution.py:508
  57.7 5.8 %collective-permute-start.14 = (bf16[128,128]{1,0:T(8,128)(2,1)S(1)}, bf16[128,128]{1,0:T(8,128)(2,1)S(1)}, u32[]{:S(2)}, u32[]{:S(2)}) collective-permute-start(bf16[128,128]{1,0:T(8,128)(2,1)S(1)} %get-tuple-element.64), channel_id=1, source_target_pairs={{0,6},{1,7},{2,4},{3,5},{4,2},{5,3},{6,0},{7,1},{8,14},{9,15},{10,... | collective-permute-start | bytes 98312 | tf_op jit(solution)/shard_map/ppermute | solution.py:508
  60.2 5.1 %collective-permute-start.15 = (bf16[128,128]{1,0:T(8,128)(2,1)S(1)}, bf16[128,128]{1,0:T(8,128)(2,1)S(1)}, u32[]{:S(2)}, u32[]{:S(2)}) collective-permute-start(bf16[128,128]{1,0:T(8,128)(2,1)S(1)} %get-tuple-element.65), channel_id=1, source_target_pairs={{0,7},{1,6},{2,5},{3,4},{4,3},{5,2},{6,1},{7,0},{8,15},{9,14},{10,... | collective-permute-start | bytes 98312 | tf_op jit(solution)/shard_map/ppermute | solution.py:508
  66.4 0.7 collective-permute-start.16
  67.1 6.0 %collective-permute-start.19 = (bf16[160,128]{1,0:T(8,128)(2,1)S(1)}, bf16[160,128]{1,0:T(8,128)(2,1)S(1)}, u32[]{:S(2)}, u32[]{:S(2)}) collective-permute-start(bf16[160,128]{1,0:T(8,128)(2,1)S(1)} %constant_dynamic-update-slice_fusion.slab_ref), channel_id=1, source_target_pairs={{0,24},{8,16},{16,8},{24,0},{1,25},{9,17},{17,9},{25,1},{2,26},{10... | collective-permute-start | bytes 122888 | tf_op jit(solution)/shard_map/ppermute | solution.py:548
  69.6 4.0 %collective-permute-start.18 = (bf16[160,128]{1,0:T(8,128)(2,1)S(1)}, bf16[160,128]{1,0:T(8,128)(2,1)S(1)}, u32[]{:S(2)}, u32[]{:S(2)}) collective-permute-start(bf16[160,128]{1,0:T(8,128)(2,1)S(1)} %constant_dynamic-update-slice_fusion.slab_ref), channel_id=1, source_target_pairs={{0,16},{8,24},{16,0},{24,8},{1,17},{9,25},{17,1},{25,9},{2,18},{10... | collective-permute-start | bytes 122888 | tf_op jit(solution)/shard_map/ppermute | solution.py:548
  70.1 4.0 %collective-permute-start.17 = (bf16[160,128]{1,0:T(8,128)(2,1)S(1)}, bf16[160,128]{1,0:T(8,128)(2,1)S(1)}, u32[]{:S(2)}, u32[]{:S(2)}) collective-permute-start(bf16[160,128]{1,0:T(8,128)(2,1)S(1)} %constant_dynamic-update-slice_fusion.slab_ref), channel_id=1, source_target_pairs={{0,8},{8,0},{16,24},{24,16},{1,9},{9,1},{17,25},{25,17},{2,10},{10... | collective-permute-start | bytes 122888 | tf_op jit(solution)/shard_map/ppermute | solution.py:548
  (7 other events, 24.1 us)
